TPU v7x, 32 devices: a whole 2x2x4 slice. The times are simulated.
32 devices in a mesh: grp: 2 (over y), comp: 16 (over z, x, core).
Axes of the slice: x: 2, y: 2, z: 4, core: 2. Of those that a mesh axis runs over, the one named last changes fastest.
Arguments:
- features: bfloat16 [65536, 256], P(('grp', 'comp')), may hold values from -8 to 8
- means: float32 [1024, 256], P('comp'), may hold values from -1 to 1
- variances: float32 [1024, 256], P('comp'), may hold values from 0.5 to 2
- weight_logits: float32 [1024], replicated, may hold values from -1 to 1
Outputs:
- new_means: float32 [1024, 256], replicated
- new_variances: float32 [1024, 256], replicated
- new_log_weights: float32 [1024], replicated
- row_scores: float32 [65536], P(('grp', 'comp'))
All inputs are finite; a program needn't handle non-finite values.
Results may differ from a plain program's by a relative error of at most 0.00085.
Values sent between devices are 32-bit elements; how exact they have to be, the bound alone decides.
No kernel may reach another device: no remote copies, remote signals or barrier semaphores. Data moves between devices by JAX's collectives and lax.ppermute only.
A program may use at most 64 MiB of HBM per device.

v0:
```python
import math

import jax
import jax.numpy as jnp
from jax import lax
from jax.sharding import PartitionSpec as P


def update_step(moments, counts, total_rows):
    width = moments.shape[1] // 2
    denominator = (counts + 1.0)[:, None]
    fresh_means = moments[:, :width] / denominator
    fresh_variances = (moments[:, width:] + 1.0) / denominator - fresh_means * fresh_means + 0.01
    fresh_weights = jnp.log((counts + 1.0) / total_rows)
    return (fresh_means, fresh_variances, fresh_weights)


def on_device(features, means, variances, weight_logits):
    owned_count = means.shape[0]
    width = means.shape[1]
    first_owned = lax.axis_index("comp") * owned_count
    log_weights = lax.dynamic_slice_in_dim(
        jax.nn.log_softmax(weight_logits), first_owned, owned_count
    )
    inverse = 1.0 / variances
    coefficient = jnp.concatenate([-0.5 * inverse, means * inverse], axis=1)
    offsets = (
        log_weights
        - 0.5 * jnp.sum(jnp.log(variances) + means * means * inverse, axis=1)
        - 0.5 * width * math.log(2.0 * math.pi)
    )
    all_coefficient, all_offsets = (
        lax.all_gather(coefficient, "comp", axis=0, tiled=True),
        lax.all_gather(offsets, "comp", axis=0, tiled=True),
    )
    total_comps = all_coefficient.shape[0]
    local_rows = features.shape[0]
    block_size = min(512, local_rows)
    moments = jnp.zeros((total_comps, 2 * width), jnp.float32)
    counts = jnp.zeros((total_comps,), jnp.float32)
    score_pieces = []
    ones_row = jnp.ones((block_size,), jnp.bfloat16)
    for block_index in range(local_rows // block_size):
        block_rows = features[block_index * block_size : (block_index + 1) * block_size]
        values = block_rows.astype(jnp.float32)
        squared = values * values
        scores = (
            jnp.dot(
                jnp.concatenate([squared, values], axis=1),
                all_coefficient.T,
                precision=lax.Precision.HIGHEST,
            )
            + all_offsets
        )
        highest = jnp.max(scores, axis=1, keepdims=True)
        exponent = jnp.exp(scores - highest)
        totals = jnp.sum(exponent, axis=1, keepdims=True)
        responsibility = (exponent / totals).astype(jnp.bfloat16)
        score_pieces.append((highest[:, 0] + jnp.log(totals[:, 0])) / width)
        moment_inputs = jnp.concatenate([block_rows, squared.astype(jnp.bfloat16)], axis=1)
        moments = moments + jnp.dot(
            responsibility.T, moment_inputs, preferred_element_type=jnp.float32
        )
        counts = counts + jnp.dot(ones_row, responsibility, preferred_element_type=jnp.float32)
    row_scores = jnp.concatenate(score_pieces, axis=0)
    total_rows = jnp.float32(
        local_rows * lax.axis_size("grp") * lax.axis_size("comp") + total_comps
    )
    owned_moments, owned_counts = (
        lax.psum_scatter(moments, "comp", scatter_dimension=0, tiled=True),
        lax.psum_scatter(counts, "comp", scatter_dimension=0, tiled=True),
    )
    summed_moments, summed_counts = lax.psum((owned_moments, owned_counts), "grp")
    owned_means, owned_variances, owned_weights = update_step(
        summed_moments, summed_counts, total_rows
    )
    fresh_means, fresh_variances, fresh_weights = (
        lax.all_gather(owned_means, "comp", axis=0, tiled=True),
        lax.all_gather(owned_variances, "comp", axis=0, tiled=True),
        lax.all_gather(owned_weights, "comp", axis=0, tiled=True),
    )
    return (fresh_means, fresh_variances, fresh_weights, row_scores)


def solution(mesh):
    return jax.shard_map(
        on_device,
        mesh=mesh,
        in_specs=(P(("grp", "comp"), None), P("comp", None), P("comp", None), P()),
        out_specs=(P(), P(), P(), P(("grp", "comp"))),
        check_vma=False,
    )
```

profile of v0, /device:TPU:0, one launch (start us, length us, event | category | flops | bytes accessed | tf_op | source)
XLA Modules:
  0.0 253.6 jit_solution(14218386838677652206)
XLA Ops:
  7.2 0.0 all-gather.4.cloned.1.call-start
  7.2 1.0 add_reduce_fusion.4
  8.2 0.7 pad_maximum_fusion
  8.9 0.0 all-gather.4.cloned.1.call-update
  8.9 0.0 reduce-scatter.2.cloned.1.call-start
  9.0 1.3 reduce_max.46
  10.2 1.9 exponential_reduce_fusion
  12.9 1.3 fusion.64
  14.9 1.3 subtract_subtract_fusion
  16.2 0.2 add_dynamic-update-slice_fusion
  16.4 35.2 %all-reduce = f32[1024]{0:T(1024)S(1)} all-reduce(f32[1024]{0:T(1024)S(1)} %add_dynamic-update-slice_fusion), channel_id=1, replica_groups=mesh['grp'=2,'comp'=16] {'comp'}, use_global_device_ids=true, to_apply=%add | all-reduce | flops 1024 | bytes 8192
  51.6 2.3 fusion.63
  53.9 0.0 copy-done.3
  53.9 1.4 fusion.38
  55.3 5.5 %fusion.4 = f32[512,1024]{1,0:T(8,128)S(1)} fusion(f32[1024,512]{1,0:T(8,128)} %all-gather.4.cloned.1.call-done, f32[512,256]{1,0:T(8,128)S(1)} %get-tuple-element.13, f32[512,256]{1,0:T(8,128)} %get-tuple-element.21), kind=kOutput, calls=%fused_computation.17 | convolution fusion | flops 3221487616 | bytes 5242880 | tf_op jit(solution)/shard_map/dot_general | solution.py:48
  60.8 0.0 copy-done
  60.8 0.0 copy-done.4
  60.8 3.6 %fusion.12 = f32[512,1024]{1,0:T(8,128)S(1)} fusion(f32[1024,512]{1,0:T(8,128)S(1)} %copy-done, f32[512,256]{1,0:T(8,128)S(1)} %get-tuple-element.15, f32[512,256]{1,0:T(8,128)S(1)} %copy-done.4), kind=kOutput, calls=%fused_computation.25 | convolution fusion | flops 3221487616 | bytes 5242880 | tf_op jit(solution)/shard_map/dot_general | solution.py:48
  64.4 3.7 %add_reduce_fusion = (f32[512]{0:T(512)S(1)}, f32[512]{0:T(512)S(1)}, f32[512,1024]{1,0:T(8,128)S(1)}) fusion(f32[1024]{0:T(1024)S(1)} %all-reduce, f32[512,1024]{1,0:T(8,128)S(1)} %fusion.4, f32[1024,512]{1,0:T(8,128)S(1)} %copy-done, f32[512,256]{1,0:T(8,128)S(1)} %get-tuple-element.16, f32[512,256]{1,0:T(8,128)S(1)} %get-tuple-element.27), kind=kOutput, calls=%fused_computation.9 | convolution fusion | flops 3223583744 | bytes 7348224 | tf_op jit(solution)/shard_map/dot_general | solution.py:48
  68.1 4.4 %fusion.3 = (f32[512]{0:T(512)S(1)}, f32[512]{0:T(512)S(1)}, f32[512]{0:T(512)S(1)}, f32[512]{0:T(512)S(1)}, f32[512,1024]{1,0:T(8,128)S(1)}) fusion(f32[512,1024]{1,0:T(8,128)S(1)} %get-tuple-element.41, f32[512]{0:T(512)S(1)} %get-tuple-element.8, f32[1024]{0:T(1024)S(1)} %all-reduce, f32[512,1024]{1,0:T(8,128)S(1)} %fusion.12, ...), kind=kOutput, calls=%fused_computation.16 | convolution fusion | flops 3226728448 | bytes 11550720 | tf_op jit(solution)/shard_map/dot_general | solution.py:48
  72.6 1.5 fusion.1
  74.1 0.0 copy-start.1
  74.1 0.0 copy-start.8
  74.1 0.0 copy-start.11
  74.2 1.4 divide_convert_fusion.2
  75.5 0.0 copy-done.8
  75.5 0.0 copy-done.11
  75.6 0.0 copy-start.6
  75.6 0.0 copy-start.10
  75.6 0.8 fusion.24
  76.3 0.2 copy-done.6
  76.5 0.1 copy-done.10
  76.6 0.8 fusion.20
  77.3 0.2 copy-done.5
  77.5 0.1 copy-done.9
  77.6 0.8 fusion.28
  78.4 0.2 copy-done.7
  78.6 2.1 add_add_fusion
  80.7 0.0 reduce-scatter.2.cloned.1.call-update
  80.7 0.0 all-reduce.5.cloned.1.call-start
  81.4 0.0 copy-start.2
  81.4 0.2 fusion.49
  81.7 0.2 fusion.47
  81.9 0.3 fusion.45
  82.2 0.5 copy-done.2
  82.6 0.2 fusion.43
  82.9 30.7 %all-reduce.2 = f32[1024]{0:T(1024)S(1)} all-reduce(f32[1024]{0:T(1024)S(1)} %add_add_fusion.1), channel_id=3, replica_groups=mesh['grp'=2,'comp'=16] {'comp'}, use_global_device_ids=true, to_apply=%region_13.14.clone | all-reduce | flops 1024 | bytes 8192
  113.6 0.1 dynamic-slice.3
  113.7 4.9 %psum.15 = f32[64]{0:T(128)S(1)} all-reduce(f32[64]{0:T(128)S(1)} %dynamic-slice.3), channel_id=1, replica_groups=mesh['grp'=2,'comp'=16] {'grp'}, use_global_device_ids=true, to_apply=%region_14.15 | all-reduce | flops 64 | bytes 512 | tf_op jit(solution)/shard_map/psum | solution.py:73
  118.6 21.8 %reduce-scatter.2.cloned.1.call-done = f32[64,512]{1,0:T(8,128)} async-done(((f32[1024,512]{1,0:T(8,128)}), f32[64,512]{1,0:T(8,128)}) %reduce-scatter.2.cloned.1.call-update) | async-done | bytes 131088 | tf_op jit(solution)/shard_map/reduce_scatter | solution.py:70
  140.4 0.0 all-reduce.5.cloned.1.call-update
  140.4 0.0 all-gather.6.cloned.1.call-start
  140.5 0.1 log_dynamic-update-slice_fusion
  140.6 22.6 %all-reduce.5.cloned.1.call-done = f32[64,512]{1,0:T(8,128)} async-done(((f32[64,512]{1,0:T(8,128)}), f32[64,512]{1,0:T(8,128)}) %all-reduce.5.cloned.1.call-update) | async-done | bytes 131088 | tf_op jit(solution)/shard_map/psum | solution.py:73
  163.2 1.6 fusion.41
  164.8 0.0 all-gather.6.cloned.1.call-update
  164.8 0.0 all-gather.8.cloned.1.call-start
  164.9 0.5 all-gather.8.cloned.1.call-update
  165.4 33.5 %all-reduce.1 = f32[1024]{0:T(1024)} all-reduce(f32[1024]{0:T(1024)S(1)} %get-tuple-element.37), channel_id=1, replica_groups=mesh['grp'=2,'comp'=16] {'comp'}, use_global_device_ids=true, to_apply=%add.1 | all-reduce | flops 1024 | bytes 8192
  199.0 0.6 pad_maximum_fusion.1
  199.6 4.4 %all-gather.6.cloned.1.call-done = f32[1024,256]{1,0:T(8,128)} async-done(((f32[64,256]{1,0:T(8,128)}), f32[1024,256]{1,0:T(8,128)}) %all-gather.6.cloned.1.call-update) | async-done | bytes 1048592 | tf_op jit(solution)/shard_map/all_gather | solution.py:78
  204.0 39.8 %all-gather.8.cloned.1.call-done = f32[1024,256]{1,0:T(8,128)} async-done(((f32[64,256]{1,0:T(8,128)}), f32[1024,256]{1,0:T(8,128)}) %all-gather.8.cloned.1.call-update) | async-done | bytes 1048592 | tf_op jit(solution)/shard_map/all_gather | solution.py:79
  243.7 2.4 copy.13
  246.1 1.0 copy.14
  (15 shorter events, 0.0 us)
Async XLA Ops:
  7.2 48.2 %all-gather.4.cloned.1.call-start = ((), (), s32[]{:S(2)}) async-start(), calls=%async_computation.1 | async-start | bytes 2228224 | tf_op jit(solution)/shard_map/all_gather | solution.py:33
  8.9 131.5 %reduce-scatter.2.cloned.1.call-start = ((), (), s32[]{:S(2)}) async-start(), calls=%async_computation.2 | async-start | bytes 2228224 | tf_op jit(solution)/shard_map/reduce_scatter | solution.py:70
  51.6 2.3 copy-start.3
  55.3 5.5 %copy-start = (f32[1024,512]{1,0:T(8,128)S(1)}, f32[1024,512]{1,0:T(8,128)}, u32[]{:S(2)}) copy-start(f32[1024,512]{1,0:T(8,128)} %all-gather.4.cloned.1.call-done) | copy-start | bytes 6291460
  55.3 5.5 %copy-start.4 = (f32[512,256]{1,0:T(8,128)S(1)}, f32[512,256]{1,0:T(8,128)}, u32[]{:S(2)}) copy-start(f32[512,256]{1,0:T(8,128)} %get-tuple-element.25) | copy-start | bytes 1572868
  74.1 4.3 %copy-start.1 = (bf16[512,1024]{1,0:T(8,128)(2,1)}, bf16[512,1024]{1,0:T(8,128)(2,1)S(1)}, u32[]{:S(2)}) copy-start(bf16[512,1024]{1,0:T(8,128)(2,1)S(1)} %get-tuple-element.33) | copy-start | bytes 3145732
  74.1 1.4 copy-start.8
  74.1 1.4 copy-start.11
  75.6 1.0 copy-start.6
  75.6 1.0 copy-start.10
  76.6 0.9 copy-start.5
  76.6 1.0 copy-start.9
  77.6 0.9 copy-start.7
  80.7 82.5 %all-reduce.5.cloned.1.call-start = ((), (), s32[]{:S(2)}) async-start(), calls=%async_computation.3 | async-start | bytes 262144 | tf_op jit(solution)/shard_map/psum | solution.py:73
  81.4 1.2 copy-start.2
  140.4 63.6 %all-gather.6.cloned.1.call-start = ((), (), s32[]{:S(2)}) async-start(), calls=%async_computation.4 | async-start | bytes 1114112 | tf_op jit(solution)/shard_map/all_gather | solution.py:78
  164.8 78.9 %all-gather.8.cloned.1.call-start = ((), (), s32[]{:S(2)}) async-start(), calls=%async_computation.5 | async-start | bytes 1114112 | tf_op jit(solution)/shard_map/all_gather | solution.py:79
  243.7 2.4 copy-start.12
Sparse Core Ops, SparseCore 0:
  10.2 44.2 all-gather.3
  80.8 59.5 reduce-scatter.1
  142.7 20.4 all-reduce.4
  166.0 37.8 all-gather.5
  206.8 36.9 all-gather.7
where the time goes:
time: 254 us
  blocking collectives  104 us (41%)
  waiting for transfers between devices  89.2 us (35%)
  matrix products  22.6 us (9%)
  between operations  16 us (6%)
  other arithmetic  15.4 us (6%)
  local copies, waits for them, and re-layouts  5.93 us (2%)
    unnamed x3, blocking collectives  99.4 us
    all_gather x1, waiting for transfers between devices, on_device(): lax.all_gather(owned_variances, 'comp', axis=0, tiled=True)  39.8 us
    psum x1, waiting for transfers between devices, on_device(): lax.psum((owned_moments, owned_counts), 'grp')  22.6 us
    reduce_scatter x1, waiting for transfers between devices, on_device(): lax.psum_scatter(moments, 'comp', scatter_dimension=0, tiled=True)  21.8 us
    dot_general x4, matrix products, on_device(): jnp.dot(jnp.concatenate([squared, values], axis=1), all_coefficient.T, pr...  17.2 us
    unnamed x32, local copies, waits for them, and re-layouts  5.93 us
  transfers between devices with their start and end apart: 5, of which 4 were waited for; matrix products, arithmetic and copies ran while one was open for 5% of the time, Pallas kernels for 0%

commit v1 on v0

v1 whole, which is shorter than its diff:
```python
import functools
import math

import jax
import jax.numpy as jnp
import numpy as np
from jax import lax
from jax.experimental import pallas as pl
from jax.experimental.pallas import tpu as pltpu
from jax.sharding import PartitionSpec as P

F32 = jnp.float32
BF16 = jnp.bfloat16
LANES = 128
COUNT_ROWS = 8
LOG2E = math.log2(math.e)
LN2 = math.log(2.0)


class Plan:
    def __init__(self, groups, owners, comps):
        self.devices = groups * owners
        self.owners = owners
        owner_bits = owners.bit_length() - 1
        group_bits = groups.bit_length() - 1
        assert owners == 1 << owner_bits and groups == 1 << group_bits and owner_bits >= 3
        self.piece = comps // owners
        self.unit = max(comps // self.devices, min(16, self.piece))
        splits = (comps // self.unit).bit_length() - 1
        group_split = splits - owner_bits
        grp = [owner_bits + b for b in range(group_bits)]
        rest = [1] + grp[:group_split] + list(range(2, owner_bits))
        swapped = [rest[1], rest[0]] + rest[2:]
        self.halving = [(0, 0)] + list(zip(rest, swapped))
        self.whole = [(b, b) for b in grp[group_split:]]
        down = list(range(owner_bits - 1, 0, -1))
        self.gather = list(zip(down, down[:-2] + [down[-1], down[-2]]))
        self.units = comps // self.unit
        per = self.piece // self.unit
        n = self.devices
        gather_at = np.zeros((n, owners), np.int32)
        slot_chunk = np.zeros((n, self.units), np.int32)
        steps = self.gather + [(0, 0)]
        for d in range(n):
            for p in range(owners):
                e = d
                for t in reversed(range(len(steps))):
                    if p >> t & 1:
                        e ^= 1 << steps[t][e & 1]
                gather_at[d, p] = e % owners
            for j in range(self.units):
                e = d
                for s, step in enumerate(self.halving):
                    if j >> (splits - 1 - s) & 1:
                        e ^= 1 << step[e & 1]
                slot_chunk[d, j] = (e % owners) * per + (e // owners) % per
        unit_chunk = (gather_at[:, :, None] * per + np.arange(per)).reshape(n, self.units)
        chunk_slot = np.argsort(slot_chunk, axis=1)
        unit_slot = np.take_along_axis(chunk_slot, unit_chunk, axis=1)
        self.tables = np.stack([unit_chunk, unit_slot, slot_chunk], axis=1).astype(np.int32)

    def pairs(self, step):
        return [(d, d ^ (1 << step[d & 1])) for d in range(self.devices)]

    def swap(self, value, step):
        return lax.ppermute(value, ("grp", "comp"), self.pairs(step))


def columns(row, height):
    return jnp.broadcast_to(row, (height, LANES)).T


def features_kernel(rows_ref, stack_ref, inputs_ref):
    rows = rows_ref[...]
    values = rows.astype(F32)
    squares = values * values
    high = squares.astype(BF16)
    low = (squares - high.astype(F32)).astype(BF16)
    width = rows.shape[1]
    high_t, low_t, rows_t = high.T, low.T, rows.T
    for at, part in enumerate((low_t, high_t, rows_t, high_t, rows_t)):
        stack_ref[at * width : (at + 1) * width, :] = part
    inputs_ref[:, :width] = rows
    inputs_ref[:, width:] = high


def prepare_features(features):
    count, width = features.shape
    block = min(512, count)
    return pl.pallas_call(
        features_kernel,
        grid=(count // block,),
        in_specs=[pl.BlockSpec((block, width), lambda i: (i, 0))],
        out_specs=[
            pl.BlockSpec((5 * width, block), lambda i: (0, i)),
            pl.BlockSpec((block, 2 * width), lambda i: (i, 0)),
        ],
        out_shape=[
            jax.ShapeDtypeStruct((5 * width, count), BF16),
            jax.ShapeDtypeStruct((count, 2 * width), BF16),
        ],
        compiler_params=pltpu.CompilerParams(vmem_limit_bytes=48 * 2**20),
        cost_estimate=pl.CostEstimate(flops=8 * count * width, bytes_accessed=16 * count * width, transcendentals=0),
    )(features)


def mixture_kernel(plan, pieces, table, *refs):
    logits_ref, stack_ref, inputs_ref = refs[pieces : pieces + 3]
    sent_ref, kept_ref, scores_ref = refs[pieces + 3 : pieces + 6]
    weights, offsets, moments, partial, staged = refs[pieces + 6 :]
    comps, depth = weights.shape
    width = depth // 5
    unit = plan.unit
    step = pl.program_id(0)

    @pl.when(step == 0)
    def _():
        logits = logits_ref[...]
        top = jnp.max(logits)
        shifted = logits - top
        log_weights = shifted - jnp.log(jnp.sum(jnp.exp(shifted)))
        for b in range(comps // LANES):
            staged[b * LANES : (b + 1) * LANES, :] = columns(log_weights[b : b + 1, :], LANES)
        at = 0
        for ref in refs[:pieces]:
            for first in range(0, ref.shape[0], unit):
                here = slice(at, at + unit)
                mean = ref[first : first + unit, :width]
                variance = ref[first : first + unit, width:]
                inverse = 1.0 / variance
                linear = mean * inverse
                constant = jnp.sum(jnp.log(variance) + mean * linear, axis=1, keepdims=True)
                chunk = pl.multiple_of(table[0, at // unit] * unit, unit)
                log_weight = staged[pl.ds(chunk, unit), :]
                offsets[here, :] = (
                    log_weight - 0.5 * constant - 0.5 * width * math.log(2.0 * math.pi)
                ) * LOG2E
                square = inverse * (-0.5 * LOG2E)
                linear = linear * LOG2E
                square_high = square.astype(BF16)
                linear_high = linear.astype(BF16)
                weights[here, :width] = square_high
                weights[here, width : 2 * width] = square_high
                weights[here, 2 * width : 3 * width] = linear_high
                weights[here, 3 * width : 4 * width] = (square - square_high.astype(F32)).astype(BF16)
                weights[here, 4 * width :] = (linear - linear_high.astype(F32)).astype(BF16)
                at += unit
        moments[...] = jnp.zeros_like(moments)
        partial[...] = jnp.zeros_like(partial)

    block = stack_ref.shape[1]
    scores = jnp.dot(weights[...], stack_ref[...], preferred_element_type=F32)
    scores = scores + jnp.tile(offsets[...], (1, block // LANES))
    highest = jnp.max(scores, axis=0, keepdims=True)
    exponent = jnp.exp2(scores - highest)
    totals = jnp.sum(exponent, axis=0, keepdims=True)
    responsibility = (exponent * (1.0 / totals)).astype(BF16)
    scores_ref[...] = ((highest + jnp.log2(totals)) * (LN2 / width)).reshape(scores_ref.shape)
    moments[...] += jnp.dot(responsibility, inputs_ref[...], preferred_element_type=F32)
    rounded = responsibility.astype(F32)
    counted = rounded[:, :LANES]
    for b in range(1, block // LANES):
        counted = counted + rounded[:, b * LANES : (b + 1) * LANES]
    partial[...] += counted

    @pl.when(step == pl.num_programs(0) - 1)
    def _():
        parts = 2 * width // LANES
        half = comps // 2 * parts
        for u in range(comps // unit):
            chunk = pl.multiple_of(table[0, u] * unit, unit)
            staged[pl.ds(chunk, unit), :] = partial[u * unit : (u + 1) * unit, :]
        for b in range(comps // LANES):
            line = jnp.sum(staged[b * LANES : (b + 1) * LANES, :].T, axis=0, keepdims=True)
            sent_ref[half + b : half + b + 1, :] = line
            kept_ref[half + b : half + b + 1, :] = line
        for u in range(comps // unit):
            target = kept_ref if u < comps // unit // 2 else sent_ref
            slot = table[1, u] % (comps // unit // 2)
            first = pl.multiple_of(slot * unit * parts, unit)
            for part in range(parts):
                target[pl.ds(first + part * unit, unit), :] = moments[
                    u * unit : (u + 1) * unit, part * LANES : (part + 1) * LANES
                ]


def mixture(plan, table, parameters, logits, stack, inputs):
    depth, count = stack.shape
    width = depth // 5
    comps = sum(p.shape[0] for p in parameters)
    block = min(512, count)
    half = comps // 2 * (2 * width // LANES) + COUNT_ROWS
    whole = lambda shape: pl.BlockSpec(shape, lambda i, t: (0,) * len(shape))
    return pl.pallas_call(
        functools.partial(mixture_kernel, plan, len(parameters)),
        grid_spec=pltpu.PrefetchScalarGridSpec(
            num_scalar_prefetch=1,
            grid=(count // block,),
            in_specs=[whole(p.shape) for p in parameters]
            + [
                whole(logits.shape),
                pl.BlockSpec((depth, block), lambda i, t: (0, i)),
                pl.BlockSpec((block, 2 * width), lambda i, t: (i, 0)),
            ],
            out_specs=[
                whole((half, LANES)),
                whole((half, LANES)),
                pl.BlockSpec((1, block), lambda i, t: (0, i)),
            ],
            scratch_shapes=[
                pltpu.VMEM((comps, depth), BF16),
                pltpu.VMEM((comps, LANES), F32),
                pltpu.VMEM((comps, 2 * width), F32),
                pltpu.VMEM((comps, LANES), F32),
                pltpu.VMEM((comps, LANES), F32),
            ],
        ),
        out_shape=[
            jax.ShapeDtypeStruct((half, LANES), F32),
            jax.ShapeDtypeStruct((half, LANES), F32),
            jax.ShapeDtypeStruct((1, count), F32),
        ],
        compiler_params=pltpu.CompilerParams(vmem_limit_bytes=56 * 2**20),
        cost_estimate=pl.CostEstimate(
            flops=14 * comps * count * width, bytes_accessed=12 * 2**20, transcendentals=comps * count
        ),
    )(table, *parameters, logits, stack, inputs)


def update_kernel(plan, pieces, total_rows, table, *refs):
    counts_ref = refs[pieces]
    means_ref, variances_ref, log_weights_ref = refs[pieces + 1 : pieces + 4]
    staged = refs[pieces + 4]
    comps, width = means_ref.shape
    unit = plan.unit
    parts = width // LANES
    denominator = counts_ref[...] + 1.0
    log_weights_ref[...] = jnp.log(denominator / total_rows)
    inverse = 1.0 / denominator
    for b in range(comps // LANES):
        staged[b * LANES : (b + 1) * LANES, :] = columns(inverse[b : b + 1, :], LANES)
    slot = 0
    for ref in refs[:pieces]:
        for first in range(0, ref.shape[0], unit * 2 * parts):
            chunk = pl.ds(pl.multiple_of(table[2, slot] * unit, unit), unit)
            scale = staged[chunk, :]
            for part in range(parts):
                lanes = slice(part * LANES, (part + 1) * LANES)
                at = first + part * unit
                mean = ref[at : at + unit, :] * scale
                at += parts * unit
                means_ref[chunk, lanes] = mean
                variances_ref[chunk, lanes] = (ref[at : at + unit, :] + 1.0) * scale - mean * mean + 0.01
            slot += 1


def update(plan, table, moments, counts, comps, width, total_rows):
    whole = lambda shape: pl.BlockSpec(shape, lambda i, t: (0,) * len(shape))
    shapes = [(comps, width), (comps, width), counts.shape]
    return pl.pallas_call(
        functools.partial(update_kernel, plan, len(moments), total_rows),
        grid_spec=pltpu.PrefetchScalarGridSpec(
            num_scalar_prefetch=1,
            grid=(1,),
            in_specs=[whole(m.shape) for m in moments] + [whole(counts.shape)],
            out_specs=[whole(s) for s in shapes],
            scratch_shapes=[pltpu.VMEM((comps, LANES), F32)],
        ),
        out_shape=[jax.ShapeDtypeStruct(s, F32) for s in shapes],
        compiler_params=pltpu.CompilerParams(vmem_limit_bytes=32 * 2**20),
        cost_estimate=pl.CostEstimate(flops=8 * comps * width, bytes_accessed=16 * comps * width, transcendentals=0),
    )(table, *moments, counts)


def on_device(plan, features, means, variances, weight_logits):
    comps = weight_logits.shape[0]
    width = means.shape[1]
    me = lax.axis_index(("grp", "comp"))
    table = lax.dynamic_index_in_dim(jnp.asarray(plan.tables), me, 0, keepdims=False)
    stack, inputs = prepare_features(features)

    with jax.named_scope("gather_parameters"):
        parameters = [jnp.concatenate([means, variances], axis=1)]
        for step in plan.gather:
            held = parameters[0] if len(parameters) == 1 else jnp.concatenate(parameters, axis=0)
            parameters.append(plan.swap(held, step))
        parameters += [plan.swap(p, (0, 0)) for p in parameters]

    sent, kept, row_scores = mixture(
        plan, table, parameters, weight_logits.reshape(comps // LANES, LANES), stack, inputs
    )

    with jax.named_scope("scatter_moments"):
        counts = kept[-COUNT_ROWS:]
        kept = kept[:-COUNT_ROWS]
        for at, step in enumerate(plan.halving):
            arrived = plan.swap(sent, step)
            kept = kept + arrived[:-COUNT_ROWS]
            counts = counts + arrived[-COUNT_ROWS:]
            if at + 1 < len(plan.halving):
                half = kept.shape[0] // 2
                sent = jnp.concatenate([kept[half:], counts], axis=0)
                kept = kept[:half]
        for step in plan.whole:
            arrived = plan.swap(jnp.concatenate([kept, counts], axis=0), step)
            kept = kept + arrived[:-COUNT_ROWS]
            counts = counts + arrived[-COUNT_ROWS:]

    with jax.named_scope("gather_moments"):
        moments = [kept]
        for step in reversed(plan.halving[1:]):
            held = moments[0] if len(moments) == 1 else jnp.concatenate(moments, axis=0)
            moments.append(plan.swap(held, step))
        moments += [plan.swap(m, (0, 0)) for m in moments]

    total_rows = float(features.shape[0] * plan.devices + comps)
    fresh_means, fresh_variances, fresh_weights = update(
        plan, table, moments, counts, comps, width, total_rows
    )
    return fresh_means, fresh_variances, fresh_weights.reshape(comps), row_scores.reshape(-1)


def solution(mesh):
    def whole(features, means, variances, weight_logits):
        plan = Plan(mesh.shape["grp"], mesh.shape["comp"], weight_logits.shape[0])
        return jax.shard_map(
            functools.partial(on_device, plan),
            mesh=mesh,
            in_specs=(P(("grp", "comp"), None), P("comp", None), P("comp", None), P()),
            out_specs=(P(), P(), P(), P(("grp", "comp"))),
            check_vma=False,
        )(features, means, variances, weight_logits)

    return whole
```

time: 254 us -> 121 us (0.48)
  blocking collectives: 104 us -> 0 us
  matrix products: 22.6 us -> 0 us
  Pallas kernels: 0 us -> 22.1 us
  starting transfers between devices: 0.2 us -> 19.6 us
  waiting for transfers between devices: 89.2 us -> 70.2 us
  between operations: 16 us -> 0.86 us
  other arithmetic: 15.4 us -> 2.35 us
    unnamed x3 -> x0, blocking collectives: 99.4 us -> none
    ppermute x0 -> x21, waiting for transfers between devices: none -> 70.2 us  [swap(): return lax.ppermute(value, ('grp', 'comp'), self.pairs(step))]
    all_gather x3 -> x0, waiting for transfers between devices: 44.2 us -> none  [the longest x1 39.8 us: on_device(): lax.all_gather(owned_variances, 'comp', axis=0, tiled=True)]
    psum x1 -> x0, waiting for transfers between devices: 22.6 us -> none  [on_device(): lax.psum((owned_moments, owned_counts), 'grp')]
    dot_general x12 -> x0, matrix products: 22.6 us -> none  [the longest x4 17.2 us: on_device(): jnp.dot(jnp.concatenate([squared, values], axis=1), all_coefficient.T, pr...]
    pallas_call x0 -> x3, Pallas kernels: none -> 22.1 us  [the longest x1 16.5 us: mixture(): pl.pallas_call(functools.partial(mixture_kernel, plan, len(parameters)),...]
    reduce_scatter x1 -> x0, waiting for transfers between devices: 21.8 us -> none  [on_device(): lax.psum_scatter(moments, 'comp', scatter_dimension=0, tiled=True)]
    ppermute x0 -> x21, starting transfers between devices: none -> 19.6 us  [swap(): return lax.ppermute(value, ('grp', 'comp'), self.pairs(step))]
  transfers between devices with their start and end apart: 5 -> 21, of which waited for: 4 -> 15; matrix products, arithmetic and copies ran while one was open for 5% -> 1% of each run, Pallas kernels for 0% -> 3%
where the time goes in v1:
time: 121 us; the launch traced here: 120 us
  waiting for transfers between devices  70.2 us (58%)
  Pallas kernels  22.1 us (18%)
  starting transfers between devices  19.6 us (16%)
  local copies, waits for them, and re-layouts  5.35 us (4%)
  other arithmetic  2.35 us (2%)
    ppermute x21, waiting for transfers between devices, swap(): return lax.ppermute(value, ('grp', 'comp'), self.pairs(step))  70.2 us
    ppermute x21, starting transfers between devices, swap(): return lax.ppermute(value, ('grp', 'comp'), self.pairs(step))  19.6 us
    pallas_call x1, Pallas kernels, mixture(): pl.pallas_call(functools.partial(mixture_kernel, plan, len(parameters)),...  16.5 us
    pallas_call x1, Pallas kernels, prepare_features(): pl.pallas_call(features_kernel, grid=(count // block,), in_specs=[pl.Bloc...  3.25 us
    unnamed x23, local copies, waits for them, and re-layouts  3.18 us
  transfers between devices with their start and end apart: 21, of which 15 were waited for; matrix products, arithmetic and copies ran while one was open for 1% of the time, Pallas kernels for 3%

profile of v1, /device:TPU:0, one launch (start us, length us, event | category | flops | bytes accessed | tf_op | source)
XLA Modules:
  0.0 120.5 jit_solution(14943661336365945694)
XLA Ops:
  0.6 0.0 copy-start
  0.6 0.9 constant_dynamic-update-slice_fusion.1
  1.6 0.8 constant_dynamic-update-slice_fusion.refs_0_
  2.4 4.0 %collective-permute-start = (f32[64,512]{1,0:T(8,128)S(1)}, f32[64,512]{1,0:T(8,128)S(1)}, u32[]{:S(2)}, u32[]{:S(2)}) collective-permute-start(f32[64,512]{1,0:T(8,128)S(1)} %constant_dynamic-update-slice_fusion.refs_0_), channel_id=1, source_target_pairs={{0,8},{1,9},{2,10},{3,11},{4,12},{5,13},{6,14},{7,15},{8,0},{9,1},... | collective-permute-start | bytes 393224 | tf_op jit(solution)/shard_map/gather_parameters/ppermute | solution.py:66
  6.5 6.3 %collective-permute-done.refs_1_ = f32[64,512]{1,0:T(8,128)S(1)} collective-permute-done((f32[64,512]{1,0:T(8,128)S(1)}, f32[64,512]{1,0:T(8,128)S(1)}, u32[]{:S(2)}, u32[]{:S(2)}) %collective-permute-start) | collective-permute-done | bytes 131104 | tf_op jit(solution)/shard_map/gather_parameters/ppermute | solution.py:66
  12.8 0.8 collective-permute-start.1
  13.6 5.6 %collective-permute-done.1.refs_2_ = f32[128,512]{1,0:T(8,128)S(1)} collective-permute-done((f32[128,512]{1,0:T(8,128)S(1)}, f32[128,512]{1,0:T(8,128)S(1)}, u32[]{:S(2)}, u32[]{:S(2)}) %collective-permute-start.1) | collective-permute-done | bytes 262176 | tf_op jit(solution)/shard_map/gather_parameters/ppermute | solution.py:66
  19.3 1.6 %collective-permute-start.2 = (f32[256,512]{1,0:T(8,128)S(1)}, f32[256,512]{1,0:T(8,128)S(1)}, u32[]{:S(2)}, u32[]{:S(2)}) collective-permute-start(f32[256,512]{1,0:T(8,128)S(1)} %pad_maximum_fusion.1), channel_id=1, source_target_pairs={{0,2},{1,5},{2,0},{3,7},{4,6},{5,1},{6,4},{7,3},{8,10},{9,13},{10,... | collective-permute-start | bytes 1572872 | tf_op jit(solution)/shard_map/gather_parameters/ppermute | solution.py:66
  20.9 7.6 %collective-permute-done.2.refs_3_ = f32[256,512]{1,0:T(8,128)S(1)} collective-permute-done((f32[256,512]{1,0:T(8,128)S(1)}, f32[256,512]{1,0:T(8,128)S(1)}, u32[]{:S(2)}, u32[]{:S(2)}) %collective-permute-start.2) | collective-permute-done | bytes 524320 | tf_op jit(solution)/shard_map/gather_parameters/ppermute | solution.py:66
  28.5 0.0 collective-permute-start.6
  28.5 0.5 collective-permute-start.5
  29.0 0.0 collective-permute-start.3
  29.0 0.5 collective-permute-start.4
  29.5 0.0 copy-done
  29.5 3.2 %shard_map.84 = (bf16[1280,2048]{1,0:T(8,128)(2,1)}, bf16[2048,512]{1,0:T(8,128)(2,1)S(1)}) custom-call(bf16[2048,256]{1,0:T(8,128)(2,1)S(1)} %copy-done), custom_call_target="tpu_custom_call" | custom-call | flops 4194304 | bytes 8388608 | tf_op jit(solution)/shard_map/pallas_call | solution.py:90
  32.8 0.0 copy-done.3
  32.8 0.0 copy-done.4
  32.8 0.0 copy-done.5
  32.8 1.3 %copy-done.2 = bf16[2048,512]{1,0:T(8,128)(2,1)} copy-done((bf16[2048,512]{1,0:T(8,128)(2,1)}, bf16[2048,512]{1,0:T(8,128)(2,1)S(1)}, u32[]{:S(2)}) %copy-start.2) | copy-done | bytes 2097176
  34.1 1.3 %dynamic-slice_bitcast_fusion.table = s32[3,32]{1,0:T(4,128)} fusion(s32[32,3,32]{2,1,0:T(4,128)} %constant.19.clone, s32[]{:T(128)S(6)} %select_n.4), kind=kLoop, calls=%fused_computation.21 | loop fusion | bytes 772 | tf_op jit(solution)/shard_map/jit(dynamic_index_in_dim)/squeeze | solution.py:279
  35.4 0.0 collective-permute-done.3.refs_4_
  35.4 0.0 collective-permute-done.4.refs_5_
  35.4 0.0 collective-permute-done.5.refs_6_
  35.4 0.0 copy-start.8
  35.4 0.0 collective-permute-done.6.refs_7_
  35.4 0.0 copy-start.7
  35.5 0.6 copy-done.9
  36.0 0.0 copy-done.10
  36.1 0.1 copy-done.8
  36.2 0.2 copy-done.7
  36.3 16.5 %shard_map.85 = (f32[2056,128]{1,0:T(8,128)}, f32[2056,128]{1,0:T(8,128)}, f32[1,2048]{1,0:T(1,128)}) custom-call(s32[3,32]{1,0:T(4,128)} %dynamic-slice_bitcast_fusion.table, f32[64,512]{1,0:T(8,128)} %copy-done.3, f32[64,512]{1,0:T(8,128)} %copy-done.4, f32[128,512]{1,0:T(8,128)} %copy-done.5, f32[256,512]{1,0:T(8,128)} %copy-done.6, f32[64,512]{1,0:T(8,128)} %copy-done.9, ...), custom_call_target="tpu_custom_call" | custom-call | flops 7516192768 | bytes 12582912 | tf_op jit(solution)/shard_map/pallas_call | solution.py:194
  52.8 0.1 collective-permute-start.7
  52.9 2.9 %collective-permute-done.7 = f32[2056,128]{1,0:T(8,128)S(1)} collective-permute-done((f32[2056,128]{1,0:T(8,128)}, f32[2056,128]{1,0:T(8,128)S(1)}, u32[]{:S(2)}, u32[]{:S(2)}) %collective-permute-start.7) | collective-permute-done | bytes 1052704 | tf_op jit(solution)/shard_map/scatter_moments/ppermute | solution.py:66
  55.8 1.3 %slice_add_fusion = f32[2048,128]{1,0:T(8,128)S(1)} fusion(f32[2056,128]{1,0:T(8,128)S(1)} %collective-permute-done.7, f32[2056,128]{1,0:T(8,128)} %get-tuple-element.14), kind=kLoop, calls=%fused_computation | loop fusion | flops 262144 | bytes 3145728 | tf_op jit(solution)/shard_map/scatter_moments/add | solution.py:298
  57.2 0.7 slice_add_fusion.9
  57.9 1.6 %collective-permute-start.8 = (f32[1032,128]{1,0:T(8,128)S(1)}, f32[1032,128]{1,0:T(8,128)S(1)}, u32[]{:S(2)}, u32[]{:S(2)}) collective-permute-start(f32[1032,128]{1,0:T(8,128)S(1)} %pad_maximum_fusion), channel_id=1, source_target_pairs={{0,2},{1,17},{2,0},{3,19},{4,6},{5,21},{6,4},{7,23},{8,10},{9,25},... | collective-permute-start | bytes 1585160 | tf_op jit(solution)/shard_map/scatter_moments/ppermute | solution.py:66
  59.5 7.7 %collective-permute-done.8 = f32[1032,128]{1,0:T(8,128)S(1)} collective-permute-done((f32[1032,128]{1,0:T(8,128)S(1)}, f32[1032,128]{1,0:T(8,128)S(1)}, u32[]{:S(2)}, u32[]{:S(2)}) %collective-permute-start.8) | collective-permute-done | bytes 528416 | tf_op jit(solution)/shard_map/scatter_moments/ppermute | solution.py:66
  67.2 0.1 slice_add_fusion.1
  67.3 1.6 %collective-permute-start.9 = (f32[520,128]{1,0:T(8,128)S(1)}, f32[520,128]{1,0:T(8,128)S(1)}, u32[]{:S(2)}, u32[]{:S(2)}) collective-permute-start(f32[520,128]{1,0:T(8,128)S(1)} %pad_maximum_fusion.3), channel_id=1, source_target_pairs={{0,16},{1,3},{2,18},{3,1},{4,20},{5,7},{6,22},{7,5},{8,24},{9,11},... | collective-permute-start | bytes 798728 | tf_op jit(solution)/shard_map/scatter_moments/ppermute | solution.py:66
  68.9 4.8 %collective-permute-done.9 = f32[520,128]{1,0:T(8,128)S(1)} collective-permute-done((f32[520,128]{1,0:T(8,128)S(1)}, f32[520,128]{1,0:T(8,128)S(1)}, u32[]{:S(2)}, u32[]{:S(2)}) %collective-permute-start.9) | collective-permute-done | bytes 266272 | tf_op jit(solution)/shard_map/scatter_moments/ppermute | solution.py:66
  73.9 0.8 collective-permute-start.10
  74.7 4.3 %collective-permute-done.10 = f32[264,128]{1,0:T(8,128)S(1)} collective-permute-done((f32[264,128]{1,0:T(8,128)S(1)}, f32[264,128]{1,0:T(8,128)S(1)}, u32[]{:S(2)}, u32[]{:S(2)}) %collective-permute-start.10) | collective-permute-done | bytes 135200 | tf_op jit(solution)/shard_map/scatter_moments/ppermute | solution.py:66
  79.0 0.0 copy-start.1
  79.0 2.2 %collective-permute-start.11 = (f32[136,128]{1,0:T(8,128)S(1)}, f32[136,128]{1,0:T(8,128)S(1)}, u32[]{:S(2)}, u32[]{:S(2)}) collective-permute-start(f32[136,128]{1,0:T(8,128)S(1)} %pad_maximum_fusion.8), channel_id=1, source_target_pairs={{0,8},{1,9},{2,10},{3,11},{4,12},{5,13},{6,14},{7,15},{8,0},{9,1},... | collective-permute-start | bytes 208904 | tf_op jit(solution)/shard_map/scatter_moments/ppermute | solution.py:66
  81.2 4.9 %collective-permute-done.11 = f32[136,128]{1,0:T(8,128)S(1)} collective-permute-done((f32[136,128]{1,0:T(8,128)S(1)}, f32[136,128]{1,0:T(8,128)S(1)}, u32[]{:S(2)}, u32[]{:S(2)}) %collective-permute-start.11) | collective-permute-done | bytes 69664 | tf_op jit(solution)/shard_map/scatter_moments/ppermute | solution.py:66
  86.1 0.3 collective-permute-start.12
  86.5 5.3 %collective-permute-done.12.refs_1_ = f32[128,128]{1,0:T(8,128)S(1)} collective-permute-done((f32[128,128]{1,0:T(8,128)S(1)}, f32[128,128]{1,0:T(8,128)S(1)}, u32[]{:S(2)}, u32[]{:S(2)}) %collective-permute-start.12) | collective-permute-done | bytes 65568 | tf_op jit(solution)/shard_map/gather_moments/ppermute | solution.py:66
  91.8 1.2 collective-permute-start.13
  93.0 3.8 %collective-permute-done.13.refs_2_ = f32[256,128]{1,0:T(8,128)S(1)} collective-permute-done((f32[256,128]{1,0:T(8,128)S(1)}, f32[256,128]{1,0:T(8,128)S(1)}, u32[]{:S(2)}, u32[]{:S(2)}) %collective-permute-start.13) | collective-permute-done | bytes 131104 | tf_op jit(solution)/shard_map/gather_moments/ppermute | solution.py:66
  96.8 1.7 %collective-permute-start.14 = (f32[512,128]{1,0:T(8,128)S(1)}, f32[512,128]{1,0:T(8,128)S(1)}, u32[]{:S(2)}, u32[]{:S(2)}) collective-permute-start(f32[512,128]{1,0:T(8,128)S(1)} %pad_maximum_fusion.5), channel_id=1, source_target_pairs={{0,16},{1,3},{2,18},{3,1},{4,20},{5,7},{6,22},{7,5},{8,24},{9,11},... | collective-permute-start | bytes 786440 | tf_op jit(solution)/shard_map/gather_moments/ppermute | solution.py:66
  98.5 7.6 %collective-permute-done.14.refs_3_ = f32[512,128]{1,0:T(8,128)S(1)} collective-permute-done((f32[512,128]{1,0:T(8,128)S(1)}, f32[512,128]{1,0:T(8,128)S(1)}, u32[]{:S(2)}, u32[]{:S(2)}) %collective-permute-start.14) | collective-permute-done | bytes 262176 | tf_op jit(solution)/shard_map/gather_moments/ppermute | solution.py:66
  106.2 1.7 %collective-permute-start.15 = (f32[1024,128]{1,0:T(8,128)S(1)}, f32[1024,128]{1,0:T(8,128)S(1)}, u32[]{:S(2)}, u32[]{:S(2)}) collective-permute-start(f32[1024,128]{1,0:T(8,128)S(1)} %pad_maximum_fusion.2), channel_id=1, source_target_pairs={{0,2},{1,17},{2,0},{3,19},{4,6},{5,21},{6,4},{7,23},{8,10},{9,25},... | collective-permute-start | bytes 1572872 | tf_op jit(solution)/shard_map/gather_moments/ppermute | solution.py:66
  107.9 7.6 %collective-permute-done.15.refs_4_ = f32[1024,128]{1,0:T(8,128)S(1)} collective-permute-done((f32[1024,128]{1,0:T(8,128)S(1)}, f32[1024,128]{1,0:T(8,128)S(1)}, u32[]{:S(2)}, u32[]{:S(2)}) %collective-permute-start.15) | collective-permute-done | bytes 524320 | tf_op jit(solution)/shard_map/gather_moments/ppermute | solution.py:66
  115.4 0.0 collective-permute-start.20
  115.4 0.5 collective-permute-start.19
  116.0 0.0 collective-permute-start.16
  116.0 0.5 collective-permute-start.17
  116.5 0.0 collective-permute-start.18
  116.5 1.4 %collective-permute-done.16.refs_5_ = f32[128,128]{1,0:T(8,128)S(1)} collective-permute-done((f32[128,128]{1,0:T(8,128)S(1)}, f32[128,128]{1,0:T(8,128)S(1)}, u32[]{:S(2)}, u32[]{:S(2)}) %collective-permute-start.16) | collective-permute-done | bytes 65568 | tf_op jit(solution)/shard_map/gather_moments/ppermute | solution.py:66
  117.8 0.1 collective-permute-done.17.refs_6_
  117.9 0.2 collective-permute-done.18.refs_7_
  118.1 0.0 collective-permute-done.19.refs_8_
  118.1 0.0 collective-permute-done.20.refs_9_
  118.1 2.4 %shard_map.86 = (f32[1024,256]{1,0:T(8,128)}, f32[1024,256]{1,0:T(8,128)}, f32[8,128]{1,0:T(8,128)}) custom-call(s32[3,32]{1,0:T(4,128)S(1)} %copy-done.1, f32[128,128]{1,0:T(8,128)S(1)} %slice_add_fusion.4.refs_0_, f32[128,128]{1,0:T(8,128)S(1)} %collective-permute-done.12.refs_1_, f32[256,128]{1,0:T(8,128)S(1)} %collective-permute-done.13.refs_2_, ...), custom_call_target="tpu_custom_call" | custom-call | flops 2097152 | bytes 4194304 | tf_op jit(solution)/shard_map/pallas_call | solution.py:260
  (29 shorter events, 0.4 us)
Async XLA Ops:
  0.6 28.9 %copy-start = (bf16[2048,256]{1,0:T(8,128)(2,1)S(1)}, bf16[2048,256]{1,0:T(8,128)(2,1)}, u32[]{:S(2)}) copy-start(bf16[2048,256]{1,0:T(8,128)(2,1)} %rows_ref.1) | copy-start | bytes 3145732
  2.4 30.4 %copy-start.3 = (f32[64,512]{1,0:T(8,128)}, f32[64,512]{1,0:T(8,128)S(1)}, u32[]{:S(2)}) copy-start(f32[64,512]{1,0:T(8,128)S(1)} %constant_dynamic-update-slice_fusion.refs_0_) | copy-start | bytes 393220
  2.4 10.3 %collective-permute-start = (f32[64,512]{1,0:T(8,128)S(1)}, f32[64,512]{1,0:T(8,128)S(1)}, u32[]{:S(2)}, u32[]{:S(2)}) collective-permute-start(f32[64,512]{1,0:T(8,128)S(1)} %constant_dynamic-update-slice_fusion.refs_0_), channel_id=1, source_target_pairs={{0,8},{1,9},{2,10},{3,11},{4,12},{5,13},{6,14},{7,15},{8,0},{9,1},... | collective-permute-start | bytes 393224 | tf_op jit(solution)/shard_map/gather_parameters/ppermute | solution.py:66
  12.8 20.0 %copy-start.4 = (f32[64,512]{1,0:T(8,128)}, f32[64,512]{1,0:T(8,128)S(1)}, u32[]{:S(2)}) copy-start(f32[64,512]{1,0:T(8,128)S(1)} %collective-permute-done.refs_1_) | copy-start | bytes 393220
  12.8 6.4 %collective-permute-start.1 = (f32[128,512]{1,0:T(8,128)S(1)}, f32[128,512]{1,0:T(8,128)S(1)}, u32[]{:S(2)}, u32[]{:S(2)}) collective-permute-start(f32[128,512]{1,0:T(8,128)S(1)} %pad_maximum_fusion.4), channel_id=1, source_target_pairs={{0,4},{1,3},{2,6},{3,1},{4,0},{5,7},{6,2},{7,5},{8,12},{9,11},{10,... | collective-permute-start | bytes 786440 | tf_op jit(solution)/shard_map/gather_parameters/ppermute | solution.py:66
  19.2 13.6 %copy-start.5 = (f32[128,512]{1,0:T(8,128)}, f32[128,512]{1,0:T(8,128)S(1)}, u32[]{:S(2)}) copy-start(f32[128,512]{1,0:T(8,128)S(1)} %collective-permute-done.1.refs_2_) | copy-start | bytes 786436
  19.3 9.2 %collective-permute-start.2 = (f32[256,512]{1,0:T(8,128)S(1)}, f32[256,512]{1,0:T(8,128)S(1)}, u32[]{:S(2)}, u32[]{:S(2)}) collective-permute-start(f32[256,512]{1,0:T(8,128)S(1)} %pad_maximum_fusion.1), channel_id=1, source_target_pairs={{0,2},{1,5},{2,0},{3,7},{4,6},{5,1},{6,4},{7,3},{8,10},{9,13},{10,... | collective-permute-start | bytes 1572872 | tf_op jit(solution)/shard_map/gather_parameters/ppermute | solution.py:66
  28.5 6.9 %copy-start.6 = (f32[256,512]{1,0:T(8,128)}, f32[256,512]{1,0:T(8,128)S(1)}, u32[]{:S(2)}) copy-start(f32[256,512]{1,0:T(8,128)S(1)} %collective-permute-done.2.refs_3_) | copy-start | bytes 1572868
  28.5 6.9 %collective-permute-start.6 = (f32[256,512]{1,0:T(8,128)S(1)}, f32[256,512]{1,0:T(8,128)S(1)}, u32[]{:S(2)}, u32[]{:S(2)}) collective-permute-start(f32[256,512]{1,0:T(8,128)S(1)} %collective-permute-done.2.refs_3_), channel_id=1, source_target_pairs={{0,1},{1,0},{2,3},{3,2},{4,5},{5,4},{6,7},{7,6},{8,9},{9,8},{10,11... | collective-permute-start | bytes 1572872 | tf_op jit(solution)/shard_map/gather_parameters/ppermute | solution.py:66
  28.5 6.9 %collective-permute-start.5 = (f32[128,512]{1,0:T(8,128)S(1)}, f32[128,512]{1,0:T(8,128)S(1)}, u32[]{:S(2)}, u32[]{:S(2)}) collective-permute-start(f32[128,512]{1,0:T(8,128)S(1)} %collective-permute-done.1.refs_2_), channel_id=1, source_target_pairs={{0,1},{1,0},{2,3},{3,2},{4,5},{5,4},{6,7},{7,6},{8,9},{9,8},{10,11... | collective-permute-start | bytes 786440 | tf_op jit(solution)/shard_map/gather_parameters/ppermute | solution.py:66
  29.0 6.4 %collective-permute-start.3 = (f32[64,512]{1,0:T(8,128)S(1)}, f32[64,512]{1,0:T(8,128)S(1)}, u32[]{:S(2)}, u32[]{:S(2)}) collective-permute-start(f32[64,512]{1,0:T(8,128)S(1)} %constant_dynamic-update-slice_fusion.refs_0_), channel_id=1, source_target_pairs={{0,1},{1,0},{2,3},{3,2},{4,5},{5,4},{6,7},{7,6},{8,9},{9,8},{10,11... | collective-permute-start | bytes 393224 | tf_op jit(solution)/shard_map/gather_parameters/ppermute | solution.py:66
  29.0 6.4 %collective-permute-start.4 = (f32[64,512]{1,0:T(8,128)S(1)}, f32[64,512]{1,0:T(8,128)S(1)}, u32[]{:S(2)}, u32[]{:S(2)}) collective-permute-start(f32[64,512]{1,0:T(8,128)S(1)} %collective-permute-done.refs_1_), channel_id=1, source_target_pairs={{0,1},{1,0},{2,3},{3,2},{4,5},{5,4},{6,7},{7,6},{8,9},{9,8},{10,11... | collective-permute-start | bytes 393224 | tf_op jit(solution)/shard_map/gather_parameters/ppermute | solution.py:66
  32.8 1.3 %copy-start.2 = (bf16[2048,512]{1,0:T(8,128)(2,1)}, bf16[2048,512]{1,0:T(8,128)(2,1)S(1)}, u32[]{:S(2)}) copy-start(bf16[2048,512]{1,0:T(8,128)(2,1)S(1)} %get-tuple-element.13.refs_10_) | copy-start | bytes 6291460
  35.4 0.7 copy-start.9
  35.4 0.7 copy-start.10
  35.4 0.8 copy-start.8
  35.4 0.9 copy-start.7
  52.8 2.9 %collective-permute-start.7 = (f32[2056,128]{1,0:T(8,128)}, f32[2056,128]{1,0:T(8,128)S(1)}, u32[]{:S(2)}, u32[]{:S(2)}) collective-permute-start(f32[2056,128]{1,0:T(8,128)} %get-tuple-element.15), channel_id=1, source_target_pairs={{0,1},{1,0},{2,3},{3,2},{4,5},{5,4},{6,7},{7,6},{8,9},{9,8},{10,11... | collective-permute-start | bytes 3158024 | tf_op jit(solution)/shard_map/scatter_moments/ppermute | solution.py:66
  57.9 9.3 %collective-permute-start.8 = (f32[1032,128]{1,0:T(8,128)S(1)}, f32[1032,128]{1,0:T(8,128)S(1)}, u32[]{:S(2)}, u32[]{:S(2)}) collective-permute-start(f32[1032,128]{1,0:T(8,128)S(1)} %pad_maximum_fusion), channel_id=1, source_target_pairs={{0,2},{1,17},{2,0},{3,19},{4,6},{5,21},{6,4},{7,23},{8,10},{9,25},... | collective-permute-start | bytes 1585160 | tf_op jit(solution)/shard_map/scatter_moments/ppermute | solution.py:66
  67.3 6.5 %collective-permute-start.9 = (f32[520,128]{1,0:T(8,128)S(1)}, f32[520,128]{1,0:T(8,128)S(1)}, u32[]{:S(2)}, u32[]{:S(2)}) collective-permute-start(f32[520,128]{1,0:T(8,128)S(1)} %pad_maximum_fusion.3), channel_id=1, source_target_pairs={{0,16},{1,3},{2,18},{3,1},{4,20},{5,7},{6,22},{7,5},{8,24},{9,11},... | collective-permute-start | bytes 798728 | tf_op jit(solution)/shard_map/scatter_moments/ppermute | solution.py:66
  73.9 5.1 %collective-permute-start.10 = (f32[264,128]{1,0:T(8,128)S(1)}, f32[264,128]{1,0:T(8,128)S(1)}, u32[]{:S(2)}, u32[]{:S(2)}) collective-permute-start(f32[264,128]{1,0:T(8,128)S(1)} %pad_maximum_fusion.6), channel_id=1, source_target_pairs={{0,4},{1,5},{2,6},{3,7},{4,0},{5,1},{6,2},{7,3},{8,12},{9,13},{10,... | collective-permute-start | bytes 405512 | tf_op jit(solution)/shard_map/scatter_moments/ppermute | solution.py:66
  79.0 39.1 %copy-start.1 = (s32[3,32]{1,0:T(4,128)S(1)}, s32[3,32]{1,0:T(4,128)}, u32[]{:S(2)}) copy-start(s32[3,32]{1,0:T(4,128)} %dynamic-slice_bitcast_fusion.table) | copy-start | bytes 1156
  79.0 7.1 %collective-permute-start.11 = (f32[136,128]{1,0:T(8,128)S(1)}, f32[136,128]{1,0:T(8,128)S(1)}, u32[]{:S(2)}, u32[]{:S(2)}) collective-permute-start(f32[136,128]{1,0:T(8,128)S(1)} %pad_maximum_fusion.8), channel_id=1, source_target_pairs={{0,8},{1,9},{2,10},{3,11},{4,12},{5,13},{6,14},{7,15},{8,0},{9,1},... | collective-permute-start | bytes 208904 | tf_op jit(solution)/shard_map/scatter_moments/ppermute | solution.py:66
  86.1 5.6 %collective-permute-start.12 = (f32[128,128]{1,0:T(8,128)S(1)}, f32[128,128]{1,0:T(8,128)S(1)}, u32[]{:S(2)}, u32[]{:S(2)}) collective-permute-start(f32[128,128]{1,0:T(8,128)S(1)} %slice_add_fusion.4.refs_0_), channel_id=1, source_target_pairs={{0,8},{1,9},{2,10},{3,11},{4,12},{5,13},{6,14},{7,15},{8,0},{9,1},... | collective-permute-start | bytes 196616 | tf_op jit(solution)/shard_map/gather_moments/ppermute | solution.py:66
  91.8 5.0 %collective-permute-start.13 = (f32[256,128]{1,0:T(8,128)S(1)}, f32[256,128]{1,0:T(8,128)S(1)}, u32[]{:S(2)}, u32[]{:S(2)}) collective-permute-start(f32[256,128]{1,0:T(8,128)S(1)} %pad_maximum_fusion.7), channel_id=1, source_target_pairs={{0,4},{1,5},{2,6},{3,7},{4,0},{5,1},{6,2},{7,3},{8,12},{9,13},{10,... | collective-permute-start | bytes 393224 | tf_op jit(solution)/shard_map/gather_moments/ppermute | solution.py:66
  96.8 9.3 %collective-permute-start.14 = (f32[512,128]{1,0:T(8,128)S(1)}, f32[512,128]{1,0:T(8,128)S(1)}, u32[]{:S(2)}, u32[]{:S(2)}) collective-permute-start(f32[512,128]{1,0:T(8,128)S(1)} %pad_maximum_fusion.5), channel_id=1, source_target_pairs={{0,16},{1,3},{2,18},{3,1},{4,20},{5,7},{6,22},{7,5},{8,24},{9,11},... | collective-permute-start | bytes 786440 | tf_op jit(solution)/shard_map/gather_moments/ppermute | solution.py:66
  106.2 9.2 %collective-permute-start.15 = (f32[1024,128]{1,0:T(8,128)S(1)}, f32[1024,128]{1,0:T(8,128)S(1)}, u32[]{:S(2)}, u32[]{:S(2)}) collective-permute-start(f32[1024,128]{1,0:T(8,128)S(1)} %pad_maximum_fusion.2), channel_id=1, source_target_pairs={{0,2},{1,17},{2,0},{3,19},{4,6},{5,21},{6,4},{7,23},{8,10},{9,25},... | collective-permute-start | bytes 1572872 | tf_op jit(solution)/shard_map/gather_moments/ppermute | solution.py:66
  115.4 2.7 %collective-permute-start.20 = (f32[1024,128]{1,0:T(8,128)S(1)}, f32[1024,128]{1,0:T(8,128)S(1)}, u32[]{:S(2)}, u32[]{:S(2)}) collective-permute-start(f32[1024,128]{1,0:T(8,128)S(1)} %collective-permute-done.15.refs_4_), channel_id=1, source_target_pairs={{0,1},{1,0},{2,3},{3,2},{4,5},{5,4},{6,7},{7,6},{8,9},{9,8},{10,11... | collective-permute-start | bytes 1572872 | tf_op jit(solution)/shard_map/gather_moments/ppermute | solution.py:66
  115.4 2.7 %collective-permute-start.19 = (f32[512,128]{1,0:T(8,128)S(1)}, f32[512,128]{1,0:T(8,128)S(1)}, u32[]{:S(2)}, u32[]{:S(2)}) collective-permute-start(f32[512,128]{1,0:T(8,128)S(1)} %collective-permute-done.14.refs_3_), channel_id=1, source_target_pairs={{0,1},{1,0},{2,3},{3,2},{4,5},{5,4},{6,7},{7,6},{8,9},{9,8},{10,11... | collective-permute-start | bytes 786440 | tf_op jit(solution)/shard_map/gather_moments/ppermute | solution.py:66
  116.0 1.9 %collective-permute-start.16 = (f32[128,128]{1,0:T(8,128)S(1)}, f32[128,128]{1,0:T(8,128)S(1)}, u32[]{:S(2)}, u32[]{:S(2)}) collective-permute-start(f32[128,128]{1,0:T(8,128)S(1)} %slice_add_fusion.4.refs_0_), channel_id=1, source_target_pairs={{0,1},{1,0},{2,3},{3,2},{4,5},{5,4},{6,7},{7,6},{8,9},{9,8},{10,11... | collective-permute-start | bytes 196616 | tf_op jit(solution)/shard_map/gather_moments/ppermute | solution.py:66
  116.0 2.0 %collective-permute-start.17 = (f32[128,128]{1,0:T(8,128)S(1)}, f32[128,128]{1,0:T(8,128)S(1)}, u32[]{:S(2)}, u32[]{:S(2)}) collective-permute-start(f32[128,128]{1,0:T(8,128)S(1)} %collective-permute-done.12.refs_1_), channel_id=1, source_target_pairs={{0,1},{1,0},{2,3},{3,2},{4,5},{5,4},{6,7},{7,6},{8,9},{9,8},{10,11... | collective-permute-start | bytes 196616 | tf_op jit(solution)/shard_map/gather_moments/ppermute | solution.py:66
  116.5 1.6 %collective-permute-start.18 = (f32[256,128]{1,0:T(8,128)S(1)}, f32[256,128]{1,0:T(8,128)S(1)}, u32[]{:S(2)}, u32[]{:S(2)}) collective-permute-start(f32[256,128]{1,0:T(8,128)S(1)} %collective-permute-done.13.refs_2_), channel_id=1, source_target_pairs={{0,1},{1,0},{2,3},{3,2},{4,5},{5,4},{6,7},{7,6},{8,9},{9,8},{10,11... | collective-permute-start | bytes 393224 | tf_op jit(solution)/shard_map/gather_moments/ppermute | solution.py:66

commit v2 on v0

v2 whole, which is shorter than its diff:
```python
import functools
import math

import jax
import jax.numpy as jnp
import numpy as np
from jax import lax
from jax.experimental import pallas as pl
from jax.experimental.pallas import tpu as pltpu
from jax.sharding import PartitionSpec as P

F32 = jnp.float32
BF16 = jnp.bfloat16
LANES = 128
COUNT_ROWS = 8
LOG2E = math.log2(math.e)
LN2 = math.log(2.0)
BLOCK = 1024
VMEM_MIB = 40


class Plan:
    def __init__(self, groups, owners, comps):
        self.devices = groups * owners
        self.owners = owners
        owner_bits = owners.bit_length() - 1
        group_bits = groups.bit_length() - 1
        assert owners == 1 << owner_bits and groups == 1 << group_bits and owner_bits >= 4
        piece = comps // owners
        self.unit = max(comps // self.devices, min(16, piece))
        self.units = comps // self.unit
        per = piece // self.unit
        splits = self.units.bit_length() - 1
        group_split = splits - owner_bits
        grp = [owner_bits + b for b in range(group_bits)]
        first, second, third, *others = [1] + grp[:group_split] + list(range(2, owner_bits))
        orders = (
            ((first, second, third), (third, first, second)),
            ((second, third, first), (second, first, third)),
        )
        self.halving = [
            [(0, 0)] + list(zip(zero, one)) + [(b, b) for b in others] for zero, one in orders
        ]
        self.whole = [(b, b) for b in grp[group_split:]]
        down = list(range(owner_bits - 1, 0, -1))
        self.gather = list(zip(down, down[:-2] + [down[-1], down[-2]]))
        n = self.devices
        gather_at = np.zeros((n, owners), np.int32)
        slot_chunk = np.zeros((2, n, self.units), np.int32)
        steps = self.gather + [(0, 0)]
        for d in range(n):
            for p in range(owners):
                e = d
                for t in reversed(range(len(steps))):
                    if p >> t & 1:
                        e ^= 1 << steps[t][e & 1]
                gather_at[d, p] = e % owners
            for stream, halving in enumerate(self.halving):
                for j in range(self.units):
                    e = d
                    for s, step in enumerate(halving):
                        if j >> (splits - 1 - s) & 1:
                            e ^= 1 << step[e & 1]
                    slot_chunk[stream, d, j] = (e % owners) * per + (e // owners) % per
        unit_chunk = (gather_at[:, :, None] * per + np.arange(per)).reshape(n, self.units)
        unit_slot = [np.take_along_axis(np.argsort(c, axis=1), unit_chunk, axis=1) for c in slot_chunk]
        self.tables = np.stack([unit_chunk, *unit_slot, *slot_chunk], axis=1).astype(np.int32)

    def swap(self, value, step):
        pairs = [(d, d ^ (1 << step[d & 1])) for d in range(self.devices)]
        return lax.ppermute(value, ("grp", "comp"), pairs)


def columns(row, height):
    return jnp.broadcast_to(row, (height, LANES)).T


def mixture_kernel(plan, pieces, block, table, *refs):
    mean_refs, variance_refs = refs[:pieces], refs[pieces : 2 * pieces]
    logits_ref, features_ref = refs[2 * pieces : 2 * pieces + 2]
    sent_refs = refs[2 * pieces + 2 : 2 * pieces + 4]
    kept_refs = refs[2 * pieces + 4 : 2 * pieces + 6]
    scores_ref = refs[2 * pieces + 6]
    weights, offsets, moments, partial, staged = refs[2 * pieces + 7 :]
    comps = weights.shape[0]
    count, width = features_ref.shape
    unit = plan.unit

    logits = logits_ref[...]
    shifted = logits - jnp.max(logits)
    log_weights = shifted - jnp.log(jnp.sum(jnp.exp(shifted)))
    for b in range(comps // LANES):
        staged[b * LANES : (b + 1) * LANES, :] = columns(log_weights[b : b + 1, :], LANES)
    at = 0
    for mean_ref, variance_ref in zip(mean_refs, variance_refs):
        for first in range(0, mean_ref.shape[0], unit):
            here = slice(at, at + unit)
            mean = mean_ref[first : first + unit, :]
            variance = variance_ref[first : first + unit, :]
            inverse = 1.0 / variance
            linear = mean * inverse
            constant = jnp.sum(jnp.log(variance) + mean * linear, axis=1, keepdims=True)
            chunk = pl.multiple_of(table[0, at // unit] * unit, unit)
            log_weight = staged[pl.ds(chunk, unit), :]
            offsets[here, :] = (
                log_weight - 0.5 * constant - 0.5 * width * math.log(2.0 * math.pi)
            ) * LOG2E
            square = inverse * (-0.5 * LOG2E)
            linear = linear * LOG2E
            square_high = square.astype(BF16)
            linear_high = linear.astype(BF16)
            weights[here, :width] = square_high
            weights[here, width : 2 * width] = square_high
            weights[here, 2 * width : 3 * width] = linear_high
            weights[here, 3 * width : 4 * width] = (square - square_high.astype(F32)).astype(BF16)
            weights[here, 4 * width :] = (linear - linear_high.astype(F32)).astype(BF16)
            at += unit

    for first in range(0, count, block):
        rows = features_ref[first : first + block, :]
        values = rows.astype(F32)
        squares = values * values
        high = squares.astype(BF16)
        low = (squares - high.astype(F32)).astype(BF16)
        scores = lax.dot_general(
            weights[...],
            jnp.concatenate([low, high, rows, high, rows], axis=1),
            (((1,), (1,)), ((), ())),
            preferred_element_type=F32,
        )
        scores = scores + jnp.tile(offsets[...], (1, block // LANES))
        highest = jnp.max(scores, axis=0, keepdims=True)
        exponent = jnp.exp2(scores - highest)
        totals = jnp.sum(exponent, axis=0, keepdims=True)
        responsibility = (exponent * (1.0 / totals)).astype(BF16)
        scores_ref[:, first : first + block] = (highest + jnp.log2(totals)) * (LN2 / width)
        added = jnp.dot(
            responsibility, jnp.concatenate([rows, high], axis=1), preferred_element_type=F32
        )
        rounded = responsibility.astype(F32)
        counted = rounded[:, :LANES]
        for b in range(1, block // LANES):
            counted = counted + rounded[:, b * LANES : (b + 1) * LANES]
        if first == 0:
            moments[...] = added
            partial[...] = counted
        else:
            moments[...] += added
            partial[...] += counted

    parts = width // LANES
    units = comps // unit
    half = comps // 2 * parts
    for u in range(units):
        chunk = pl.multiple_of(table[0, u] * unit, unit)
        staged[pl.ds(chunk, unit), :] = partial[u * unit : (u + 1) * unit, :]
    for b in range(comps // LANES):
        line = jnp.sum(staged[b * LANES : (b + 1) * LANES, :].T, axis=0, keepdims=True)
        sent_refs[0][half + b : half + b + 1, :] = line
        kept_refs[0][half + b : half + b + 1, :] = line
    for u in range(units):
        targets = kept_refs if u < units // 2 else sent_refs
        for stream, target in enumerate(targets):
            first = pl.multiple_of(table[1 + stream, u] % (units // 2) * (unit * parts), unit)
            for part in range(parts):
                at = stream * width + part * LANES
                target[pl.ds(first + part * unit, unit), :] = moments[
                    u * unit : (u + 1) * unit, at : at + LANES
                ]


def mixture(plan, table, means, variances, logits, features):
    count, width = features.shape
    comps = sum(p.shape[0] for p in means)
    half = comps // 2 * (width // LANES)
    shapes = [(half + COUNT_ROWS, LANES), (half, LANES)] * 2 + [(1, count)]
    vmem = pl.BlockSpec(memory_space=pltpu.VMEM)
    outs = pl.pallas_call(
        functools.partial(mixture_kernel, plan, len(means), min(BLOCK, count)),
        in_specs=[pl.BlockSpec(memory_space=pltpu.SMEM)] + [vmem] * (2 * len(means) + 2),
        out_specs=[vmem] * 5,
        out_shape=[jax.ShapeDtypeStruct(s, F32) for s in shapes],
        scratch_shapes=[
            pltpu.VMEM((comps, 5 * width), BF16),
            pltpu.VMEM((comps, LANES), F32),
            pltpu.VMEM((comps, 2 * width), F32),
            pltpu.VMEM((comps, LANES), F32),
            pltpu.VMEM((comps, LANES), F32),
        ],
        compiler_params=pltpu.CompilerParams(vmem_limit_bytes=VMEM_MIB * 2**20),
        cost_estimate=pl.CostEstimate(
            flops=14 * comps * count * width, bytes_accessed=8 * 2**20, transcendentals=comps * count
        ),
    )(table, *means, *variances, logits, features)
    return outs[:2], outs[2:4], outs[4]


def update_kernel(plan, pieces, total_rows, table, *refs):
    first_refs, second_refs = refs[:pieces], refs[pieces : 2 * pieces]
    counts_ref = refs[2 * pieces]
    means_ref, variances_ref, log_weights_ref, staged = refs[2 * pieces + 1 :]
    comps, width = means_ref.shape
    unit = plan.unit
    parts = width // LANES
    denominator = counts_ref[...] + 1.0
    log_weights_ref[...] = jnp.log(denominator / total_rows)
    inverse = 1.0 / denominator
    for b in range(comps // LANES):
        staged[b * LANES : (b + 1) * LANES, :] = columns(inverse[b : b + 1, :], LANES)
    for stream, stream_refs in enumerate((first_refs, second_refs)):
        slot = 0
        for ref in stream_refs:
            for first in range(0, ref.shape[0], unit * parts):
                chunk = pl.ds(pl.multiple_of(table[3 + stream, slot] * unit, unit), unit)
                scale = staged[chunk, :]
                for part in range(parts):
                    lanes = slice(part * LANES, (part + 1) * LANES)
                    moment = ref[first + part * unit : first + (part + 1) * unit, :]
                    if stream == 0:
                        means_ref[chunk, lanes] = moment * scale
                    else:
                        mean = means_ref[chunk, lanes]
                        variances_ref[chunk, lanes] = (moment + 1.0) * scale - mean * mean + 0.01
                slot += 1


def update(plan, table, first, second, counts, comps, width, total_rows):
    vmem = pl.BlockSpec(memory_space=pltpu.VMEM)
    shapes = [(comps, width), (comps, width), counts.shape]
    return pl.pallas_call(
        functools.partial(update_kernel, plan, len(first), total_rows),
        in_specs=[pl.BlockSpec(memory_space=pltpu.SMEM)] + [vmem] * (2 * len(first) + 1),
        out_specs=[vmem] * 3,
        scratch_shapes=[pltpu.VMEM((comps, LANES), F32)],
        out_shape=[jax.ShapeDtypeStruct(s, F32) for s in shapes],
        compiler_params=pltpu.CompilerParams(vmem_limit_bytes=16 * 2**20),
        cost_estimate=pl.CostEstimate(flops=8 * comps * width, bytes_accessed=16 * comps * width, transcendentals=0),
    )(table, *first, *second, counts)


def gather(plan, streams, steps):
    held = streams
    for step in steps[:-1]:
        held = [jnp.concatenate([h, plan.swap(h, at)], axis=0) for h, at in zip(held, step)]
    last = [plan.swap(h, at) for h, at in zip(held, steps[-1])]
    mates = [plan.swap(h, (0, 0)) for h in held]
    return [[h, l, m, plan.swap(l, (0, 0))] for h, l, m in zip(held, last, mates)]


def scatter(plan, sent, kept):
    rows = kept[1].shape[0]
    counts = kept[0][rows:]
    kept = [kept[0][:rows], kept[1]]
    for at, step in enumerate(zip(*plan.halving)):
        arrived = [plan.swap(s, pair) for s, pair in zip(sent, step)]
        counts = counts + arrived[0][rows:]
        kept = [k + a[:rows] for k, a in zip(kept, arrived)]
        if at + 1 < len(plan.halving[0]):
            rows //= 2
            sent = [jnp.concatenate([kept[0][rows:], counts], axis=0), kept[1][rows:]]
            kept = [k[:rows] for k in kept]
    for pair in plan.whole:
        arrived = [plan.swap(jnp.concatenate([kept[0], counts], axis=0), pair), plan.swap(kept[1], pair)]
        counts = counts + arrived[0][rows:]
        kept = [k + a[:rows] for k, a in zip(kept, arrived)]
    return kept, 0.5 * (counts + plan.swap(counts, (0, 0)))


def on_device(plan, features, means, variances, weight_logits):
    comps = weight_logits.shape[0]
    width = means.shape[1]
    me = lax.axis_index(("grp", "comp"))
    table = lax.dynamic_index_in_dim(jnp.asarray(plan.tables), me, 0, keepdims=False)

    with jax.named_scope("gather_parameters"):
        all_means, all_variances = gather(plan, [means, variances], [(g, g) for g in plan.gather])
    sent, kept, row_scores = mixture(
        plan, table, all_means, all_variances, weight_logits.reshape(comps // LANES, LANES), features
    )
    with jax.named_scope("scatter_moments"):
        kept, counts = scatter(plan, sent, kept)
    with jax.named_scope("gather_moments"):
        first, second = gather(plan, kept, list(zip(*plan.halving))[:0:-1])

    total_rows = float(features.shape[0] * plan.devices + comps)
    fresh_means, fresh_variances, fresh_weights = update(
        plan, table, first, second, counts, comps, width, total_rows
    )
    return fresh_means, fresh_variances, fresh_weights.reshape(comps), row_scores.reshape(-1)


def solution(mesh):
    def whole(features, means, variances, weight_logits):
        plan = Plan(mesh.shape["grp"], mesh.shape["comp"], weight_logits.shape[0])
        return jax.shard_map(
            functools.partial(on_device, plan),
            mesh=mesh,
            in_specs=(P(("grp", "comp"), None), P("comp", None), P("comp", None), P()),
            out_specs=(P(), P(), P(), P(("grp", "comp"))),
            check_vma=False,
        )(features, means, variances, weight_logits)

    return whole
```

time: 254 us -> 92.2 us (0.36)
  blocking collectives: 104 us -> 0 us
  waiting for transfers between devices: 89.2 us -> 37.1 us
  starting transfers between devices: 0.2 us -> 38.7 us
  matrix products: 22.6 us -> 0 us
  between operations: 16 us -> 0.89 us
  other arithmetic: 15.4 us -> 1.24 us
  Pallas kernels: 0 us -> 12.3 us
  local copies, waits for them, and re-layouts: 5.93 us -> 1.67 us
    unnamed x3 -> x0, blocking collectives: 99.4 us -> none
    all_gather x3 -> x0, waiting for transfers between devices: 44.2 us -> none  [the longest x1 39.8 us: on_device(): lax.all_gather(owned_variances, 'comp', axis=0, tiled=True)]
    ppermute x0 -> x33, starting transfers between devices: none -> 38.7 us  [swap(): return lax.ppermute(value, ('grp', 'comp'), pairs)]
    ppermute x0 -> x33, waiting for transfers between devices: none -> 37.1 us  [swap(): return lax.ppermute(value, ('grp', 'comp'), pairs)]
    psum x1 -> x0, waiting for transfers between devices: 22.6 us -> none  [on_device(): lax.psum((owned_moments, owned_counts), 'grp')]
    dot_general x12 -> x0, matrix products: 22.6 us -> none  [the longest x4 17.2 us: on_device(): jnp.dot(jnp.concatenate([squared, values], axis=1), all_coefficient.T, pr...]
    reduce_scatter x1 -> x0, waiting for transfers between devices: 21.8 us -> none  [on_device(): lax.psum_scatter(moments, 'comp', scatter_dimension=0, tiled=True)]
    pallas_call x0 -> x2, Pallas kernels: none -> 12.3 us  [the longest x1 9.88 us: mixture(): pl.pallas_call(functools.partial(mixture_kernel, plan, len(means), min(BL...]
  transfers between devices with their start and end apart: 5 -> 33, of which waited for: 4 -> 19; matrix products, arithmetic and copies ran while one was open for 5% -> 3% of each run, Pallas kernels for 0% -> 0%
where the time goes in v2:
time: 92.2 us; the launch traced here: 91.9 us
  starting transfers between devices  38.7 us (42%)
  waiting for transfers between devices  37.1 us (40%)
  Pallas kernels  12.3 us (13%)
  local copies, waits for them, and re-layouts  1.67 us (2%)
  other arithmetic  1.24 us (1%)
    ppermute x33, starting transfers between devices, swap(): return lax.ppermute(value, ('grp', 'comp'), pairs)  38.7 us
    ppermute x33, waiting for transfers between devices, swap(): return lax.ppermute(value, ('grp', 'comp'), pairs)  37.1 us
    pallas_call x1, Pallas kernels, mixture(): pl.pallas_call(functools.partial(mixture_kernel, plan, len(means), min(BL...  9.88 us
    pallas_call x1, Pallas kernels, update(): pl.pallas_call(functools.partial(update_kernel, plan, len(first), total_r...  2.37 us
  transfers between devices with their start and end apart: 33, of which 19 were waited for; matrix products, arithmetic and copies ran while one was open for 3% of the time, Pallas kernels for 0%

profile of v2, /device:TPU:0, one launch (start us, length us, event | category | flops | bytes accessed | tf_op | source)
XLA Modules:
  0.0 91.9 jit_solution(10232966546500058666)
XLA Ops:
  0.7 4.1 %collective-permute-start = (f32[64,256]{1,0:T(8,128)}, f32[64,256]{1,0:T(8,128)S(1)}, u32[]{:S(2)}, u32[]{:S(2)}) collective-permute-start(f32[64,256]{1,0:T(8,128)} %param.6), channel_id=1, source_target_pairs={{0,8},{1,9},{2,10},{3,11},{4,12},{5,13},{6,14},{7,15},{8,0},{9,1},... | collective-permute-start | bytes 196616 | tf_op jit(solution)/shard_map/gather_parameters/ppermute | solution.py:71
  4.8 0.1 collective-permute-start.5
  4.8 0.8 constant_dynamic-update-slice_fusion.2
  5.7 2.9 %collective-permute-done = f32[64,256]{1,0:T(8,128)S(1)} collective-permute-done((f32[64,256]{1,0:T(8,128)}, f32[64,256]{1,0:T(8,128)S(1)}, u32[]{:S(2)}, u32[]{:S(2)}) %collective-permute-start) | collective-permute-done | bytes 65568 | tf_op jit(solution)/shard_map/gather_parameters/ppermute | solution.py:71
  8.6 0.8 pad_maximum_fusion.4
  9.5 2.2 %collective-permute-start.1 = (f32[128,256]{1,0:T(8,128)S(1)}, f32[128,256]{1,0:T(8,128)S(1)}, u32[]{:S(2)}, u32[]{:S(2)}) collective-permute-start(f32[128,256]{1,0:T(8,128)S(1)} %pad_maximum_fusion.4), channel_id=1, source_target_pairs={{0,4},{1,3},{2,6},{3,1},{4,0},{5,7},{6,2},{7,5},{8,12},{9,11},{10,... | collective-permute-start | bytes 393224 | tf_op jit(solution)/shard_map/gather_parameters/ppermute | solution.py:71
  11.7 0.5 collective-permute-start.6
  12.2 4.6 %collective-permute-done.6 = f32[128,256]{1,0:T(8,128)S(1)} collective-permute-done((f32[128,256]{1,0:T(8,128)S(1)}, f32[128,256]{1,0:T(8,128)S(1)}, u32[]{:S(2)}, u32[]{:S(2)}) %collective-permute-start.6) | collective-permute-done | bytes 131104 | tf_op jit(solution)/shard_map/gather_parameters/ppermute | solution.py:71
  16.8 1.6 %collective-permute-start.7 = (f32[256,256]{1,0:T(8,128)S(1)}, f32[256,256]{1,0:T(8,128)S(1)}, u32[]{:S(2)}, u32[]{:S(2)}) collective-permute-start(f32[256,256]{1,0:T(8,128)S(1)} %constant_dynamic-update-slice_fusion.3.refs_4_), channel_id=1, source_target_pairs={{0,2},{1,5},{2,0},{3,7},{4,6},{5,1},{6,4},{7,3},{8,10},{9,13},{10,... | collective-permute-start | bytes 786440 | tf_op jit(solution)/shard_map/gather_parameters/ppermute | solution.py:71
  18.3 0.0 collective-permute-done.1
  18.3 0.6 collective-permute-start.2
  18.9 0.0 collective-permute-start.8
  18.9 0.5 collective-permute-start.3
  19.5 3.8 %collective-permute-done.7.refs_5_ = f32[256,256]{1,0:T(8,128)S(1)} collective-permute-done((f32[256,256]{1,0:T(8,128)S(1)}, f32[256,256]{1,0:T(8,128)S(1)}, u32[]{:S(2)}, u32[]{:S(2)}) %collective-permute-start.7) | collective-permute-done | bytes 262176 | tf_op jit(solution)/shard_map/gather_parameters/ppermute | solution.py:71
  23.2 0.0 collective-permute-start.9
  23.2 2.8 %collective-permute-done.2.refs_1_ = f32[256,256]{1,0:T(8,128)S(1)} collective-permute-done((f32[256,256]{1,0:T(8,128)S(1)}, f32[256,256]{1,0:T(8,128)S(1)}, u32[]{:S(2)}, u32[]{:S(2)}) %collective-permute-start.2) | collective-permute-done | bytes 262176 | tf_op jit(solution)/shard_map/gather_parameters/ppermute | solution.py:71
  26.0 0.0 collective-permute-start.4
  26.0 0.7 dynamic-slice_bitcast_fusion.table
  26.7 0.0 collective-permute-done.8.refs_6_
  26.7 0.0 collective-permute-done.3.refs_2_
  26.7 0.0 collective-permute-done.9.refs_7_
  26.7 0.8 collective-permute-done.4.refs_3_
  27.6 9.9 %shard_map.84 = (f32[1032,128]{1,0:T(8,128)S(1)}, f32[1024,128]{1,0:T(8,128)S(1)}, f32[1032,128]{1,0:T(8,128)S(1)}, f32[1024,128]{1,0:T(8,128)S(1)}, f32[1,2048]{1,0:T(1,128)}) custom-call(s32[5,32]{1,0:T(8,128)S(1)} %dynamic-slice_bitcast_fusion.table, f32[256,256]{1,0:T(8,128)S(1)} %constant_dynamic-update-slice_fusion.refs_0_, ...), custom_call_target="tpu_custom_call" | custom-call | flops 7516192768 | bytes 8388608 | tf_op jit(solution)/shard_map/pallas_call | solution.py:178
  37.4 0.1 collective-permute-start.10
  37.6 0.4 collective-permute-start.21
  37.9 2.2 %collective-permute-done.21 = f32[1024,128]{1,0:T(8,128)S(1)} collective-permute-done((f32[1024,128]{1,0:T(8,128)S(1)}, f32[1024,128]{1,0:T(8,128)S(1)}, u32[]{:S(2)}, u32[]{:S(2)}) %collective-permute-start.21) | collective-permute-done | bytes 524320 | tf_op jit(solution)/shard_map/scatter_moments/ppermute | solution.py:71
  40.1 0.1 add.66
  40.2 1.6 %collective-permute-start.22 = (f32[512,128]{1,0:T(8,128)S(1)}, f32[512,128]{1,0:T(8,128)S(1)}, u32[]{:S(2)}, u32[]{:S(2)}) collective-permute-start(f32[512,128]{1,0:T(8,128)S(1)} %slice.130), channel_id=1, source_target_pairs={{0,16},{1,17},{2,18},{3,19},{4,20},{5,21},{6,22},{7,23},{8,24},{9,... | collective-permute-start | bytes 786440 | tf_op jit(solution)/shard_map/scatter_moments/ppermute | solution.py:71
  41.8 0.0 collective-permute-done.10
  41.8 0.1 slice_add_fusion
  41.9 1.6 %collective-permute-start.11 = (f32[520,128]{1,0:T(8,128)S(1)}, f32[520,128]{1,0:T(8,128)S(1)}, u32[]{:S(2)}, u32[]{:S(2)}) collective-permute-start(f32[520,128]{1,0:T(8,128)S(1)} %pad_maximum_fusion), channel_id=1, source_target_pairs={{0,2},{1,5},{2,0},{3,7},{4,6},{5,1},{6,4},{7,3},{8,10},{9,13},{10,... | collective-permute-start | bytes 798728 | tf_op jit(solution)/shard_map/scatter_moments/ppermute | solution.py:71
  43.5 5.1 %collective-permute-done.22 = f32[512,128]{1,0:T(8,128)S(1)} collective-permute-done((f32[512,128]{1,0:T(8,128)S(1)}, f32[512,128]{1,0:T(8,128)S(1)}, u32[]{:S(2)}, u32[]{:S(2)}) %collective-permute-start.22) | collective-permute-done | bytes 262176 | tf_op jit(solution)/shard_map/scatter_moments/ppermute | solution.py:71
  48.7 1.4 %collective-permute-start.23 = (f32[256,128]{1,0:T(8,128)S(1)}, f32[256,128]{1,0:T(8,128)S(1)}, u32[]{:S(2)}, u32[]{:S(2)}) collective-permute-start(f32[256,128]{1,0:T(8,128)S(1)} %slice.132), channel_id=1, source_target_pairs={{0,4},{1,3},{2,6},{3,1},{4,0},{5,7},{6,2},{7,5},{8,12},{9,11},{10,... | collective-permute-start | bytes 393224 | tf_op jit(solution)/shard_map/scatter_moments/ppermute | solution.py:71
  50.1 1.6 %collective-permute-start.12 = (f32[264,128]{1,0:T(8,128)S(1)}, f32[264,128]{1,0:T(8,128)S(1)}, u32[]{:S(2)}, u32[]{:S(2)}) collective-permute-start(f32[264,128]{1,0:T(8,128)S(1)} %pad_maximum_fusion.3), channel_id=1, source_target_pairs={{0,16},{1,3},{2,18},{3,1},{4,20},{5,7},{6,22},{7,5},{8,24},{9,11},... | collective-permute-start | bytes 405512 | tf_op jit(solution)/shard_map/scatter_moments/ppermute | solution.py:71
  51.7 2.0 %collective-permute-done.23 = f32[256,128]{1,0:T(8,128)S(1)} collective-permute-done((f32[256,128]{1,0:T(8,128)S(1)}, f32[256,128]{1,0:T(8,128)S(1)}, u32[]{:S(2)}, u32[]{:S(2)}) %collective-permute-start.23) | collective-permute-done | bytes 131104 | tf_op jit(solution)/shard_map/scatter_moments/ppermute | solution.py:71
  53.7 1.5 %collective-permute-start.24 = (f32[128,128]{1,0:T(8,128)S(1)}, f32[128,128]{1,0:T(8,128)S(1)}, u32[]{:S(2)}, u32[]{:S(2)}) collective-permute-start(f32[128,128]{1,0:T(8,128)S(1)} %slice.134), channel_id=1, source_target_pairs={{0,2},{1,5},{2,0},{3,7},{4,6},{5,1},{6,4},{7,3},{8,10},{9,13},{10,... | collective-permute-start | bytes 196616 | tf_op jit(solution)/shard_map/scatter_moments/ppermute | solution.py:71
  55.3 1.4 %collective-permute-start.13 = (f32[136,128]{1,0:T(8,128)S(1)}, f32[136,128]{1,0:T(8,128)S(1)}, u32[]{:S(2)}, u32[]{:S(2)}) collective-permute-start(f32[136,128]{1,0:T(8,128)S(1)} %pad_maximum_fusion.8), channel_id=1, source_target_pairs={{0,4},{1,17},{2,6},{3,19},{4,0},{5,21},{6,2},{7,23},{8,12},{9,25},... | collective-permute-start | bytes 208904 | tf_op jit(solution)/shard_map/scatter_moments/ppermute | solution.py:71
  56.7 1.3 %collective-permute-done.24 = f32[128,128]{1,0:T(8,128)S(1)} collective-permute-done((f32[128,128]{1,0:T(8,128)S(1)}, f32[128,128]{1,0:T(8,128)S(1)}, u32[]{:S(2)}, u32[]{:S(2)}) %collective-permute-start.24) | collective-permute-done | bytes 65568 | tf_op jit(solution)/shard_map/scatter_moments/ppermute | solution.py:71
  58.1 3.3 %collective-permute-start.25 = (f32[64,128]{1,0:T(8,128)S(1)}, f32[64,128]{1,0:T(8,128)S(1)}, u32[]{:S(2)}, u32[]{:S(2)}) collective-permute-start(f32[64,128]{1,0:T(8,128)S(1)} %slice.136), channel_id=1, source_target_pairs={{0,8},{1,9},{2,10},{3,11},{4,12},{5,13},{6,14},{7,15},{8,0},{9,1},... | collective-permute-start | bytes 98312 | tf_op jit(solution)/shard_map/scatter_moments/ppermute | solution.py:71
  61.5 1.6 %collective-permute-start.14 = (f32[72,128]{1,0:T(8,128)S(1)}, f32[72,128]{1,0:T(8,128)S(1)}, u32[]{:S(2)}, u32[]{:S(2)}) collective-permute-start(f32[72,128]{1,0:T(8,128)S(1)} %pad_maximum_fusion.11), channel_id=1, source_target_pairs={{0,8},{1,9},{2,10},{3,11},{4,12},{5,13},{6,14},{7,15},{8,0},{9,1},... | collective-permute-start | bytes 110600 | tf_op jit(solution)/shard_map/scatter_moments/ppermute | solution.py:71
  63.1 0.2 collective-permute-done.25
  63.3 3.3 %collective-permute-start.26 = (f32[64,128]{1,0:T(8,128)S(1)}, f32[64,128]{1,0:T(8,128)S(1)}, u32[]{:S(2)}, u32[]{:S(2)}) collective-permute-start(f32[64,128]{1,0:T(8,128)S(1)} %slice_add_fusion.7), channel_id=1, source_target_pairs={{0,8},{1,9},{2,10},{3,11},{4,12},{5,13},{6,14},{7,15},{8,0},{9,1},... | collective-permute-start | bytes 98312 | tf_op jit(solution)/shard_map/gather_moments/ppermute | solution.py:71
  66.7 0.6 collective-permute-done.14
  67.2 1.2 %collective-permute-start.15 = (f32[64,128]{1,0:T(8,128)S(1)}, f32[64,128]{1,0:T(8,128)S(1)}, u32[]{:S(2)}, u32[]{:S(2)}) collective-permute-start(f32[64,128]{1,0:T(8,128)S(1)} %slice_add_fusion.8), channel_id=1, source_target_pairs={{0,8},{1,9},{2,10},{3,11},{4,12},{5,13},{6,14},{7,15},{8,0},{9,1},... | collective-permute-start | bytes 98312 | tf_op jit(solution)/shard_map/gather_moments/ppermute | solution.py:71
  68.4 0.1 collective-permute-done.26
  68.6 1.5 %collective-permute-start.27 = (f32[128,128]{1,0:T(8,128)S(1)}, f32[128,128]{1,0:T(8,128)S(1)}, u32[]{:S(2)}, u32[]{:S(2)}) collective-permute-start(f32[128,128]{1,0:T(8,128)S(1)} %pad_maximum_fusion.10), channel_id=1, source_target_pairs={{0,2},{1,5},{2,0},{3,7},{4,6},{5,1},{6,4},{7,3},{8,10},{9,13},{10,... | collective-permute-start | bytes 196616 | tf_op jit(solution)/shard_map/gather_moments/ppermute | solution.py:71
  70.1 2.0 %collective-permute-done.15 = f32[64,128]{1,0:T(8,128)S(1)} collective-permute-done((f32[64,128]{1,0:T(8,128)S(1)}, f32[64,128]{1,0:T(8,128)S(1)}, u32[]{:S(2)}, u32[]{:S(2)}) %collective-permute-start.15) | collective-permute-done | bytes 32800 | tf_op jit(solution)/shard_map/gather_moments/ppermute | solution.py:71
  72.1 1.2 %collective-permute-start.16 = (f32[128,128]{1,0:T(8,128)S(1)}, f32[128,128]{1,0:T(8,128)S(1)}, u32[]{:S(2)}, u32[]{:S(2)}) collective-permute-start(f32[128,128]{1,0:T(8,128)S(1)} %pad_maximum_fusion.9), channel_id=1, source_target_pairs={{0,4},{1,17},{2,6},{3,19},{4,0},{5,21},{6,2},{7,23},{8,12},{9,25},... | collective-permute-start | bytes 196616 | tf_op jit(solution)/shard_map/gather_moments/ppermute | solution.py:71
  73.2 0.3 collective-permute-done.27
  73.5 1.7 %collective-permute-start.28 = (f32[256,128]{1,0:T(8,128)S(1)}, f32[256,128]{1,0:T(8,128)S(1)}, u32[]{:S(2)}, u32[]{:S(2)}) collective-permute-start(f32[256,128]{1,0:T(8,128)S(1)} %pad_maximum_fusion.7), channel_id=1, source_target_pairs={{0,4},{1,3},{2,6},{3,1},{4,0},{5,7},{6,2},{7,5},{8,12},{9,11},{10,... | collective-permute-start | bytes 393224 | tf_op jit(solution)/shard_map/gather_moments/ppermute | solution.py:71
  75.3 1.1 %collective-permute-done.16 = f32[128,128]{1,0:T(8,128)S(1)} collective-permute-done((f32[128,128]{1,0:T(8,128)S(1)}, f32[128,128]{1,0:T(8,128)S(1)}, u32[]{:S(2)}, u32[]{:S(2)}) %collective-permute-start.16) | collective-permute-done | bytes 65568 | tf_op jit(solution)/shard_map/gather_moments/ppermute | solution.py:71
  76.3 1.6 %collective-permute-start.17 = (f32[256,128]{1,0:T(8,128)S(1)}, f32[256,128]{1,0:T(8,128)S(1)}, u32[]{:S(2)}, u32[]{:S(2)}) collective-permute-start(f32[256,128]{1,0:T(8,128)S(1)} %pad_maximum_fusion.6), channel_id=1, source_target_pairs={{0,16},{1,3},{2,18},{3,1},{4,20},{5,7},{6,22},{7,5},{8,24},{9,11},... | collective-permute-start | bytes 393224 | tf_op jit(solution)/shard_map/gather_moments/ppermute | solution.py:71
  77.9 2.0 %collective-permute-done.28 = f32[256,128]{1,0:T(8,128)S(1)} collective-permute-done((f32[256,128]{1,0:T(8,128)S(1)}, f32[256,128]{1,0:T(8,128)S(1)}, u32[]{:S(2)}, u32[]{:S(2)}) %collective-permute-start.28) | collective-permute-done | bytes 131104 | tf_op jit(solution)/shard_map/gather_moments/ppermute | solution.py:71
  79.9 1.6 %collective-permute-start.29 = (f32[512,128]{1,0:T(8,128)S(1)}, f32[512,128]{1,0:T(8,128)S(1)}, u32[]{:S(2)}, u32[]{:S(2)}) collective-permute-start(f32[512,128]{1,0:T(8,128)S(1)} %pad_maximum_fusion.2.refs_4_), channel_id=1, source_target_pairs={{0,16},{1,17},{2,18},{3,19},{4,20},{5,21},{6,22},{7,23},{8,24},{9,... | collective-permute-start | bytes 786440 | tf_op jit(solution)/shard_map/gather_moments/ppermute | solution.py:71
  81.5 1.6 %collective-permute-start.18 = (f32[512,128]{1,0:T(8,128)S(1)}, f32[512,128]{1,0:T(8,128)S(1)}, u32[]{:S(2)}, u32[]{:S(2)}) collective-permute-start(f32[512,128]{1,0:T(8,128)S(1)} %pad_maximum_fusion.1.refs_0_), channel_id=1, source_target_pairs={{0,2},{1,5},{2,0},{3,7},{4,6},{5,1},{6,4},{7,3},{8,10},{9,13},{10,... | collective-permute-start | bytes 786440 | tf_op jit(solution)/shard_map/gather_moments/ppermute | solution.py:71
  83.1 0.5 collective-permute-start.19
  83.6 2.8 %collective-permute-done.29.refs_5_ = f32[512,128]{1,0:T(8,128)S(1)} collective-permute-done((f32[512,128]{1,0:T(8,128)S(1)}, f32[512,128]{1,0:T(8,128)S(1)}, u32[]{:S(2)}, u32[]{:S(2)}) %collective-permute-start.29) | collective-permute-done | bytes 262176 | tf_op jit(solution)/shard_map/gather_moments/ppermute | solution.py:71
  86.4 1.6 %collective-permute-done.18.refs_1_ = f32[512,128]{1,0:T(8,128)S(1)} collective-permute-done((f32[512,128]{1,0:T(8,128)S(1)}, f32[512,128]{1,0:T(8,128)S(1)}, u32[]{:S(2)}, u32[]{:S(2)}) %collective-permute-start.18) | collective-permute-done | bytes 262176 | tf_op jit(solution)/shard_map/gather_moments/ppermute | solution.py:71
  88.0 0.5 collective-permute-start.32
  88.5 1.0 %collective-permute-done.32 = f32[8,128]{1,0:T(8,128)S(1)} collective-permute-done((f32[8,128]{1,0:T(8,128)S(1)}, f32[8,128]{1,0:T(8,128)S(1)}, u32[]{:S(2)}, u32[]{:S(2)}) %collective-permute-start.32) | collective-permute-done | bytes 4128 | tf_op jit(solution)/shard_map/scatter_moments/ppermute | solution.py:71
  89.5 0.0 collective-permute-done.30.refs_6_
  89.5 0.0 collective-permute-done.19.refs_2_
  89.5 0.0 collective-permute-done.31.refs_7_
  89.5 2.4 %shard_map.85 = (f32[1024,256]{1,0:T(8,128)}, f32[1024,256]{1,0:T(8,128)}, f32[8,128]{1,0:T(8,128)}) custom-call(s32[5,32]{1,0:T(8,128)S(1)} %dynamic-slice_bitcast_fusion.table, f32[512,128]{1,0:T(8,128)S(1)} %pad_maximum_fusion.1.refs_0_, f32[512,128]{1,0:T(8,128)S(1)} %collective-permute-done.18.refs_1_, f32[512,128]{1,0:T(8,128)S(1)} %collective-permute-done.19.refs_2_, ...), custom_call_target="tpu_custom_call" | custom-call | flops 2097152 | bytes 4194304 | tf_op jit(solution)/shard_map/pallas_call | solution.py:230
  (53 shorter events, 0.4 us)
Async XLA Ops:
  0.6 5.0 %copy-start.2 = (f32[64,256]{1,0:T(8,128)S(1)}, f32[64,256]{1,0:T(8,128)}, u32[]{:S(2)}) copy-start(f32[64,256]{1,0:T(8,128)} %param.7) | copy-start | bytes 196612
  0.6 26.9 %copy-start = (bf16[2048,256]{1,0:T(8,128)(2,1)S(1)}, bf16[2048,256]{1,0:T(8,128)(2,1)}, u32[]{:S(2)}) copy-start(bf16[2048,256]{1,0:T(8,128)(2,1)} %refs_9_.1) | copy-start | bytes 3145732
  0.7 8.0 %collective-permute-start = (f32[64,256]{1,0:T(8,128)}, f32[64,256]{1,0:T(8,128)S(1)}, u32[]{:S(2)}, u32[]{:S(2)}) collective-permute-start(f32[64,256]{1,0:T(8,128)} %param.6), channel_id=1, source_target_pairs={{0,8},{1,9},{2,10},{3,11},{4,12},{5,13},{6,14},{7,15},{8,0},{9,1},... | collective-permute-start | bytes 196616 | tf_op jit(solution)/shard_map/gather_parameters/ppermute | solution.py:71
  4.8 7.0 %collective-permute-start.5 = (f32[64,256]{1,0:T(8,128)}, f32[64,256]{1,0:T(8,128)S(1)}, u32[]{:S(2)}, u32[]{:S(2)}) collective-permute-start(f32[64,256]{1,0:T(8,128)} %param.7), channel_id=1, source_target_pairs={{0,8},{1,9},{2,10},{3,11},{4,12},{5,13},{6,14},{7,15},{8,0},{9,1},... | collective-permute-start | bytes 196616 | tf_op jit(solution)/shard_map/gather_parameters/ppermute | solution.py:71
  9.5 8.9 %collective-permute-start.1 = (f32[128,256]{1,0:T(8,128)S(1)}, f32[128,256]{1,0:T(8,128)S(1)}, u32[]{:S(2)}, u32[]{:S(2)}) collective-permute-start(f32[128,256]{1,0:T(8,128)S(1)} %pad_maximum_fusion.4), channel_id=1, source_target_pairs={{0,4},{1,3},{2,6},{3,1},{4,0},{5,7},{6,2},{7,5},{8,12},{9,11},{10,... | collective-permute-start | bytes 393224 | tf_op jit(solution)/shard_map/gather_parameters/ppermute | solution.py:71
  11.7 5.0 %collective-permute-start.6 = (f32[128,256]{1,0:T(8,128)S(1)}, f32[128,256]{1,0:T(8,128)S(1)}, u32[]{:S(2)}, u32[]{:S(2)}) collective-permute-start(f32[128,256]{1,0:T(8,128)S(1)} %pad_maximum_fusion.5), channel_id=1, source_target_pairs={{0,4},{1,3},{2,6},{3,1},{4,0},{5,7},{6,2},{7,5},{8,12},{9,11},{10,... | collective-permute-start | bytes 393224 | tf_op jit(solution)/shard_map/gather_parameters/ppermute | solution.py:71
  16.8 6.4 %collective-permute-start.7 = (f32[256,256]{1,0:T(8,128)S(1)}, f32[256,256]{1,0:T(8,128)S(1)}, u32[]{:S(2)}, u32[]{:S(2)}) collective-permute-start(f32[256,256]{1,0:T(8,128)S(1)} %constant_dynamic-update-slice_fusion.3.refs_4_), channel_id=1, source_target_pairs={{0,2},{1,5},{2,0},{3,7},{4,6},{5,1},{6,4},{7,3},{8,10},{9,13},{10,... | collective-permute-start | bytes 786440 | tf_op jit(solution)/shard_map/gather_parameters/ppermute | solution.py:71
  18.3 7.7 %collective-permute-start.2 = (f32[256,256]{1,0:T(8,128)S(1)}, f32[256,256]{1,0:T(8,128)S(1)}, u32[]{:S(2)}, u32[]{:S(2)}) collective-permute-start(f32[256,256]{1,0:T(8,128)S(1)} %constant_dynamic-update-slice_fusion.refs_0_), channel_id=1, source_target_pairs={{0,2},{1,5},{2,0},{3,7},{4,6},{5,1},{6,4},{7,3},{8,10},{9,13},{10,... | collective-permute-start | bytes 786440 | tf_op jit(solution)/shard_map/gather_parameters/ppermute | solution.py:71
  18.9 7.8 %collective-permute-start.8 = (f32[256,256]{1,0:T(8,128)S(1)}, f32[256,256]{1,0:T(8,128)S(1)}, u32[]{:S(2)}, u32[]{:S(2)}) collective-permute-start(f32[256,256]{1,0:T(8,128)S(1)} %constant_dynamic-update-slice_fusion.3.refs_4_), channel_id=1, source_target_pairs={{0,1},{1,0},{2,3},{3,2},{4,5},{5,4},{6,7},{7,6},{8,9},{9,8},{10,11... | collective-permute-start | bytes 786440 | tf_op jit(solution)/shard_map/gather_parameters/ppermute | solution.py:71
  18.9 7.8 %collective-permute-start.3 = (f32[256,256]{1,0:T(8,128)S(1)}, f32[256,256]{1,0:T(8,128)S(1)}, u32[]{:S(2)}, u32[]{:S(2)}) collective-permute-start(f32[256,256]{1,0:T(8,128)S(1)} %constant_dynamic-update-slice_fusion.refs_0_), channel_id=1, source_target_pairs={{0,1},{1,0},{2,3},{3,2},{4,5},{5,4},{6,7},{7,6},{8,9},{9,8},{10,11... | collective-permute-start | bytes 786440 | tf_op jit(solution)/shard_map/gather_parameters/ppermute | solution.py:71
  23.2 3.5 %collective-permute-start.9 = (f32[256,256]{1,0:T(8,128)S(1)}, f32[256,256]{1,0:T(8,128)S(1)}, u32[]{:S(2)}, u32[]{:S(2)}) collective-permute-start(f32[256,256]{1,0:T(8,128)S(1)} %collective-permute-done.7.refs_5_), channel_id=1, source_target_pairs={{0,1},{1,0},{2,3},{3,2},{4,5},{5,4},{6,7},{7,6},{8,9},{9,8},{10,11... | collective-permute-start | bytes 786440 | tf_op jit(solution)/shard_map/gather_parameters/ppermute | solution.py:71
  26.0 1.5 %collective-permute-start.4 = (f32[256,256]{1,0:T(8,128)S(1)}, f32[256,256]{1,0:T(8,128)S(1)}, u32[]{:S(2)}, u32[]{:S(2)}) collective-permute-start(f32[256,256]{1,0:T(8,128)S(1)} %collective-permute-done.2.refs_1_), channel_id=1, source_target_pairs={{0,1},{1,0},{2,3},{3,2},{4,5},{5,4},{6,7},{7,6},{8,9},{9,8},{10,11... | collective-permute-start | bytes 786440 | tf_op jit(solution)/shard_map/gather_parameters/ppermute | solution.py:71
  26.0 1.5 %copy-start.1 = (f32[1024]{0:T(1024)S(1)}, f32[1024]{0:T(1024)}, u32[]{:S(2)}) copy-start(f32[1024]{0:T(1024)} %param.8) | copy-start | bytes 12292
  37.4 4.3 %collective-permute-start.10 = (f32[1032,128]{1,0:T(8,128)S(1)}, f32[1032,128]{1,0:T(8,128)S(1)}, u32[]{:S(2)}, u32[]{:S(2)}) collective-permute-start(f32[1032,128]{1,0:T(8,128)S(1)} %get-tuple-element.13), channel_id=1, source_target_pairs={{0,1},{1,0},{2,3},{3,2},{4,5},{5,4},{6,7},{7,6},{8,9},{9,8},{10,11... | collective-permute-start | bytes 1585160 | tf_op jit(solution)/shard_map/scatter_moments/ppermute | solution.py:71
  37.6 2.5 %collective-permute-start.21 = (f32[1024,128]{1,0:T(8,128)S(1)}, f32[1024,128]{1,0:T(8,128)S(1)}, u32[]{:S(2)}, u32[]{:S(2)}) collective-permute-start(f32[1024,128]{1,0:T(8,128)S(1)} %get-tuple-element.15), channel_id=1, source_target_pairs={{0,1},{1,0},{2,3},{3,2},{4,5},{5,4},{6,7},{7,6},{8,9},{9,8},{10,11... | collective-permute-start | bytes 1572872 | tf_op jit(solution)/shard_map/scatter_moments/ppermute | solution.py:71
  40.2 8.4 %collective-permute-start.22 = (f32[512,128]{1,0:T(8,128)S(1)}, f32[512,128]{1,0:T(8,128)S(1)}, u32[]{:S(2)}, u32[]{:S(2)}) collective-permute-start(f32[512,128]{1,0:T(8,128)S(1)} %slice.130), channel_id=1, source_target_pairs={{0,16},{1,17},{2,18},{3,19},{4,20},{5,21},{6,22},{7,23},{8,24},{9,... | collective-permute-start | bytes 786440 | tf_op jit(solution)/shard_map/scatter_moments/ppermute | solution.py:71
  41.9 8.1 %collective-permute-start.11 = (f32[520,128]{1,0:T(8,128)S(1)}, f32[520,128]{1,0:T(8,128)S(1)}, u32[]{:S(2)}, u32[]{:S(2)}) collective-permute-start(f32[520,128]{1,0:T(8,128)S(1)} %pad_maximum_fusion), channel_id=1, source_target_pairs={{0,2},{1,5},{2,0},{3,7},{4,6},{5,1},{6,4},{7,3},{8,10},{9,13},{10,... | collective-permute-start | bytes 798728 | tf_op jit(solution)/shard_map/scatter_moments/ppermute | solution.py:71
  48.7 5.0 %collective-permute-start.23 = (f32[256,128]{1,0:T(8,128)S(1)}, f32[256,128]{1,0:T(8,128)S(1)}, u32[]{:S(2)}, u32[]{:S(2)}) collective-permute-start(f32[256,128]{1,0:T(8,128)S(1)} %slice.132), channel_id=1, source_target_pairs={{0,4},{1,3},{2,6},{3,1},{4,0},{5,7},{6,2},{7,5},{8,12},{9,11},{10,... | collective-permute-start | bytes 393224 | tf_op jit(solution)/shard_map/scatter_moments/ppermute | solution.py:71
  50.1 5.2 %collective-permute-start.12 = (f32[264,128]{1,0:T(8,128)S(1)}, f32[264,128]{1,0:T(8,128)S(1)}, u32[]{:S(2)}, u32[]{:S(2)}) collective-permute-start(f32[264,128]{1,0:T(8,128)S(1)} %pad_maximum_fusion.3), channel_id=1, source_target_pairs={{0,16},{1,3},{2,18},{3,1},{4,20},{5,7},{6,22},{7,5},{8,24},{9,11},... | collective-permute-start | bytes 405512 | tf_op jit(solution)/shard_map/scatter_moments/ppermute | solution.py:71
  53.7 4.3 %collective-permute-start.24 = (f32[128,128]{1,0:T(8,128)S(1)}, f32[128,128]{1,0:T(8,128)S(1)}, u32[]{:S(2)}, u32[]{:S(2)}) collective-permute-start(f32[128,128]{1,0:T(8,128)S(1)} %slice.134), channel_id=1, source_target_pairs={{0,2},{1,5},{2,0},{3,7},{4,6},{5,1},{6,4},{7,3},{8,10},{9,13},{10,... | collective-permute-start | bytes 196616 | tf_op jit(solution)/shard_map/scatter_moments/ppermute | solution.py:71
  55.3 6.1 %collective-permute-start.13 = (f32[136,128]{1,0:T(8,128)S(1)}, f32[136,128]{1,0:T(8,128)S(1)}, u32[]{:S(2)}, u32[]{:S(2)}) collective-permute-start(f32[136,128]{1,0:T(8,128)S(1)} %pad_maximum_fusion.8), channel_id=1, source_target_pairs={{0,4},{1,17},{2,6},{3,19},{4,0},{5,21},{6,2},{7,23},{8,12},{9,25},... | collective-permute-start | bytes 208904 | tf_op jit(solution)/shard_map/scatter_moments/ppermute | solution.py:71
  58.1 5.2 %collective-permute-start.25 = (f32[64,128]{1,0:T(8,128)S(1)}, f32[64,128]{1,0:T(8,128)S(1)}, u32[]{:S(2)}, u32[]{:S(2)}) collective-permute-start(f32[64,128]{1,0:T(8,128)S(1)} %slice.136), channel_id=1, source_target_pairs={{0,8},{1,9},{2,10},{3,11},{4,12},{5,13},{6,14},{7,15},{8,0},{9,1},... | collective-permute-start | bytes 98312 | tf_op jit(solution)/shard_map/scatter_moments/ppermute | solution.py:71
  61.5 5.8 %collective-permute-start.14 = (f32[72,128]{1,0:T(8,128)S(1)}, f32[72,128]{1,0:T(8,128)S(1)}, u32[]{:S(2)}, u32[]{:S(2)}) collective-permute-start(f32[72,128]{1,0:T(8,128)S(1)} %pad_maximum_fusion.11), channel_id=1, source_target_pairs={{0,8},{1,9},{2,10},{3,11},{4,12},{5,13},{6,14},{7,15},{8,0},{9,1},... | collective-permute-start | bytes 110600 | tf_op jit(solution)/shard_map/scatter_moments/ppermute | solution.py:71
  63.3 5.2 %collective-permute-start.26 = (f32[64,128]{1,0:T(8,128)S(1)}, f32[64,128]{1,0:T(8,128)S(1)}, u32[]{:S(2)}, u32[]{:S(2)}) collective-permute-start(f32[64,128]{1,0:T(8,128)S(1)} %slice_add_fusion.7), channel_id=1, source_target_pairs={{0,8},{1,9},{2,10},{3,11},{4,12},{5,13},{6,14},{7,15},{8,0},{9,1},... | collective-permute-start | bytes 98312 | tf_op jit(solution)/shard_map/gather_moments/ppermute | solution.py:71
  67.2 4.8 %collective-permute-start.15 = (f32[64,128]{1,0:T(8,128)S(1)}, f32[64,128]{1,0:T(8,128)S(1)}, u32[]{:S(2)}, u32[]{:S(2)}) collective-permute-start(f32[64,128]{1,0:T(8,128)S(1)} %slice_add_fusion.8), channel_id=1, source_target_pairs={{0,8},{1,9},{2,10},{3,11},{4,12},{5,13},{6,14},{7,15},{8,0},{9,1},... | collective-permute-start | bytes 98312 | tf_op jit(solution)/shard_map/gather_moments/ppermute | solution.py:71
  68.6 5.0 %collective-permute-start.27 = (f32[128,128]{1,0:T(8,128)S(1)}, f32[128,128]{1,0:T(8,128)S(1)}, u32[]{:S(2)}, u32[]{:S(2)}) collective-permute-start(f32[128,128]{1,0:T(8,128)S(1)} %pad_maximum_fusion.10), channel_id=1, source_target_pairs={{0,2},{1,5},{2,0},{3,7},{4,6},{5,1},{6,4},{7,3},{8,10},{9,13},{10,... | collective-permute-start | bytes 196616 | tf_op jit(solution)/shard_map/gather_moments/ppermute | solution.py:71
  72.1 4.3 %collective-permute-start.16 = (f32[128,128]{1,0:T(8,128)S(1)}, f32[128,128]{1,0:T(8,128)S(1)}, u32[]{:S(2)}, u32[]{:S(2)}) collective-permute-start(f32[128,128]{1,0:T(8,128)S(1)} %pad_maximum_fusion.9), channel_id=1, source_target_pairs={{0,4},{1,17},{2,6},{3,19},{4,0},{5,21},{6,2},{7,23},{8,12},{9,25},... | collective-permute-start | bytes 196616 | tf_op jit(solution)/shard_map/gather_moments/ppermute | solution.py:71
  73.5 6.4 %collective-permute-start.28 = (f32[256,128]{1,0:T(8,128)S(1)}, f32[256,128]{1,0:T(8,128)S(1)}, u32[]{:S(2)}, u32[]{:S(2)}) collective-permute-start(f32[256,128]{1,0:T(8,128)S(1)} %pad_maximum_fusion.7), channel_id=1, source_target_pairs={{0,4},{1,3},{2,6},{3,1},{4,0},{5,7},{6,2},{7,5},{8,12},{9,11},{10,... | collective-permute-start | bytes 393224 | tf_op jit(solution)/shard_map/gather_moments/ppermute | solution.py:71
  76.3 5.2 %collective-permute-start.17 = (f32[256,128]{1,0:T(8,128)S(1)}, f32[256,128]{1,0:T(8,128)S(1)}, u32[]{:S(2)}, u32[]{:S(2)}) collective-permute-start(f32[256,128]{1,0:T(8,128)S(1)} %pad_maximum_fusion.6), channel_id=1, source_target_pairs={{0,16},{1,3},{2,18},{3,1},{4,20},{5,7},{6,22},{7,5},{8,24},{9,11},... | collective-permute-start | bytes 393224 | tf_op jit(solution)/shard_map/gather_moments/ppermute | solution.py:71
  79.9 6.4 %collective-permute-start.29 = (f32[512,128]{1,0:T(8,128)S(1)}, f32[512,128]{1,0:T(8,128)S(1)}, u32[]{:S(2)}, u32[]{:S(2)}) collective-permute-start(f32[512,128]{1,0:T(8,128)S(1)} %pad_maximum_fusion.2.refs_4_), channel_id=1, source_target_pairs={{0,16},{1,17},{2,18},{3,19},{4,20},{5,21},{6,22},{7,23},{8,24},{9,... | collective-permute-start | bytes 786440 | tf_op jit(solution)/shard_map/gather_moments/ppermute | solution.py:71
  81.5 6.4 %collective-permute-start.18 = (f32[512,128]{1,0:T(8,128)S(1)}, f32[512,128]{1,0:T(8,128)S(1)}, u32[]{:S(2)}, u32[]{:S(2)}) collective-permute-start(f32[512,128]{1,0:T(8,128)S(1)} %pad_maximum_fusion.1.refs_0_), channel_id=1, source_target_pairs={{0,2},{1,5},{2,0},{3,7},{4,6},{5,1},{6,4},{7,3},{8,10},{9,13},{10,... | collective-permute-start | bytes 786440 | tf_op jit(solution)/shard_map/gather_moments/ppermute | solution.py:71
  83.1 6.4 %collective-permute-start.30 = (f32[512,128]{1,0:T(8,128)S(1)}, f32[512,128]{1,0:T(8,128)S(1)}, u32[]{:S(2)}, u32[]{:S(2)}) collective-permute-start(f32[512,128]{1,0:T(8,128)S(1)} %pad_maximum_fusion.2.refs_4_), channel_id=1, source_target_pairs={{0,1},{1,0},{2,3},{3,2},{4,5},{5,4},{6,7},{7,6},{8,9},{9,8},{10,11... | collective-permute-start | bytes 786440 | tf_op jit(solution)/shard_map/gather_moments/ppermute | solution.py:71
  83.1 6.4 %collective-permute-start.19 = (f32[512,128]{1,0:T(8,128)S(1)}, f32[512,128]{1,0:T(8,128)S(1)}, u32[]{:S(2)}, u32[]{:S(2)}) collective-permute-start(f32[512,128]{1,0:T(8,128)S(1)} %pad_maximum_fusion.1.refs_0_), channel_id=1, source_target_pairs={{0,1},{1,0},{2,3},{3,2},{4,5},{5,4},{6,7},{7,6},{8,9},{9,8},{10,11... | collective-permute-start | bytes 786440 | tf_op jit(solution)/shard_map/gather_moments/ppermute | solution.py:71
  86.3 3.2 %collective-permute-start.31 = (f32[512,128]{1,0:T(8,128)S(1)}, f32[512,128]{1,0:T(8,128)S(1)}, u32[]{:S(2)}, u32[]{:S(2)}) collective-permute-start(f32[512,128]{1,0:T(8,128)S(1)} %collective-permute-done.29.refs_5_), channel_id=1, source_target_pairs={{0,1},{1,0},{2,3},{3,2},{4,5},{5,4},{6,7},{7,6},{8,9},{9,8},{10,11... | collective-permute-start | bytes 786440 | tf_op jit(solution)/shard_map/gather_moments/ppermute | solution.py:71
  88.0 1.6 %collective-permute-start.20 = (f32[512,128]{1,0:T(8,128)S(1)}, f32[512,128]{1,0:T(8,128)S(1)}, u32[]{:S(2)}, u32[]{:S(2)}) collective-permute-start(f32[512,128]{1,0:T(8,128)S(1)} %collective-permute-done.18.refs_1_), channel_id=1, source_target_pairs={{0,1},{1,0},{2,3},{3,2},{4,5},{5,4},{6,7},{7,6},{8,9},{9,8},{10,11... | collective-permute-start | bytes 786440 | tf_op jit(solution)/shard_map/gather_moments/ppermute | solution.py:71
  88.0 1.5 %collective-permute-start.32 = (f32[8,128]{1,0:T(8,128)S(1)}, f32[8,128]{1,0:T(8,128)S(1)}, u32[]{:S(2)}, u32[]{:S(2)}) collective-permute-start(f32[8,128]{1,0:T(8,128)S(1)} %slice_add_fusion.9), channel_id=1, source_target_pairs={{0,1},{1,0},{2,3},{3,2},{4,5},{5,4},{6,7},{7,6},{8,9},{9,8},{10,11... | collective-permute-start | bytes 12296 | tf_op jit(solution)/shard_map/scatter_moments/ppermute | solution.py:71

commit v3 on v2

v3 whole, which is shorter than its diff:
```python
import functools
import math

import jax
import jax.numpy as jnp
import numpy as np
from jax import lax
from jax.experimental import pallas as pl
from jax.experimental.pallas import tpu as pltpu
from jax.sharding import PartitionSpec as P

F32 = jnp.float32
BF16 = jnp.bfloat16
LANES = 128
COUNT_ROWS = 8
LOG2E = math.log2(math.e)
LN2 = math.log(2.0)
BLOCK = 1024


class Plan:
    def __init__(self, groups, owners, comps):
        self.devices = groups * owners
        self.owners = owners
        owner_bits = owners.bit_length() - 1
        group_bits = groups.bit_length() - 1
        assert owners == 1 << owner_bits and groups == 1 << group_bits and owner_bits >= 4
        piece = comps // owners
        group = list(range(owner_bits, owner_bits + group_bits))
        split = [1] + group[:1] + list(range(2, owner_bits - 1))
        while comps >> (len(split) + 1) < 16:
            split.pop()
        rest = [b for b in range(1, owner_bits + group_bits) if b not in split]
        self.units = 1 << (len(split) + 1)
        self.unit = comps // self.units
        assert piece % self.unit == 0
        per = piece // self.unit
        first, second, third, *others = split
        orders = (
            ((first, second, third), (third, first, second)),
            ((second, third, first), (second, first, third)),
        )
        self.halving = [
            [(0, 0)] + list(zip(zero, one)) + [(b, b) for b in others] for zero, one in orders
        ]
        self.whole = [(b, b) for b in rest]
        down = list(range(owner_bits - 1, 0, -1))
        self.gather = list(zip(down, down[:-2] + [down[-1], down[-2]]))

        def reach(device, steps, place):
            for t in reversed(range(len(steps))):
                if place >> t & 1:
                    device ^= 1 << steps[t][device & 1]
            return device

        n = range(self.devices)
        places = range(owners)
        gather_at = np.array([[reach(d, self.gather + [(0, 0)], p) % owners for p in places] for d in n])
        unit_chunk = (gather_at[:, :, None] * per + np.arange(per)).reshape(self.devices, self.units)
        owned = sorted([0] + split)
        slot_chunk = []
        for halving in self.halving:
            at = np.array([[reach(d, halving[::-1], j) for j in range(self.units)] for d in n])
            slot_chunk.append(sum((at >> b & 1) << i for i, b in enumerate(owned)))
        unit_slot = [np.take_along_axis(np.argsort(c, axis=1), unit_chunk, axis=1) for c in slot_chunk]
        self.tables = np.stack([unit_chunk, *unit_slot, *slot_chunk], axis=1).astype(np.int32)

    def swap(self, value, step):
        pairs = [(d, d ^ (1 << step[d & 1])) for d in range(self.devices)]
        return lax.ppermute(value, ("grp", "comp"), pairs)


def columns(row, height):
    return jnp.broadcast_to(row, (height, LANES)).T


def prepare_kernel(plan, table, *refs):
    sources, copies, (stack_ref, staged, features_ref, logits_ref, sems) = refs[:4], refs[4:6], refs[6:]
    targets = (features_ref, logits_ref, *copies)
    moves = [pltpu.make_async_copy(s, t, sems.at[i]) for i, (s, t) in enumerate(zip(sources, targets))]
    for move in moves:
        move.start()
    for move in moves:
        move.wait()
    logits = logits_ref[...]
    shifted = logits - jnp.max(logits)
    log_weights = shifted - jnp.log(jnp.sum(jnp.exp(shifted)))
    for b in range(logits.shape[0]):
        staged[b * LANES : (b + 1) * LANES, :] = columns(log_weights[b : b + 1, :], LANES)
    width = features_ref.shape[1]
    rows = features_ref[...]
    values = rows.astype(F32)
    squares = values * values
    high = squares.astype(BF16)
    stack_ref[:, :width] = (squares - high.astype(F32)).astype(BF16)
    stack_ref[:, width : 2 * width] = high
    stack_ref[:, 2 * width :] = rows


def build_weights(unit, table, first_units, mean_refs, variance_refs, log_weights, weights, offsets):
    at = 0
    width = mean_refs[0].shape[1]
    for mean_ref, variance_ref, first_unit in zip(mean_refs, variance_refs, first_units):
        for first in range(0, mean_ref.shape[0], unit):
            here = slice(at, at + unit)
            mean = mean_ref[first : first + unit, :]
            variance = variance_ref[first : first + unit, :]
            inverse = 1.0 / variance
            linear = mean * inverse
            constant = jnp.sum(jnp.log(variance) + mean * linear, axis=1, keepdims=True)
            chunk = pl.multiple_of(table[0, first_unit + first // unit] * unit, unit)
            log_weight = log_weights[pl.ds(chunk, unit), :]
            offsets[here, :] = (
                log_weight - 0.5 * constant - 0.5 * width * math.log(2.0 * math.pi)
            ) * LOG2E
            square = inverse * (-0.5 * LOG2E)
            linear = linear * LOG2E
            square_high = square.astype(BF16)
            linear_high = linear.astype(BF16)
            weights[here, :width] = square_high
            weights[here, width : 2 * width] = square_high
            weights[here, 2 * width : 3 * width] = linear_high
            weights[here, 3 * width : 4 * width] = (square - square_high.astype(F32)).astype(BF16)
            weights[here, 4 * width :] = (linear - linear_high.astype(F32)).astype(BF16)
            at += unit


def block_scores(stack, weights, offsets):
    width = stack.shape[1] // 3
    scores = lax.dot_general(
        weights[...],
        jnp.concatenate([stack, stack[:, width:]], axis=1),
        (((1,), (1,)), ((), ())),
        preferred_element_type=F32,
    )
    return scores + jnp.tile(offsets[...], (1, stack.shape[0] // LANES))


def store_moments(plan, table, first_unit, moments, targets):
    unit = plan.unit
    width = moments.shape[1] // 2
    parts = width // LANES
    for u in range(moments.shape[0] // unit):
        for column, target in enumerate(targets):
            slot = table[2 - column, first_unit + u] % (plan.units // 2)
            first = pl.multiple_of(slot * (unit * parts), unit)
            for part in range(parts):
                at = column * width + part * LANES
                target[pl.ds(first + part * unit, unit), :] = moments[
                    u * unit : (u + 1) * unit, at : at + LANES
                ]


def early_kernel(plan, table, *refs):
    mean_refs, variance_refs = refs[0:2], refs[2:4]
    log_weights, stack_ref, scores_ref = refs[4:7]
    weights, offsets = refs[7:]
    count = stack_ref.shape[0]
    block = min(BLOCK, count)
    firsts = (0, plan.units // 2)
    build_weights(plan.unit, table, firsts, mean_refs, variance_refs, log_weights, weights, offsets)
    for first in range(0, count, block):
        scores_ref[:, first : first + block] = block_scores(
            stack_ref[first : first + block, :], weights, offsets
        )


def late_kernel(plan, table, *refs):
    mean_refs, variance_refs = refs[0:2], refs[2:4]
    log_weights, stack_ref, early_ref = refs[4:7]
    sent_refs, counts_ref, scores_ref, own_ref = refs[7:9], refs[9], refs[10], refs[11]
    weights, offsets, moments, partial, staged = refs[12:]
    count, width = stack_ref.shape[0], stack_ref.shape[1] // 3
    block = min(BLOCK, count)
    quarter = weights.shape[0] // 2
    quarters = plan.units // 4
    firsts = (quarters, 3 * quarters)
    build_weights(plan.unit, table, firsts, mean_refs, variance_refs, log_weights, weights, offsets)
    for first in range(0, count, block):
        stack = stack_ref[first : first + block, :]
        late = block_scores(stack, weights, offsets)
        early = early_ref[:, first : first + block]
        highest = jnp.maximum(
            jnp.max(early, axis=0, keepdims=True), jnp.max(late, axis=0, keepdims=True)
        )
        early = jnp.exp2(early - highest)
        late = jnp.exp2(late - highest)
        totals = jnp.sum(early, axis=0, keepdims=True) + jnp.sum(late, axis=0, keepdims=True)
        scores_ref[:, first : first + block] = (highest + jnp.log2(totals)) * (LN2 / width)
        inverse = 1.0 / totals
        early = (early * inverse).astype(BF16)
        late = (late * inverse).astype(BF16)
        own_ref[:quarter, first : first + block] = early[:quarter]
        own_ref[quarter:, first : first + block] = late[:quarter]
        added = jnp.dot(
            jnp.concatenate([early[quarter:], late[quarter:]], axis=0),
            stack[:, width:],
            preferred_element_type=F32,
        )
        if first == 0:
            moments[...] = added
        else:
            moments[...] += added
        for at, part in enumerate((early[:quarter], late[:quarter], early[quarter:], late[quarter:])):
            rounded = part.astype(F32)
            counted = rounded[:, :LANES]
            for b in range(1, block // LANES):
                counted = counted + rounded[:, b * LANES : (b + 1) * LANES]
            here = slice(at * quarter, (at + 1) * quarter)
            if first == 0:
                partial[here, :] = counted
            else:
                partial[here, :] += counted

    unit = plan.unit
    for u in range(plan.units):
        chunk = pl.multiple_of(table[0, u] * unit, unit)
        staged[pl.ds(chunk, unit), :] = partial[u * unit : (u + 1) * unit, :]
    half = sent_refs[1].shape[0]
    for b in range(4 * quarter // LANES):
        line = jnp.sum(staged[b * LANES : (b + 1) * LANES, :].T, axis=0, keepdims=True)
        counts_ref[b : b + 1, :] = line
        sent_refs[0][half + b : half + b + 1, :] = line
    store_moments(plan, table, plan.units // 2, moments, sent_refs[::-1])


def own_kernel(plan, table, own_ref, stack_ref, first_ref, second_ref, moments):
    count, width = stack_ref.shape[0], stack_ref.shape[1] // 3
    block = min(BLOCK, count)
    for first in range(0, count, block):
        here = slice(first, first + block)
        added = jnp.dot(own_ref[:, here], stack_ref[here, width:], preferred_element_type=F32)
        if first == 0:
            moments[...] = added
        else:
            moments[...] += added
    store_moments(plan, table, 0, moments, (second_ref, first_ref))


def call(kernel, plan, table, operands, shapes, scratch, flops, vmem_mib, space=pltpu.VMEM):
    vmem = pl.BlockSpec(memory_space=pltpu.VMEM)
    moved = sum(math.prod(o.shape) * o.dtype.itemsize for o in operands)
    return pl.pallas_call(
        functools.partial(kernel, plan),
        in_specs=[pl.BlockSpec(memory_space=pltpu.SMEM)] + [pl.BlockSpec(memory_space=space)] * len(operands),
        out_specs=[vmem] * len(shapes),
        out_shape=[jax.ShapeDtypeStruct(*s) for s in shapes],
        scratch_shapes=[pltpu.VMEM(*s) if isinstance(s, tuple) else s for s in scratch],
        compiler_params=pltpu.CompilerParams(vmem_limit_bytes=vmem_mib * 2**20),
        cost_estimate=pl.CostEstimate(flops=flops, bytes_accessed=2 * moved, transcendentals=0),
    )(table, *operands)


def prepare(plan, table, features, logits, means, variances):
    count, width = features.shape
    comps = math.prod(logits.shape)
    *held, stack, log_weights = call(
        prepare_kernel,
        plan,
        table,
        [pltpu.with_memory_space_constraint(a, pltpu.HBM) for a in (features, logits, means, variances)],
        [(means.shape, F32)] * 2 + [((count, 3 * width), BF16), ((comps, LANES), F32)],
        [((count, width), BF16), (logits.shape, F32), pltpu.SemaphoreType.DMA((4,))],
        8 * count * width,
        16,
        pltpu.HBM,
    )
    return held, stack, log_weights


def early_scores(plan, table, means, variances, log_weights, stack):
    count, width = stack.shape[0], stack.shape[1] // 3
    comps = sum(m.shape[0] for m in means)
    return call(
        early_kernel,
        plan,
        table,
        [*means, *variances, log_weights, stack],
        [((comps, count), F32)],
        [((comps, 5 * width), BF16), ((comps, LANES), F32)],
        10 * comps * count * width,
        24,
    )[0]


def mixture(plan, table, means, variances, log_weights, stack, early):
    count, width = stack.shape[0], stack.shape[1] // 3
    half = sum(m.shape[0] for m in means)
    rows = half * (width // LANES)
    *sent, counts, row_scores, own = call(
        late_kernel,
        plan,
        table,
        [*means, *variances, log_weights, stack, early],
        [
            ((rows + COUNT_ROWS, LANES), F32),
            ((rows, LANES), F32),
            ((COUNT_ROWS, LANES), F32),
            ((1, count), F32),
            ((half, count), BF16),
        ],
        [
            ((half, 5 * width), BF16),
            ((half, LANES), F32),
            ((half, 2 * width), F32),
            ((2 * half, LANES), F32),
            ((2 * half, LANES), F32),
        ],
        16 * half * count * width,
        32,
    )
    kept = call(
        own_kernel,
        plan,
        table,
        [own, stack],
        [((rows, LANES), F32)] * 2,
        [((half, 2 * width), F32)],
        4 * half * count * width,
        16,
    )
    return sent, kept, counts, row_scores


def update_kernel(plan, pieces, total_rows, table, *refs):
    first_refs, second_refs = refs[:pieces], refs[pieces : 2 * pieces]
    counts_ref = refs[2 * pieces]
    means_ref, variances_ref, log_weights_ref, staged = refs[2 * pieces + 1 :]
    comps, width = means_ref.shape
    unit = plan.unit
    parts = width // LANES
    denominator = counts_ref[...] + 1.0
    log_weights_ref[...] = jnp.log(denominator / total_rows)
    inverse = 1.0 / denominator
    for b in range(comps // LANES):
        staged[b * LANES : (b + 1) * LANES, :] = columns(inverse[b : b + 1, :], LANES)
    for stream, stream_refs in enumerate((first_refs, second_refs)):
        slot = 0
        for ref in stream_refs:
            for first in range(0, ref.shape[0], unit * parts):
                chunk = pl.ds(pl.multiple_of(table[3 + stream, slot] * unit, unit), unit)
                scale = staged[chunk, :]
                for part in range(parts):
                    lanes = slice(part * LANES, (part + 1) * LANES)
                    moment = ref[first + part * unit : first + (part + 1) * unit, :]
                    if stream == 0:
                        means_ref[chunk, lanes] = moment * scale
                    else:
                        mean = means_ref[chunk, lanes]
                        variances_ref[chunk, lanes] = (moment + 1.0) * scale - mean * mean + 0.01
                slot += 1


def update(plan, table, first, second, counts, comps, width, total_rows):
    vmem = pl.BlockSpec(memory_space=pltpu.VMEM)
    shapes = [(comps, width), (comps, width), counts.shape]
    return pl.pallas_call(
        functools.partial(update_kernel, plan, len(first), total_rows),
        in_specs=[pl.BlockSpec(memory_space=pltpu.SMEM)] + [vmem] * (2 * len(first) + 1),
        out_specs=[vmem] * 3,
        scratch_shapes=[pltpu.VMEM((comps, LANES), F32)],
        out_shape=[jax.ShapeDtypeStruct(s, F32) for s in shapes],
        compiler_params=pltpu.CompilerParams(vmem_limit_bytes=16 * 2**20),
        cost_estimate=pl.CostEstimate(flops=8 * comps * width, bytes_accessed=16 * comps * width, transcendentals=0),
    )(table, *first, *second, counts)


def double(plan, held, step, arrived=None):
    arrived = [plan.swap(h, at) for h, at in zip(held, step)] if arrived is None else arrived
    return [jnp.concatenate(pair, axis=0) for pair in zip(held, arrived)]


def scatter(plan, sent, kept, counts):
    rows = kept[1].shape[0]
    for at, step in enumerate(zip(*plan.halving)):
        if at:
            rows //= 2
            sent = [jnp.concatenate([kept[0][rows:], counts], axis=0), kept[1][rows:]]
            kept = [k[:rows] for k in kept]
        arrived = [plan.swap(s, pair) for s, pair in zip(sent, step)]
        counts = counts + arrived[0][rows:]
        kept = [k + a[:rows] for k, a in zip(kept, arrived)]
    for pair in plan.whole:
        arrived = [plan.swap(jnp.concatenate([kept[0], counts], axis=0), pair), plan.swap(kept[1], pair)]
        counts = counts + arrived[0][rows:]
        kept = [k + a[:rows] for k, a in zip(kept, arrived)]
    return kept, 0.5 * (counts + plan.swap(counts, (0, 0)))


def on_device(plan, features, means, variances, weight_logits):
    comps = weight_logits.shape[0]
    width = means.shape[1]
    me = lax.axis_index(("grp", "comp"))
    table = lax.dynamic_index_in_dim(jnp.asarray(plan.tables), me, 0, keepdims=False)
    logits = weight_logits.reshape(comps // LANES, LANES)

    with jax.named_scope("gather_parameters"):
        arrived = [plan.swap(h, plan.gather[0]) for h in (means, variances)]
        held, stack, log_weights = prepare(plan, table, features, logits, means, variances)
        arrived, held, stack, log_weights, table = lax.optimization_barrier(
            (arrived, held, stack, log_weights, table)
        )
        held = double(plan, held, None, arrived)
        for step in plan.gather[1:-1]:
            held = double(plan, held, (step, step))
        last = [plan.swap(h, plan.gather[-1]) for h in held]
        pairs = [(h, plan.swap(h, (0, 0))) for h in held]
        early = early_scores(plan, table, *pairs, log_weights, stack)
        last, early = lax.optimization_barrier((last, early))
        pairs = [(l, plan.swap(l, (0, 0))) for l in last]
    sent, kept, counts, row_scores = mixture(plan, table, *pairs, log_weights, stack, early)
    with jax.named_scope("scatter_moments"):
        kept, counts = scatter(plan, sent, kept, counts)
    with jax.named_scope("gather_moments"):
        steps = list(zip(*plan.halving))[:0:-1]
        held = kept
        for step in steps[:-1]:
            held = double(plan, held, step)
        last = [plan.swap(h, at) for h, at in zip(held, steps[-1])]
        mates = [plan.swap(h, (0, 0)) for h in held]
        first, second = [[h, l, m, plan.swap(l, (0, 0))] for h, l, m in zip(held, last, mates)]

    total_rows = float(features.shape[0] * plan.devices + comps)
    fresh_means, fresh_variances, fresh_weights = update(
        plan, table, first, second, counts, comps, width, total_rows
    )
    return fresh_means, fresh_variances, fresh_weights.reshape(comps), row_scores.reshape(-1)


def solution(mesh):
    def whole(features, means, variances, weight_logits):
        plan = Plan(mesh.shape["grp"], mesh.shape["comp"], weight_logits.shape[0])
        return jax.shard_map(
            functools.partial(on_device, plan),
            mesh=mesh,
            in_specs=(P(("grp", "comp"), None), P("comp", None), P("comp", None), P()),
            out_specs=(P(), P(), P(), P(("grp", "comp"))),
            check_vma=False,
        )(features, means, variances, weight_logits)

    return whole
```

time: 92.2 us -> 86.8 us (0.941)
  waiting for transfers between devices: 37.1 us -> 31.2 us
  Pallas kernels: 12.3 us -> 17.9 us
  starting transfers between devices: 38.7 us -> 35.4 us
    ppermute x33 -> x31, waiting for transfers between devices: 37.1 us -> 31.2 us  [swap(): return lax.ppermute(value, ('grp', 'comp'), pairs)]
    pallas_call x1 -> x4, Pallas kernels: 9.88 us -> 15.5 us  [call(): pl.pallas_call(functools.partial(kernel, plan), in_specs=[pl.BlockSpec(me...]
    ppermute x33 -> x31, starting transfers between devices: 38.7 us -> 35.4 us  [swap(): return lax.ppermute(value, ('grp', 'comp'), pairs)]
  transfers between devices with their start and end apart: 33 -> 31, of which waited for: 19 -> 18; matrix products, arithmetic and copies ran while one was open for 3% -> 1% of each run, Pallas kernels for 0% -> 10%
where the time goes in v3:
time: 86.8 us; the launch traced here: 86.6 us
  starting transfers between devices  35.4 us (41%)
  waiting for transfers between devices  31.2 us (36%)
  Pallas kernels  17.9 us (21%)
  between operations  0.92 us (1%)
    ppermute x31, starting transfers between devices, swap(): return lax.ppermute(value, ('grp', 'comp'), pairs)  35.4 us
    ppermute x31, waiting for transfers between devices, swap(): return lax.ppermute(value, ('grp', 'comp'), pairs)  31.2 us
    pallas_call x4, Pallas kernels, call(): pl.pallas_call(functools.partial(kernel, plan), in_specs=[pl.BlockSpec(me...  15.5 us
    pallas_call x1, Pallas kernels, update(): pl.pallas_call(functools.partial(update_kernel, plan, len(first), total_r...  2.4 us
  transfers between devices with their start and end apart: 31, of which 18 were waited for; matrix products, arithmetic and copies ran while one was open for 1% of the time, Pallas kernels for 10%

profile of v3, /device:TPU:0, one launch (start us, length us, event | category | flops | bytes accessed | tf_op | source)
XLA Modules:
  0.0 86.6 jit_solution(13698642776329536874)
XLA Ops:
  0.6 4.1 %collective-permute-start = (f32[64,256]{1,0:T(8,128)}, f32[64,256]{1,0:T(8,128)S(1)}, u32[]{:S(2)}, u32[]{:S(2)}) collective-permute-start(f32[64,256]{1,0:T(8,128)} %refs_2_.1), channel_id=1, source_target_pairs={{0,8},{1,9},{2,10},{3,11},{4,12},{5,13},{6,14},{7,15},{8,0},{9,1},... | collective-permute-start | bytes 196616 | tf_op jit(solution)/shard_map/gather_parameters/ppermute | solution.py:70
  4.7 0.1 collective-permute-start.1
  4.8 0.7 dynamic-slice_bitcast_fusion.table
  5.5 3.1 %gather_parameters.2 = (f32[64,256]{1,0:T(8,128)S(1)}, f32[64,256]{1,0:T(8,128)S(1)}, bf16[2048,768]{1,0:T(8,128)(2,1)S(1)}, f32[1024,128]{1,0:T(8,128)S(1)}) custom-call(s32[5,16]{1,0:T(8,128)S(1)} %dynamic-slice_bitcast_fusion.table, bf16[2048,256]{1,0:T(8,128)(2,1)} %refs_0_.1, f32[8,128]{1,0:T(8,128)} %bitcast.5, f32[64,256]{1,0:T(8,128)} %refs_2_.1, ...), custom_call_target="tpu_custom_call" | custom-call | flops 4194304 | bytes 2367488 | tf_op jit(solution)/shard_map/gather_parameters/pallas_call | solution.py:243
  8.6 0.0 collective-permute-done
  8.6 2.8 %collective-permute-done.1 = f32[64,256]{1,0:T(8,128)S(1)} collective-permute-done((f32[64,256]{1,0:T(8,128)}, f32[64,256]{1,0:T(8,128)S(1)}, u32[]{:S(2)}, u32[]{:S(2)}) %collective-permute-start.1) | collective-permute-done | bytes 65568 | tf_op jit(solution)/shard_map/gather_parameters/ppermute | solution.py:70
  11.5 0.7 collective-permute-start.4
  12.2 1.4 %collective-permute-start.2 = (f32[128,256]{1,0:T(8,128)S(1)}, f32[128,256]{1,0:T(8,128)S(1)}, u32[]{:S(2)}, u32[]{:S(2)}) collective-permute-start(f32[128,256]{1,0:T(8,128)S(1)} %pad_maximum_fusion.4), channel_id=1, source_target_pairs={{0,4},{1,3},{2,6},{3,1},{4,0},{5,7},{6,2},{7,5},{8,12},{9,11},{10,... | collective-permute-start | bytes 393224 | tf_op jit(solution)/shard_map/gather_parameters/ppermute | solution.py:70
  13.6 4.3 %collective-permute-done.2 = f32[128,256]{1,0:T(8,128)S(1)} collective-permute-done((f32[128,256]{1,0:T(8,128)S(1)}, f32[128,256]{1,0:T(8,128)S(1)}, u32[]{:S(2)}, u32[]{:S(2)}) %collective-permute-start.2) | collective-permute-done | bytes 131104 | tf_op jit(solution)/shard_map/gather_parameters/ppermute | solution.py:70
  17.9 0.1 collective-permute-start.6
  18.0 0.0 collective-permute-done.4
  18.0 0.5 collective-permute-start.7
  18.6 1.7 %collective-permute-start.3 = (f32[256,256]{1,0:T(8,128)S(1)}, f32[256,256]{1,0:T(8,128)S(1)}, u32[]{:S(2)}, u32[]{:S(2)}) collective-permute-start(f32[256,256]{1,0:T(8,128)S(1)} %constant_dynamic-update-slice_fusion.refs_0_), channel_id=1, source_target_pairs={{0,2},{1,5},{2,0},{3,7},{4,6},{5,1},{6,4},{7,3},{8,10},{9,13},{10,... | collective-permute-start | bytes 786440 | tf_op jit(solution)/shard_map/gather_parameters/ppermute | solution.py:70
  20.3 0.3 collective-permute-start.5
  20.6 0.0 collective-permute-done.6.refs_1_
  20.6 0.0 collective-permute-done.7.refs_3_
  20.6 3.6 %gather_parameters.3.refs_6_ = f32[512,2048]{1,0:T(8,128)S(1)} custom-call(s32[5,16]{1,0:T(8,128)S(1)} %dynamic-slice_bitcast_fusion.table, f32[256,256]{1,0:T(8,128)S(1)} %constant_dynamic-update-slice_fusion.refs_0_, f32[256,256]{1,0:T(8,128)S(1)} %collective-permute-done.6.refs_1_, f32[256,256]{1,0:T(8,128)S(1)} %constant_dynamic-update-slice_fusion.3.refs_2_, ...), custom_call_target="tpu_custom_call" | custom-call | flops 2684354560 | bytes 9437184 | tf_op jit(solution)/shard_map/gather_parameters/pallas_call | solution.py:243
  24.2 0.7 collective-permute-done.3.refs_0_
  24.9 2.8 %collective-permute-done.5.refs_2_ = f32[256,256]{1,0:T(8,128)S(1)} collective-permute-done((f32[256,256]{1,0:T(8,128)S(1)}, f32[256,256]{1,0:T(8,128)S(1)}, u32[]{:S(2)}, u32[]{:S(2)}) %collective-permute-start.5) | collective-permute-done | bytes 262176 | tf_op jit(solution)/shard_map/gather_parameters/ppermute | solution.py:70
  27.7 0.0 collective-permute-start.8
  27.8 0.5 collective-permute-start.9
  28.3 1.0 %collective-permute-done.8.refs_1_ = f32[256,256]{1,0:T(8,128)S(1)} collective-permute-done((f32[256,256]{1,0:T(8,128)S(1)}, f32[256,256]{1,0:T(8,128)S(1)}, u32[]{:S(2)}, u32[]{:S(2)}) %collective-permute-start.8) | collective-permute-done | bytes 262176 | tf_op jit(solution)/shard_map/gather_parameters/ppermute | solution.py:70
  29.3 0.4 collective-permute-done.9.refs_3_
  29.7 7.0 %shard_map.84 = (f32[1032,128]{1,0:T(8,128)S(1)}, f32[1024,128]{1,0:T(8,128)S(1)}, f32[8,128]{1,0:T(8,128)S(1)}, f32[1,2048]{1,0:T(1,128)}, bf16[512,2048]{1,0:T(8,128)(2,1)S(1)}) custom-call(s32[5,16]{1,0:T(8,128)S(1)} %dynamic-slice_bitcast_fusion.table, f32[256,256]{1,0:T(8,128)S(1)} %collective-permute-done.3.refs_0_, ...), custom_call_target="tpu_custom_call" | custom-call | flops 4294967296 | bytes 17825792 | tf_op jit(solution)/shard_map/pallas_call | solution.py:243
  36.6 0.1 collective-permute-start.10
  36.8 0.4 collective-permute-start.20
  37.1 1.8 %shard_map.85 = (f32[1024,128]{1,0:T(8,128)S(1)}, f32[1024,128]{1,0:T(8,128)S(1)}) custom-call(s32[5,16]{1,0:T(8,128)S(1)} %dynamic-slice_bitcast_fusion.table, bf16[512,2048]{1,0:T(8,128)(2,1)S(1)} %get-tuple-element.42.own_ref, bf16[2048,768]{1,0:T(8,128)(2,1)S(1)} %get-tuple-element.38.refs_5_.stack_ref), custom_call_target="tpu_custom_call" | custom-call | flops 1073741824 | bytes 10485760 | tf_op jit(solution)/shard_map/pallas_call | solution.py:243
  39.0 0.0 collective-permute-done.10
  39.0 0.1 slice_add_fusion
  39.1 1.8 %collective-permute-start.11 = (f32[520,128]{1,0:T(8,128)S(1)}, f32[520,128]{1,0:T(8,128)S(1)}, u32[]{:S(2)}, u32[]{:S(2)}) collective-permute-start(f32[520,128]{1,0:T(8,128)S(1)} %pad_maximum_fusion), channel_id=1, source_target_pairs={{0,2},{1,5},{2,0},{3,7},{4,6},{5,1},{6,4},{7,3},{8,10},{9,13},{10,... | collective-permute-start | bytes 798728 | tf_op jit(solution)/shard_map/scatter_moments/ppermute | solution.py:70
  40.9 0.0 collective-permute-done.20
  40.9 0.1 add.66
  41.0 1.6 %collective-permute-start.21 = (f32[512,128]{1,0:T(8,128)S(1)}, f32[512,128]{1,0:T(8,128)S(1)}, u32[]{:S(2)}, u32[]{:S(2)}) collective-permute-start(f32[512,128]{1,0:T(8,128)S(1)} %slice.104), channel_id=1, source_target_pairs={{0,16},{1,17},{2,18},{3,19},{4,20},{5,21},{6,22},{7,23},{8,24},{9,... | collective-permute-start | bytes 786440 | tf_op jit(solution)/shard_map/scatter_moments/ppermute | solution.py:70
  42.6 3.0 %collective-permute-done.11 = f32[520,128]{1,0:T(8,128)S(1)} collective-permute-done((f32[520,128]{1,0:T(8,128)S(1)}, f32[520,128]{1,0:T(8,128)S(1)}, u32[]{:S(2)}, u32[]{:S(2)}) %collective-permute-start.11) | collective-permute-done | bytes 266272 | tf_op jit(solution)/shard_map/scatter_moments/ppermute | solution.py:70
  45.7 1.8 %collective-permute-start.12 = (f32[264,128]{1,0:T(8,128)S(1)}, f32[264,128]{1,0:T(8,128)S(1)}, u32[]{:S(2)}, u32[]{:S(2)}) collective-permute-start(f32[264,128]{1,0:T(8,128)S(1)} %pad_maximum_fusion.3), channel_id=1, source_target_pairs={{0,16},{1,3},{2,18},{3,1},{4,20},{5,7},{6,22},{7,5},{8,24},{9,11},... | collective-permute-start | bytes 405512 | tf_op jit(solution)/shard_map/scatter_moments/ppermute | solution.py:70
  47.5 0.6 collective-permute-done.21
  48.2 1.4 %collective-permute-start.22 = (f32[256,128]{1,0:T(8,128)S(1)}, f32[256,128]{1,0:T(8,128)S(1)}, u32[]{:S(2)}, u32[]{:S(2)}) collective-permute-start(f32[256,128]{1,0:T(8,128)S(1)} %slice.106), channel_id=1, source_target_pairs={{0,4},{1,3},{2,6},{3,1},{4,0},{5,7},{6,2},{7,5},{8,12},{9,11},{10,... | collective-permute-start | bytes 393224 | tf_op jit(solution)/shard_map/scatter_moments/ppermute | solution.py:70
  49.6 1.2 %collective-permute-done.12 = f32[264,128]{1,0:T(8,128)S(1)} collective-permute-done((f32[264,128]{1,0:T(8,128)S(1)}, f32[264,128]{1,0:T(8,128)S(1)}, u32[]{:S(2)}, u32[]{:S(2)}) %collective-permute-start.12) | collective-permute-done | bytes 135200 | tf_op jit(solution)/shard_map/scatter_moments/ppermute | solution.py:70
  50.8 0.7 collective-permute-start.13
  51.6 1.6 %collective-permute-done.22 = f32[256,128]{1,0:T(8,128)S(1)} collective-permute-done((f32[256,128]{1,0:T(8,128)S(1)}, f32[256,128]{1,0:T(8,128)S(1)}, u32[]{:S(2)}, u32[]{:S(2)}) %collective-permute-start.22) | collective-permute-done | bytes 131104 | tf_op jit(solution)/shard_map/scatter_moments/ppermute | solution.py:70
  53.2 1.7 %collective-permute-start.23 = (f32[128,128]{1,0:T(8,128)S(1)}, f32[128,128]{1,0:T(8,128)S(1)}, u32[]{:S(2)}, u32[]{:S(2)}) collective-permute-start(f32[128,128]{1,0:T(8,128)S(1)} %slice.108), channel_id=1, source_target_pairs={{0,2},{1,5},{2,0},{3,7},{4,6},{5,1},{6,4},{7,3},{8,10},{9,13},{10,... | collective-permute-start | bytes 196616 | tf_op jit(solution)/shard_map/scatter_moments/ppermute | solution.py:70
  54.9 0.9 %collective-permute-done.13 = f32[136,128]{1,0:T(8,128)S(1)} collective-permute-done((f32[136,128]{1,0:T(8,128)S(1)}, f32[136,128]{1,0:T(8,128)S(1)}, u32[]{:S(2)}, u32[]{:S(2)}) %collective-permute-start.13) | collective-permute-done | bytes 69664 | tf_op jit(solution)/shard_map/scatter_moments/ppermute | solution.py:70
  55.8 2.3 %collective-permute-start.14 = (f32[136,128]{1,0:T(8,128)S(1)}, f32[136,128]{1,0:T(8,128)S(1)}, u32[]{:S(2)}, u32[]{:S(2)}) collective-permute-start(f32[136,128]{1,0:T(8,128)S(1)} %pad_maximum_fusion.9), channel_id=1, source_target_pairs={{0,8},{1,9},{2,10},{3,11},{4,12},{5,13},{6,14},{7,15},{8,0},{9,1},... | collective-permute-start | bytes 208904 | tf_op jit(solution)/shard_map/scatter_moments/ppermute | solution.py:70
  58.2 2.7 %collective-permute-start.24 = (f32[128,128]{1,0:T(8,128)S(1)}, f32[128,128]{1,0:T(8,128)S(1)}, u32[]{:S(2)}, u32[]{:S(2)}) collective-permute-start(f32[128,128]{1,0:T(8,128)S(1)} %slice_add_fusion.5), channel_id=1, source_target_pairs={{0,8},{1,9},{2,10},{3,11},{4,12},{5,13},{6,14},{7,15},{8,0},{9,1},... | collective-permute-start | bytes 196616 | tf_op jit(solution)/shard_map/scatter_moments/ppermute | solution.py:70
  60.9 2.5 %collective-permute-done.24 = f32[128,128]{1,0:T(8,128)S(1)} collective-permute-done((f32[128,128]{1,0:T(8,128)S(1)}, f32[128,128]{1,0:T(8,128)S(1)}, u32[]{:S(2)}, u32[]{:S(2)}) %collective-permute-start.24) | collective-permute-done | bytes 65568 | tf_op jit(solution)/shard_map/scatter_moments/ppermute | solution.py:70
  63.4 1.4 %collective-permute-start.25 = (f32[128,128]{1,0:T(8,128)S(1)}, f32[128,128]{1,0:T(8,128)S(1)}, u32[]{:S(2)}, u32[]{:S(2)}) collective-permute-start(f32[128,128]{1,0:T(8,128)S(1)} %add.70), channel_id=1, source_target_pairs={{0,2},{1,5},{2,0},{3,7},{4,6},{5,1},{6,4},{7,3},{8,10},{9,13},{10,... | collective-permute-start | bytes 196616 | tf_op jit(solution)/shard_map/gather_moments/ppermute | solution.py:70
  64.8 2.0 %collective-permute-start.15 = (f32[128,128]{1,0:T(8,128)S(1)}, f32[128,128]{1,0:T(8,128)S(1)}, u32[]{:S(2)}, u32[]{:S(2)}) collective-permute-start(f32[128,128]{1,0:T(8,128)S(1)} %slice_add_fusion.6), channel_id=1, source_target_pairs={{0,4},{1,17},{2,6},{3,19},{4,0},{5,21},{6,2},{7,23},{8,12},{9,25},... | collective-permute-start | bytes 196616 | tf_op jit(solution)/shard_map/gather_moments/ppermute | solution.py:70
  66.9 0.9 %collective-permute-done.25 = f32[128,128]{1,0:T(8,128)S(1)} collective-permute-done((f32[128,128]{1,0:T(8,128)S(1)}, f32[128,128]{1,0:T(8,128)S(1)}, u32[]{:S(2)}, u32[]{:S(2)}) %collective-permute-start.25) | collective-permute-done | bytes 65568 | tf_op jit(solution)/shard_map/gather_moments/ppermute | solution.py:70
  67.8 2.4 %collective-permute-start.26 = (f32[256,128]{1,0:T(8,128)S(1)}, f32[256,128]{1,0:T(8,128)S(1)}, u32[]{:S(2)}, u32[]{:S(2)}) collective-permute-start(f32[256,128]{1,0:T(8,128)S(1)} %pad_maximum_fusion.7), channel_id=1, source_target_pairs={{0,4},{1,3},{2,6},{3,1},{4,0},{5,7},{6,2},{7,5},{8,12},{9,11},{10,... | collective-permute-start | bytes 393224 | tf_op jit(solution)/shard_map/gather_moments/ppermute | solution.py:70
  70.1 0.0 collective-permute-done.15
  70.1 1.6 %collective-permute-start.16 = (f32[256,128]{1,0:T(8,128)S(1)}, f32[256,128]{1,0:T(8,128)S(1)}, u32[]{:S(2)}, u32[]{:S(2)}) collective-permute-start(f32[256,128]{1,0:T(8,128)S(1)} %pad_maximum_fusion.6), channel_id=1, source_target_pairs={{0,16},{1,3},{2,18},{3,1},{4,20},{5,7},{6,22},{7,5},{8,24},{9,11},... | collective-permute-start | bytes 393224 | tf_op jit(solution)/shard_map/gather_moments/ppermute | solution.py:70
  71.7 1.3 %collective-permute-done.26 = f32[256,128]{1,0:T(8,128)S(1)} collective-permute-done((f32[256,128]{1,0:T(8,128)S(1)}, f32[256,128]{1,0:T(8,128)S(1)}, u32[]{:S(2)}, u32[]{:S(2)}) %collective-permute-start.26) | collective-permute-done | bytes 131104 | tf_op jit(solution)/shard_map/gather_moments/ppermute | solution.py:70
  73.1 1.8 %collective-permute-start.27 = (f32[512,128]{1,0:T(8,128)S(1)}, f32[512,128]{1,0:T(8,128)S(1)}, u32[]{:S(2)}, u32[]{:S(2)}) collective-permute-start(f32[512,128]{1,0:T(8,128)S(1)} %pad_maximum_fusion.2.refs_4_), channel_id=1, source_target_pairs={{0,16},{1,17},{2,18},{3,19},{4,20},{5,21},{6,22},{7,23},{8,24},{9,... | collective-permute-start | bytes 786440 | tf_op jit(solution)/shard_map/gather_moments/ppermute | solution.py:70
  74.9 1.3 %collective-permute-done.16 = f32[256,128]{1,0:T(8,128)S(1)} collective-permute-done((f32[256,128]{1,0:T(8,128)S(1)}, f32[256,128]{1,0:T(8,128)S(1)}, u32[]{:S(2)}, u32[]{:S(2)}) %collective-permute-start.16) | collective-permute-done | bytes 131104 | tf_op jit(solution)/shard_map/gather_moments/ppermute | solution.py:70
  76.2 1.3 %collective-permute-start.17 = (f32[512,128]{1,0:T(8,128)S(1)}, f32[512,128]{1,0:T(8,128)S(1)}, u32[]{:S(2)}, u32[]{:S(2)}) collective-permute-start(f32[512,128]{1,0:T(8,128)S(1)} %pad_maximum_fusion.1.refs_0_), channel_id=1, source_target_pairs={{0,2},{1,5},{2,0},{3,7},{4,6},{5,1},{6,4},{7,3},{8,10},{9,13},{10,... | collective-permute-start | bytes 786440 | tf_op jit(solution)/shard_map/gather_moments/ppermute | solution.py:70
  77.5 0.5 collective-permute-start.18
  78.0 1.5 %collective-permute-done.27.refs_5_ = f32[512,128]{1,0:T(8,128)S(1)} collective-permute-done((f32[512,128]{1,0:T(8,128)S(1)}, f32[512,128]{1,0:T(8,128)S(1)}, u32[]{:S(2)}, u32[]{:S(2)}) %collective-permute-start.27) | collective-permute-done | bytes 262176 | tf_op jit(solution)/shard_map/gather_moments/ppermute | solution.py:70
  79.5 3.1 %collective-permute-done.17.refs_1_ = f32[512,128]{1,0:T(8,128)S(1)} collective-permute-done((f32[512,128]{1,0:T(8,128)S(1)}, f32[512,128]{1,0:T(8,128)S(1)}, u32[]{:S(2)}, u32[]{:S(2)}) %collective-permute-start.17) | collective-permute-done | bytes 262176 | tf_op jit(solution)/shard_map/gather_moments/ppermute | solution.py:70
  82.6 0.5 collective-permute-start.30
  83.1 1.0 %collective-permute-done.30 = f32[8,128]{1,0:T(8,128)S(1)} collective-permute-done((f32[8,128]{1,0:T(8,128)S(1)}, f32[8,128]{1,0:T(8,128)S(1)}, u32[]{:S(2)}, u32[]{:S(2)}) %collective-permute-start.30) | collective-permute-done | bytes 4128 | tf_op jit(solution)/shard_map/scatter_moments/ppermute | solution.py:70
  84.2 0.0 collective-permute-done.28.refs_6_
  84.2 0.0 collective-permute-done.18.refs_2_
  84.2 0.0 collective-permute-done.29.refs_7_
  84.2 2.4 %shard_map.86 = (f32[1024,256]{1,0:T(8,128)}, f32[1024,256]{1,0:T(8,128)}, f32[8,128]{1,0:T(8,128)}) custom-call(s32[5,16]{1,0:T(8,128)S(1)} %dynamic-slice_bitcast_fusion.table, f32[512,128]{1,0:T(8,128)S(1)} %pad_maximum_fusion.1.refs_0_, f32[512,128]{1,0:T(8,128)S(1)} %collective-permute-done.17.refs_1_, f32[512,128]{1,0:T(8,128)S(1)} %collective-permute-done.18.refs_2_, ...), custom_call_target="tpu_custom_call" | custom-call | flops 2097152 | bytes 4194304 | tf_op jit(solution)/shard_map/pallas_call | solution.py:357
  (42 shorter events, 0.4 us)
Async XLA Ops:
  0.6 8.0 %collective-permute-start = (f32[64,256]{1,0:T(8,128)}, f32[64,256]{1,0:T(8,128)S(1)}, u32[]{:S(2)}, u32[]{:S(2)}) collective-permute-start(f32[64,256]{1,0:T(8,128)} %refs_2_.1), channel_id=1, source_target_pairs={{0,8},{1,9},{2,10},{3,11},{4,12},{5,13},{6,14},{7,15},{8,0},{9,1},... | collective-permute-start | bytes 196616 | tf_op jit(solution)/shard_map/gather_parameters/ppermute | solution.py:70
  4.7 6.7 %collective-permute-start.1 = (f32[64,256]{1,0:T(8,128)}, f32[64,256]{1,0:T(8,128)S(1)}, u32[]{:S(2)}, u32[]{:S(2)}) collective-permute-start(f32[64,256]{1,0:T(8,128)} %refs_3_.1), channel_id=1, source_target_pairs={{0,8},{1,9},{2,10},{3,11},{4,12},{5,13},{6,14},{7,15},{8,0},{9,1},... | collective-permute-start | bytes 196616 | tf_op jit(solution)/shard_map/gather_parameters/ppermute | solution.py:70
  11.5 6.5 %collective-permute-start.4 = (f32[128,256]{1,0:T(8,128)S(1)}, f32[128,256]{1,0:T(8,128)S(1)}, u32[]{:S(2)}, u32[]{:S(2)}) collective-permute-start(f32[128,256]{1,0:T(8,128)S(1)} %pad_maximum_fusion.5), channel_id=1, source_target_pairs={{0,4},{1,3},{2,6},{3,1},{4,0},{5,7},{6,2},{7,5},{8,12},{9,11},{10,... | collective-permute-start | bytes 393224 | tf_op jit(solution)/shard_map/gather_parameters/ppermute | solution.py:70
  12.2 5.7 %collective-permute-start.2 = (f32[128,256]{1,0:T(8,128)S(1)}, f32[128,256]{1,0:T(8,128)S(1)}, u32[]{:S(2)}, u32[]{:S(2)}) collective-permute-start(f32[128,256]{1,0:T(8,128)S(1)} %pad_maximum_fusion.4), channel_id=1, source_target_pairs={{0,4},{1,3},{2,6},{3,1},{4,0},{5,7},{6,2},{7,5},{8,12},{9,11},{10,... | collective-permute-start | bytes 393224 | tf_op jit(solution)/shard_map/gather_parameters/ppermute | solution.py:70
  17.9 2.7 %collective-permute-start.6 = (f32[256,256]{1,0:T(8,128)S(1)}, f32[256,256]{1,0:T(8,128)S(1)}, u32[]{:S(2)}, u32[]{:S(2)}) collective-permute-start(f32[256,256]{1,0:T(8,128)S(1)} %constant_dynamic-update-slice_fusion.refs_0_), channel_id=1, source_target_pairs={{0,1},{1,0},{2,3},{3,2},{4,5},{5,4},{6,7},{7,6},{8,9},{9,8},{10,11... | collective-permute-start | bytes 786440 | tf_op jit(solution)/shard_map/gather_parameters/ppermute | solution.py:70
  18.0 2.6 %collective-permute-start.7 = (f32[256,256]{1,0:T(8,128)S(1)}, f32[256,256]{1,0:T(8,128)S(1)}, u32[]{:S(2)}, u32[]{:S(2)}) collective-permute-start(f32[256,256]{1,0:T(8,128)S(1)} %constant_dynamic-update-slice_fusion.3.refs_2_), channel_id=1, source_target_pairs={{0,1},{1,0},{2,3},{3,2},{4,5},{5,4},{6,7},{7,6},{8,9},{9,8},{10,11... | collective-permute-start | bytes 786440 | tf_op jit(solution)/shard_map/gather_parameters/ppermute | solution.py:70
  18.6 6.4 %collective-permute-start.3 = (f32[256,256]{1,0:T(8,128)S(1)}, f32[256,256]{1,0:T(8,128)S(1)}, u32[]{:S(2)}, u32[]{:S(2)}) collective-permute-start(f32[256,256]{1,0:T(8,128)S(1)} %constant_dynamic-update-slice_fusion.refs_0_), channel_id=1, source_target_pairs={{0,2},{1,5},{2,0},{3,7},{4,6},{5,1},{6,4},{7,3},{8,10},{9,13},{10,... | collective-permute-start | bytes 786440 | tf_op jit(solution)/shard_map/gather_parameters/ppermute | solution.py:70
  20.3 7.5 %collective-permute-start.5 = (f32[256,256]{1,0:T(8,128)S(1)}, f32[256,256]{1,0:T(8,128)S(1)}, u32[]{:S(2)}, u32[]{:S(2)}) collective-permute-start(f32[256,256]{1,0:T(8,128)S(1)} %constant_dynamic-update-slice_fusion.3.refs_2_), channel_id=1, source_target_pairs={{0,2},{1,5},{2,0},{3,7},{4,6},{5,1},{6,4},{7,3},{8,10},{9,13},{10,... | collective-permute-start | bytes 786440 | tf_op jit(solution)/shard_map/gather_parameters/ppermute | solution.py:70
  27.7 1.5 %collective-permute-start.8 = (f32[256,256]{1,0:T(8,128)S(1)}, f32[256,256]{1,0:T(8,128)S(1)}, u32[]{:S(2)}, u32[]{:S(2)}) collective-permute-start(f32[256,256]{1,0:T(8,128)S(1)} %collective-permute-done.3.refs_0_), channel_id=1, source_target_pairs={{0,1},{1,0},{2,3},{3,2},{4,5},{5,4},{6,7},{7,6},{8,9},{9,8},{10,11... | collective-permute-start | bytes 786440 | tf_op jit(solution)/shard_map/gather_parameters/ppermute | solution.py:70
  27.8 1.9 %collective-permute-start.9 = (f32[256,256]{1,0:T(8,128)S(1)}, f32[256,256]{1,0:T(8,128)S(1)}, u32[]{:S(2)}, u32[]{:S(2)}) collective-permute-start(f32[256,256]{1,0:T(8,128)S(1)} %collective-permute-done.5.refs_2_), channel_id=1, source_target_pairs={{0,1},{1,0},{2,3},{3,2},{4,5},{5,4},{6,7},{7,6},{8,9},{9,8},{10,11... | collective-permute-start | bytes 786440 | tf_op jit(solution)/shard_map/gather_parameters/ppermute | solution.py:70
  36.6 2.4 %collective-permute-start.10 = (f32[1032,128]{1,0:T(8,128)S(1)}, f32[1032,128]{1,0:T(8,128)S(1)}, u32[]{:S(2)}, u32[]{:S(2)}) collective-permute-start(f32[1032,128]{1,0:T(8,128)S(1)} %get-tuple-element.44), channel_id=1, source_target_pairs={{0,1},{1,0},{2,3},{3,2},{4,5},{5,4},{6,7},{7,6},{8,9},{9,8},{10,11... | collective-permute-start | bytes 1585160 | tf_op jit(solution)/shard_map/scatter_moments/ppermute | solution.py:70
  36.8 4.1 %collective-permute-start.20 = (f32[1024,128]{1,0:T(8,128)S(1)}, f32[1024,128]{1,0:T(8,128)S(1)}, u32[]{:S(2)}, u32[]{:S(2)}) collective-permute-start(f32[1024,128]{1,0:T(8,128)S(1)} %get-tuple-element.47), channel_id=1, source_target_pairs={{0,1},{1,0},{2,3},{3,2},{4,5},{5,4},{6,7},{7,6},{8,9},{9,8},{10,11... | collective-permute-start | bytes 1572872 | tf_op jit(solution)/shard_map/scatter_moments/ppermute | solution.py:70
  39.1 6.5 %collective-permute-start.11 = (f32[520,128]{1,0:T(8,128)S(1)}, f32[520,128]{1,0:T(8,128)S(1)}, u32[]{:S(2)}, u32[]{:S(2)}) collective-permute-start(f32[520,128]{1,0:T(8,128)S(1)} %pad_maximum_fusion), channel_id=1, source_target_pairs={{0,2},{1,5},{2,0},{3,7},{4,6},{5,1},{6,4},{7,3},{8,10},{9,13},{10,... | collective-permute-start | bytes 798728 | tf_op jit(solution)/shard_map/scatter_moments/ppermute | solution.py:70
  41.0 7.1 %collective-permute-start.21 = (f32[512,128]{1,0:T(8,128)S(1)}, f32[512,128]{1,0:T(8,128)S(1)}, u32[]{:S(2)}, u32[]{:S(2)}) collective-permute-start(f32[512,128]{1,0:T(8,128)S(1)} %slice.104), channel_id=1, source_target_pairs={{0,16},{1,17},{2,18},{3,19},{4,20},{5,21},{6,22},{7,23},{8,24},{9,... | collective-permute-start | bytes 786440 | tf_op jit(solution)/shard_map/scatter_moments/ppermute | solution.py:70
  45.7 5.1 %collective-permute-start.12 = (f32[264,128]{1,0:T(8,128)S(1)}, f32[264,128]{1,0:T(8,128)S(1)}, u32[]{:S(2)}, u32[]{:S(2)}) collective-permute-start(f32[264,128]{1,0:T(8,128)S(1)} %pad_maximum_fusion.3), channel_id=1, source_target_pairs={{0,16},{1,3},{2,18},{3,1},{4,20},{5,7},{6,22},{7,5},{8,24},{9,11},... | collective-permute-start | bytes 405512 | tf_op jit(solution)/shard_map/scatter_moments/ppermute | solution.py:70
  48.2 5.0 %collective-permute-start.22 = (f32[256,128]{1,0:T(8,128)S(1)}, f32[256,128]{1,0:T(8,128)S(1)}, u32[]{:S(2)}, u32[]{:S(2)}) collective-permute-start(f32[256,128]{1,0:T(8,128)S(1)} %slice.106), channel_id=1, source_target_pairs={{0,4},{1,3},{2,6},{3,1},{4,0},{5,7},{6,2},{7,5},{8,12},{9,11},{10,... | collective-permute-start | bytes 393224 | tf_op jit(solution)/shard_map/scatter_moments/ppermute | solution.py:70
  50.8 5.0 %collective-permute-start.13 = (f32[136,128]{1,0:T(8,128)S(1)}, f32[136,128]{1,0:T(8,128)S(1)}, u32[]{:S(2)}, u32[]{:S(2)}) collective-permute-start(f32[136,128]{1,0:T(8,128)S(1)} %pad_maximum_fusion.8), channel_id=1, source_target_pairs={{0,4},{1,17},{2,6},{3,19},{4,0},{5,21},{6,2},{7,23},{8,12},{9,25},... | collective-permute-start | bytes 208904 | tf_op jit(solution)/shard_map/scatter_moments/ppermute | solution.py:70
  53.2 5.0 %collective-permute-start.23 = (f32[128,128]{1,0:T(8,128)S(1)}, f32[128,128]{1,0:T(8,128)S(1)}, u32[]{:S(2)}, u32[]{:S(2)}) collective-permute-start(f32[128,128]{1,0:T(8,128)S(1)} %slice.108), channel_id=1, source_target_pairs={{0,2},{1,5},{2,0},{3,7},{4,6},{5,1},{6,4},{7,3},{8,10},{9,13},{10,... | collective-permute-start | bytes 196616 | tf_op jit(solution)/shard_map/scatter_moments/ppermute | solution.py:70
  55.8 9.0 %collective-permute-start.14 = (f32[136,128]{1,0:T(8,128)S(1)}, f32[136,128]{1,0:T(8,128)S(1)}, u32[]{:S(2)}, u32[]{:S(2)}) collective-permute-start(f32[136,128]{1,0:T(8,128)S(1)} %pad_maximum_fusion.9), channel_id=1, source_target_pairs={{0,8},{1,9},{2,10},{3,11},{4,12},{5,13},{6,14},{7,15},{8,0},{9,1},... | collective-permute-start | bytes 208904 | tf_op jit(solution)/shard_map/scatter_moments/ppermute | solution.py:70
  58.2 5.2 %collective-permute-start.24 = (f32[128,128]{1,0:T(8,128)S(1)}, f32[128,128]{1,0:T(8,128)S(1)}, u32[]{:S(2)}, u32[]{:S(2)}) collective-permute-start(f32[128,128]{1,0:T(8,128)S(1)} %slice_add_fusion.5), channel_id=1, source_target_pairs={{0,8},{1,9},{2,10},{3,11},{4,12},{5,13},{6,14},{7,15},{8,0},{9,1},... | collective-permute-start | bytes 196616 | tf_op jit(solution)/shard_map/scatter_moments/ppermute | solution.py:70
  63.4 4.3 %collective-permute-start.25 = (f32[128,128]{1,0:T(8,128)S(1)}, f32[128,128]{1,0:T(8,128)S(1)}, u32[]{:S(2)}, u32[]{:S(2)}) collective-permute-start(f32[128,128]{1,0:T(8,128)S(1)} %add.70), channel_id=1, source_target_pairs={{0,2},{1,5},{2,0},{3,7},{4,6},{5,1},{6,4},{7,3},{8,10},{9,13},{10,... | collective-permute-start | bytes 196616 | tf_op jit(solution)/shard_map/gather_moments/ppermute | solution.py:70
  64.8 5.3 %collective-permute-start.15 = (f32[128,128]{1,0:T(8,128)S(1)}, f32[128,128]{1,0:T(8,128)S(1)}, u32[]{:S(2)}, u32[]{:S(2)}) collective-permute-start(f32[128,128]{1,0:T(8,128)S(1)} %slice_add_fusion.6), channel_id=1, source_target_pairs={{0,4},{1,17},{2,6},{3,19},{4,0},{5,21},{6,2},{7,23},{8,12},{9,25},... | collective-permute-start | bytes 196616 | tf_op jit(solution)/shard_map/gather_moments/ppermute | solution.py:70
  67.8 5.3 %collective-permute-start.26 = (f32[256,128]{1,0:T(8,128)S(1)}, f32[256,128]{1,0:T(8,128)S(1)}, u32[]{:S(2)}, u32[]{:S(2)}) collective-permute-start(f32[256,128]{1,0:T(8,128)S(1)} %pad_maximum_fusion.7), channel_id=1, source_target_pairs={{0,4},{1,3},{2,6},{3,1},{4,0},{5,7},{6,2},{7,5},{8,12},{9,11},{10,... | collective-permute-start | bytes 393224 | tf_op jit(solution)/shard_map/gather_moments/ppermute | solution.py:70
  70.1 6.0 %collective-permute-start.16 = (f32[256,128]{1,0:T(8,128)S(1)}, f32[256,128]{1,0:T(8,128)S(1)}, u32[]{:S(2)}, u32[]{:S(2)}) collective-permute-start(f32[256,128]{1,0:T(8,128)S(1)} %pad_maximum_fusion.6), channel_id=1, source_target_pairs={{0,16},{1,3},{2,18},{3,1},{4,20},{5,7},{6,22},{7,5},{8,24},{9,11},... | collective-permute-start | bytes 393224 | tf_op jit(solution)/shard_map/gather_moments/ppermute | solution.py:70
  73.1 6.4 %collective-permute-start.27 = (f32[512,128]{1,0:T(8,128)S(1)}, f32[512,128]{1,0:T(8,128)S(1)}, u32[]{:S(2)}, u32[]{:S(2)}) collective-permute-start(f32[512,128]{1,0:T(8,128)S(1)} %pad_maximum_fusion.2.refs_4_), channel_id=1, source_target_pairs={{0,16},{1,17},{2,18},{3,19},{4,20},{5,21},{6,22},{7,23},{8,24},{9,... | collective-permute-start | bytes 786440 | tf_op jit(solution)/shard_map/gather_moments/ppermute | solution.py:70
  76.2 6.4 %collective-permute-start.17 = (f32[512,128]{1,0:T(8,128)S(1)}, f32[512,128]{1,0:T(8,128)S(1)}, u32[]{:S(2)}, u32[]{:S(2)}) collective-permute-start(f32[512,128]{1,0:T(8,128)S(1)} %pad_maximum_fusion.1.refs_0_), channel_id=1, source_target_pairs={{0,2},{1,5},{2,0},{3,7},{4,6},{5,1},{6,4},{7,3},{8,10},{9,13},{10,... | collective-permute-start | bytes 786440 | tf_op jit(solution)/shard_map/gather_moments/ppermute | solution.py:70
  77.5 6.7 %collective-permute-start.28 = (f32[512,128]{1,0:T(8,128)S(1)}, f32[512,128]{1,0:T(8,128)S(1)}, u32[]{:S(2)}, u32[]{:S(2)}) collective-permute-start(f32[512,128]{1,0:T(8,128)S(1)} %pad_maximum_fusion.2.refs_4_), channel_id=1, source_target_pairs={{0,1},{1,0},{2,3},{3,2},{4,5},{5,4},{6,7},{7,6},{8,9},{9,8},{10,11... | collective-permute-start | bytes 786440 | tf_op jit(solution)/shard_map/gather_moments/ppermute | solution.py:70
  77.5 6.7 %collective-permute-start.18 = (f32[512,128]{1,0:T(8,128)S(1)}, f32[512,128]{1,0:T(8,128)S(1)}, u32[]{:S(2)}, u32[]{:S(2)}) collective-permute-start(f32[512,128]{1,0:T(8,128)S(1)} %pad_maximum_fusion.1.refs_0_), channel_id=1, source_target_pairs={{0,1},{1,0},{2,3},{3,2},{4,5},{5,4},{6,7},{7,6},{8,9},{9,8},{10,11... | collective-permute-start | bytes 786440 | tf_op jit(solution)/shard_map/gather_moments/ppermute | solution.py:70
  79.5 4.7 %collective-permute-start.29 = (f32[512,128]{1,0:T(8,128)S(1)}, f32[512,128]{1,0:T(8,128)S(1)}, u32[]{:S(2)}, u32[]{:S(2)}) collective-permute-start(f32[512,128]{1,0:T(8,128)S(1)} %collective-permute-done.27.refs_5_), channel_id=1, source_target_pairs={{0,1},{1,0},{2,3},{3,2},{4,5},{5,4},{6,7},{7,6},{8,9},{9,8},{10,11... | collective-permute-start | bytes 786440 | tf_op jit(solution)/shard_map/gather_moments/ppermute | solution.py:70
  82.6 1.6 %collective-permute-start.19 = (f32[512,128]{1,0:T(8,128)S(1)}, f32[512,128]{1,0:T(8,128)S(1)}, u32[]{:S(2)}, u32[]{:S(2)}) collective-permute-start(f32[512,128]{1,0:T(8,128)S(1)} %collective-permute-done.17.refs_1_), channel_id=1, source_target_pairs={{0,1},{1,0},{2,3},{3,2},{4,5},{5,4},{6,7},{7,6},{8,9},{9,8},{10,11... | collective-permute-start | bytes 786440 | tf_op jit(solution)/shard_map/gather_moments/ppermute | solution.py:70
  82.6 1.5 %collective-permute-start.30 = (f32[8,128]{1,0:T(8,128)S(1)}, f32[8,128]{1,0:T(8,128)S(1)}, u32[]{:S(2)}, u32[]{:S(2)}) collective-permute-start(f32[8,128]{1,0:T(8,128)S(1)} %slice_add_fusion.8), channel_id=1, source_target_pairs={{0,1},{1,0},{2,3},{3,2},{4,5},{5,4},{6,7},{7,6},{8,9},{9,8},{10,11... | collective-permute-start | bytes 12296 | tf_op jit(solution)/shard_map/scatter_moments/ppermute | solution.py:70

commit v4 on v3

--- a/solution.py
+++ b/solution.py
@@ -37,8 +37,8 @@
         per = piece // self.unit
         first, second, third, *others = split
         orders = (
-            ((first, second, third), (third, first, second)),
-            ((second, third, first), (second, first, third)),
+            ((third, first, second), (second, third, first)),
+            ((first, third, second), (second, first, third)),
         )
         self.halving = [
             [(0, 0)] + list(zip(zero, one)) + [(b, b) for b in others] for zero, one in orders
@@ -151,49 +151,62 @@
                 ]
 
 
-def early_kernel(plan, table, *refs):
-    mean_refs, variance_refs = refs[0:2], refs[2:4]
-    log_weights, stack_ref, scores_ref = refs[4:7]
-    weights, offsets = refs[7:]
+def early_kernel(plan, first_units, table, *refs):
+    pieces = len(first_units)
+    mean_refs, variance_refs = refs[:pieces], refs[pieces : 2 * pieces]
+    log_weights, stack_ref, powers_ref, highest_ref, totals_ref, weights, offsets = refs[2 * pieces :]
     count = stack_ref.shape[0]
     block = min(BLOCK, count)
-    firsts = (0, plan.units // 2)
-    build_weights(plan.unit, table, firsts, mean_refs, variance_refs, log_weights, weights, offsets)
+    build_weights(plan.unit, table, first_units, mean_refs, variance_refs, log_weights, weights, offsets)
     for first in range(0, count, block):
-        scores_ref[:, first : first + block] = block_scores(
-            stack_ref[first : first + block, :], weights, offsets
-        )
+        here = slice(first, first + block)
+        scores = block_scores(stack_ref[here, :], weights, offsets)
+        highest = jnp.max(scores, axis=0, keepdims=True)
+        powers = jnp.exp2(scores - highest)
+        powers_ref[:, here] = powers
+        highest_ref[:, here] = highest
+        totals_ref[:, here] = jnp.sum(powers, axis=0, keepdims=True)
 
 
 def late_kernel(plan, table, *refs):
-    mean_refs, variance_refs = refs[0:2], refs[2:4]
-    log_weights, stack_ref, early_ref = refs[4:7]
-    sent_refs, counts_ref, scores_ref, own_ref = refs[7:9], refs[9], refs[10], refs[11]
-    weights, offsets, moments, partial, staged = refs[12:]
+    mean_ref, variance_ref, log_weights, stack_ref = refs[:4]
+    (powers_1, highest_1, totals_1), (powers_2, highest_2, totals_2) = refs[4:7], refs[7:10]
+    sent_refs, counts_ref, scores_ref, own_ref = refs[10:12], refs[12], refs[13], refs[14]
+    weights, offsets, moments, partial, staged = refs[15:]
     count, width = stack_ref.shape[0], stack_ref.shape[1] // 3
-    block = min(BLOCK, count)
-    quarter = weights.shape[0] // 2
-    quarters = plan.units // 4
-    firsts = (quarters, 3 * quarters)
-    build_weights(plan.unit, table, firsts, mean_refs, variance_refs, log_weights, weights, offsets)
+    block = min(2 * BLOCK, count)
+    quarter = weights.shape[0]
+    firsts = (3 * plan.units // 4,)
+    build_weights(plan.unit, table, firsts, (mean_ref,), (variance_ref,), log_weights, weights, offsets)
     for first in range(0, count, block):
-        stack = stack_ref[first : first + block, :]
-        late = block_scores(stack, weights, offsets)
-        early = early_ref[:, first : first + block]
+        here = slice(first, first + block)
+        stack = stack_ref[here, :]
+        scores = block_scores(stack, weights, offsets)
         highest = jnp.maximum(
-            jnp.max(early, axis=0, keepdims=True), jnp.max(late, axis=0, keepdims=True)
-        )
-        early = jnp.exp2(early - highest)
-        late = jnp.exp2(late - highest)
-        totals = jnp.sum(early, axis=0, keepdims=True) + jnp.sum(late, axis=0, keepdims=True)
-        scores_ref[:, first : first + block] = (highest + jnp.log2(totals)) * (LN2 / width)
+            jnp.maximum(highest_1[:, here], highest_2[:, here]), jnp.max(scores, axis=0, keepdims=True)
+        )
+        scale_1 = jnp.exp2(highest_1[:, here] - highest)
+        scale_2 = jnp.exp2(highest_2[:, here] - highest)
+        powers = jnp.exp2(scores - highest)
+        totals = (
+            totals_1[:, here] * scale_1
+            + totals_2[:, here] * scale_2
+            + jnp.sum(powers, axis=0, keepdims=True)
+        )
+        scores_ref[:, here] = (highest + jnp.log2(totals)) * (LN2 / width)
         inverse = 1.0 / totals
-        early = (early * inverse).astype(BF16)
-        late = (late * inverse).astype(BF16)
-        own_ref[:quarter, first : first + block] = early[:quarter]
-        own_ref[quarter:, first : first + block] = late[:quarter]
+        scale_1 = scale_1 * inverse
+        scale_2 = scale_2 * inverse
+        parts = (
+            (powers_1[:quarter, here] * scale_1).astype(BF16),
+            (powers_2[:, here] * scale_2).astype(BF16),
+            (powers_1[quarter:, here] * scale_1).astype(BF16),
+            (powers * inverse).astype(BF16),
+        )
+        own_ref[:quarter, here] = parts[0]
+        own_ref[quarter:, here] = parts[1]
         added = jnp.dot(
-            jnp.concatenate([early[quarter:], late[quarter:]], axis=0),
+            jnp.concatenate(parts[2:], axis=0),
             stack[:, width:],
             preferred_element_type=F32,
         )
@@ -201,7 +214,7 @@
             moments[...] = added
         else:
             moments[...] += added
-        for at, part in enumerate((early[:quarter], late[:quarter], early[quarter:], late[quarter:])):
+        for at, part in enumerate(parts):
             rounded = part.astype(F32)
             counted = rounded[:, :LANES]
             for b in range(1, block // LANES):
@@ -268,30 +281,30 @@
     return held, stack, log_weights
 
 
-def early_scores(plan, table, means, variances, log_weights, stack):
+def early_scores(plan, table, first_units, means, variances, log_weights, stack):
     count, width = stack.shape[0], stack.shape[1] // 3
     comps = sum(m.shape[0] for m in means)
     return call(
-        early_kernel,
+        lambda plan, *refs: early_kernel(plan, first_units, *refs),
         plan,
         table,
         [*means, *variances, log_weights, stack],
-        [((comps, count), F32)],
+        [((comps, count), F32), ((1, count), F32), ((1, count), F32)],
         [((comps, 5 * width), BF16), ((comps, LANES), F32)],
         10 * comps * count * width,
         24,
-    )[0]
-
-
-def mixture(plan, table, means, variances, log_weights, stack, early):
+    )
+
+
+def mixture(plan, table, mean, variance, log_weights, stack, early):
     count, width = stack.shape[0], stack.shape[1] // 3
-    half = sum(m.shape[0] for m in means)
+    half = 2 * mean.shape[0]
     rows = half * (width // LANES)
     *sent, counts, row_scores, own = call(
         late_kernel,
         plan,
         table,
-        [*means, *variances, log_weights, stack, early],
+        [mean, variance, log_weights, stack, *early],
         [
             ((rows + COUNT_ROWS, LANES), F32),
             ((rows, LANES), F32),
@@ -300,13 +313,13 @@
             ((half, count), BF16),
         ],
         [
-            ((half, 5 * width), BF16),
-            ((half, LANES), F32),
+            ((half // 2, 5 * width), BF16),
+            ((half // 2, LANES), F32),
             ((half, 2 * width), F32),
             ((2 * half, LANES), F32),
             ((2 * half, LANES), F32),
         ],
-        16 * half * count * width,
+        9 * half * count * width,
         32,
     )
     kept = call(
@@ -405,10 +418,13 @@
             held = double(plan, held, (step, step))
         last = [plan.swap(h, plan.gather[-1]) for h in held]
         pairs = [(h, plan.swap(h, (0, 0))) for h in held]
-        early = early_scores(plan, table, *pairs, log_weights, stack)
+        firsts = (0, plan.units // 2)
+        early = early_scores(plan, table, firsts, *pairs, log_weights, stack)
         last, early = lax.optimization_barrier((last, early))
-        pairs = [(l, plan.swap(l, (0, 0))) for l in last]
-    sent, kept, counts, row_scores = mixture(plan, table, *pairs, log_weights, stack, early)
+        mates = [plan.swap(l, (0, 0)) for l in last]
+        firsts = (plan.units // 4,)
+        early += early_scores(plan, table, firsts, last[:1], last[1:], log_weights, stack)
+    sent, kept, counts, row_scores = mixture(plan, table, *mates, log_weights, stack, early)
     with jax.named_scope("scatter_moments"):
         kept, counts = scatter(plan, sent, kept, counts)
     with jax.named_scope("gather_moments"):

time: 86.8 us -> 84.6 us (0.975)
  starting transfers between devices: 35.4 us -> 30.7 us
  waiting for transfers between devices: 31.2 us -> 32.8 us
  Pallas kernels: 17.9 us -> 18.8 us
    ppermute x31, starting transfers between devices: 35.4 us -> 30.7 us  [swap(): return lax.ppermute(value, ('grp', 'comp'), pairs)]
    ppermute x31, waiting for transfers between devices: 31.2 us -> 32.8 us  [swap(): return lax.ppermute(value, ('grp', 'comp'), pairs)]
    pallas_call x4 -> x5, Pallas kernels: 15.5 us -> 16.4 us  [call(): pl.pallas_call(functools.partial(kernel, plan), in_specs=[pl.BlockSpec(me...]
  transfers between devices with their start and end apart: 31 -> 31, of which waited for: 18 -> 14; matrix products, arithmetic and copies ran while one was open for 1% -> 1% of each run, Pallas kernels for 10% -> 14%
where the time goes in v4:
time: 84.6 us; the launch traced here: 84.4 us
  waiting for transfers between devices  32.8 us (39%)
  starting transfers between devices  30.7 us (36%)
  Pallas kernels  18.8 us (22%)
  between operations  0.93 us (1%)
    ppermute x31, waiting for transfers between devices, swap(): return lax.ppermute(value, ('grp', 'comp'), pairs)  32.8 us
    ppermute x31, starting transfers between devices, swap(): return lax.ppermute(value, ('grp', 'comp'), pairs)  30.7 us
    pallas_call x5, Pallas kernels, call(): pl.pallas_call(functools.partial(kernel, plan), in_specs=[pl.BlockSpec(me...  16.4 us
    pallas_call x1, Pallas kernels, update(): pl.pallas_call(functools.partial(update_kernel, plan, len(first), total_r...  2.4 us
  transfers between devices with their start and end apart: 31, of which 14 were waited for; matrix products, arithmetic and copies ran while one was open for 1% of the time, Pallas kernels for 14%

profile of v4, /device:TPU:0, one launch (start us, length us, event | category | flops | bytes accessed | tf_op | source)
XLA Modules:
  0.0 84.4 jit_solution(12335369408227006242)
XLA Ops:
  0.6 4.1 %collective-permute-start = (f32[64,256]{1,0:T(8,128)}, f32[64,256]{1,0:T(8,128)S(1)}, u32[]{:S(2)}, u32[]{:S(2)}) collective-permute-start(f32[64,256]{1,0:T(8,128)} %refs_2_.1), channel_id=1, source_target_pairs={{0,8},{1,9},{2,10},{3,11},{4,12},{5,13},{6,14},{7,15},{8,0},{9,1},... | collective-permute-start | bytes 196616 | tf_op jit(solution)/shard_map/gather_parameters/ppermute | solution.py:70
  4.7 0.1 collective-permute-start.1
  4.8 0.7 dynamic-slice_bitcast_fusion.table.refs_0_
  5.5 3.1 %gather_parameters.3 = (f32[64,256]{1,0:T(8,128)S(1)}, f32[64,256]{1,0:T(8,128)S(1)}, bf16[2048,768]{1,0:T(8,128)(2,1)S(1)}, f32[1024,128]{1,0:T(8,128)S(1)}) custom-call(s32[5,16]{1,0:T(8,128)S(1)} %dynamic-slice_bitcast_fusion.table.refs_0_, bf16[2048,256]{1,0:T(8,128)(2,1)} %refs_0_.1, f32[8,128]{1,0:T(8,128)} %bitcast.5, f32[64,256]{1,0:T(8,128)} %refs_2_.1, ...), custom_call_target="tpu_custom_call" | custom-call | flops 4194304 | bytes 2367488 | tf_op jit(solution)/shard_map/gather_parameters/pallas_call | solution.py:256
  8.6 0.0 collective-permute-done
  8.6 2.8 %collective-permute-done.1 = f32[64,256]{1,0:T(8,128)S(1)} collective-permute-done((f32[64,256]{1,0:T(8,128)}, f32[64,256]{1,0:T(8,128)S(1)}, u32[]{:S(2)}, u32[]{:S(2)}) %collective-permute-start.1) | collective-permute-done | bytes 65568 | tf_op jit(solution)/shard_map/gather_parameters/ppermute | solution.py:70
  11.5 0.7 collective-permute-start.4
  12.2 1.4 %collective-permute-start.2 = (f32[128,256]{1,0:T(8,128)S(1)}, f32[128,256]{1,0:T(8,128)S(1)}, u32[]{:S(2)}, u32[]{:S(2)}) collective-permute-start(f32[128,256]{1,0:T(8,128)S(1)} %pad_maximum_fusion.4), channel_id=1, source_target_pairs={{0,4},{1,3},{2,6},{3,1},{4,0},{5,7},{6,2},{7,5},{8,12},{9,11},{10,... | collective-permute-start | bytes 393224 | tf_op jit(solution)/shard_map/gather_parameters/ppermute | solution.py:70
  13.6 4.3 %collective-permute-done.2 = f32[128,256]{1,0:T(8,128)S(1)} collective-permute-done((f32[128,256]{1,0:T(8,128)S(1)}, f32[128,256]{1,0:T(8,128)S(1)}, u32[]{:S(2)}, u32[]{:S(2)}) %collective-permute-start.2) | collective-permute-done | bytes 131104 | tf_op jit(solution)/shard_map/gather_parameters/ppermute | solution.py:70
  17.9 0.1 collective-permute-start.6
  18.0 0.0 collective-permute-done.4
  18.0 0.5 collective-permute-start.7
  18.6 1.7 %collective-permute-start.3 = (f32[256,256]{1,0:T(8,128)S(1)}, f32[256,256]{1,0:T(8,128)S(1)}, u32[]{:S(2)}, u32[]{:S(2)}) collective-permute-start(f32[256,256]{1,0:T(8,128)S(1)} %constant_dynamic-update-slice_fusion.refs_1_), channel_id=1, source_target_pairs={{0,2},{1,5},{2,0},{3,7},{4,6},{5,1},{6,4},{7,3},{8,10},{9,13},{10,... | collective-permute-start | bytes 786440 | tf_op jit(solution)/shard_map/gather_parameters/ppermute | solution.py:70
  20.3 0.3 collective-permute-start.5
  20.6 0.0 collective-permute-done.6.refs_2_
  20.6 4.2 %gather_parameters.4 = (f32[512,2048]{1,0:T(8,128)S(1)}, f32[1,2048]{1,0:T(1,128)S(1)}, f32[1,2048]{1,0:T(1,128)S(1)}) custom-call(s32[5,16]{1,0:T(8,128)S(1)} %dynamic-slice_bitcast_fusion.table.refs_0_, f32[256,256]{1,0:T(8,128)S(1)} %constant_dynamic-update-slice_fusion.refs_1_, f32[256,256]{1,0:T(8,128)S(1)} %collective-permute-done.6.refs_2_, ...), custom_call_target="tpu_custom_call" | custom-call | flops 2684354560 | bytes 9437184 | tf_op jit(solution)/shard_map/gather_parameters/pallas_call | solution.py:256
  24.8 0.2 collective-permute-done.3.refs_1_
  24.9 2.8 %collective-permute-done.5.refs_2_ = f32[256,256]{1,0:T(8,128)S(1)} collective-permute-done((f32[256,256]{1,0:T(8,128)S(1)}, f32[256,256]{1,0:T(8,128)S(1)}, u32[]{:S(2)}, u32[]{:S(2)}) %collective-permute-start.5) | collective-permute-done | bytes 262176 | tf_op jit(solution)/shard_map/gather_parameters/ppermute | solution.py:70
  27.8 0.5 collective-permute-start.9
  28.3 2.4 %gather_parameters.5 = (f32[256,2048]{1,0:T(8,128)S(1)}, f32[1,2048]{1,0:T(1,128)S(1)}, f32[1,2048]{1,0:T(1,128)S(1)}) custom-call(s32[5,16]{1,0:T(8,128)S(1)} %dynamic-slice_bitcast_fusion.table.refs_0_, f32[256,256]{1,0:T(8,128)S(1)} %collective-permute-done.3.refs_1_, f32[256,256]{1,0:T(8,128)S(1)} %collective-permute-done.5.refs_2_, ...), custom_call_target="tpu_custom_call" | custom-call | flops 1342177280 | bytes 8388608 | tf_op jit(solution)/shard_map/gather_parameters/pallas_call | solution.py:256
  30.6 0.0 collective-permute-done.8.refs_0_
  30.6 0.0 collective-permute-done.9.refs_1_
  30.6 5.0 %shard_map.84 = (f32[1032,128]{1,0:T(8,128)S(1)}, f32[1024,128]{1,0:T(8,128)S(1)}, f32[8,128]{1,0:T(8,128)S(1)}, f32[1,2048]{1,0:T(1,128)}, bf16[512,2048]{1,0:T(8,128)(2,1)S(1)}) custom-call(s32[5,16]{1,0:T(8,128)S(1)} %dynamic-slice_bitcast_fusion.table.refs_0_, f32[256,256]{1,0:T(8,128)S(1)} %collective-permute-done.8.refs_0_, ...), custom_call_target="tpu_custom_call" | custom-call | flops 2415919104 | bytes 21037056 | tf_op jit(solution)/shard_map/pallas_call | solution.py:256
  35.6 0.0 collective-permute-start.10
  35.6 0.5 collective-permute-start.20
  36.1 1.8 %shard_map.85 = (f32[1024,128]{1,0:T(8,128)S(1)}, f32[1024,128]{1,0:T(8,128)S(1)}) custom-call(s32[5,16]{1,0:T(8,128)S(1)} %dynamic-slice_bitcast_fusion.table.refs_0_, bf16[512,2048]{1,0:T(8,128)(2,1)S(1)} %get-tuple-element.58.own_ref, bf16[2048,768]{1,0:T(8,128)(2,1)S(1)} %get-tuple-element.46.refs_6_.refs_4_.refs_3_.stack_ref), custom_call_target="tpu_custom_call" | custom-call | flops 1073741824 | bytes 10485760 | tf_op jit(solution)/shard_map/pallas_call | solution.py:256
  38.0 0.0 collective-permute-done.10
  38.0 0.1 slice_add_fusion
  38.1 0.7 collective-permute-start.11
  38.9 0.0 collective-permute-done.20
  38.9 0.1 add.66
  39.0 1.7 %collective-permute-start.21 = (f32[512,128]{1,0:T(8,128)S(1)}, f32[512,128]{1,0:T(8,128)S(1)}, u32[]{:S(2)}, u32[]{:S(2)}) collective-permute-start(f32[512,128]{1,0:T(8,128)S(1)} %slice.104), channel_id=1, source_target_pairs={{0,2},{1,17},{2,0},{3,19},{4,6},{5,21},{6,4},{7,23},{8,10},{9,25},... | collective-permute-start | bytes 786440 | tf_op jit(solution)/shard_map/scatter_moments/ppermute | solution.py:70
  40.7 3.9 %collective-permute-done.11 = f32[520,128]{1,0:T(8,128)S(1)} collective-permute-done((f32[520,128]{1,0:T(8,128)S(1)}, f32[520,128]{1,0:T(8,128)S(1)}, u32[]{:S(2)}, u32[]{:S(2)}) %collective-permute-start.11) | collective-permute-done | bytes 266272 | tf_op jit(solution)/shard_map/scatter_moments/ppermute | solution.py:70
  44.7 1.8 %collective-permute-start.12 = (f32[264,128]{1,0:T(8,128)S(1)}, f32[264,128]{1,0:T(8,128)S(1)}, u32[]{:S(2)}, u32[]{:S(2)}) collective-permute-start(f32[264,128]{1,0:T(8,128)S(1)} %pad_maximum_fusion.3), channel_id=1, source_target_pairs={{0,2},{1,5},{2,0},{3,7},{4,6},{5,1},{6,4},{7,3},{8,10},{9,13},{10,... | collective-permute-start | bytes 405512 | tf_op jit(solution)/shard_map/scatter_moments/ppermute | solution.py:70
  46.5 0.7 collective-permute-start.22
  47.2 3.4 %collective-permute-done.12 = f32[264,128]{1,0:T(8,128)S(1)} collective-permute-done((f32[264,128]{1,0:T(8,128)S(1)}, f32[264,128]{1,0:T(8,128)S(1)}, u32[]{:S(2)}, u32[]{:S(2)}) %collective-permute-start.12) | collective-permute-done | bytes 135200 | tf_op jit(solution)/shard_map/scatter_moments/ppermute | solution.py:70
  50.7 1.8 %collective-permute-start.13 = (f32[136,128]{1,0:T(8,128)S(1)}, f32[136,128]{1,0:T(8,128)S(1)}, u32[]{:S(2)}, u32[]{:S(2)}) collective-permute-start(f32[136,128]{1,0:T(8,128)S(1)} %pad_maximum_fusion.8), channel_id=1, source_target_pairs={{0,16},{1,3},{2,18},{3,1},{4,20},{5,7},{6,22},{7,5},{8,24},{9,11},... | collective-permute-start | bytes 208904 | tf_op jit(solution)/shard_map/scatter_moments/ppermute | solution.py:70
  52.4 0.0 collective-permute-done.22
  52.5 0.7 collective-permute-start.23
  53.2 1.9 %collective-permute-done.13 = f32[136,128]{1,0:T(8,128)S(1)} collective-permute-done((f32[136,128]{1,0:T(8,128)S(1)}, f32[136,128]{1,0:T(8,128)S(1)}, u32[]{:S(2)}, u32[]{:S(2)}) %collective-permute-start.13) | collective-permute-done | bytes 69664 | tf_op jit(solution)/shard_map/scatter_moments/ppermute | solution.py:70
  55.1 2.6 %collective-permute-start.14 = (f32[136,128]{1,0:T(8,128)S(1)}, f32[136,128]{1,0:T(8,128)S(1)}, u32[]{:S(2)}, u32[]{:S(2)}) collective-permute-start(f32[136,128]{1,0:T(8,128)S(1)} %pad_maximum_fusion.9), channel_id=1, source_target_pairs={{0,8},{1,9},{2,10},{3,11},{4,12},{5,13},{6,14},{7,15},{8,0},{9,1},... | collective-permute-start | bytes 208904 | tf_op jit(solution)/shard_map/scatter_moments/ppermute | solution.py:70
  57.7 1.5 %collective-permute-start.24 = (f32[128,128]{1,0:T(8,128)S(1)}, f32[128,128]{1,0:T(8,128)S(1)}, u32[]{:S(2)}, u32[]{:S(2)}) collective-permute-start(f32[128,128]{1,0:T(8,128)S(1)} %slice_add_fusion.5), channel_id=1, source_target_pairs={{0,8},{1,9},{2,10},{3,11},{4,12},{5,13},{6,14},{7,15},{8,0},{9,1},... | collective-permute-start | bytes 196616 | tf_op jit(solution)/shard_map/scatter_moments/ppermute | solution.py:70
  59.2 3.8 %collective-permute-done.24 = f32[128,128]{1,0:T(8,128)S(1)} collective-permute-done((f32[128,128]{1,0:T(8,128)S(1)}, f32[128,128]{1,0:T(8,128)S(1)}, u32[]{:S(2)}, u32[]{:S(2)}) %collective-permute-start.24) | collective-permute-done | bytes 65568 | tf_op jit(solution)/shard_map/scatter_moments/ppermute | solution.py:70
  63.1 1.5 %collective-permute-start.25 = (f32[128,128]{1,0:T(8,128)S(1)}, f32[128,128]{1,0:T(8,128)S(1)}, u32[]{:S(2)}, u32[]{:S(2)}) collective-permute-start(f32[128,128]{1,0:T(8,128)S(1)} %add.70), channel_id=1, source_target_pairs={{0,16},{1,5},{2,18},{3,7},{4,20},{5,1},{6,22},{7,3},{8,24},{9,13},... | collective-permute-start | bytes 196616 | tf_op jit(solution)/shard_map/gather_moments/ppermute | solution.py:70
  64.5 0.0 collective-permute-done.14
  64.6 0.7 collective-permute-start.15
  65.2 2.2 %collective-permute-done.25 = f32[128,128]{1,0:T(8,128)S(1)} collective-permute-done((f32[128,128]{1,0:T(8,128)S(1)}, f32[128,128]{1,0:T(8,128)S(1)}, u32[]{:S(2)}, u32[]{:S(2)}) %collective-permute-start.25) | collective-permute-done | bytes 65568 | tf_op jit(solution)/shard_map/gather_moments/ppermute | solution.py:70
  67.4 1.4 %collective-permute-start.26 = (f32[256,128]{1,0:T(8,128)S(1)}, f32[256,128]{1,0:T(8,128)S(1)}, u32[]{:S(2)}, u32[]{:S(2)}) collective-permute-start(f32[256,128]{1,0:T(8,128)S(1)} %pad_maximum_fusion.7), channel_id=1, source_target_pairs={{0,4},{1,3},{2,6},{3,1},{4,0},{5,7},{6,2},{7,5},{8,12},{9,11},{10,... | collective-permute-start | bytes 393224 | tf_op jit(solution)/shard_map/gather_moments/ppermute | solution.py:70
  68.8 0.1 collective-permute-done.15
  68.9 1.7 %collective-permute-start.16 = (f32[256,128]{1,0:T(8,128)S(1)}, f32[256,128]{1,0:T(8,128)S(1)}, u32[]{:S(2)}, u32[]{:S(2)}) collective-permute-start(f32[256,128]{1,0:T(8,128)S(1)} %pad_maximum_fusion.6), channel_id=1, source_target_pairs={{0,2},{1,5},{2,0},{3,7},{4,6},{5,1},{6,4},{7,3},{8,10},{9,13},{10,... | collective-permute-start | bytes 393224 | tf_op jit(solution)/shard_map/gather_moments/ppermute | solution.py:70
  70.6 1.9 %collective-permute-done.26 = f32[256,128]{1,0:T(8,128)S(1)} collective-permute-done((f32[256,128]{1,0:T(8,128)S(1)}, f32[256,128]{1,0:T(8,128)S(1)}, u32[]{:S(2)}, u32[]{:S(2)}) %collective-permute-start.26) | collective-permute-done | bytes 131104 | tf_op jit(solution)/shard_map/gather_moments/ppermute | solution.py:70
  72.5 1.6 %collective-permute-start.27 = (f32[512,128]{1,0:T(8,128)S(1)}, f32[512,128]{1,0:T(8,128)S(1)}, u32[]{:S(2)}, u32[]{:S(2)}) collective-permute-start(f32[512,128]{1,0:T(8,128)S(1)} %pad_maximum_fusion.2.refs_4_), channel_id=1, source_target_pairs={{0,2},{1,17},{2,0},{3,19},{4,6},{5,21},{6,4},{7,23},{8,10},{9,25},... | collective-permute-start | bytes 786440 | tf_op jit(solution)/shard_map/gather_moments/ppermute | solution.py:70
  74.0 0.0 collective-permute-done.16
  74.0 1.6 %collective-permute-start.17 = (f32[512,128]{1,0:T(8,128)S(1)}, f32[512,128]{1,0:T(8,128)S(1)}, u32[]{:S(2)}, u32[]{:S(2)}) collective-permute-start(f32[512,128]{1,0:T(8,128)S(1)} %pad_maximum_fusion.1.refs_0_), channel_id=1, source_target_pairs={{0,4},{1,17},{2,6},{3,19},{4,0},{5,21},{6,2},{7,23},{8,12},{9,25},... | collective-permute-start | bytes 786440 | tf_op jit(solution)/shard_map/gather_moments/ppermute | solution.py:70
  75.6 0.0 collective-permute-start.28
  75.6 0.5 collective-permute-start.18
  76.1 2.8 %collective-permute-done.27.refs_5_ = f32[512,128]{1,0:T(8,128)S(1)} collective-permute-done((f32[512,128]{1,0:T(8,128)S(1)}, f32[512,128]{1,0:T(8,128)S(1)}, u32[]{:S(2)}, u32[]{:S(2)}) %collective-permute-start.27) | collective-permute-done | bytes 262176 | tf_op jit(solution)/shard_map/gather_moments/ppermute | solution.py:70
  78.9 0.0 collective-permute-start.29
  78.9 1.6 %collective-permute-done.17.refs_1_ = f32[512,128]{1,0:T(8,128)S(1)} collective-permute-done((f32[512,128]{1,0:T(8,128)S(1)}, f32[512,128]{1,0:T(8,128)S(1)}, u32[]{:S(2)}, u32[]{:S(2)}) %collective-permute-start.17) | collective-permute-done | bytes 262176 | tf_op jit(solution)/shard_map/gather_moments/ppermute | solution.py:70
  80.5 0.0 collective-permute-start.19
  80.5 0.5 collective-permute-start.30
  81.0 1.0 %collective-permute-done.30 = f32[8,128]{1,0:T(8,128)S(1)} collective-permute-done((f32[8,128]{1,0:T(8,128)S(1)}, f32[8,128]{1,0:T(8,128)S(1)}, u32[]{:S(2)}, u32[]{:S(2)}) %collective-permute-start.30) | collective-permute-done | bytes 4128 | tf_op jit(solution)/shard_map/scatter_moments/ppermute | solution.py:70
  82.0 0.0 collective-permute-done.19.refs_3_
  82.0 2.4 %shard_map.86 = (f32[1024,256]{1,0:T(8,128)}, f32[1024,256]{1,0:T(8,128)}, f32[8,128]{1,0:T(8,128)}) custom-call(s32[5,16]{1,0:T(8,128)S(1)} %dynamic-slice_bitcast_fusion.table.refs_0_, f32[512,128]{1,0:T(8,128)S(1)} %pad_maximum_fusion.1.refs_0_, f32[512,128]{1,0:T(8,128)S(1)} %collective-permute-done.17.refs_1_, ...), custom_call_target="tpu_custom_call" | custom-call | flops 2097152 | bytes 4194304 | tf_op jit(solution)/shard_map/pallas_call | solution.py:370
  (43 shorter events, 0.4 us)
Async XLA Ops:
  0.6 8.0 %collective-permute-start = (f32[64,256]{1,0:T(8,128)}, f32[64,256]{1,0:T(8,128)S(1)}, u32[]{:S(2)}, u32[]{:S(2)}) collective-permute-start(f32[64,256]{1,0:T(8,128)} %refs_2_.1), channel_id=1, source_target_pairs={{0,8},{1,9},{2,10},{3,11},{4,12},{5,13},{6,14},{7,15},{8,0},{9,1},... | collective-permute-start | bytes 196616 | tf_op jit(solution)/shard_map/gather_parameters/ppermute | solution.py:70
  4.7 6.7 %collective-permute-start.1 = (f32[64,256]{1,0:T(8,128)}, f32[64,256]{1,0:T(8,128)S(1)}, u32[]{:S(2)}, u32[]{:S(2)}) collective-permute-start(f32[64,256]{1,0:T(8,128)} %refs_3_.1), channel_id=1, source_target_pairs={{0,8},{1,9},{2,10},{3,11},{4,12},{5,13},{6,14},{7,15},{8,0},{9,1},... | collective-permute-start | bytes 196616 | tf_op jit(solution)/shard_map/gather_parameters/ppermute | solution.py:70
  11.5 6.5 %collective-permute-start.4 = (f32[128,256]{1,0:T(8,128)S(1)}, f32[128,256]{1,0:T(8,128)S(1)}, u32[]{:S(2)}, u32[]{:S(2)}) collective-permute-start(f32[128,256]{1,0:T(8,128)S(1)} %pad_maximum_fusion.5), channel_id=1, source_target_pairs={{0,4},{1,3},{2,6},{3,1},{4,0},{5,7},{6,2},{7,5},{8,12},{9,11},{10,... | collective-permute-start | bytes 393224 | tf_op jit(solution)/shard_map/gather_parameters/ppermute | solution.py:70
  12.2 5.7 %collective-permute-start.2 = (f32[128,256]{1,0:T(8,128)S(1)}, f32[128,256]{1,0:T(8,128)S(1)}, u32[]{:S(2)}, u32[]{:S(2)}) collective-permute-start(f32[128,256]{1,0:T(8,128)S(1)} %pad_maximum_fusion.4), channel_id=1, source_target_pairs={{0,4},{1,3},{2,6},{3,1},{4,0},{5,7},{6,2},{7,5},{8,12},{9,11},{10,... | collective-permute-start | bytes 393224 | tf_op jit(solution)/shard_map/gather_parameters/ppermute | solution.py:70
  17.9 2.7 %collective-permute-start.6 = (f32[256,256]{1,0:T(8,128)S(1)}, f32[256,256]{1,0:T(8,128)S(1)}, u32[]{:S(2)}, u32[]{:S(2)}) collective-permute-start(f32[256,256]{1,0:T(8,128)S(1)} %constant_dynamic-update-slice_fusion.refs_1_), channel_id=1, source_target_pairs={{0,1},{1,0},{2,3},{3,2},{4,5},{5,4},{6,7},{7,6},{8,9},{9,8},{10,11... | collective-permute-start | bytes 786440 | tf_op jit(solution)/shard_map/gather_parameters/ppermute | solution.py:70
  18.0 2.6 %collective-permute-start.7 = (f32[256,256]{1,0:T(8,128)S(1)}, f32[256,256]{1,0:T(8,128)S(1)}, u32[]{:S(2)}, u32[]{:S(2)}) collective-permute-start(f32[256,256]{1,0:T(8,128)S(1)} %constant_dynamic-update-slice_fusion.3.refs_3_), channel_id=1, source_target_pairs={{0,1},{1,0},{2,3},{3,2},{4,5},{5,4},{6,7},{7,6},{8,9},{9,8},{10,11... | collective-permute-start | bytes 786440 | tf_op jit(solution)/shard_map/gather_parameters/ppermute | solution.py:70
  18.6 6.4 %collective-permute-start.3 = (f32[256,256]{1,0:T(8,128)S(1)}, f32[256,256]{1,0:T(8,128)S(1)}, u32[]{:S(2)}, u32[]{:S(2)}) collective-permute-start(f32[256,256]{1,0:T(8,128)S(1)} %constant_dynamic-update-slice_fusion.refs_1_), channel_id=1, source_target_pairs={{0,2},{1,5},{2,0},{3,7},{4,6},{5,1},{6,4},{7,3},{8,10},{9,13},{10,... | collective-permute-start | bytes 786440 | tf_op jit(solution)/shard_map/gather_parameters/ppermute | solution.py:70
  20.3 7.5 %collective-permute-start.5 = (f32[256,256]{1,0:T(8,128)S(1)}, f32[256,256]{1,0:T(8,128)S(1)}, u32[]{:S(2)}, u32[]{:S(2)}) collective-permute-start(f32[256,256]{1,0:T(8,128)S(1)} %constant_dynamic-update-slice_fusion.3.refs_3_), channel_id=1, source_target_pairs={{0,2},{1,5},{2,0},{3,7},{4,6},{5,1},{6,4},{7,3},{8,10},{9,13},{10,... | collective-permute-start | bytes 786440 | tf_op jit(solution)/shard_map/gather_parameters/ppermute | solution.py:70
  27.7 2.9 %collective-permute-start.8 = (f32[256,256]{1,0:T(8,128)S(1)}, f32[256,256]{1,0:T(8,128)S(1)}, u32[]{:S(2)}, u32[]{:S(2)}) collective-permute-start(f32[256,256]{1,0:T(8,128)S(1)} %collective-permute-done.3.refs_1_), channel_id=1, source_target_pairs={{0,1},{1,0},{2,3},{3,2},{4,5},{5,4},{6,7},{7,6},{8,9},{9,8},{10,11... | collective-permute-start | bytes 786440 | tf_op jit(solution)/shard_map/gather_parameters/ppermute | solution.py:70
  27.8 2.9 %collective-permute-start.9 = (f32[256,256]{1,0:T(8,128)S(1)}, f32[256,256]{1,0:T(8,128)S(1)}, u32[]{:S(2)}, u32[]{:S(2)}) collective-permute-start(f32[256,256]{1,0:T(8,128)S(1)} %collective-permute-done.5.refs_2_), channel_id=1, source_target_pairs={{0,1},{1,0},{2,3},{3,2},{4,5},{5,4},{6,7},{7,6},{8,9},{9,8},{10,11... | collective-permute-start | bytes 786440 | tf_op jit(solution)/shard_map/gather_parameters/ppermute | solution.py:70
  35.6 2.4 %collective-permute-start.10 = (f32[1032,128]{1,0:T(8,128)S(1)}, f32[1032,128]{1,0:T(8,128)S(1)}, u32[]{:S(2)}, u32[]{:S(2)}) collective-permute-start(f32[1032,128]{1,0:T(8,128)S(1)} %get-tuple-element.60), channel_id=1, source_target_pairs={{0,1},{1,0},{2,3},{3,2},{4,5},{5,4},{6,7},{7,6},{8,9},{9,8},{10,11... | collective-permute-start | bytes 1585160 | tf_op jit(solution)/shard_map/scatter_moments/ppermute | solution.py:70
  35.6 3.2 %collective-permute-start.20 = (f32[1024,128]{1,0:T(8,128)S(1)}, f32[1024,128]{1,0:T(8,128)S(1)}, u32[]{:S(2)}, u32[]{:S(2)}) collective-permute-start(f32[1024,128]{1,0:T(8,128)S(1)} %get-tuple-element.63), channel_id=1, source_target_pairs={{0,1},{1,0},{2,3},{3,2},{4,5},{5,4},{6,7},{7,6},{8,9},{9,8},{10,11... | collective-permute-start | bytes 1572872 | tf_op jit(solution)/shard_map/scatter_moments/ppermute | solution.py:70
  38.1 6.5 %collective-permute-start.11 = (f32[520,128]{1,0:T(8,128)S(1)}, f32[520,128]{1,0:T(8,128)S(1)}, u32[]{:S(2)}, u32[]{:S(2)}) collective-permute-start(f32[520,128]{1,0:T(8,128)S(1)} %pad_maximum_fusion), channel_id=1, source_target_pairs={{0,4},{1,17},{2,6},{3,19},{4,0},{5,21},{6,2},{7,23},{8,12},{9,25},... | collective-permute-start | bytes 798728 | tf_op jit(solution)/shard_map/scatter_moments/ppermute | solution.py:70
  39.0 7.5 %collective-permute-start.21 = (f32[512,128]{1,0:T(8,128)S(1)}, f32[512,128]{1,0:T(8,128)S(1)}, u32[]{:S(2)}, u32[]{:S(2)}) collective-permute-start(f32[512,128]{1,0:T(8,128)S(1)} %slice.104), channel_id=1, source_target_pairs={{0,2},{1,17},{2,0},{3,19},{4,6},{5,21},{6,4},{7,23},{8,10},{9,25},... | collective-permute-start | bytes 786440 | tf_op jit(solution)/shard_map/scatter_moments/ppermute | solution.py:70
  44.7 5.9 %collective-permute-start.12 = (f32[264,128]{1,0:T(8,128)S(1)}, f32[264,128]{1,0:T(8,128)S(1)}, u32[]{:S(2)}, u32[]{:S(2)}) collective-permute-start(f32[264,128]{1,0:T(8,128)S(1)} %pad_maximum_fusion.3), channel_id=1, source_target_pairs={{0,2},{1,5},{2,0},{3,7},{4,6},{5,1},{6,4},{7,3},{8,10},{9,13},{10,... | collective-permute-start | bytes 405512 | tf_op jit(solution)/shard_map/scatter_moments/ppermute | solution.py:70
  46.5 5.9 %collective-permute-start.22 = (f32[256,128]{1,0:T(8,128)S(1)}, f32[256,128]{1,0:T(8,128)S(1)}, u32[]{:S(2)}, u32[]{:S(2)}) collective-permute-start(f32[256,128]{1,0:T(8,128)S(1)} %slice.106), channel_id=1, source_target_pairs={{0,4},{1,3},{2,6},{3,1},{4,0},{5,7},{6,2},{7,5},{8,12},{9,11},{10,... | collective-permute-start | bytes 393224 | tf_op jit(solution)/shard_map/scatter_moments/ppermute | solution.py:70
  50.7 4.4 %collective-permute-start.13 = (f32[136,128]{1,0:T(8,128)S(1)}, f32[136,128]{1,0:T(8,128)S(1)}, u32[]{:S(2)}, u32[]{:S(2)}) collective-permute-start(f32[136,128]{1,0:T(8,128)S(1)} %pad_maximum_fusion.8), channel_id=1, source_target_pairs={{0,16},{1,3},{2,18},{3,1},{4,20},{5,7},{6,22},{7,5},{8,24},{9,11},... | collective-permute-start | bytes 208904 | tf_op jit(solution)/shard_map/scatter_moments/ppermute | solution.py:70
  52.5 5.2 %collective-permute-start.23 = (f32[128,128]{1,0:T(8,128)S(1)}, f32[128,128]{1,0:T(8,128)S(1)}, u32[]{:S(2)}, u32[]{:S(2)}) collective-permute-start(f32[128,128]{1,0:T(8,128)S(1)} %slice.108), channel_id=1, source_target_pairs={{0,16},{1,5},{2,18},{3,7},{4,20},{5,1},{6,22},{7,3},{8,24},{9,13},... | collective-permute-start | bytes 196616 | tf_op jit(solution)/shard_map/scatter_moments/ppermute | solution.py:70
  55.1 9.5 %collective-permute-start.14 = (f32[136,128]{1,0:T(8,128)S(1)}, f32[136,128]{1,0:T(8,128)S(1)}, u32[]{:S(2)}, u32[]{:S(2)}) collective-permute-start(f32[136,128]{1,0:T(8,128)S(1)} %pad_maximum_fusion.9), channel_id=1, source_target_pairs={{0,8},{1,9},{2,10},{3,11},{4,12},{5,13},{6,14},{7,15},{8,0},{9,1},... | collective-permute-start | bytes 208904 | tf_op jit(solution)/shard_map/scatter_moments/ppermute | solution.py:70
  57.7 5.3 %collective-permute-start.24 = (f32[128,128]{1,0:T(8,128)S(1)}, f32[128,128]{1,0:T(8,128)S(1)}, u32[]{:S(2)}, u32[]{:S(2)}) collective-permute-start(f32[128,128]{1,0:T(8,128)S(1)} %slice_add_fusion.5), channel_id=1, source_target_pairs={{0,8},{1,9},{2,10},{3,11},{4,12},{5,13},{6,14},{7,15},{8,0},{9,1},... | collective-permute-start | bytes 196616 | tf_op jit(solution)/shard_map/scatter_moments/ppermute | solution.py:70
  63.1 4.3 %collective-permute-start.25 = (f32[128,128]{1,0:T(8,128)S(1)}, f32[128,128]{1,0:T(8,128)S(1)}, u32[]{:S(2)}, u32[]{:S(2)}) collective-permute-start(f32[128,128]{1,0:T(8,128)S(1)} %add.70), channel_id=1, source_target_pairs={{0,16},{1,5},{2,18},{3,7},{4,20},{5,1},{6,22},{7,3},{8,24},{9,13},... | collective-permute-start | bytes 196616 | tf_op jit(solution)/shard_map/gather_moments/ppermute | solution.py:70
  64.6 4.3 %collective-permute-start.15 = (f32[128,128]{1,0:T(8,128)S(1)}, f32[128,128]{1,0:T(8,128)S(1)}, u32[]{:S(2)}, u32[]{:S(2)}) collective-permute-start(f32[128,128]{1,0:T(8,128)S(1)} %slice_add_fusion.6), channel_id=1, source_target_pairs={{0,16},{1,3},{2,18},{3,1},{4,20},{5,7},{6,22},{7,5},{8,24},{9,11},... | collective-permute-start | bytes 196616 | tf_op jit(solution)/shard_map/gather_moments/ppermute | solution.py:70
  67.4 5.0 %collective-permute-start.26 = (f32[256,128]{1,0:T(8,128)S(1)}, f32[256,128]{1,0:T(8,128)S(1)}, u32[]{:S(2)}, u32[]{:S(2)}) collective-permute-start(f32[256,128]{1,0:T(8,128)S(1)} %pad_maximum_fusion.7), channel_id=1, source_target_pairs={{0,4},{1,3},{2,6},{3,1},{4,0},{5,7},{6,2},{7,5},{8,12},{9,11},{10,... | collective-permute-start | bytes 393224 | tf_op jit(solution)/shard_map/gather_moments/ppermute | solution.py:70
  68.9 5.1 %collective-permute-start.16 = (f32[256,128]{1,0:T(8,128)S(1)}, f32[256,128]{1,0:T(8,128)S(1)}, u32[]{:S(2)}, u32[]{:S(2)}) collective-permute-start(f32[256,128]{1,0:T(8,128)S(1)} %pad_maximum_fusion.6), channel_id=1, source_target_pairs={{0,2},{1,5},{2,0},{3,7},{4,6},{5,1},{6,4},{7,3},{8,10},{9,13},{10,... | collective-permute-start | bytes 393224 | tf_op jit(solution)/shard_map/gather_moments/ppermute | solution.py:70
  72.5 6.4 %collective-permute-start.27 = (f32[512,128]{1,0:T(8,128)S(1)}, f32[512,128]{1,0:T(8,128)S(1)}, u32[]{:S(2)}, u32[]{:S(2)}) collective-permute-start(f32[512,128]{1,0:T(8,128)S(1)} %pad_maximum_fusion.2.refs_4_), channel_id=1, source_target_pairs={{0,2},{1,17},{2,0},{3,19},{4,6},{5,21},{6,4},{7,23},{8,10},{9,25},... | collective-permute-start | bytes 786440 | tf_op jit(solution)/shard_map/gather_moments/ppermute | solution.py:70
  74.0 6.4 %collective-permute-start.17 = (f32[512,128]{1,0:T(8,128)S(1)}, f32[512,128]{1,0:T(8,128)S(1)}, u32[]{:S(2)}, u32[]{:S(2)}) collective-permute-start(f32[512,128]{1,0:T(8,128)S(1)} %pad_maximum_fusion.1.refs_0_), channel_id=1, source_target_pairs={{0,4},{1,17},{2,6},{3,19},{4,0},{5,21},{6,2},{7,23},{8,12},{9,25},... | collective-permute-start | bytes 786440 | tf_op jit(solution)/shard_map/gather_moments/ppermute | solution.py:70
  75.6 6.4 %collective-permute-start.28 = (f32[512,128]{1,0:T(8,128)S(1)}, f32[512,128]{1,0:T(8,128)S(1)}, u32[]{:S(2)}, u32[]{:S(2)}) collective-permute-start(f32[512,128]{1,0:T(8,128)S(1)} %pad_maximum_fusion.2.refs_4_), channel_id=1, source_target_pairs={{0,1},{1,0},{2,3},{3,2},{4,5},{5,4},{6,7},{7,6},{8,9},{9,8},{10,11... | collective-permute-start | bytes 786440 | tf_op jit(solution)/shard_map/gather_moments/ppermute | solution.py:70
  75.6 6.4 %collective-permute-start.18 = (f32[512,128]{1,0:T(8,128)S(1)}, f32[512,128]{1,0:T(8,128)S(1)}, u32[]{:S(2)}, u32[]{:S(2)}) collective-permute-start(f32[512,128]{1,0:T(8,128)S(1)} %pad_maximum_fusion.1.refs_0_), channel_id=1, source_target_pairs={{0,1},{1,0},{2,3},{3,2},{4,5},{5,4},{6,7},{7,6},{8,9},{9,8},{10,11... | collective-permute-start | bytes 786440 | tf_op jit(solution)/shard_map/gather_moments/ppermute | solution.py:70
  78.9 3.1 %collective-permute-start.29 = (f32[512,128]{1,0:T(8,128)S(1)}, f32[512,128]{1,0:T(8,128)S(1)}, u32[]{:S(2)}, u32[]{:S(2)}) collective-permute-start(f32[512,128]{1,0:T(8,128)S(1)} %collective-permute-done.27.refs_5_), channel_id=1, source_target_pairs={{0,1},{1,0},{2,3},{3,2},{4,5},{5,4},{6,7},{7,6},{8,9},{9,8},{10,11... | collective-permute-start | bytes 786440 | tf_op jit(solution)/shard_map/gather_moments/ppermute | solution.py:70
  80.5 1.6 %collective-permute-start.19 = (f32[512,128]{1,0:T(8,128)S(1)}, f32[512,128]{1,0:T(8,128)S(1)}, u32[]{:S(2)}, u32[]{:S(2)}) collective-permute-start(f32[512,128]{1,0:T(8,128)S(1)} %collective-permute-done.17.refs_1_), channel_id=1, source_target_pairs={{0,1},{1,0},{2,3},{3,2},{4,5},{5,4},{6,7},{7,6},{8,9},{9,8},{10,11... | collective-permute-start | bytes 786440 | tf_op jit(solution)/shard_map/gather_moments/ppermute | solution.py:70
  80.5 1.5 %collective-permute-start.30 = (f32[8,128]{1,0:T(8,128)S(1)}, f32[8,128]{1,0:T(8,128)S(1)}, u32[]{:S(2)}, u32[]{:S(2)}) collective-permute-start(f32[8,128]{1,0:T(8,128)S(1)} %slice_add_fusion.8), channel_id=1, source_target_pairs={{0,1},{1,0},{2,3},{3,2},{4,5},{5,4},{6,7},{7,6},{8,9},{9,8},{10,11... | collective-permute-start | bytes 12296 | tf_op jit(solution)/shard_map/scatter_moments/ppermute | solution.py:70

commit v5 on v4

--- a/solution.py
+++ b/solution.py
@@ -24,21 +24,18 @@
         self.owners = owners
         owner_bits = owners.bit_length() - 1
         group_bits = groups.bit_length() - 1
-        assert owners == 1 << owner_bits and groups == 1 << group_bits and owner_bits >= 4
-        piece = comps // owners
-        group = list(range(owner_bits, owner_bits + group_bits))
-        split = [1] + group[:1] + list(range(2, owner_bits - 1))
-        while comps >> (len(split) + 1) < 16:
-            split.pop()
+        assert owners == 1 << owner_bits and groups == 1 << group_bits
+        assert owner_bits >= 4 and group_bits >= 1 and comps % owners == 0
+        self.units = owners
+        self.unit = comps // owners
+        self.masks = [1] + [1 << b | 1 for b in range(1, owner_bits)]
+        self.masks += [1 << b for b in range(owner_bits, owner_bits + group_bits)]
+        split = [1, owner_bits] + list(range(2, owner_bits - 1))
         rest = [b for b in range(1, owner_bits + group_bits) if b not in split]
-        self.units = 1 << (len(split) + 1)
-        self.unit = comps // self.units
-        assert piece % self.unit == 0
-        per = piece // self.unit
         first, second, third, *others = split
         orders = (
             ((third, first, second), (second, third, first)),
-            ((first, third, second), (second, first, third)),
+            ((first, second, third), (second, third, first)),
         )
         self.halving = [
             [(0, 0)] + list(zip(zero, one)) + [(b, b) for b in others] for zero, one in orders
@@ -50,23 +47,30 @@
         def reach(device, steps, place):
             for t in reversed(range(len(steps))):
                 if place >> t & 1:
-                    device ^= 1 << steps[t][device & 1]
+                    device = self.partner(device, steps[t])
             return device
 
+        def chunk(device):
+            place = sum((device >> b & 1) << i for i, b in enumerate(split)) << 1
+            return place | (self.colour(place) ^ self.colour(device))
+
         n = range(self.devices)
-        places = range(owners)
-        gather_at = np.array([[reach(d, self.gather + [(0, 0)], p) % owners for p in places] for d in n])
-        unit_chunk = (gather_at[:, :, None] * per + np.arange(per)).reshape(self.devices, self.units)
-        owned = sorted([0] + split)
-        slot_chunk = []
-        for halving in self.halving:
-            at = np.array([[reach(d, halving[::-1], j) for j in range(self.units)] for d in n])
-            slot_chunk.append(sum((at >> b & 1) << i for i, b in enumerate(owned)))
+        places = range(self.units)
+        unit_chunk = np.array([[reach(d, self.gather + [(0, 0)], p) % owners for p in places] for d in n])
+        slot_chunk = [
+            np.array([[chunk(reach(d, halving[::-1], j)) for j in places] for d in n]) for halving in self.halving
+        ]
         unit_slot = [np.take_along_axis(np.argsort(c, axis=1), unit_chunk, axis=1) for c in slot_chunk]
         self.tables = np.stack([unit_chunk, *unit_slot, *slot_chunk], axis=1).astype(np.int32)
 
+    def colour(self, device):
+        return (device % self.owners).bit_count() & 1
+
+    def partner(self, device, step):
+        return device ^ self.masks[step[self.colour(device)]]
+
     def swap(self, value, step):
-        pairs = [(d, d ^ (1 << step[d & 1])) for d in range(self.devices)]
+        pairs = [(d, self.partner(d, step)) for d in range(self.devices)]
         return lax.ppermute(value, ("grp", "comp"), pairs)
 
 
@@ -335,47 +339,64 @@
     return sent, kept, counts, row_scores
 
 
-def update_kernel(plan, pieces, total_rows, table, *refs):
-    first_refs, second_refs = refs[:pieces], refs[pieces : 2 * pieces]
-    counts_ref = refs[2 * pieces]
-    means_ref, variances_ref, log_weights_ref, staged = refs[2 * pieces + 1 :]
-    comps, width = means_ref.shape
-    unit = plan.unit
-    parts = width // LANES
+def scale_kernel(plan, total_rows, table, counts_ref, log_weights_ref, scale_ref):
     denominator = counts_ref[...] + 1.0
     log_weights_ref[...] = jnp.log(denominator / total_rows)
     inverse = 1.0 / denominator
-    for b in range(comps // LANES):
-        staged[b * LANES : (b + 1) * LANES, :] = columns(inverse[b : b + 1, :], LANES)
-    for stream, stream_refs in enumerate((first_refs, second_refs)):
-        slot = 0
-        for ref in stream_refs:
+    for b in range(counts_ref.shape[0]):
+        scale_ref[b * LANES : (b + 1) * LANES, :] = columns(inverse[b : b + 1, :], LANES)
+
+
+def update_kernel(plan, first_slot, table, *refs):
+    piece_refs, scale_ref = (refs[:2], refs[2:4]), refs[4]
+    means_ref, variances_ref, mean_buffer, variance_buffer, sems = refs[-5:]
+    width = mean_buffer.shape[1]
+    unit = plan.unit
+    parts = width // LANES
+    moves = []
+    for stream, buffer, target in ((0, mean_buffer, means_ref), (1, variance_buffer, variances_ref)):
+        slot = first_slot
+        for ref in piece_refs[stream]:
             for first in range(0, ref.shape[0], unit * parts):
                 chunk = pl.ds(pl.multiple_of(table[3 + stream, slot] * unit, unit), unit)
-                scale = staged[chunk, :]
+                scale = scale_ref[chunk, :]
                 for part in range(parts):
                     lanes = slice(part * LANES, (part + 1) * LANES)
                     moment = ref[first + part * unit : first + (part + 1) * unit, :]
                     if stream == 0:
-                        means_ref[chunk, lanes] = moment * scale
+                        buffer[chunk, lanes] = moment * scale
                     else:
-                        mean = means_ref[chunk, lanes]
-                        variances_ref[chunk, lanes] = (moment + 1.0) * scale - mean * mean + 0.01
+                        mean = mean_buffer[chunk, lanes]
+                        buffer[chunk, lanes] = (moment + 1.0) * scale - mean * mean + 0.01
+                sem = sems.at[stream, slot - first_slot]
+                move = pltpu.make_async_copy(buffer.at[chunk, :], target.at[chunk, :], sem)
+                move.start()
+                moves.append(move)
                 slot += 1
-
-
-def update(plan, table, first, second, counts, comps, width, total_rows):
+    for move in moves:
+        move.wait()
+
+
+def update(plan, table, first_slot, first, second, scale, shape, earlier=()):
     vmem = pl.BlockSpec(memory_space=pltpu.VMEM)
-    shapes = [(comps, width), (comps, width), counts.shape]
+    hbm = pl.BlockSpec(memory_space=pl.ANY)
+    operands = [*first, *second, scale]
     return pl.pallas_call(
-        functools.partial(update_kernel, plan, len(first), total_rows),
-        in_specs=[pl.BlockSpec(memory_space=pltpu.SMEM)] + [vmem] * (2 * len(first) + 1),
-        out_specs=[vmem] * 3,
-        scratch_shapes=[pltpu.VMEM((comps, LANES), F32)],
-        out_shape=[jax.ShapeDtypeStruct(s, F32) for s in shapes],
+        functools.partial(update_kernel, plan, first_slot),
+        in_specs=[pl.BlockSpec(memory_space=pltpu.SMEM)] + [vmem] * len(operands) + [hbm] * len(earlier),
+        out_specs=[hbm] * 2,
+        out_shape=[jax.ShapeDtypeStruct(shape, F32)] * 2,
+        scratch_shapes=[
+            pltpu.VMEM(shape, F32),
+            pltpu.VMEM(shape, F32),
+            pltpu.SemaphoreType.DMA((2, plan.units // 2)),
+        ],
+        input_output_aliases={1 + len(operands) + i: i for i in range(len(earlier))},
         compiler_params=pltpu.CompilerParams(vmem_limit_bytes=16 * 2**20),
-        cost_estimate=pl.CostEstimate(flops=8 * comps * width, bytes_accessed=16 * comps * width, transcendentals=0),
-    )(table, *first, *second, counts)
+        cost_estimate=pl.CostEstimate(
+            flops=4 * math.prod(shape), bytes_accessed=8 * math.prod(shape), transcendentals=0
+        ),
+    )(table, *operands, *earlier)
 
 
 def double(plan, held, step, arrived=None):
@@ -428,19 +449,31 @@
     with jax.named_scope("scatter_moments"):
         kept, counts = scatter(plan, sent, kept, counts)
     with jax.named_scope("gather_moments"):
+        total_rows = float(features.shape[0] * plan.devices + comps)
+        log_weights, scale = call(
+            lambda plan, *refs: scale_kernel(plan, total_rows, *refs),
+            plan,
+            table,
+            [counts],
+            [(counts.shape, F32), ((comps, LANES), F32)],
+            [],
+            comps,
+            8,
+        )
         steps = list(zip(*plan.halving))[:0:-1]
         held = kept
         for step in steps[:-1]:
             held = double(plan, held, step)
         last = [plan.swap(h, at) for h, at in zip(held, steps[-1])]
         mates = [plan.swap(h, (0, 0)) for h in held]
-        first, second = [[h, l, m, plan.swap(l, (0, 0))] for h, l, m in zip(held, last, mates)]
-
-    total_rows = float(features.shape[0] * plan.devices + comps)
-    fresh_means, fresh_variances, fresh_weights = update(
-        plan, table, first, second, counts, comps, width, total_rows
-    )
-    return fresh_means, fresh_variances, fresh_weights.reshape(comps), row_scores.reshape(-1)
+        last, scale = lax.optimization_barrier((last, scale))
+        own = [[h, l] for h, l in zip(held, last)]
+        others = [[m, plan.swap(l, (0, 0))] for m, l in zip(mates, last)]
+    fresh = update(plan, table, 0, *own, scale, (comps, width))
+    fresh_means, fresh_variances = update(
+        plan, table, plan.units // 2, *others, scale, (comps, width), fresh
+    )
+    return fresh_means, fresh_variances, log_weights.reshape(comps), row_scores.reshape(-1)
 
 
 def solution(mesh):

time: 84.6 us -> 82.2 us (0.972)
  waiting for transfers between devices: 32.8 us -> 28.9 us
  Pallas kernels: 18.8 us -> 21.1 us
  starting transfers between devices: 30.7 us -> 29.8 us
    ppermute x31, waiting for transfers between devices: 32.8 us -> 28.9 us  [swap(): return lax.ppermute(value, ('grp', 'comp'), pairs)]
    pallas_call x5 -> x6, Pallas kernels: 16.4 us -> 17.7 us  [call(): pl.pallas_call(functools.partial(kernel, plan), in_specs=[pl.BlockSpec(me...]
    pallas_call x1 -> x2, Pallas kernels: 2.4 us -> 3.4 us  [update(): pl.pallas_call(functools.partial(update_kernel, plan, first_slot), in_spe...]
    ppermute x31, starting transfers between devices: 30.7 us -> 29.8 us  [swap(): return lax.ppermute(value, ('grp', 'comp'), pairs)]
  transfers between devices with their start and end apart: 31 -> 31, of which waited for: 14 -> 14; matrix products, arithmetic and copies ran while one was open for 1% -> 1% of each run, Pallas kernels for 14% -> 18%
where the time goes in v5:
time: 82.2 us; the launch traced here: 82 us
  starting transfers between devices  29.8 us (36%)
  waiting for transfers between devices  28.9 us (35%)
  Pallas kernels  21.1 us (26%)
  between operations  0.94 us (1%)
    ppermute x31, starting transfers between devices, swap(): return lax.ppermute(value, ('grp', 'comp'), pairs)  29.8 us
    ppermute x31, waiting for transfers between devices, swap(): return lax.ppermute(value, ('grp', 'comp'), pairs)  28.9 us
    pallas_call x6, Pallas kernels, call(): pl.pallas_call(functools.partial(kernel, plan), in_specs=[pl.BlockSpec(me...  17.7 us
    pallas_call x2, Pallas kernels, update(): pl.pallas_call(functools.partial(update_kernel, plan, first_slot), in_spe...  3.4 us
  transfers between devices with their start and end apart: 31, of which 14 were waited for; matrix products, arithmetic and copies ran while one was open for 1% of the time, Pallas kernels for 18%

profile of v5, /device:TPU:0, one launch (start us, length us, event | category | flops | bytes accessed | tf_op | source)
XLA Modules:
  0.0 82.0 jit_solution(709808834034738825)
XLA Ops:
  0.6 3.5 %collective-permute-start = (f32[64,256]{1,0:T(8,128)}, f32[64,256]{1,0:T(8,128)S(1)}, u32[]{:S(2)}, u32[]{:S(2)}) collective-permute-start(f32[64,256]{1,0:T(8,128)} %refs_2_.1), channel_id=1, source_target_pairs={{0,9},{1,8},{2,11},{3,10},{4,13},{5,12},{6,15},{7,14},{8,1},{9,0},... | collective-permute-start | bytes 196616 | tf_op jit(solution)/shard_map/gather_parameters/ppermute | solution.py:74
  4.2 0.1 collective-permute-start.1
  4.3 0.7 dynamic-slice_bitcast_fusion.table.refs_0_
  4.9 3.1 %gather_parameters.3 = (f32[64,256]{1,0:T(8,128)S(1)}, f32[64,256]{1,0:T(8,128)S(1)}, bf16[2048,768]{1,0:T(8,128)(2,1)S(1)}, f32[1024,128]{1,0:T(8,128)S(1)}) custom-call(s32[5,16]{1,0:T(8,128)S(1)} %dynamic-slice_bitcast_fusion.table.refs_0_, bf16[2048,256]{1,0:T(8,128)(2,1)} %refs_0_.1, f32[8,128]{1,0:T(8,128)} %bitcast.5, f32[64,256]{1,0:T(8,128)} %refs_2_.1, ...), custom_call_target="tpu_custom_call" | custom-call | flops 4194304 | bytes 2367488 | tf_op jit(solution)/shard_map/gather_parameters/pallas_call | solution.py:260
  8.0 0.0 collective-permute-done
  8.0 3.0 %collective-permute-done.1 = f32[64,256]{1,0:T(8,128)S(1)} collective-permute-done((f32[64,256]{1,0:T(8,128)}, f32[64,256]{1,0:T(8,128)S(1)}, u32[]{:S(2)}, u32[]{:S(2)}) %collective-permute-start.1) | collective-permute-done | bytes 65568 | tf_op jit(solution)/shard_map/gather_parameters/ppermute | solution.py:74
  11.1 1.4 %collective-permute-start.4 = (f32[128,256]{1,0:T(8,128)S(1)}, f32[128,256]{1,0:T(8,128)S(1)}, u32[]{:S(2)}, u32[]{:S(2)}) collective-permute-start(f32[128,256]{1,0:T(8,128)S(1)} %pad_maximum_fusion.5), channel_id=1, source_target_pairs={{0,5},{1,2},{2,1},{3,6},{4,7},{5,0},{6,3},{7,4},{8,11},{9,12},{10,... | collective-permute-start | bytes 393224 | tf_op jit(solution)/shard_map/gather_parameters/ppermute | solution.py:74
  12.5 0.4 collective-permute-start.2
  12.9 4.0 %collective-permute-done.2 = f32[128,256]{1,0:T(8,128)S(1)} collective-permute-done((f32[128,256]{1,0:T(8,128)S(1)}, f32[128,256]{1,0:T(8,128)S(1)}, u32[]{:S(2)}, u32[]{:S(2)}) %collective-permute-start.2) | collective-permute-done | bytes 131104 | tf_op jit(solution)/shard_map/gather_parameters/ppermute | solution.py:74
  16.9 0.9 %collective-permute-start.6 = (f32[256,256]{1,0:T(8,128)S(1)}, f32[256,256]{1,0:T(8,128)S(1)}, u32[]{:S(2)}, u32[]{:S(2)}) collective-permute-start(f32[256,256]{1,0:T(8,128)S(1)} %constant_dynamic-update-slice_fusion.refs_1_), channel_id=1, source_target_pairs={{0,1},{1,0},{2,3},{3,2},{4,5},{5,4},{6,7},{7,6},{8,9},{9,8},{10,11... | collective-permute-start | bytes 786440 | tf_op jit(solution)/shard_map/gather_parameters/ppermute | solution.py:74
  17.8 0.0 collective-permute-done.4
  17.8 0.1 collective-permute-start.7
  17.9 1.5 %collective-permute-start.3 = (f32[256,256]{1,0:T(8,128)S(1)}, f32[256,256]{1,0:T(8,128)S(1)}, u32[]{:S(2)}, u32[]{:S(2)}) collective-permute-start(f32[256,256]{1,0:T(8,128)S(1)} %constant_dynamic-update-slice_fusion.refs_1_), channel_id=1, source_target_pairs={{0,3},{1,4},{2,7},{3,0},{4,1},{5,6},{6,5},{7,2},{8,13},{9,10},{10,... | collective-permute-start | bytes 786440 | tf_op jit(solution)/shard_map/gather_parameters/ppermute | solution.py:74
  19.4 0.3 collective-permute-start.5
  19.7 0.0 collective-permute-done.6.refs_2_
  19.7 0.0 collective-permute-done.7.refs_4_
  19.7 4.2 %gather_parameters.4 = (f32[512,2048]{1,0:T(8,128)S(1)}, f32[1,2048]{1,0:T(1,128)S(1)}, f32[1,2048]{1,0:T(1,128)S(1)}) custom-call(s32[5,16]{1,0:T(8,128)S(1)} %dynamic-slice_bitcast_fusion.table.refs_0_, f32[256,256]{1,0:T(8,128)S(1)} %constant_dynamic-update-slice_fusion.refs_1_, f32[256,256]{1,0:T(8,128)S(1)} %collective-permute-done.6.refs_2_, ...), custom_call_target="tpu_custom_call" | custom-call | flops 2684354560 | bytes 9437184 | tf_op jit(solution)/shard_map/gather_parameters/pallas_call | solution.py:260
  23.9 2.7 %collective-permute-done.5.refs_2_ = f32[256,256]{1,0:T(8,128)S(1)} collective-permute-done((f32[256,256]{1,0:T(8,128)S(1)}, f32[256,256]{1,0:T(8,128)S(1)}, u32[]{:S(2)}, u32[]{:S(2)}) %collective-permute-start.5) | collective-permute-done | bytes 262176 | tf_op jit(solution)/shard_map/gather_parameters/ppermute | solution.py:74
  26.6 0.4 collective-permute-start.8
  27.0 0.1 collective-permute-start.9
  27.1 2.4 %gather_parameters.5 = (f32[256,2048]{1,0:T(8,128)S(1)}, f32[1,2048]{1,0:T(1,128)S(1)}, f32[1,2048]{1,0:T(1,128)S(1)}) custom-call(s32[5,16]{1,0:T(8,128)S(1)} %dynamic-slice_bitcast_fusion.table.refs_0_, f32[256,256]{1,0:T(8,128)S(1)} %collective-permute-done.3.refs_1_, f32[256,256]{1,0:T(8,128)S(1)} %collective-permute-done.5.refs_2_, ...), custom_call_target="tpu_custom_call" | custom-call | flops 1342177280 | bytes 8388608 | tf_op jit(solution)/shard_map/gather_parameters/pallas_call | solution.py:260
  29.5 5.0 %shard_map.84 = (f32[1032,128]{1,0:T(8,128)S(1)}, f32[1024,128]{1,0:T(8,128)S(1)}, f32[8,128]{1,0:T(8,128)S(1)}, f32[1,2048]{1,0:T(1,128)}, bf16[512,2048]{1,0:T(8,128)(2,1)S(1)}) custom-call(s32[5,16]{1,0:T(8,128)S(1)} %dynamic-slice_bitcast_fusion.table.refs_0_, f32[256,256]{1,0:T(8,128)S(1)} %collective-permute-done.8.refs_0_, ...), custom_call_target="tpu_custom_call" | custom-call | flops 2415919104 | bytes 21037056 | tf_op jit(solution)/shard_map/pallas_call | solution.py:260
  34.5 0.4 collective-permute-start.10
  34.9 0.1 collective-permute-start.19
  35.0 1.8 %shard_map.85 = (f32[1024,128]{1,0:T(8,128)S(1)}, f32[1024,128]{1,0:T(8,128)S(1)}) custom-call(s32[5,16]{1,0:T(8,128)S(1)} %dynamic-slice_bitcast_fusion.table.refs_0_, bf16[512,2048]{1,0:T(8,128)(2,1)S(1)} %get-tuple-element.64.own_ref, bf16[2048,768]{1,0:T(8,128)(2,1)S(1)} %get-tuple-element.52.refs_6_.refs_4_.refs_3_.stack_ref), custom_call_target="tpu_custom_call" | custom-call | flops 1073741824 | bytes 10485760 | tf_op jit(solution)/shard_map/pallas_call | solution.py:260
  36.8 0.1 slice_add_fusion
  37.0 1.0 %collective-permute-start.11 = (f32[520,128]{1,0:T(8,128)S(1)}, f32[520,128]{1,0:T(8,128)S(1)}, u32[]{:S(2)}, u32[]{:S(2)}) collective-permute-start(f32[520,128]{1,0:T(8,128)S(1)} %pad_maximum_fusion), channel_id=1, source_target_pairs={{0,5},{1,17},{2,18},{3,6},{4,20},{5,0},{6,3},{7,23},{8,24},{9,12},... | collective-permute-start | bytes 798728 | tf_op jit(solution)/shard_map/scatter_moments/ppermute | solution.py:74
  38.0 0.1 add.66
  38.1 1.6 %collective-permute-start.20 = (f32[512,128]{1,0:T(8,128)S(1)}, f32[512,128]{1,0:T(8,128)S(1)}, u32[]{:S(2)}, u32[]{:S(2)}) collective-permute-start(f32[512,128]{1,0:T(8,128)S(1)} %slice.104), channel_id=1, source_target_pairs={{0,3},{1,17},{2,18},{3,0},{4,20},{5,6},{6,5},{7,23},{8,24},{9,10},... | collective-permute-start | bytes 786440 | tf_op jit(solution)/shard_map/scatter_moments/ppermute | solution.py:74
  39.7 3.2 %collective-permute-done.11 = f32[520,128]{1,0:T(8,128)S(1)} collective-permute-done((f32[520,128]{1,0:T(8,128)S(1)}, f32[520,128]{1,0:T(8,128)S(1)}, u32[]{:S(2)}, u32[]{:S(2)}) %collective-permute-start.11) | collective-permute-done | bytes 266272 | tf_op jit(solution)/shard_map/scatter_moments/ppermute | solution.py:74
  42.9 1.8 %collective-permute-start.12 = (f32[264,128]{1,0:T(8,128)S(1)}, f32[264,128]{1,0:T(8,128)S(1)}, u32[]{:S(2)}, u32[]{:S(2)}) collective-permute-start(f32[264,128]{1,0:T(8,128)S(1)} %pad_maximum_fusion.3), channel_id=1, source_target_pairs={{0,3},{1,4},{2,7},{3,0},{4,1},{5,6},{6,5},{7,2},{8,13},{9,10},{10,... | collective-permute-start | bytes 405512 | tf_op jit(solution)/shard_map/scatter_moments/ppermute | solution.py:74
  44.8 1.6 %collective-permute-start.21 = (f32[256,128]{1,0:T(8,128)S(1)}, f32[256,128]{1,0:T(8,128)S(1)}, u32[]{:S(2)}, u32[]{:S(2)}) collective-permute-start(f32[256,128]{1,0:T(8,128)S(1)} %slice.106), channel_id=1, source_target_pairs={{0,16},{1,4},{2,7},{3,19},{4,1},{5,21},{6,22},{7,2},{8,13},{9,25},... | collective-permute-start | bytes 393224 | tf_op jit(solution)/shard_map/scatter_moments/ppermute | solution.py:74
  46.4 1.1 %collective-permute-done.12 = f32[264,128]{1,0:T(8,128)S(1)} collective-permute-done((f32[264,128]{1,0:T(8,128)S(1)}, f32[264,128]{1,0:T(8,128)S(1)}, u32[]{:S(2)}, u32[]{:S(2)}) %collective-permute-start.12) | collective-permute-done | bytes 135200 | tf_op jit(solution)/shard_map/scatter_moments/ppermute | solution.py:74
  47.5 1.8 %collective-permute-start.13 = (f32[136,128]{1,0:T(8,128)S(1)}, f32[136,128]{1,0:T(8,128)S(1)}, u32[]{:S(2)}, u32[]{:S(2)}) collective-permute-start(f32[136,128]{1,0:T(8,128)S(1)} %pad_maximum_fusion.8), channel_id=1, source_target_pairs={{0,16},{1,2},{2,1},{3,19},{4,7},{5,21},{6,22},{7,4},{8,11},{9,25},... | collective-permute-start | bytes 208904 | tf_op jit(solution)/shard_map/scatter_moments/ppermute | solution.py:74
  49.3 0.5 collective-permute-done.21
  49.9 0.6 collective-permute-start.22
  50.5 1.4 %collective-permute-done.13 = f32[136,128]{1,0:T(8,128)S(1)} collective-permute-done((f32[136,128]{1,0:T(8,128)S(1)}, f32[136,128]{1,0:T(8,128)S(1)}, u32[]{:S(2)}, u32[]{:S(2)}) %collective-permute-start.13) | collective-permute-done | bytes 69664 | tf_op jit(solution)/shard_map/scatter_moments/ppermute | solution.py:74
  51.9 2.3 %collective-permute-start.14 = (f32[136,128]{1,0:T(8,128)S(1)}, f32[136,128]{1,0:T(8,128)S(1)}, u32[]{:S(2)}, u32[]{:S(2)}) collective-permute-start(f32[136,128]{1,0:T(8,128)S(1)} %pad_maximum_fusion.9), channel_id=1, source_target_pairs={{0,9},{1,8},{2,11},{3,10},{4,13},{5,12},{6,15},{7,14},{8,1},{9,0},... | collective-permute-start | bytes 208904 | tf_op jit(solution)/shard_map/scatter_moments/ppermute | solution.py:74
  54.3 1.7 %collective-permute-start.23 = (f32[128,128]{1,0:T(8,128)S(1)}, f32[128,128]{1,0:T(8,128)S(1)}, u32[]{:S(2)}, u32[]{:S(2)}) collective-permute-start(f32[128,128]{1,0:T(8,128)S(1)} %slice_add_fusion.5), channel_id=1, source_target_pairs={{0,9},{1,8},{2,11},{3,10},{4,13},{5,12},{6,15},{7,14},{8,1},{9,0},... | collective-permute-start | bytes 196616 | tf_op jit(solution)/shard_map/scatter_moments/ppermute | solution.py:74
  56.0 5.8 %collective-permute-done.23 = f32[128,128]{1,0:T(8,128)S(1)} collective-permute-done((f32[128,128]{1,0:T(8,128)S(1)}, f32[128,128]{1,0:T(8,128)S(1)}, u32[]{:S(2)}, u32[]{:S(2)}) %collective-permute-start.23) | collective-permute-done | bytes 65568 | tf_op jit(solution)/shard_map/scatter_moments/ppermute | solution.py:74
  61.8 0.5 collective-permute-start.24
  62.3 0.0 collective-permute-done.14
  62.4 1.6 %collective-permute-start.15 = (f32[128,128]{1,0:T(8,128)S(1)}, f32[128,128]{1,0:T(8,128)S(1)}, u32[]{:S(2)}, u32[]{:S(2)}) collective-permute-start(f32[128,128]{1,0:T(8,128)S(1)} %slice_add_fusion.6), channel_id=1, source_target_pairs={{0,16},{1,2},{2,1},{3,19},{4,7},{5,21},{6,22},{7,4},{8,11},{9,25},... | collective-permute-start | bytes 196616 | tf_op jit(solution)/shard_map/gather_moments/ppermute | solution.py:74
  63.9 1.6 %collective-permute-done.24 = f32[128,128]{1,0:T(8,128)S(1)} collective-permute-done((f32[128,128]{1,0:T(8,128)S(1)}, f32[128,128]{1,0:T(8,128)S(1)}, u32[]{:S(2)}, u32[]{:S(2)}) %collective-permute-start.24) | collective-permute-done | bytes 65568 | tf_op jit(solution)/shard_map/gather_moments/ppermute | solution.py:74
  65.6 1.6 %collective-permute-start.25 = (f32[256,128]{1,0:T(8,128)S(1)}, f32[256,128]{1,0:T(8,128)S(1)}, u32[]{:S(2)}, u32[]{:S(2)}) collective-permute-start(f32[256,128]{1,0:T(8,128)S(1)} %pad_maximum_fusion.7), channel_id=1, source_target_pairs={{0,16},{1,4},{2,7},{3,19},{4,1},{5,21},{6,22},{7,2},{8,13},{9,25},... | collective-permute-start | bytes 393224 | tf_op jit(solution)/shard_map/gather_moments/ppermute | solution.py:74
  67.1 0.0 collective-permute-done.15
  67.2 1.1 %collective-permute-start.16 = (f32[256,128]{1,0:T(8,128)S(1)}, f32[256,128]{1,0:T(8,128)S(1)}, u32[]{:S(2)}, u32[]{:S(2)}) collective-permute-start(f32[256,128]{1,0:T(8,128)S(1)} %pad_maximum_fusion.6), channel_id=1, source_target_pairs={{0,3},{1,4},{2,7},{3,0},{4,1},{5,6},{6,5},{7,2},{8,13},{9,10},{10,... | collective-permute-start | bytes 393224 | tf_op jit(solution)/shard_map/gather_moments/ppermute | solution.py:74
  68.3 2.3 %collective-permute-done.25 = f32[256,128]{1,0:T(8,128)S(1)} collective-permute-done((f32[256,128]{1,0:T(8,128)S(1)}, f32[256,128]{1,0:T(8,128)S(1)}, u32[]{:S(2)}, u32[]{:S(2)}) %collective-permute-start.25) | collective-permute-done | bytes 131104 | tf_op jit(solution)/shard_map/gather_moments/ppermute | solution.py:74
  70.6 0.6 collective-permute-start.26
  71.2 0.4 collective-permute-done.16
  71.6 1.2 %collective-permute-start.18 = (f32[512,128]{1,0:T(8,128)S(1)}, f32[512,128]{1,0:T(8,128)S(1)}, u32[]{:S(2)}, u32[]{:S(2)}) collective-permute-start(f32[512,128]{1,0:T(8,128)S(1)} %pad_maximum_fusion.1.refs_0_), channel_id=1, source_target_pairs={{0,5},{1,17},{2,18},{3,6},{4,20},{5,0},{6,3},{7,23},{8,24},{9,12},... | collective-permute-start | bytes 786440 | tf_op jit(solution)/shard_map/gather_moments/ppermute | solution.py:74
  72.8 0.1 collective-permute-start.27
  72.9 1.1 %collective-permute-done.27 = f32[8,128]{1,0:T(8,128)S(1)} collective-permute-done((f32[8,128]{1,0:T(8,128)S(1)}, f32[8,128]{1,0:T(8,128)S(1)}, u32[]{:S(2)}, u32[]{:S(2)}) %collective-permute-start.27) | collective-permute-done | bytes 4128 | tf_op jit(solution)/shard_map/scatter_moments/ppermute | solution.py:74
  74.0 1.3 %gather_moments.1 = (f32[8,128]{1,0:T(8,128)}, f32[1024,128]{1,0:T(8,128)S(1)}) custom-call(s32[5,16]{1,0:T(8,128)S(1)} %dynamic-slice_bitcast_fusion.table.refs_0_, f32[8,128]{1,0:T(8,128)S(1)} %add_multiply_fusion.refs_1_), custom_call_target="tpu_custom_call" | custom-call | flops 1024 | bytes 8192 | tf_op jit(solution)/shard_map/gather_moments/pallas_call | solution.py:260
  75.2 0.2 collective-permute-start.29
  75.4 0.3 collective-permute-start.17
  75.8 0.7 collective-permute-done.26.refs_3_
  76.5 1.0 %collective-permute-done.18.refs_1_ = f32[512,128]{1,0:T(8,128)S(1)} collective-permute-done((f32[512,128]{1,0:T(8,128)S(1)}, f32[512,128]{1,0:T(8,128)S(1)}, u32[]{:S(2)}, u32[]{:S(2)}) %collective-permute-start.18) | collective-permute-done | bytes 262176 | tf_op jit(solution)/shard_map/gather_moments/ppermute | solution.py:74
  77.5 1.0 %collective-permute-start.28 = (f32[512,128]{1,0:T(8,128)S(1)}, f32[512,128]{1,0:T(8,128)S(1)}, u32[]{:S(2)}, u32[]{:S(2)}) collective-permute-start(f32[512,128]{1,0:T(8,128)S(1)} %collective-permute-done.18.refs_1_), channel_id=1, source_target_pairs={{0,1},{1,0},{2,3},{3,2},{4,5},{5,4},{6,7},{7,6},{8,9},{9,8},{10,11... | collective-permute-start | bytes 786440 | tf_op jit(solution)/shard_map/gather_moments/ppermute | solution.py:74
  78.5 0.0 collective-permute-start.30
  78.6 1.7 %shard_map.86 = (f32[1024,256]{1,0:T(8,128)}, f32[1024,256]{1,0:T(8,128)}) custom-call(s32[5,16]{1,0:T(8,128)S(1)} %dynamic-slice_bitcast_fusion.table.refs_0_, f32[512,128]{1,0:T(8,128)S(1)} %pad_maximum_fusion.1.refs_0_, f32[512,128]{1,0:T(8,128)S(1)} %collective-permute-done.18.refs_1_, f32[512,128]{1,0:T(8,128)S(1)} %pad_maximum_fusion.2.refs_2_, ...), custom_call_target="tpu_custom_call" | custom-call | flops 1048576 | bytes 2097152 | tf_op jit(solution)/shard_map/pallas_call | solution.py:384
  80.3 0.0 collective-permute-done.28.refs_1_
  80.3 0.0 collective-permute-done.30.refs_3_
  80.3 1.7 %shard_map.87 = (f32[1024,256]{1,0:T(8,128)}, f32[1024,256]{1,0:T(8,128)}) custom-call(s32[5,16]{1,0:T(8,128)S(1)} %dynamic-slice_bitcast_fusion.table.refs_0_, f32[512,128]{1,0:T(8,128)S(1)} %collective-permute-done.17.refs_0_, f32[512,128]{1,0:T(8,128)S(1)} %collective-permute-done.28.refs_1_, ...), custom_call_target="tpu_custom_call", output_to_operand_aliasing={{0}: (6, {}), {1}: (7, {})} | custom-call | flops 1048576 | bytes 2097152 | tf_op jit(solution)/shard_map/pallas_call | solution.py:384
  (45 shorter events, 0.4 us)
Async XLA Ops:
  0.6 7.4 %collective-permute-start = (f32[64,256]{1,0:T(8,128)}, f32[64,256]{1,0:T(8,128)S(1)}, u32[]{:S(2)}, u32[]{:S(2)}) collective-permute-start(f32[64,256]{1,0:T(8,128)} %refs_2_.1), channel_id=1, source_target_pairs={{0,9},{1,8},{2,11},{3,10},{4,13},{5,12},{6,15},{7,14},{8,1},{9,0},... | collective-permute-start | bytes 196616 | tf_op jit(solution)/shard_map/gather_parameters/ppermute | solution.py:74
  4.2 6.8 %collective-permute-start.1 = (f32[64,256]{1,0:T(8,128)}, f32[64,256]{1,0:T(8,128)S(1)}, u32[]{:S(2)}, u32[]{:S(2)}) collective-permute-start(f32[64,256]{1,0:T(8,128)} %refs_3_.1), channel_id=1, source_target_pairs={{0,9},{1,8},{2,11},{3,10},{4,13},{5,12},{6,15},{7,14},{8,1},{9,0},... | collective-permute-start | bytes 196616 | tf_op jit(solution)/shard_map/gather_parameters/ppermute | solution.py:74
  11.1 6.7 %collective-permute-start.4 = (f32[128,256]{1,0:T(8,128)S(1)}, f32[128,256]{1,0:T(8,128)S(1)}, u32[]{:S(2)}, u32[]{:S(2)}) collective-permute-start(f32[128,256]{1,0:T(8,128)S(1)} %pad_maximum_fusion.5), channel_id=1, source_target_pairs={{0,5},{1,2},{2,1},{3,6},{4,7},{5,0},{6,3},{7,4},{8,11},{9,12},{10,... | collective-permute-start | bytes 393224 | tf_op jit(solution)/shard_map/gather_parameters/ppermute | solution.py:74
  12.5 4.5 %collective-permute-start.2 = (f32[128,256]{1,0:T(8,128)S(1)}, f32[128,256]{1,0:T(8,128)S(1)}, u32[]{:S(2)}, u32[]{:S(2)}) collective-permute-start(f32[128,256]{1,0:T(8,128)S(1)} %pad_maximum_fusion.4), channel_id=1, source_target_pairs={{0,5},{1,2},{2,1},{3,6},{4,7},{5,0},{6,3},{7,4},{8,11},{9,12},{10,... | collective-permute-start | bytes 393224 | tf_op jit(solution)/shard_map/gather_parameters/ppermute | solution.py:74
  16.9 2.8 %collective-permute-start.6 = (f32[256,256]{1,0:T(8,128)S(1)}, f32[256,256]{1,0:T(8,128)S(1)}, u32[]{:S(2)}, u32[]{:S(2)}) collective-permute-start(f32[256,256]{1,0:T(8,128)S(1)} %constant_dynamic-update-slice_fusion.refs_1_), channel_id=1, source_target_pairs={{0,1},{1,0},{2,3},{3,2},{4,5},{5,4},{6,7},{7,6},{8,9},{9,8},{10,11... | collective-permute-start | bytes 786440 | tf_op jit(solution)/shard_map/gather_parameters/ppermute | solution.py:74
  17.8 1.9 %collective-permute-start.7 = (f32[256,256]{1,0:T(8,128)S(1)}, f32[256,256]{1,0:T(8,128)S(1)}, u32[]{:S(2)}, u32[]{:S(2)}) collective-permute-start(f32[256,256]{1,0:T(8,128)S(1)} %constant_dynamic-update-slice_fusion.3.refs_3_), channel_id=1, source_target_pairs={{0,1},{1,0},{2,3},{3,2},{4,5},{5,4},{6,7},{7,6},{8,9},{9,8},{10,11... | collective-permute-start | bytes 786440 | tf_op jit(solution)/shard_map/gather_parameters/ppermute | solution.py:74
  17.9 6.0 %collective-permute-start.3 = (f32[256,256]{1,0:T(8,128)S(1)}, f32[256,256]{1,0:T(8,128)S(1)}, u32[]{:S(2)}, u32[]{:S(2)}) collective-permute-start(f32[256,256]{1,0:T(8,128)S(1)} %constant_dynamic-update-slice_fusion.refs_1_), channel_id=1, source_target_pairs={{0,3},{1,4},{2,7},{3,0},{4,1},{5,6},{6,5},{7,2},{8,13},{9,10},{10,... | collective-permute-start | bytes 786440 | tf_op jit(solution)/shard_map/gather_parameters/ppermute | solution.py:74
  19.4 7.2 %collective-permute-start.5 = (f32[256,256]{1,0:T(8,128)S(1)}, f32[256,256]{1,0:T(8,128)S(1)}, u32[]{:S(2)}, u32[]{:S(2)}) collective-permute-start(f32[256,256]{1,0:T(8,128)S(1)} %constant_dynamic-update-slice_fusion.3.refs_3_), channel_id=1, source_target_pairs={{0,3},{1,4},{2,7},{3,0},{4,1},{5,6},{6,5},{7,2},{8,13},{9,10},{10,... | collective-permute-start | bytes 786440 | tf_op jit(solution)/shard_map/gather_parameters/ppermute | solution.py:74
  26.6 2.9 %collective-permute-start.8 = (f32[256,256]{1,0:T(8,128)S(1)}, f32[256,256]{1,0:T(8,128)S(1)}, u32[]{:S(2)}, u32[]{:S(2)}) collective-permute-start(f32[256,256]{1,0:T(8,128)S(1)} %collective-permute-done.3.refs_1_), channel_id=1, source_target_pairs={{0,1},{1,0},{2,3},{3,2},{4,5},{5,4},{6,7},{7,6},{8,9},{9,8},{10,11... | collective-permute-start | bytes 786440 | tf_op jit(solution)/shard_map/gather_parameters/ppermute | solution.py:74
  27.0 2.5 %collective-permute-start.9 = (f32[256,256]{1,0:T(8,128)S(1)}, f32[256,256]{1,0:T(8,128)S(1)}, u32[]{:S(2)}, u32[]{:S(2)}) collective-permute-start(f32[256,256]{1,0:T(8,128)S(1)} %collective-permute-done.5.refs_2_), channel_id=1, source_target_pairs={{0,1},{1,0},{2,3},{3,2},{4,5},{5,4},{6,7},{7,6},{8,9},{9,8},{10,11... | collective-permute-start | bytes 786440 | tf_op jit(solution)/shard_map/gather_parameters/ppermute | solution.py:74
  34.5 2.4 %collective-permute-start.10 = (f32[1032,128]{1,0:T(8,128)S(1)}, f32[1032,128]{1,0:T(8,128)S(1)}, u32[]{:S(2)}, u32[]{:S(2)}) collective-permute-start(f32[1032,128]{1,0:T(8,128)S(1)} %get-tuple-element.66), channel_id=1, source_target_pairs={{0,1},{1,0},{2,3},{3,2},{4,5},{5,4},{6,7},{7,6},{8,9},{9,8},{10,11... | collective-permute-start | bytes 1585160 | tf_op jit(solution)/shard_map/scatter_moments/ppermute | solution.py:74
  34.9 3.1 %collective-permute-start.19 = (f32[1024,128]{1,0:T(8,128)S(1)}, f32[1024,128]{1,0:T(8,128)S(1)}, u32[]{:S(2)}, u32[]{:S(2)}) collective-permute-start(f32[1024,128]{1,0:T(8,128)S(1)} %get-tuple-element.69), channel_id=1, source_target_pairs={{0,1},{1,0},{2,3},{3,2},{4,5},{5,4},{6,7},{7,6},{8,9},{9,8},{10,11... | collective-permute-start | bytes 1572872 | tf_op jit(solution)/shard_map/scatter_moments/ppermute | solution.py:74
  37.0 5.9 %collective-permute-start.11 = (f32[520,128]{1,0:T(8,128)S(1)}, f32[520,128]{1,0:T(8,128)S(1)}, u32[]{:S(2)}, u32[]{:S(2)}) collective-permute-start(f32[520,128]{1,0:T(8,128)S(1)} %pad_maximum_fusion), channel_id=1, source_target_pairs={{0,5},{1,17},{2,18},{3,6},{4,20},{5,0},{6,3},{7,23},{8,24},{9,12},... | collective-permute-start | bytes 798728 | tf_op jit(solution)/shard_map/scatter_moments/ppermute | solution.py:74
  38.1 6.6 %collective-permute-start.20 = (f32[512,128]{1,0:T(8,128)S(1)}, f32[512,128]{1,0:T(8,128)S(1)}, u32[]{:S(2)}, u32[]{:S(2)}) collective-permute-start(f32[512,128]{1,0:T(8,128)S(1)} %slice.104), channel_id=1, source_target_pairs={{0,3},{1,17},{2,18},{3,0},{4,20},{5,6},{6,5},{7,23},{8,24},{9,10},... | collective-permute-start | bytes 786440 | tf_op jit(solution)/shard_map/scatter_moments/ppermute | solution.py:74
  42.9 4.5 %collective-permute-start.12 = (f32[264,128]{1,0:T(8,128)S(1)}, f32[264,128]{1,0:T(8,128)S(1)}, u32[]{:S(2)}, u32[]{:S(2)}) collective-permute-start(f32[264,128]{1,0:T(8,128)S(1)} %pad_maximum_fusion.3), channel_id=1, source_target_pairs={{0,3},{1,4},{2,7},{3,0},{4,1},{5,6},{6,5},{7,2},{8,13},{9,10},{10,... | collective-permute-start | bytes 405512 | tf_op jit(solution)/shard_map/scatter_moments/ppermute | solution.py:74
  44.8 5.0 %collective-permute-start.21 = (f32[256,128]{1,0:T(8,128)S(1)}, f32[256,128]{1,0:T(8,128)S(1)}, u32[]{:S(2)}, u32[]{:S(2)}) collective-permute-start(f32[256,128]{1,0:T(8,128)S(1)} %slice.106), channel_id=1, source_target_pairs={{0,16},{1,4},{2,7},{3,19},{4,1},{5,21},{6,22},{7,2},{8,13},{9,25},... | collective-permute-start | bytes 393224 | tf_op jit(solution)/shard_map/scatter_moments/ppermute | solution.py:74
  47.5 4.4 %collective-permute-start.13 = (f32[136,128]{1,0:T(8,128)S(1)}, f32[136,128]{1,0:T(8,128)S(1)}, u32[]{:S(2)}, u32[]{:S(2)}) collective-permute-start(f32[136,128]{1,0:T(8,128)S(1)} %pad_maximum_fusion.8), channel_id=1, source_target_pairs={{0,16},{1,2},{2,1},{3,19},{4,7},{5,21},{6,22},{7,4},{8,11},{9,25},... | collective-permute-start | bytes 208904 | tf_op jit(solution)/shard_map/scatter_moments/ppermute | solution.py:74
  49.9 4.4 %collective-permute-start.22 = (f32[128,128]{1,0:T(8,128)S(1)}, f32[128,128]{1,0:T(8,128)S(1)}, u32[]{:S(2)}, u32[]{:S(2)}) collective-permute-start(f32[128,128]{1,0:T(8,128)S(1)} %slice.108), channel_id=1, source_target_pairs={{0,5},{1,2},{2,1},{3,6},{4,7},{5,0},{6,3},{7,4},{8,11},{9,12},{10,... | collective-permute-start | bytes 196616 | tf_op jit(solution)/shard_map/scatter_moments/ppermute | solution.py:74
  51.9 10.4 %collective-permute-start.14 = (f32[136,128]{1,0:T(8,128)S(1)}, f32[136,128]{1,0:T(8,128)S(1)}, u32[]{:S(2)}, u32[]{:S(2)}) collective-permute-start(f32[136,128]{1,0:T(8,128)S(1)} %pad_maximum_fusion.9), channel_id=1, source_target_pairs={{0,9},{1,8},{2,11},{3,10},{4,13},{5,12},{6,15},{7,14},{8,1},{9,0},... | collective-permute-start | bytes 208904 | tf_op jit(solution)/shard_map/scatter_moments/ppermute | solution.py:74
  54.3 7.5 %collective-permute-start.23 = (f32[128,128]{1,0:T(8,128)S(1)}, f32[128,128]{1,0:T(8,128)S(1)}, u32[]{:S(2)}, u32[]{:S(2)}) collective-permute-start(f32[128,128]{1,0:T(8,128)S(1)} %slice_add_fusion.5), channel_id=1, source_target_pairs={{0,9},{1,8},{2,11},{3,10},{4,13},{5,12},{6,15},{7,14},{8,1},{9,0},... | collective-permute-start | bytes 196616 | tf_op jit(solution)/shard_map/scatter_moments/ppermute | solution.py:74
  61.8 3.8 %collective-permute-start.24 = (f32[128,128]{1,0:T(8,128)S(1)}, f32[128,128]{1,0:T(8,128)S(1)}, u32[]{:S(2)}, u32[]{:S(2)}) collective-permute-start(f32[128,128]{1,0:T(8,128)S(1)} %add.70), channel_id=1, source_target_pairs={{0,5},{1,2},{2,1},{3,6},{4,7},{5,0},{6,3},{7,4},{8,11},{9,12},{10,... | collective-permute-start | bytes 196616 | tf_op jit(solution)/shard_map/gather_moments/ppermute | solution.py:74
  62.4 4.8 %collective-permute-start.15 = (f32[128,128]{1,0:T(8,128)S(1)}, f32[128,128]{1,0:T(8,128)S(1)}, u32[]{:S(2)}, u32[]{:S(2)}) collective-permute-start(f32[128,128]{1,0:T(8,128)S(1)} %slice_add_fusion.6), channel_id=1, source_target_pairs={{0,16},{1,2},{2,1},{3,19},{4,7},{5,21},{6,22},{7,4},{8,11},{9,25},... | collective-permute-start | bytes 196616 | tf_op jit(solution)/shard_map/gather_moments/ppermute | solution.py:74
  65.6 5.0 %collective-permute-start.25 = (f32[256,128]{1,0:T(8,128)S(1)}, f32[256,128]{1,0:T(8,128)S(1)}, u32[]{:S(2)}, u32[]{:S(2)}) collective-permute-start(f32[256,128]{1,0:T(8,128)S(1)} %pad_maximum_fusion.7), channel_id=1, source_target_pairs={{0,16},{1,4},{2,7},{3,19},{4,1},{5,21},{6,22},{7,2},{8,13},{9,25},... | collective-permute-start | bytes 393224 | tf_op jit(solution)/shard_map/gather_moments/ppermute | solution.py:74
  67.2 4.5 %collective-permute-start.16 = (f32[256,128]{1,0:T(8,128)S(1)}, f32[256,128]{1,0:T(8,128)S(1)}, u32[]{:S(2)}, u32[]{:S(2)}) collective-permute-start(f32[256,128]{1,0:T(8,128)S(1)} %pad_maximum_fusion.6), channel_id=1, source_target_pairs={{0,3},{1,4},{2,7},{3,0},{4,1},{5,6},{6,5},{7,2},{8,13},{9,10},{10,... | collective-permute-start | bytes 393224 | tf_op jit(solution)/shard_map/gather_moments/ppermute | solution.py:74
  70.6 5.9 %collective-permute-start.26 = (f32[512,128]{1,0:T(8,128)S(1)}, f32[512,128]{1,0:T(8,128)S(1)}, u32[]{:S(2)}, u32[]{:S(2)}) collective-permute-start(f32[512,128]{1,0:T(8,128)S(1)} %pad_maximum_fusion.2.refs_2_), channel_id=1, source_target_pairs={{0,3},{1,17},{2,18},{3,0},{4,20},{5,6},{6,5},{7,23},{8,24},{9,10},... | collective-permute-start | bytes 786440 | tf_op jit(solution)/shard_map/gather_moments/ppermute | solution.py:74
  71.6 5.9 %collective-permute-start.18 = (f32[512,128]{1,0:T(8,128)S(1)}, f32[512,128]{1,0:T(8,128)S(1)}, u32[]{:S(2)}, u32[]{:S(2)}) collective-permute-start(f32[512,128]{1,0:T(8,128)S(1)} %pad_maximum_fusion.1.refs_0_), channel_id=1, source_target_pairs={{0,5},{1,17},{2,18},{3,6},{4,20},{5,0},{6,3},{7,23},{8,24},{9,12},... | collective-permute-start | bytes 786440 | tf_op jit(solution)/shard_map/gather_moments/ppermute | solution.py:74
  72.8 1.2 %collective-permute-start.27 = (f32[8,128]{1,0:T(8,128)S(1)}, f32[8,128]{1,0:T(8,128)S(1)}, u32[]{:S(2)}, u32[]{:S(2)}) collective-permute-start(f32[8,128]{1,0:T(8,128)S(1)} %slice_add_fusion.8), channel_id=1, source_target_pairs={{0,1},{1,0},{2,3},{3,2},{4,5},{5,4},{6,7},{7,6},{8,9},{9,8},{10,11... | collective-permute-start | bytes 12296 | tf_op jit(solution)/shard_map/scatter_moments/ppermute | solution.py:74
  75.2 5.0 %collective-permute-start.29 = (f32[512,128]{1,0:T(8,128)S(1)}, f32[512,128]{1,0:T(8,128)S(1)}, u32[]{:S(2)}, u32[]{:S(2)}) collective-permute-start(f32[512,128]{1,0:T(8,128)S(1)} %pad_maximum_fusion.2.refs_2_), channel_id=1, source_target_pairs={{0,1},{1,0},{2,3},{3,2},{4,5},{5,4},{6,7},{7,6},{8,9},{9,8},{10,11... | collective-permute-start | bytes 786440 | tf_op jit(solution)/shard_map/gather_moments/ppermute | solution.py:74
  75.4 4.9 %collective-permute-start.17 = (f32[512,128]{1,0:T(8,128)S(1)}, f32[512,128]{1,0:T(8,128)S(1)}, u32[]{:S(2)}, u32[]{:S(2)}) collective-permute-start(f32[512,128]{1,0:T(8,128)S(1)} %pad_maximum_fusion.1.refs_0_), channel_id=1, source_target_pairs={{0,1},{1,0},{2,3},{3,2},{4,5},{5,4},{6,7},{7,6},{8,9},{9,8},{10,11... | collective-permute-start | bytes 786440 | tf_op jit(solution)/shard_map/gather_moments/ppermute | solution.py:74
  77.5 2.8 %collective-permute-start.28 = (f32[512,128]{1,0:T(8,128)S(1)}, f32[512,128]{1,0:T(8,128)S(1)}, u32[]{:S(2)}, u32[]{:S(2)}) collective-permute-start(f32[512,128]{1,0:T(8,128)S(1)} %collective-permute-done.18.refs_1_), channel_id=1, source_target_pairs={{0,1},{1,0},{2,3},{3,2},{4,5},{5,4},{6,7},{7,6},{8,9},{9,8},{10,11... | collective-permute-start | bytes 786440 | tf_op jit(solution)/shard_map/gather_moments/ppermute | solution.py:74
  78.5 1.7 %collective-permute-start.30 = (f32[512,128]{1,0:T(8,128)S(1)}, f32[512,128]{1,0:T(8,128)S(1)}, u32[]{:S(2)}, u32[]{:S(2)}) collective-permute-start(f32[512,128]{1,0:T(8,128)S(1)} %collective-permute-done.26.refs_3_), channel_id=1, source_target_pairs={{0,1},{1,0},{2,3},{3,2},{4,5},{5,4},{6,7},{7,6},{8,9},{9,8},{10,11... | collective-permute-start | bytes 786440 | tf_op jit(solution)/shard_map/gather_moments/ppermute | solution.py:74

commit v6 on v5

--- a/solution.py
+++ b/solution.py
@@ -78,9 +78,18 @@
     return jnp.broadcast_to(row, (height, LANES)).T
 
 
+def copy_kernel(plan, table, *refs):
+    sources, copies, sems = refs[:2], refs[2:4], refs[4]
+    moves = [pltpu.make_async_copy(s, t, sems.at[i]) for i, (s, t) in enumerate(zip(sources, copies))]
+    for move in moves:
+        move.start()
+    for move in moves:
+        move.wait()
+
+
 def prepare_kernel(plan, table, *refs):
-    sources, copies, (stack_ref, staged, features_ref, logits_ref, sems) = refs[:4], refs[4:6], refs[6:]
-    targets = (features_ref, logits_ref, *copies)
+    sources, (stack_ref, staged, features_ref, logits_ref, sems) = refs[:2], refs[2:]
+    targets = (features_ref, logits_ref)
     moves = [pltpu.make_async_copy(s, t, sems.at[i]) for i, (s, t) in enumerate(zip(sources, targets))]
     for move in moves:
         move.start()
@@ -268,21 +277,24 @@
     )(table, *operands)
 
 
-def prepare(plan, table, features, logits, means, variances):
+def in_hbm(arrays):
+    return [pltpu.with_memory_space_constraint(a, pltpu.HBM) for a in arrays]
+
+
+def prepare(plan, table, features, logits):
     count, width = features.shape
     comps = math.prod(logits.shape)
-    *held, stack, log_weights = call(
+    return call(
         prepare_kernel,
         plan,
         table,
-        [pltpu.with_memory_space_constraint(a, pltpu.HBM) for a in (features, logits, means, variances)],
-        [(means.shape, F32)] * 2 + [((count, 3 * width), BF16), ((comps, LANES), F32)],
-        [((count, width), BF16), (logits.shape, F32), pltpu.SemaphoreType.DMA((4,))],
+        in_hbm([features, logits]),
+        [((count, 3 * width), BF16), ((comps, LANES), F32)],
+        [((count, width), BF16), (logits.shape, F32), pltpu.SemaphoreType.DMA((2,))],
         8 * count * width,
         16,
         pltpu.HBM,
     )
-    return held, stack, log_weights
 
 
 def early_scores(plan, table, first_units, means, variances, log_weights, stack):
@@ -430,15 +442,20 @@
 
     with jax.named_scope("gather_parameters"):
         arrived = [plan.swap(h, plan.gather[0]) for h in (means, variances)]
-        held, stack, log_weights = prepare(plan, table, features, logits, means, variances)
-        arrived, held, stack, log_weights, table = lax.optimization_barrier(
-            (arrived, held, stack, log_weights, table)
+        held = call(
+            copy_kernel, plan, table, in_hbm([means, variances]), [(means.shape, F32)] * 2,
+            [pltpu.SemaphoreType.DMA((2,))], 0, 8, pltpu.HBM,
         )
         held = double(plan, held, None, arrived)
+        features, _ = lax.optimization_barrier((features, held[0]))
+        stack, log_weights = prepare(plan, table, features, logits)
         for step in plan.gather[1:-1]:
-            held = double(plan, held, (step, step))
+            arrived = [plan.swap(h, step) for h in held]
+            arrived[0], stack, log_weights = lax.optimization_barrier((arrived[0], stack, log_weights))
+            held = double(plan, held, None, arrived)
         last = [plan.swap(h, plan.gather[-1]) for h in held]
-        pairs = [(h, plan.swap(h, (0, 0))) for h in held]
+        both = lax.optimization_barrier(held)
+        pairs = [(h, plan.swap(b, (0, 0))) for h, b in zip(held, both)]
         firsts = (0, plan.units // 2)
         early = early_scores(plan, table, firsts, *pairs, log_weights, stack)
         last, early = lax.optimization_barrier((last, early))

time: 82.2 us -> 80.8 us (0.983)
  waiting for transfers between devices: 28.9 us -> 22.7 us
  starting transfers between devices: 29.8 us -> 33 us
  Pallas kernels: 21.1 us -> 22.6 us
    ppermute x31, waiting for transfers between devices: 28.9 us -> 22.7 us  [swap(): return lax.ppermute(value, ('grp', 'comp'), pairs)]
    ppermute x31, starting transfers between devices: 29.8 us -> 33 us  [swap(): return lax.ppermute(value, ('grp', 'comp'), pairs)]
    pallas_call x6 -> x7, Pallas kernels: 17.7 us -> 19.2 us  [call(): pl.pallas_call(functools.partial(kernel, plan), in_specs=[pl.BlockSpec(me...]
  transfers between devices with their start and end apart: 31 -> 31, of which waited for: 14 -> 13; matrix products, arithmetic and copies ran while one was open for 1% -> 1% of each run, Pallas kernels for 18% -> 20%
where the time goes in v6:
time: 80.8 us; the launch traced here: 80.5 us
  starting transfers between devices  33 us (41%)
  waiting for transfers between devices  22.7 us (28%)
  Pallas kernels  22.6 us (28%)
  between operations  0.97 us (1%)
  local copies, waits for them, and re-layouts  0.81 us (1%)
    ppermute x31, starting transfers between devices, swap(): return lax.ppermute(value, ('grp', 'comp'), pairs)  33 us
    ppermute x31, waiting for transfers between devices, swap(): return lax.ppermute(value, ('grp', 'comp'), pairs)  22.7 us
    pallas_call x7, Pallas kernels, call(): pl.pallas_call(functools.partial(kernel, plan), in_specs=[pl.BlockSpec(me...  19.2 us
    pallas_call x2, Pallas kernels, update(): pl.pallas_call(functools.partial(update_kernel, plan, first_slot), in_spe...  3.4 us
  transfers between devices with their start and end apart: 31, of which 13 were waited for; matrix products, arithmetic and copies ran while one was open for 1% of the time, Pallas kernels for 20%

profile of v6, /device:TPU:0, one launch (start us, length us, event | category | flops | bytes accessed | tf_op | source)
XLA Modules:
  0.0 80.5 jit_solution(17885584056794423115)
XLA Ops:
  0.6 3.5 %collective-permute-start = (f32[64,256]{1,0:T(8,128)}, f32[64,256]{1,0:T(8,128)S(1)}, u32[]{:S(2)}, u32[]{:S(2)}) collective-permute-start(f32[64,256]{1,0:T(8,128)} %refs_0_.1), channel_id=1, source_target_pairs={{0,9},{1,8},{2,11},{3,10},{4,13},{5,12},{6,15},{7,14},{8,1},{9,0},... | collective-permute-start | bytes 196616 | tf_op jit(solution)/shard_map/gather_parameters/ppermute | solution.py:74
  4.2 0.1 collective-permute-start.3
  4.3 0.7 dynamic-slice_bitcast_fusion.table.refs_0_
  4.9 1.5 %gather_parameters.4 = (f32[64,256]{1,0:T(8,128)S(1)}, f32[64,256]{1,0:T(8,128)S(1)}) custom-call(s32[5,16]{1,0:T(8,128)S(1)} %dynamic-slice_bitcast_fusion.table.refs_0_, f32[64,256]{1,0:T(8,128)} %refs_0_.1, f32[64,256]{1,0:T(8,128)} %refs_1_.1), custom_call_target="tpu_custom_call" | custom-call | bytes 262144 | tf_op jit(solution)/shard_map/gather_parameters/pallas_call | solution.py:269
  6.5 0.5 collective-permute-done
  7.0 4.0 %collective-permute-start.1 = (f32[128,256]{1,0:T(8,128)S(1)}, f32[128,256]{1,0:T(8,128)S(1)}, u32[]{:S(2)}, u32[]{:S(2)}) collective-permute-start(f32[128,256]{1,0:T(8,128)S(1)} %get-tuple-element.78), channel_id=1, source_target_pairs={{0,5},{1,2},{2,1},{3,6},{4,7},{5,0},{6,3},{7,4},{8,11},{9,12},{10,... | collective-permute-start | bytes 393224 | tf_op jit(solution)/shard_map/gather_parameters/ppermute | solution.py:74
  11.0 0.0 collective-permute-done.3
  11.0 1.4 %collective-permute-start.4 = (f32[128,256]{1,0:T(8,128)S(1)}, f32[128,256]{1,0:T(8,128)S(1)}, u32[]{:S(2)}, u32[]{:S(2)}) collective-permute-start(f32[128,256]{1,0:T(8,128)S(1)} %pad_maximum_fusion.4), channel_id=1, source_target_pairs={{0,5},{1,2},{2,1},{3,6},{4,7},{5,0},{6,3},{7,4},{8,11},{9,12},{10,... | collective-permute-start | bytes 393224 | tf_op jit(solution)/shard_map/gather_parameters/ppermute | solution.py:74
  12.4 3.0 %gather_parameters.5 = (bf16[2048,768]{1,0:T(8,128)(2,1)S(1)}, f32[1024,128]{1,0:T(8,128)S(1)}) custom-call(s32[5,16]{1,0:T(8,128)S(1)} %dynamic-slice_bitcast_fusion.table.refs_0_, bf16[2048,256]{1,0:T(8,128)(2,1)} %refs_0_.2, f32[8,128]{1,0:T(8,128)} %bitcast.5), custom_call_target="tpu_custom_call" | custom-call | flops 4194304 | bytes 2105344 | tf_op jit(solution)/shard_map/gather_parameters/pallas_call | solution.py:269
  15.5 0.0 collective-permute-done.1
  15.5 0.0 collective-permute-done.4
  15.6 0.9 %collective-permute-start.6 = (f32[256,256]{1,0:T(8,128)S(1)}, f32[256,256]{1,0:T(8,128)S(1)}, u32[]{:S(2)}, u32[]{:S(2)}) collective-permute-start(f32[256,256]{1,0:T(8,128)S(1)} %constant_dynamic-update-slice_fusion.2.refs_1_), channel_id=1, source_target_pairs={{0,1},{1,0},{2,3},{3,2},{4,5},{5,4},{6,7},{7,6},{8,9},{9,8},{10,11... | collective-permute-start | bytes 786440 | tf_op jit(solution)/shard_map/gather_parameters/ppermute | solution.py:74
  16.5 0.1 collective-permute-start.7
  16.6 1.3 %collective-permute-start.5 = (f32[256,256]{1,0:T(8,128)S(1)}, f32[256,256]{1,0:T(8,128)S(1)}, u32[]{:S(2)}, u32[]{:S(2)}) collective-permute-start(f32[256,256]{1,0:T(8,128)S(1)} %constant_dynamic-update-slice_fusion.5.refs_3_), channel_id=1, source_target_pairs={{0,3},{1,4},{2,7},{3,0},{4,1},{5,6},{6,5},{7,2},{8,13},{9,10},{10,... | collective-permute-start | bytes 786440 | tf_op jit(solution)/shard_map/gather_parameters/ppermute | solution.py:74
  17.9 0.4 collective-permute-start.2
  18.3 0.0 collective-permute-done.6.refs_2_
  18.3 0.0 collective-permute-done.7.refs_4_
  18.3 4.2 %gather_parameters.6 = (f32[512,2048]{1,0:T(8,128)S(1)}, f32[1,2048]{1,0:T(1,128)S(1)}, f32[1,2048]{1,0:T(1,128)S(1)}) custom-call(s32[5,16]{1,0:T(8,128)S(1)} %dynamic-slice_bitcast_fusion.table.refs_0_, f32[256,256]{1,0:T(8,128)S(1)} %constant_dynamic-update-slice_fusion.2.refs_1_, f32[256,256]{1,0:T(8,128)S(1)} %collective-permute-done.6.refs_2_, ...), custom_call_target="tpu_custom_call" | custom-call | flops 2684354560 | bytes 9437184 | tf_op jit(solution)/shard_map/gather_parameters/pallas_call | solution.py:269
  22.5 0.0 collective-permute-done.5.refs_2_
  22.5 2.7 %collective-permute-done.2.refs_1_ = f32[256,256]{1,0:T(8,128)S(1)} collective-permute-done((f32[256,256]{1,0:T(8,128)S(1)}, f32[256,256]{1,0:T(8,128)S(1)}, u32[]{:S(2)}, u32[]{:S(2)}) %collective-permute-start.2) | collective-permute-done | bytes 262176 | tf_op jit(solution)/shard_map/gather_parameters/ppermute | solution.py:74
  25.2 0.4 collective-permute-start.8
  25.6 0.1 collective-permute-start.9
  25.7 2.4 %gather_parameters.7 = (f32[256,2048]{1,0:T(8,128)S(1)}, f32[1,2048]{1,0:T(1,128)S(1)}, f32[1,2048]{1,0:T(1,128)S(1)}) custom-call(s32[5,16]{1,0:T(8,128)S(1)} %dynamic-slice_bitcast_fusion.table.refs_0_, f32[256,256]{1,0:T(8,128)S(1)} %collective-permute-done.2.refs_1_, f32[256,256]{1,0:T(8,128)S(1)} %collective-permute-done.5.refs_2_, ...), custom_call_target="tpu_custom_call" | custom-call | flops 1342177280 | bytes 8388608 | tf_op jit(solution)/shard_map/gather_parameters/pallas_call | solution.py:269
  28.0 0.0 collective-permute-done.8.refs_0_
  28.1 5.0 %shard_map.84 = (f32[1032,128]{1,0:T(8,128)S(1)}, f32[1024,128]{1,0:T(8,128)S(1)}, f32[8,128]{1,0:T(8,128)S(1)}, f32[1,2048]{1,0:T(1,128)}, bf16[512,2048]{1,0:T(8,128)(2,1)S(1)}) custom-call(s32[5,16]{1,0:T(8,128)S(1)} %dynamic-slice_bitcast_fusion.table.refs_0_, f32[256,256]{1,0:T(8,128)S(1)} %collective-permute-done.8.refs_0_, ...), custom_call_target="tpu_custom_call" | custom-call | flops 2415919104 | bytes 21037056 | tf_op jit(solution)/shard_map/pallas_call | solution.py:269
  33.0 0.4 collective-permute-start.10
  33.5 0.1 collective-permute-start.19
  33.6 1.8 %shard_map.85 = (f32[1024,128]{1,0:T(8,128)S(1)}, f32[1024,128]{1,0:T(8,128)S(1)}) custom-call(s32[5,16]{1,0:T(8,128)S(1)} %dynamic-slice_bitcast_fusion.table.refs_0_, bf16[512,2048]{1,0:T(8,128)(2,1)S(1)} %get-tuple-element.62.own_ref, bf16[2048,768]{1,0:T(8,128)(2,1)S(1)} %get-tuple-element.50.refs_6_.refs_4_.refs_3_.stack_ref), custom_call_target="tpu_custom_call" | custom-call | flops 1073741824 | bytes 10485760 | tf_op jit(solution)/shard_map/pallas_call | solution.py:269
  35.4 0.0 collective-permute-done.10
  35.4 0.1 slice_add_fusion
  35.5 0.9 %collective-permute-start.11 = (f32[520,128]{1,0:T(8,128)S(1)}, f32[520,128]{1,0:T(8,128)S(1)}, u32[]{:S(2)}, u32[]{:S(2)}) collective-permute-start(f32[520,128]{1,0:T(8,128)S(1)} %pad_maximum_fusion), channel_id=1, source_target_pairs={{0,5},{1,17},{2,18},{3,6},{4,20},{5,0},{6,3},{7,23},{8,24},{9,12},... | collective-permute-start | bytes 798728 | tf_op jit(solution)/shard_map/scatter_moments/ppermute | solution.py:74
  36.5 0.1 add.66
  36.6 1.6 %collective-permute-start.20 = (f32[512,128]{1,0:T(8,128)S(1)}, f32[512,128]{1,0:T(8,128)S(1)}, u32[]{:S(2)}, u32[]{:S(2)}) collective-permute-start(f32[512,128]{1,0:T(8,128)S(1)} %slice.104), channel_id=1, source_target_pairs={{0,3},{1,17},{2,18},{3,0},{4,20},{5,6},{6,5},{7,23},{8,24},{9,10},... | collective-permute-start | bytes 786440 | tf_op jit(solution)/shard_map/scatter_moments/ppermute | solution.py:74
  38.1 3.3 %collective-permute-done.11 = f32[520,128]{1,0:T(8,128)S(1)} collective-permute-done((f32[520,128]{1,0:T(8,128)S(1)}, f32[520,128]{1,0:T(8,128)S(1)}, u32[]{:S(2)}, u32[]{:S(2)}) %collective-permute-start.11) | collective-permute-done | bytes 266272 | tf_op jit(solution)/shard_map/scatter_moments/ppermute | solution.py:74
  41.5 1.7 %collective-permute-start.12 = (f32[264,128]{1,0:T(8,128)S(1)}, f32[264,128]{1,0:T(8,128)S(1)}, u32[]{:S(2)}, u32[]{:S(2)}) collective-permute-start(f32[264,128]{1,0:T(8,128)S(1)} %pad_maximum_fusion.3), channel_id=1, source_target_pairs={{0,3},{1,4},{2,7},{3,0},{4,1},{5,6},{6,5},{7,2},{8,13},{9,10},{10,... | collective-permute-start | bytes 405512 | tf_op jit(solution)/shard_map/scatter_moments/ppermute | solution.py:74
  43.3 1.6 %collective-permute-start.21 = (f32[256,128]{1,0:T(8,128)S(1)}, f32[256,128]{1,0:T(8,128)S(1)}, u32[]{:S(2)}, u32[]{:S(2)}) collective-permute-start(f32[256,128]{1,0:T(8,128)S(1)} %slice.106), channel_id=1, source_target_pairs={{0,16},{1,4},{2,7},{3,19},{4,1},{5,21},{6,22},{7,2},{8,13},{9,25},... | collective-permute-start | bytes 393224 | tf_op jit(solution)/shard_map/scatter_moments/ppermute | solution.py:74
  44.9 1.2 %collective-permute-done.12 = f32[264,128]{1,0:T(8,128)S(1)} collective-permute-done((f32[264,128]{1,0:T(8,128)S(1)}, f32[264,128]{1,0:T(8,128)S(1)}, u32[]{:S(2)}, u32[]{:S(2)}) %collective-permute-start.12) | collective-permute-done | bytes 135200 | tf_op jit(solution)/shard_map/scatter_moments/ppermute | solution.py:74
  46.1 1.7 %collective-permute-start.13 = (f32[136,128]{1,0:T(8,128)S(1)}, f32[136,128]{1,0:T(8,128)S(1)}, u32[]{:S(2)}, u32[]{:S(2)}) collective-permute-start(f32[136,128]{1,0:T(8,128)S(1)} %pad_maximum_fusion.7), channel_id=1, source_target_pairs={{0,16},{1,2},{2,1},{3,19},{4,7},{5,21},{6,22},{7,4},{8,11},{9,25},... | collective-permute-start | bytes 208904 | tf_op jit(solution)/shard_map/scatter_moments/ppermute | solution.py:74
  47.8 0.5 collective-permute-done.21
  48.3 0.6 collective-permute-start.22
  48.9 1.6 %collective-permute-done.13 = f32[136,128]{1,0:T(8,128)S(1)} collective-permute-done((f32[136,128]{1,0:T(8,128)S(1)}, f32[136,128]{1,0:T(8,128)S(1)}, u32[]{:S(2)}, u32[]{:S(2)}) %collective-permute-start.13) | collective-permute-done | bytes 69664 | tf_op jit(solution)/shard_map/scatter_moments/ppermute | solution.py:74
  50.5 2.3 %collective-permute-start.14 = (f32[136,128]{1,0:T(8,128)S(1)}, f32[136,128]{1,0:T(8,128)S(1)}, u32[]{:S(2)}, u32[]{:S(2)}) collective-permute-start(f32[136,128]{1,0:T(8,128)S(1)} %pad_maximum_fusion.8), channel_id=1, source_target_pairs={{0,9},{1,8},{2,11},{3,10},{4,13},{5,12},{6,15},{7,14},{8,1},{9,0},... | collective-permute-start | bytes 208904 | tf_op jit(solution)/shard_map/scatter_moments/ppermute | solution.py:74
  52.9 1.6 %collective-permute-start.23 = (f32[128,128]{1,0:T(8,128)S(1)}, f32[128,128]{1,0:T(8,128)S(1)}, u32[]{:S(2)}, u32[]{:S(2)}) collective-permute-start(f32[128,128]{1,0:T(8,128)S(1)} %slice_add_fusion.5), channel_id=1, source_target_pairs={{0,9},{1,8},{2,11},{3,10},{4,13},{5,12},{6,15},{7,14},{8,1},{9,0},... | collective-permute-start | bytes 196616 | tf_op jit(solution)/shard_map/scatter_moments/ppermute | solution.py:74
  54.5 5.8 %collective-permute-done.23 = f32[128,128]{1,0:T(8,128)S(1)} collective-permute-done((f32[128,128]{1,0:T(8,128)S(1)}, f32[128,128]{1,0:T(8,128)S(1)}, u32[]{:S(2)}, u32[]{:S(2)}) %collective-permute-start.23) | collective-permute-done | bytes 65568 | tf_op jit(solution)/shard_map/scatter_moments/ppermute | solution.py:74
  60.3 0.6 collective-permute-start.24
  60.9 1.6 %collective-permute-start.15 = (f32[128,128]{1,0:T(8,128)S(1)}, f32[128,128]{1,0:T(8,128)S(1)}, u32[]{:S(2)}, u32[]{:S(2)}) collective-permute-start(f32[128,128]{1,0:T(8,128)S(1)} %slice_add_fusion.6), channel_id=1, source_target_pairs={{0,16},{1,2},{2,1},{3,19},{4,7},{5,21},{6,22},{7,4},{8,11},{9,25},... | collective-permute-start | bytes 196616 | tf_op jit(solution)/shard_map/gather_moments/ppermute | solution.py:74
  62.5 1.5 %collective-permute-done.24 = f32[128,128]{1,0:T(8,128)S(1)} collective-permute-done((f32[128,128]{1,0:T(8,128)S(1)}, f32[128,128]{1,0:T(8,128)S(1)}, u32[]{:S(2)}, u32[]{:S(2)}) %collective-permute-start.24) | collective-permute-done | bytes 65568 | tf_op jit(solution)/shard_map/gather_moments/ppermute | solution.py:74
  64.0 1.6 %collective-permute-start.25 = (f32[256,128]{1,0:T(8,128)S(1)}, f32[256,128]{1,0:T(8,128)S(1)}, u32[]{:S(2)}, u32[]{:S(2)}) collective-permute-start(f32[256,128]{1,0:T(8,128)S(1)} %pad_maximum_fusion.6), channel_id=1, source_target_pairs={{0,16},{1,4},{2,7},{3,19},{4,1},{5,21},{6,22},{7,2},{8,13},{9,25},... | collective-permute-start | bytes 393224 | tf_op jit(solution)/shard_map/gather_moments/ppermute | solution.py:74
  65.6 0.0 collective-permute-done.15
  65.6 1.1 %collective-permute-start.16 = (f32[256,128]{1,0:T(8,128)S(1)}, f32[256,128]{1,0:T(8,128)S(1)}, u32[]{:S(2)}, u32[]{:S(2)}) collective-permute-start(f32[256,128]{1,0:T(8,128)S(1)} %pad_maximum_fusion.5), channel_id=1, source_target_pairs={{0,3},{1,4},{2,7},{3,0},{4,1},{5,6},{6,5},{7,2},{8,13},{9,10},{10,... | collective-permute-start | bytes 393224 | tf_op jit(solution)/shard_map/gather_moments/ppermute | solution.py:74
  66.8 2.3 %collective-permute-done.25 = f32[256,128]{1,0:T(8,128)S(1)} collective-permute-done((f32[256,128]{1,0:T(8,128)S(1)}, f32[256,128]{1,0:T(8,128)S(1)}, u32[]{:S(2)}, u32[]{:S(2)}) %collective-permute-start.25) | collective-permute-done | bytes 131104 | tf_op jit(solution)/shard_map/gather_moments/ppermute | solution.py:74
  69.1 0.5 collective-permute-start.26
  69.6 0.5 collective-permute-done.16
  70.1 1.3 %collective-permute-start.18 = (f32[512,128]{1,0:T(8,128)S(1)}, f32[512,128]{1,0:T(8,128)S(1)}, u32[]{:S(2)}, u32[]{:S(2)}) collective-permute-start(f32[512,128]{1,0:T(8,128)S(1)} %pad_maximum_fusion.1.refs_0_), channel_id=1, source_target_pairs={{0,5},{1,17},{2,18},{3,6},{4,20},{5,0},{6,3},{7,23},{8,24},{9,12},... | collective-permute-start | bytes 786440 | tf_op jit(solution)/shard_map/gather_moments/ppermute | solution.py:74
  71.4 1.2 %collective-permute-done.27 = f32[8,128]{1,0:T(8,128)S(1)} collective-permute-done((f32[8,128]{1,0:T(8,128)S(1)}, f32[8,128]{1,0:T(8,128)S(1)}, u32[]{:S(2)}, u32[]{:S(2)}) %collective-permute-start.27) | collective-permute-done | bytes 4128 | tf_op jit(solution)/shard_map/scatter_moments/ppermute | solution.py:74
  72.6 1.3 %gather_moments.1 = (f32[8,128]{1,0:T(8,128)}, f32[1024,128]{1,0:T(8,128)S(1)}) custom-call(s32[5,16]{1,0:T(8,128)S(1)} %dynamic-slice_bitcast_fusion.table.refs_0_, f32[8,128]{1,0:T(8,128)S(1)} %add_multiply_fusion.refs_1_), custom_call_target="tpu_custom_call" | custom-call | flops 1024 | bytes 8192 | tf_op jit(solution)/shard_map/gather_moments/pallas_call | solution.py:269
  73.8 0.2 collective-permute-start.29
  74.0 0.3 collective-permute-start.17
  74.3 0.6 collective-permute-done.26.refs_3_
  75.0 1.0 %collective-permute-done.18.refs_1_ = f32[512,128]{1,0:T(8,128)S(1)} collective-permute-done((f32[512,128]{1,0:T(8,128)S(1)}, f32[512,128]{1,0:T(8,128)S(1)}, u32[]{:S(2)}, u32[]{:S(2)}) %collective-permute-start.18) | collective-permute-done | bytes 262176 | tf_op jit(solution)/shard_map/gather_moments/ppermute | solution.py:74
  76.0 1.1 %collective-permute-start.28 = (f32[512,128]{1,0:T(8,128)S(1)}, f32[512,128]{1,0:T(8,128)S(1)}, u32[]{:S(2)}, u32[]{:S(2)}) collective-permute-start(f32[512,128]{1,0:T(8,128)S(1)} %collective-permute-done.18.refs_1_), channel_id=1, source_target_pairs={{0,1},{1,0},{2,3},{3,2},{4,5},{5,4},{6,7},{7,6},{8,9},{9,8},{10,11... | collective-permute-start | bytes 786440 | tf_op jit(solution)/shard_map/gather_moments/ppermute | solution.py:74
  77.0 0.0 collective-permute-start.30
  77.0 1.7 %shard_map.86 = (f32[1024,256]{1,0:T(8,128)}, f32[1024,256]{1,0:T(8,128)}) custom-call(s32[5,16]{1,0:T(8,128)S(1)} %dynamic-slice_bitcast_fusion.table.refs_0_, f32[512,128]{1,0:T(8,128)S(1)} %pad_maximum_fusion.1.refs_0_, f32[512,128]{1,0:T(8,128)S(1)} %collective-permute-done.18.refs_1_, f32[512,128]{1,0:T(8,128)S(1)} %pad_maximum_fusion.2.refs_2_, ...), custom_call_target="tpu_custom_call" | custom-call | flops 1048576 | bytes 2097152 | tf_op jit(solution)/shard_map/pallas_call | solution.py:396
  78.8 1.7 %shard_map.87 = (f32[1024,256]{1,0:T(8,128)}, f32[1024,256]{1,0:T(8,128)}) custom-call(s32[5,16]{1,0:T(8,128)S(1)} %dynamic-slice_bitcast_fusion.table.refs_0_, f32[512,128]{1,0:T(8,128)S(1)} %collective-permute-done.17.refs_0_, f32[512,128]{1,0:T(8,128)S(1)} %collective-permute-done.28.refs_1_, ...), custom_call_target="tpu_custom_call", output_to_operand_aliasing={{0}: (6, {}), {1}: (7, {})} | custom-call | flops 1048576 | bytes 2097152 | tf_op jit(solution)/shard_map/pallas_call | solution.py:396
  (45 shorter events, 0.4 us)
Async XLA Ops:
  0.6 6.3 %collective-permute-start = (f32[64,256]{1,0:T(8,128)}, f32[64,256]{1,0:T(8,128)S(1)}, u32[]{:S(2)}, u32[]{:S(2)}) collective-permute-start(f32[64,256]{1,0:T(8,128)} %refs_0_.1), channel_id=1, source_target_pairs={{0,9},{1,8},{2,11},{3,10},{4,13},{5,12},{6,15},{7,14},{8,1},{9,0},... | collective-permute-start | bytes 196616 | tf_op jit(solution)/shard_map/gather_parameters/ppermute | solution.py:74
  4.2 6.9 %collective-permute-start.3 = (f32[64,256]{1,0:T(8,128)}, f32[64,256]{1,0:T(8,128)S(1)}, u32[]{:S(2)}, u32[]{:S(2)}) collective-permute-start(f32[64,256]{1,0:T(8,128)} %refs_1_.1), channel_id=1, source_target_pairs={{0,9},{1,8},{2,11},{3,10},{4,13},{5,12},{6,15},{7,14},{8,1},{9,0},... | collective-permute-start | bytes 196616 | tf_op jit(solution)/shard_map/gather_parameters/ppermute | solution.py:74
  7.0 8.5 %collective-permute-start.1 = (f32[128,256]{1,0:T(8,128)S(1)}, f32[128,256]{1,0:T(8,128)S(1)}, u32[]{:S(2)}, u32[]{:S(2)}) collective-permute-start(f32[128,256]{1,0:T(8,128)S(1)} %get-tuple-element.78), channel_id=1, source_target_pairs={{0,5},{1,2},{2,1},{3,6},{4,7},{5,0},{6,3},{7,4},{8,11},{9,12},{10,... | collective-permute-start | bytes 393224 | tf_op jit(solution)/shard_map/gather_parameters/ppermute | solution.py:74
  11.0 4.5 %collective-permute-start.4 = (f32[128,256]{1,0:T(8,128)S(1)}, f32[128,256]{1,0:T(8,128)S(1)}, u32[]{:S(2)}, u32[]{:S(2)}) collective-permute-start(f32[128,256]{1,0:T(8,128)S(1)} %pad_maximum_fusion.4), channel_id=1, source_target_pairs={{0,5},{1,2},{2,1},{3,6},{4,7},{5,0},{6,3},{7,4},{8,11},{9,12},{10,... | collective-permute-start | bytes 393224 | tf_op jit(solution)/shard_map/gather_parameters/ppermute | solution.py:74
  15.6 2.8 %collective-permute-start.6 = (f32[256,256]{1,0:T(8,128)S(1)}, f32[256,256]{1,0:T(8,128)S(1)}, u32[]{:S(2)}, u32[]{:S(2)}) collective-permute-start(f32[256,256]{1,0:T(8,128)S(1)} %constant_dynamic-update-slice_fusion.2.refs_1_), channel_id=1, source_target_pairs={{0,1},{1,0},{2,3},{3,2},{4,5},{5,4},{6,7},{7,6},{8,9},{9,8},{10,11... | collective-permute-start | bytes 786440 | tf_op jit(solution)/shard_map/gather_parameters/ppermute | solution.py:74
  16.5 1.8 %collective-permute-start.7 = (f32[256,256]{1,0:T(8,128)S(1)}, f32[256,256]{1,0:T(8,128)S(1)}, u32[]{:S(2)}, u32[]{:S(2)}) collective-permute-start(f32[256,256]{1,0:T(8,128)S(1)} %constant_dynamic-update-slice_fusion.5.refs_3_), channel_id=1, source_target_pairs={{0,1},{1,0},{2,3},{3,2},{4,5},{5,4},{6,7},{7,6},{8,9},{9,8},{10,11... | collective-permute-start | bytes 786440 | tf_op jit(solution)/shard_map/gather_parameters/ppermute | solution.py:74
  16.6 5.9 %collective-permute-start.5 = (f32[256,256]{1,0:T(8,128)S(1)}, f32[256,256]{1,0:T(8,128)S(1)}, u32[]{:S(2)}, u32[]{:S(2)}) collective-permute-start(f32[256,256]{1,0:T(8,128)S(1)} %constant_dynamic-update-slice_fusion.5.refs_3_), channel_id=1, source_target_pairs={{0,3},{1,4},{2,7},{3,0},{4,1},{5,6},{6,5},{7,2},{8,13},{9,10},{10,... | collective-permute-start | bytes 786440 | tf_op jit(solution)/shard_map/gather_parameters/ppermute | solution.py:74
  17.9 7.3 %collective-permute-start.2 = (f32[256,256]{1,0:T(8,128)S(1)}, f32[256,256]{1,0:T(8,128)S(1)}, u32[]{:S(2)}, u32[]{:S(2)}) collective-permute-start(f32[256,256]{1,0:T(8,128)S(1)} %constant_dynamic-update-slice_fusion.2.refs_1_), channel_id=1, source_target_pairs={{0,3},{1,4},{2,7},{3,0},{4,1},{5,6},{6,5},{7,2},{8,13},{9,10},{10,... | collective-permute-start | bytes 786440 | tf_op jit(solution)/shard_map/gather_parameters/ppermute | solution.py:74
  25.2 2.9 %collective-permute-start.8 = (f32[256,256]{1,0:T(8,128)S(1)}, f32[256,256]{1,0:T(8,128)S(1)}, u32[]{:S(2)}, u32[]{:S(2)}) collective-permute-start(f32[256,256]{1,0:T(8,128)S(1)} %collective-permute-done.2.refs_1_), channel_id=1, source_target_pairs={{0,1},{1,0},{2,3},{3,2},{4,5},{5,4},{6,7},{7,6},{8,9},{9,8},{10,11... | collective-permute-start | bytes 786440 | tf_op jit(solution)/shard_map/gather_parameters/ppermute | solution.py:74
  25.6 2.5 %collective-permute-start.9 = (f32[256,256]{1,0:T(8,128)S(1)}, f32[256,256]{1,0:T(8,128)S(1)}, u32[]{:S(2)}, u32[]{:S(2)}) collective-permute-start(f32[256,256]{1,0:T(8,128)S(1)} %collective-permute-done.5.refs_2_), channel_id=1, source_target_pairs={{0,1},{1,0},{2,3},{3,2},{4,5},{5,4},{6,7},{7,6},{8,9},{9,8},{10,11... | collective-permute-start | bytes 786440 | tf_op jit(solution)/shard_map/gather_parameters/ppermute | solution.py:74
  33.0 2.4 %collective-permute-start.10 = (f32[1032,128]{1,0:T(8,128)S(1)}, f32[1032,128]{1,0:T(8,128)S(1)}, u32[]{:S(2)}, u32[]{:S(2)}) collective-permute-start(f32[1032,128]{1,0:T(8,128)S(1)} %get-tuple-element.64), channel_id=1, source_target_pairs={{0,1},{1,0},{2,3},{3,2},{4,5},{5,4},{6,7},{7,6},{8,9},{9,8},{10,11... | collective-permute-start | bytes 1585160 | tf_op jit(solution)/shard_map/scatter_moments/ppermute | solution.py:74
  33.5 3.0 %collective-permute-start.19 = (f32[1024,128]{1,0:T(8,128)S(1)}, f32[1024,128]{1,0:T(8,128)S(1)}, u32[]{:S(2)}, u32[]{:S(2)}) collective-permute-start(f32[1024,128]{1,0:T(8,128)S(1)} %get-tuple-element.67), channel_id=1, source_target_pairs={{0,1},{1,0},{2,3},{3,2},{4,5},{5,4},{6,7},{7,6},{8,9},{9,8},{10,11... | collective-permute-start | bytes 1572872 | tf_op jit(solution)/shard_map/scatter_moments/ppermute | solution.py:74
  35.5 5.9 %collective-permute-start.11 = (f32[520,128]{1,0:T(8,128)S(1)}, f32[520,128]{1,0:T(8,128)S(1)}, u32[]{:S(2)}, u32[]{:S(2)}) collective-permute-start(f32[520,128]{1,0:T(8,128)S(1)} %pad_maximum_fusion), channel_id=1, source_target_pairs={{0,5},{1,17},{2,18},{3,6},{4,20},{5,0},{6,3},{7,23},{8,24},{9,12},... | collective-permute-start | bytes 798728 | tf_op jit(solution)/shard_map/scatter_moments/ppermute | solution.py:74
  36.6 6.6 %collective-permute-start.20 = (f32[512,128]{1,0:T(8,128)S(1)}, f32[512,128]{1,0:T(8,128)S(1)}, u32[]{:S(2)}, u32[]{:S(2)}) collective-permute-start(f32[512,128]{1,0:T(8,128)S(1)} %slice.104), channel_id=1, source_target_pairs={{0,3},{1,17},{2,18},{3,0},{4,20},{5,6},{6,5},{7,23},{8,24},{9,10},... | collective-permute-start | bytes 786440 | tf_op jit(solution)/shard_map/scatter_moments/ppermute | solution.py:74
  41.5 4.5 %collective-permute-start.12 = (f32[264,128]{1,0:T(8,128)S(1)}, f32[264,128]{1,0:T(8,128)S(1)}, u32[]{:S(2)}, u32[]{:S(2)}) collective-permute-start(f32[264,128]{1,0:T(8,128)S(1)} %pad_maximum_fusion.3), channel_id=1, source_target_pairs={{0,3},{1,4},{2,7},{3,0},{4,1},{5,6},{6,5},{7,2},{8,13},{9,10},{10,... | collective-permute-start | bytes 405512 | tf_op jit(solution)/shard_map/scatter_moments/ppermute | solution.py:74
  43.3 5.0 %collective-permute-start.21 = (f32[256,128]{1,0:T(8,128)S(1)}, f32[256,128]{1,0:T(8,128)S(1)}, u32[]{:S(2)}, u32[]{:S(2)}) collective-permute-start(f32[256,128]{1,0:T(8,128)S(1)} %slice.106), channel_id=1, source_target_pairs={{0,16},{1,4},{2,7},{3,19},{4,1},{5,21},{6,22},{7,2},{8,13},{9,25},... | collective-permute-start | bytes 393224 | tf_op jit(solution)/shard_map/scatter_moments/ppermute | solution.py:74
  46.1 4.4 %collective-permute-start.13 = (f32[136,128]{1,0:T(8,128)S(1)}, f32[136,128]{1,0:T(8,128)S(1)}, u32[]{:S(2)}, u32[]{:S(2)}) collective-permute-start(f32[136,128]{1,0:T(8,128)S(1)} %pad_maximum_fusion.7), channel_id=1, source_target_pairs={{0,16},{1,2},{2,1},{3,19},{4,7},{5,21},{6,22},{7,4},{8,11},{9,25},... | collective-permute-start | bytes 208904 | tf_op jit(solution)/shard_map/scatter_moments/ppermute | solution.py:74
  48.3 4.5 %collective-permute-start.22 = (f32[128,128]{1,0:T(8,128)S(1)}, f32[128,128]{1,0:T(8,128)S(1)}, u32[]{:S(2)}, u32[]{:S(2)}) collective-permute-start(f32[128,128]{1,0:T(8,128)S(1)} %slice.108), channel_id=1, source_target_pairs={{0,5},{1,2},{2,1},{3,6},{4,7},{5,0},{6,3},{7,4},{8,11},{9,12},{10,... | collective-permute-start | bytes 196616 | tf_op jit(solution)/shard_map/scatter_moments/ppermute | solution.py:74
  50.5 10.4 %collective-permute-start.14 = (f32[136,128]{1,0:T(8,128)S(1)}, f32[136,128]{1,0:T(8,128)S(1)}, u32[]{:S(2)}, u32[]{:S(2)}) collective-permute-start(f32[136,128]{1,0:T(8,128)S(1)} %pad_maximum_fusion.8), channel_id=1, source_target_pairs={{0,9},{1,8},{2,11},{3,10},{4,13},{5,12},{6,15},{7,14},{8,1},{9,0},... | collective-permute-start | bytes 208904 | tf_op jit(solution)/shard_map/scatter_moments/ppermute | solution.py:74
  52.9 7.4 %collective-permute-start.23 = (f32[128,128]{1,0:T(8,128)S(1)}, f32[128,128]{1,0:T(8,128)S(1)}, u32[]{:S(2)}, u32[]{:S(2)}) collective-permute-start(f32[128,128]{1,0:T(8,128)S(1)} %slice_add_fusion.5), channel_id=1, source_target_pairs={{0,9},{1,8},{2,11},{3,10},{4,13},{5,12},{6,15},{7,14},{8,1},{9,0},... | collective-permute-start | bytes 196616 | tf_op jit(solution)/shard_map/scatter_moments/ppermute | solution.py:74
  60.3 3.8 %collective-permute-start.24 = (f32[128,128]{1,0:T(8,128)S(1)}, f32[128,128]{1,0:T(8,128)S(1)}, u32[]{:S(2)}, u32[]{:S(2)}) collective-permute-start(f32[128,128]{1,0:T(8,128)S(1)} %add.70), channel_id=1, source_target_pairs={{0,5},{1,2},{2,1},{3,6},{4,7},{5,0},{6,3},{7,4},{8,11},{9,12},{10,... | collective-permute-start | bytes 196616 | tf_op jit(solution)/shard_map/gather_moments/ppermute | solution.py:74
  60.9 4.7 %collective-permute-start.15 = (f32[128,128]{1,0:T(8,128)S(1)}, f32[128,128]{1,0:T(8,128)S(1)}, u32[]{:S(2)}, u32[]{:S(2)}) collective-permute-start(f32[128,128]{1,0:T(8,128)S(1)} %slice_add_fusion.6), channel_id=1, source_target_pairs={{0,16},{1,2},{2,1},{3,19},{4,7},{5,21},{6,22},{7,4},{8,11},{9,25},... | collective-permute-start | bytes 196616 | tf_op jit(solution)/shard_map/gather_moments/ppermute | solution.py:74
  64.0 5.0 %collective-permute-start.25 = (f32[256,128]{1,0:T(8,128)S(1)}, f32[256,128]{1,0:T(8,128)S(1)}, u32[]{:S(2)}, u32[]{:S(2)}) collective-permute-start(f32[256,128]{1,0:T(8,128)S(1)} %pad_maximum_fusion.6), channel_id=1, source_target_pairs={{0,16},{1,4},{2,7},{3,19},{4,1},{5,21},{6,22},{7,2},{8,13},{9,25},... | collective-permute-start | bytes 393224 | tf_op jit(solution)/shard_map/gather_moments/ppermute | solution.py:74
  65.6 4.5 %collective-permute-start.16 = (f32[256,128]{1,0:T(8,128)S(1)}, f32[256,128]{1,0:T(8,128)S(1)}, u32[]{:S(2)}, u32[]{:S(2)}) collective-permute-start(f32[256,128]{1,0:T(8,128)S(1)} %pad_maximum_fusion.5), channel_id=1, source_target_pairs={{0,3},{1,4},{2,7},{3,0},{4,1},{5,6},{6,5},{7,2},{8,13},{9,10},{10,... | collective-permute-start | bytes 393224 | tf_op jit(solution)/shard_map/gather_moments/ppermute | solution.py:74
  69.1 5.9 %collective-permute-start.26 = (f32[512,128]{1,0:T(8,128)S(1)}, f32[512,128]{1,0:T(8,128)S(1)}, u32[]{:S(2)}, u32[]{:S(2)}) collective-permute-start(f32[512,128]{1,0:T(8,128)S(1)} %pad_maximum_fusion.2.refs_2_), channel_id=1, source_target_pairs={{0,3},{1,17},{2,18},{3,0},{4,20},{5,6},{6,5},{7,23},{8,24},{9,10},... | collective-permute-start | bytes 786440 | tf_op jit(solution)/shard_map/gather_moments/ppermute | solution.py:74
  70.1 5.9 %collective-permute-start.18 = (f32[512,128]{1,0:T(8,128)S(1)}, f32[512,128]{1,0:T(8,128)S(1)}, u32[]{:S(2)}, u32[]{:S(2)}) collective-permute-start(f32[512,128]{1,0:T(8,128)S(1)} %pad_maximum_fusion.1.refs_0_), channel_id=1, source_target_pairs={{0,5},{1,17},{2,18},{3,6},{4,20},{5,0},{6,3},{7,23},{8,24},{9,12},... | collective-permute-start | bytes 786440 | tf_op jit(solution)/shard_map/gather_moments/ppermute | solution.py:74
  71.4 1.2 %collective-permute-start.27 = (f32[8,128]{1,0:T(8,128)S(1)}, f32[8,128]{1,0:T(8,128)S(1)}, u32[]{:S(2)}, u32[]{:S(2)}) collective-permute-start(f32[8,128]{1,0:T(8,128)S(1)} %slice_add_fusion.8), channel_id=1, source_target_pairs={{0,1},{1,0},{2,3},{3,2},{4,5},{5,4},{6,7},{7,6},{8,9},{9,8},{10,11... | collective-permute-start | bytes 12296 | tf_op jit(solution)/shard_map/scatter_moments/ppermute | solution.py:74
  73.8 4.9 %collective-permute-start.29 = (f32[512,128]{1,0:T(8,128)S(1)}, f32[512,128]{1,0:T(8,128)S(1)}, u32[]{:S(2)}, u32[]{:S(2)}) collective-permute-start(f32[512,128]{1,0:T(8,128)S(1)} %pad_maximum_fusion.2.refs_2_), channel_id=1, source_target_pairs={{0,1},{1,0},{2,3},{3,2},{4,5},{5,4},{6,7},{7,6},{8,9},{9,8},{10,11... | collective-permute-start | bytes 786440 | tf_op jit(solution)/shard_map/gather_moments/ppermute | solution.py:74
  74.0 4.8 %collective-permute-start.17 = (f32[512,128]{1,0:T(8,128)S(1)}, f32[512,128]{1,0:T(8,128)S(1)}, u32[]{:S(2)}, u32[]{:S(2)}) collective-permute-start(f32[512,128]{1,0:T(8,128)S(1)} %pad_maximum_fusion.1.refs_0_), channel_id=1, source_target_pairs={{0,1},{1,0},{2,3},{3,2},{4,5},{5,4},{6,7},{7,6},{8,9},{9,8},{10,11... | collective-permute-start | bytes 786440 | tf_op jit(solution)/shard_map/gather_moments/ppermute | solution.py:74
  76.0 2.8 %collective-permute-start.28 = (f32[512,128]{1,0:T(8,128)S(1)}, f32[512,128]{1,0:T(8,128)S(1)}, u32[]{:S(2)}, u32[]{:S(2)}) collective-permute-start(f32[512,128]{1,0:T(8,128)S(1)} %collective-permute-done.18.refs_1_), channel_id=1, source_target_pairs={{0,1},{1,0},{2,3},{3,2},{4,5},{5,4},{6,7},{7,6},{8,9},{9,8},{10,11... | collective-permute-start | bytes 786440 | tf_op jit(solution)/shard_map/gather_moments/ppermute | solution.py:74
  77.0 1.7 %collective-permute-start.30 = (f32[512,128]{1,0:T(8,128)S(1)}, f32[512,128]{1,0:T(8,128)S(1)}, u32[]{:S(2)}, u32[]{:S(2)}) collective-permute-start(f32[512,128]{1,0:T(8,128)S(1)} %collective-permute-done.26.refs_3_), channel_id=1, source_target_pairs={{0,1},{1,0},{2,3},{3,2},{4,5},{5,4},{6,7},{7,6},{8,9},{9,8},{10,11... | collective-permute-start | bytes 786440 | tf_op jit(solution)/shard_map/gather_moments/ppermute | solution.py:74

commit v7 on v5

--- a/solution.py
+++ b/solution.py
@@ -78,9 +78,9 @@
     return jnp.broadcast_to(row, (height, LANES)).T
 
 
-def prepare_kernel(plan, table, *refs):
-    sources, copies, (stack_ref, staged, features_ref, logits_ref, sems) = refs[:4], refs[4:6], refs[6:]
-    targets = (features_ref, logits_ref, *copies)
+def start_kernel(plan, table, *refs):
+    sources, (*copies, staged, logits_ref, sems) = refs[:3], refs[3:]
+    targets = (*copies, logits_ref)
     moves = [pltpu.make_async_copy(s, t, sems.at[i]) for i, (s, t) in enumerate(zip(sources, targets))]
     for move in moves:
         move.start()
@@ -91,14 +91,26 @@
     log_weights = shifted - jnp.log(jnp.sum(jnp.exp(shifted)))
     for b in range(logits.shape[0]):
         staged[b * LANES : (b + 1) * LANES, :] = columns(log_weights[b : b + 1, :], LANES)
-    width = features_ref.shape[1]
-    rows = features_ref[...]
-    values = rows.astype(F32)
-    squares = values * values
-    high = squares.astype(BF16)
-    stack_ref[:, :width] = (squares - high.astype(F32)).astype(BF16)
-    stack_ref[:, width : 2 * width] = high
-    stack_ref[:, 2 * width :] = rows
+
+
+def stack_kernel(plan, table, source, stack_ref, features_ref, sems):
+    count, width = features_ref.shape
+    block = count // sems.shape[0]
+    moves = []
+    for at in range(sems.shape[0]):
+        here = pl.ds(at * block, block)
+        moves.append(pltpu.make_async_copy(source.at[here], features_ref.at[here], sems.at[at]))
+        moves[-1].start()
+    for at, move in enumerate(moves):
+        move.wait()
+        here = slice(at * block, (at + 1) * block)
+        rows = features_ref[here, :]
+        values = rows.astype(F32)
+        squares = values * values
+        high = squares.astype(BF16)
+        stack_ref[here, :width] = (squares - high.astype(F32)).astype(BF16)
+        stack_ref[here, width : 2 * width] = high
+        stack_ref[here, 2 * width :] = rows
 
 
 def build_weights(unit, table, first_units, mean_refs, variance_refs, log_weights, weights, offsets):
@@ -268,21 +280,37 @@
     )(table, *operands)
 
 
-def prepare(plan, table, features, logits, means, variances):
-    count, width = features.shape
-    comps = math.prod(logits.shape)
-    *held, stack, log_weights = call(
-        prepare_kernel,
+def in_hbm(arrays):
+    return [pltpu.with_memory_space_constraint(a, pltpu.HBM) for a in arrays]
+
+
+def own_copies(plan, table, means, variances, logits):
+    return call(
+        start_kernel,
         plan,
         table,
-        [pltpu.with_memory_space_constraint(a, pltpu.HBM) for a in (features, logits, means, variances)],
-        [(means.shape, F32)] * 2 + [((count, 3 * width), BF16), ((comps, LANES), F32)],
-        [((count, width), BF16), (logits.shape, F32), pltpu.SemaphoreType.DMA((4,))],
+        in_hbm([means, variances, logits]),
+        [(means.shape, F32)] * 2 + [((math.prod(logits.shape), LANES), F32)],
+        [(logits.shape, F32), pltpu.SemaphoreType.DMA((3,))],
+        0,
+        8,
+        pltpu.HBM,
+    )
+
+
+def feature_stack(plan, table, features):
+    count, width = features.shape
+    return call(
+        stack_kernel,
+        plan,
+        table,
+        in_hbm([features]),
+        [((count, 3 * width), BF16)],
+        [((count, width), BF16), pltpu.SemaphoreType.DMA((4,))],
         8 * count * width,
         16,
         pltpu.HBM,
-    )
-    return held, stack, log_weights
+    )[0]
 
 
 def early_scores(plan, table, first_units, means, variances, log_weights, stack):
@@ -417,7 +445,9 @@
     for pair in plan.whole:
         arrived = [plan.swap(jnp.concatenate([kept[0], counts], axis=0), pair), plan.swap(kept[1], pair)]
         counts = counts + arrived[0][rows:]
-        kept = [k + a[:rows] for k, a in zip(kept, arrived)]
+        first = kept[0] + arrived[0][:rows]
+        second, _ = lax.optimization_barrier((arrived[1], first))
+        kept = [first, kept[1] + second]
     return kept, 0.5 * (counts + plan.swap(counts, (0, 0)))
 
 
@@ -430,15 +460,15 @@
 
     with jax.named_scope("gather_parameters"):
         arrived = [plan.swap(h, plan.gather[0]) for h in (means, variances)]
-        held, stack, log_weights = prepare(plan, table, features, logits, means, variances)
-        arrived, held, stack, log_weights, table = lax.optimization_barrier(
-            (arrived, held, stack, log_weights, table)
-        )
+        *held, log_weights = own_copies(plan, table, means, variances, logits)
+        stack = feature_stack(plan, table, features)
+        arrived[1], stack = lax.optimization_barrier((arrived[1], stack))
         held = double(plan, held, None, arrived)
         for step in plan.gather[1:-1]:
             held = double(plan, held, (step, step))
         last = [plan.swap(h, plan.gather[-1]) for h in held]
-        pairs = [(h, plan.swap(h, (0, 0))) for h in held]
+        both = lax.optimization_barrier(held)
+        pairs = [(h, plan.swap(b, (0, 0))) for h, b in zip(held, both)]
         firsts = (0, plan.units // 2)
         early = early_scores(plan, table, firsts, *pairs, log_weights, stack)
         last, early = lax.optimization_barrier((last, early))

time: 82.2 us -> 79.4 us (0.966)
  waiting for transfers between devices: 28.9 us -> 20.5 us
  starting transfers between devices: 29.8 us -> 34.2 us
  Pallas kernels: 21.1 us -> 22 us
    ppermute x31, waiting for transfers between devices: 28.9 us -> 20.5 us  [swap(): return lax.ppermute(value, ('grp', 'comp'), pairs)]
    ppermute x31, starting transfers between devices: 29.8 us -> 34.2 us  [swap(): return lax.ppermute(value, ('grp', 'comp'), pairs)]
    pallas_call x6 -> x7, Pallas kernels: 17.7 us -> 18.6 us  [call(): pl.pallas_call(functools.partial(kernel, plan), in_specs=[pl.BlockSpec(me...]
  transfers between devices with their start and end apart: 31 -> 31, of which waited for: 14 -> 14; matrix products, arithmetic and copies ran while one was open for 1% -> 2% of each run, Pallas kernels for 18% -> 19%
where the time goes in v7:
time: 79.4 us; the launch traced here: 78.9 us
  starting transfers between devices  34.2 us (43%)
  Pallas kernels  22 us (28%)
  waiting for transfers between devices  20.5 us (26%)
  between operations  0.96 us (1%)
  local copies, waits for them, and re-layouts  0.8 us (1%)
    ppermute x31, starting transfers between devices, swap(): return lax.ppermute(value, ('grp', 'comp'), pairs)  34.2 us
    ppermute x31, waiting for transfers between devices, swap(): return lax.ppermute(value, ('grp', 'comp'), pairs)  20.5 us
    pallas_call x7, Pallas kernels, call(): pl.pallas_call(functools.partial(kernel, plan), in_specs=[pl.BlockSpec(me...  18.6 us
    pallas_call x2, Pallas kernels, update(): pl.pallas_call(functools.partial(update_kernel, plan, first_slot), in_spe...  3.4 us
  transfers between devices with their start and end apart: 31, of which 14 were waited for; matrix products, arithmetic and copies ran while one was open for 2% of the time, Pallas kernels for 19%

profile of v7, /device:TPU:0, one launch (start us, length us, event | category | flops | bytes accessed | tf_op | source)
XLA Modules:
  0.0 78.9 jit_solution(6957089529517388332)
XLA Ops:
  0.6 3.5 %collective-permute-start = (f32[64,256]{1,0:T(8,128)}, f32[64,256]{1,0:T(8,128)S(1)}, u32[]{:S(2)}, u32[]{:S(2)}) collective-permute-start(f32[64,256]{1,0:T(8,128)} %refs_0_.1), channel_id=1, source_target_pairs={{0,9},{1,8},{2,11},{3,10},{4,13},{5,12},{6,15},{7,14},{8,1},{9,0},... | collective-permute-start | bytes 196616 | tf_op jit(solution)/shard_map/gather_parameters/ppermute | solution.py:74
  4.2 0.1 collective-permute-start.3
  4.3 0.7 dynamic-slice_bitcast_fusion.table.refs_0_
  4.9 2.0 %gather_parameters.4 = (f32[64,256]{1,0:T(8,128)S(1)}, f32[64,256]{1,0:T(8,128)S(1)}, f32[1024,128]{1,0:T(8,128)S(1)}) custom-call(s32[5,16]{1,0:T(8,128)S(1)} %dynamic-slice_bitcast_fusion.table.refs_0_, f32[64,256]{1,0:T(8,128)} %refs_0_.1, f32[64,256]{1,0:T(8,128)} %refs_1_.1, f32[8,128]{1,0:T(8,128)} %bitcast.5), custom_call_target="tpu_custom_call" | custom-call | bytes 270336 | tf_op jit(solution)/shard_map/gather_parameters/pallas_call | solution.py:272
  6.9 2.0 %gather_parameters.5.refs_6_.refs_4_.refs_3_.stack_ref = bf16[2048,768]{1,0:T(8,128)(2,1)S(1)} custom-call(s32[5,16]{1,0:T(8,128)S(1)} %dynamic-slice_bitcast_fusion.table.refs_0_, bf16[2048,256]{1,0:T(8,128)(2,1)} %source.1), custom_call_target="tpu_custom_call" | custom-call | flops 4194304 | bytes 2097152 | tf_op jit(solution)/shard_map/gather_parameters/pallas_call | solution.py:272
  9.0 0.0 collective-permute-done
  9.0 2.0 %collective-permute-start.1 = (f32[128,256]{1,0:T(8,128)S(1)}, f32[128,256]{1,0:T(8,128)S(1)}, u32[]{:S(2)}, u32[]{:S(2)}) collective-permute-start(f32[128,256]{1,0:T(8,128)S(1)} %pad_maximum_fusion.4), channel_id=1, source_target_pairs={{0,5},{1,2},{2,1},{3,6},{4,7},{5,0},{6,3},{7,4},{8,11},{9,12},{10,... | collective-permute-start | bytes 393224 | tf_op jit(solution)/shard_map/gather_parameters/ppermute | solution.py:74
  11.1 1.4 %collective-permute-start.4 = (f32[128,256]{1,0:T(8,128)S(1)}, f32[128,256]{1,0:T(8,128)S(1)}, u32[]{:S(2)}, u32[]{:S(2)}) collective-permute-start(f32[128,256]{1,0:T(8,128)S(1)} %pad_maximum_fusion.5), channel_id=1, source_target_pairs={{0,5},{1,2},{2,1},{3,6},{4,7},{5,0},{6,3},{7,4},{8,11},{9,12},{10,... | collective-permute-start | bytes 393224 | tf_op jit(solution)/shard_map/gather_parameters/ppermute | solution.py:74
  12.5 1.2 %collective-permute-done.1 = f32[128,256]{1,0:T(8,128)S(1)} collective-permute-done((f32[128,256]{1,0:T(8,128)S(1)}, f32[128,256]{1,0:T(8,128)S(1)}, u32[]{:S(2)}, u32[]{:S(2)}) %collective-permute-start.1) | collective-permute-done | bytes 131104 | tf_op jit(solution)/shard_map/gather_parameters/ppermute | solution.py:74
  13.7 1.8 %collective-permute-done.4 = f32[128,256]{1,0:T(8,128)S(1)} collective-permute-done((f32[128,256]{1,0:T(8,128)S(1)}, f32[128,256]{1,0:T(8,128)S(1)}, u32[]{:S(2)}, u32[]{:S(2)}) %collective-permute-start.4) | collective-permute-done | bytes 131104 | tf_op jit(solution)/shard_map/gather_parameters/ppermute | solution.py:74
  15.5 0.5 collective-permute-start.6
  16.0 0.1 collective-permute-start.7
  16.1 1.8 %collective-permute-start.2 = (f32[256,256]{1,0:T(8,128)S(1)}, f32[256,256]{1,0:T(8,128)S(1)}, u32[]{:S(2)}, u32[]{:S(2)}) collective-permute-start(f32[256,256]{1,0:T(8,128)S(1)} %constant_dynamic-update-slice_fusion.refs_1_), channel_id=1, source_target_pairs={{0,3},{1,4},{2,7},{3,0},{4,1},{5,6},{6,5},{7,2},{8,13},{9,10},{10,... | collective-permute-start | bytes 786440 | tf_op jit(solution)/shard_map/gather_parameters/ppermute | solution.py:74
  17.9 0.0 collective-permute-start.5
  17.9 0.0 collective-permute-done.6.refs_2_
  17.9 0.0 collective-permute-done.7.refs_4_
  17.9 4.1 %gather_parameters.6 = (f32[512,2048]{1,0:T(8,128)S(1)}, f32[1,2048]{1,0:T(1,128)S(1)}, f32[1,2048]{1,0:T(1,128)S(1)}) custom-call(s32[5,16]{1,0:T(8,128)S(1)} %dynamic-slice_bitcast_fusion.table.refs_0_, f32[256,256]{1,0:T(8,128)S(1)} %constant_dynamic-update-slice_fusion.refs_1_, f32[256,256]{1,0:T(8,128)S(1)} %collective-permute-done.6.refs_2_, ...), custom_call_target="tpu_custom_call" | custom-call | flops 2684354560 | bytes 9437184 | tf_op jit(solution)/shard_map/gather_parameters/pallas_call | solution.py:272
  22.1 0.0 collective-permute-done.2.refs_1_
  22.1 2.7 %collective-permute-done.5.refs_2_ = f32[256,256]{1,0:T(8,128)S(1)} collective-permute-done((f32[256,256]{1,0:T(8,128)S(1)}, f32[256,256]{1,0:T(8,128)S(1)}, u32[]{:S(2)}, u32[]{:S(2)}) %collective-permute-start.5) | collective-permute-done | bytes 262176 | tf_op jit(solution)/shard_map/gather_parameters/ppermute | solution.py:74
  24.8 0.4 collective-permute-start.8
  25.2 0.1 collective-permute-start.9
  25.3 2.4 %gather_parameters.7 = (f32[256,2048]{1,0:T(8,128)S(1)}, f32[1,2048]{1,0:T(1,128)S(1)}, f32[1,2048]{1,0:T(1,128)S(1)}) custom-call(s32[5,16]{1,0:T(8,128)S(1)} %dynamic-slice_bitcast_fusion.table.refs_0_, f32[256,256]{1,0:T(8,128)S(1)} %collective-permute-done.2.refs_1_, f32[256,256]{1,0:T(8,128)S(1)} %collective-permute-done.5.refs_2_, ...), custom_call_target="tpu_custom_call" | custom-call | flops 1342177280 | bytes 8388608 | tf_op jit(solution)/shard_map/gather_parameters/pallas_call | solution.py:272
  27.6 0.0 collective-permute-done.8.refs_0_
  27.7 5.0 %shard_map.84 = (f32[1032,128]{1,0:T(8,128)S(1)}, f32[1024,128]{1,0:T(8,128)S(1)}, f32[8,128]{1,0:T(8,128)S(1)}, f32[1,2048]{1,0:T(1,128)}, bf16[512,2048]{1,0:T(8,128)(2,1)S(1)}) custom-call(s32[5,16]{1,0:T(8,128)S(1)} %dynamic-slice_bitcast_fusion.table.refs_0_, f32[256,256]{1,0:T(8,128)S(1)} %collective-permute-done.8.refs_0_, ...), custom_call_target="tpu_custom_call" | custom-call | flops 2415919104 | bytes 21037056 | tf_op jit(solution)/shard_map/pallas_call | solution.py:272
  32.6 0.4 collective-permute-start.10
  33.0 0.1 collective-permute-start.19
  33.1 1.8 %shard_map.85 = (f32[1024,128]{1,0:T(8,128)S(1)}, f32[1024,128]{1,0:T(8,128)S(1)}) custom-call(s32[5,16]{1,0:T(8,128)S(1)} %dynamic-slice_bitcast_fusion.table.refs_0_, bf16[512,2048]{1,0:T(8,128)(2,1)S(1)} %get-tuple-element.57.own_ref, bf16[2048,768]{1,0:T(8,128)(2,1)S(1)} %gather_parameters.5.refs_6_.refs_4_.refs_3_.stack_ref), custom_call_target="tpu_custom_call" | custom-call | flops 1073741824 | bytes 10485760 | tf_op jit(solution)/shard_map/pallas_call | solution.py:272
  35.0 0.1 slice_add_fusion
  35.1 1.4 %collective-permute-start.11 = (f32[520,128]{1,0:T(8,128)S(1)}, f32[520,128]{1,0:T(8,128)S(1)}, u32[]{:S(2)}, u32[]{:S(2)}) collective-permute-start(f32[520,128]{1,0:T(8,128)S(1)} %pad_maximum_fusion), channel_id=1, source_target_pairs={{0,5},{1,17},{2,18},{3,6},{4,20},{5,0},{6,3},{7,23},{8,24},{9,12},... | collective-permute-start | bytes 798728 | tf_op jit(solution)/shard_map/scatter_moments/ppermute | solution.py:74
  36.5 0.1 add.66
  36.6 1.5 %collective-permute-start.20 = (f32[512,128]{1,0:T(8,128)S(1)}, f32[512,128]{1,0:T(8,128)S(1)}, u32[]{:S(2)}, u32[]{:S(2)}) collective-permute-start(f32[512,128]{1,0:T(8,128)S(1)} %slice.104), channel_id=1, source_target_pairs={{0,3},{1,17},{2,18},{3,0},{4,20},{5,6},{6,5},{7,23},{8,24},{9,10},... | collective-permute-start | bytes 786440 | tf_op jit(solution)/shard_map/scatter_moments/ppermute | solution.py:74
  38.1 2.9 %collective-permute-done.11 = f32[520,128]{1,0:T(8,128)S(1)} collective-permute-done((f32[520,128]{1,0:T(8,128)S(1)}, f32[520,128]{1,0:T(8,128)S(1)}, u32[]{:S(2)}, u32[]{:S(2)}) %collective-permute-start.11) | collective-permute-done | bytes 266272 | tf_op jit(solution)/shard_map/scatter_moments/ppermute | solution.py:74
  41.1 2.1 %collective-permute-start.12 = (f32[264,128]{1,0:T(8,128)S(1)}, f32[264,128]{1,0:T(8,128)S(1)}, u32[]{:S(2)}, u32[]{:S(2)}) collective-permute-start(f32[264,128]{1,0:T(8,128)S(1)} %pad_maximum_fusion.3), channel_id=1, source_target_pairs={{0,3},{1,4},{2,7},{3,0},{4,1},{5,6},{6,5},{7,2},{8,13},{9,10},{10,... | collective-permute-start | bytes 405512 | tf_op jit(solution)/shard_map/scatter_moments/ppermute | solution.py:74
  43.2 0.0 collective-permute-done.20
  43.3 1.6 %collective-permute-start.21 = (f32[256,128]{1,0:T(8,128)S(1)}, f32[256,128]{1,0:T(8,128)S(1)}, u32[]{:S(2)}, u32[]{:S(2)}) collective-permute-start(f32[256,128]{1,0:T(8,128)S(1)} %slice.106), channel_id=1, source_target_pairs={{0,16},{1,4},{2,7},{3,19},{4,1},{5,21},{6,22},{7,2},{8,13},{9,25},... | collective-permute-start | bytes 393224 | tf_op jit(solution)/shard_map/scatter_moments/ppermute | solution.py:74
  44.9 1.1 %collective-permute-done.12 = f32[264,128]{1,0:T(8,128)S(1)} collective-permute-done((f32[264,128]{1,0:T(8,128)S(1)}, f32[264,128]{1,0:T(8,128)S(1)}, u32[]{:S(2)}, u32[]{:S(2)}) %collective-permute-start.12) | collective-permute-done | bytes 135200 | tf_op jit(solution)/shard_map/scatter_moments/ppermute | solution.py:74
  46.0 1.8 %collective-permute-start.13 = (f32[136,128]{1,0:T(8,128)S(1)}, f32[136,128]{1,0:T(8,128)S(1)}, u32[]{:S(2)}, u32[]{:S(2)}) collective-permute-start(f32[136,128]{1,0:T(8,128)S(1)} %pad_maximum_fusion.8), channel_id=1, source_target_pairs={{0,16},{1,2},{2,1},{3,19},{4,7},{5,21},{6,22},{7,4},{8,11},{9,25},... | collective-permute-start | bytes 208904 | tf_op jit(solution)/shard_map/scatter_moments/ppermute | solution.py:74
  47.8 0.5 collective-permute-done.21
  48.4 0.6 collective-permute-start.22
  48.9 1.4 %collective-permute-done.13 = f32[136,128]{1,0:T(8,128)S(1)} collective-permute-done((f32[136,128]{1,0:T(8,128)S(1)}, f32[136,128]{1,0:T(8,128)S(1)}, u32[]{:S(2)}, u32[]{:S(2)}) %collective-permute-start.13) | collective-permute-done | bytes 69664 | tf_op jit(solution)/shard_map/scatter_moments/ppermute | solution.py:74
  50.4 2.4 %collective-permute-start.14 = (f32[136,128]{1,0:T(8,128)S(1)}, f32[136,128]{1,0:T(8,128)S(1)}, u32[]{:S(2)}, u32[]{:S(2)}) collective-permute-start(f32[136,128]{1,0:T(8,128)S(1)} %pad_maximum_fusion.9), channel_id=1, source_target_pairs={{0,9},{1,8},{2,11},{3,10},{4,13},{5,12},{6,15},{7,14},{8,1},{9,0},... | collective-permute-start | bytes 208904 | tf_op jit(solution)/shard_map/scatter_moments/ppermute | solution.py:74
  52.9 1.6 %collective-permute-start.23 = (f32[128,128]{1,0:T(8,128)S(1)}, f32[128,128]{1,0:T(8,128)S(1)}, u32[]{:S(2)}, u32[]{:S(2)}) collective-permute-start(f32[128,128]{1,0:T(8,128)S(1)} %slice_add_fusion.5), channel_id=1, source_target_pairs={{0,9},{1,8},{2,11},{3,10},{4,13},{5,12},{6,15},{7,14},{8,1},{9,0},... | collective-permute-start | bytes 196616 | tf_op jit(solution)/shard_map/scatter_moments/ppermute | solution.py:74
  54.5 0.9 %collective-permute-done.14 = f32[136,128]{1,0:T(8,128)S(1)} collective-permute-done((f32[136,128]{1,0:T(8,128)S(1)}, f32[136,128]{1,0:T(8,128)S(1)}, u32[]{:S(2)}, u32[]{:S(2)}) %collective-permute-start.14) | collective-permute-done | bytes 69664 | tf_op jit(solution)/shard_map/scatter_moments/ppermute | solution.py:74
  55.4 1.6 %collective-permute-start.15 = (f32[128,128]{1,0:T(8,128)S(1)}, f32[128,128]{1,0:T(8,128)S(1)}, u32[]{:S(2)}, u32[]{:S(2)}) collective-permute-start(f32[128,128]{1,0:T(8,128)S(1)} %slice_add_fusion.6), channel_id=1, source_target_pairs={{0,16},{1,2},{2,1},{3,19},{4,7},{5,21},{6,22},{7,4},{8,11},{9,25},... | collective-permute-start | bytes 196616 | tf_op jit(solution)/shard_map/gather_moments/ppermute | solution.py:74
  57.0 3.3 %collective-permute-done.23 = f32[128,128]{1,0:T(8,128)S(1)} collective-permute-done((f32[128,128]{1,0:T(8,128)S(1)}, f32[128,128]{1,0:T(8,128)S(1)}, u32[]{:S(2)}, u32[]{:S(2)}) %collective-permute-start.23) | collective-permute-done | bytes 65568 | tf_op jit(solution)/shard_map/scatter_moments/ppermute | solution.py:74
  60.3 0.6 collective-permute-start.24
  60.9 0.0 collective-permute-done.15
  60.9 1.8 %collective-permute-start.16 = (f32[256,128]{1,0:T(8,128)S(1)}, f32[256,128]{1,0:T(8,128)S(1)}, u32[]{:S(2)}, u32[]{:S(2)}) collective-permute-start(f32[256,128]{1,0:T(8,128)S(1)} %pad_maximum_fusion.6), channel_id=1, source_target_pairs={{0,3},{1,4},{2,7},{3,0},{4,1},{5,6},{6,5},{7,2},{8,13},{9,10},{10,... | collective-permute-start | bytes 393224 | tf_op jit(solution)/shard_map/gather_moments/ppermute | solution.py:74
  62.7 1.3 %collective-permute-done.24 = f32[128,128]{1,0:T(8,128)S(1)} collective-permute-done((f32[128,128]{1,0:T(8,128)S(1)}, f32[128,128]{1,0:T(8,128)S(1)}, u32[]{:S(2)}, u32[]{:S(2)}) %collective-permute-start.24) | collective-permute-done | bytes 65568 | tf_op jit(solution)/shard_map/gather_moments/ppermute | solution.py:74
  64.1 1.6 %collective-permute-start.25 = (f32[256,128]{1,0:T(8,128)S(1)}, f32[256,128]{1,0:T(8,128)S(1)}, u32[]{:S(2)}, u32[]{:S(2)}) collective-permute-start(f32[256,128]{1,0:T(8,128)S(1)} %pad_maximum_fusion.7), channel_id=1, source_target_pairs={{0,16},{1,4},{2,7},{3,19},{4,1},{5,21},{6,22},{7,2},{8,13},{9,25},... | collective-permute-start | bytes 393224 | tf_op jit(solution)/shard_map/gather_moments/ppermute | solution.py:74
  65.7 0.1 collective-permute-done.16
  65.8 2.7 %collective-permute-start.18 = (f32[512,128]{1,0:T(8,128)S(1)}, f32[512,128]{1,0:T(8,128)S(1)}, u32[]{:S(2)}, u32[]{:S(2)}) collective-permute-start(f32[512,128]{1,0:T(8,128)S(1)} %pad_maximum_fusion.1.refs_0_), channel_id=1, source_target_pairs={{0,5},{1,17},{2,18},{3,6},{4,20},{5,0},{6,3},{7,23},{8,24},{9,12},... | collective-permute-start | bytes 786440 | tf_op jit(solution)/shard_map/gather_moments/ppermute | solution.py:74
  68.4 0.7 collective-permute-done.25
  69.1 0.8 %collective-permute-start.26 = (f32[512,128]{1,0:T(8,128)S(1)}, f32[512,128]{1,0:T(8,128)S(1)}, u32[]{:S(2)}, u32[]{:S(2)}) collective-permute-start(f32[512,128]{1,0:T(8,128)S(1)} %pad_maximum_fusion.2.refs_2_), channel_id=1, source_target_pairs={{0,3},{1,17},{2,18},{3,0},{4,20},{5,6},{6,5},{7,23},{8,24},{9,10},... | collective-permute-start | bytes 786440 | tf_op jit(solution)/shard_map/gather_moments/ppermute | solution.py:74
  70.0 0.7 collective-permute-start.27
  70.6 0.8 %collective-permute-done.27 = f32[8,128]{1,0:T(8,128)S(1)} collective-permute-done((f32[8,128]{1,0:T(8,128)S(1)}, f32[8,128]{1,0:T(8,128)S(1)}, u32[]{:S(2)}, u32[]{:S(2)}) %collective-permute-start.27) | collective-permute-done | bytes 4128 | tf_op jit(solution)/shard_map/scatter_moments/ppermute | solution.py:74
  71.5 1.3 %gather_moments.1 = (f32[8,128]{1,0:T(8,128)}, f32[1024,128]{1,0:T(8,128)S(1)}) custom-call(s32[5,16]{1,0:T(8,128)S(1)} %dynamic-slice_bitcast_fusion.table.refs_0_, f32[8,128]{1,0:T(8,128)S(1)} %add_multiply_fusion.refs_1_), custom_call_target="tpu_custom_call" | custom-call | flops 1024 | bytes 8192 | tf_op jit(solution)/shard_map/gather_moments/pallas_call | solution.py:272
  72.7 0.3 collective-permute-start.17
  73.1 0.2 collective-permute-start.29
  73.2 1.7 %collective-permute-done.26.refs_3_ = f32[512,128]{1,0:T(8,128)S(1)} collective-permute-done((f32[512,128]{1,0:T(8,128)S(1)}, f32[512,128]{1,0:T(8,128)S(1)}, u32[]{:S(2)}, u32[]{:S(2)}) %collective-permute-start.26) | collective-permute-done | bytes 262176 | tf_op jit(solution)/shard_map/gather_moments/ppermute | solution.py:74
  75.0 0.0 collective-permute-start.28
  75.0 0.5 collective-permute-start.30
  75.5 1.7 %shard_map.86 = (f32[1024,256]{1,0:T(8,128)}, f32[1024,256]{1,0:T(8,128)}) custom-call(s32[5,16]{1,0:T(8,128)S(1)} %dynamic-slice_bitcast_fusion.table.refs_0_, f32[512,128]{1,0:T(8,128)S(1)} %pad_maximum_fusion.1.refs_0_, f32[512,128]{1,0:T(8,128)S(1)} %collective-permute-done.18.refs_1_, f32[512,128]{1,0:T(8,128)S(1)} %pad_maximum_fusion.2.refs_2_, ...), custom_call_target="tpu_custom_call" | custom-call | flops 1048576 | bytes 2097152 | tf_op jit(solution)/shard_map/pallas_call | solution.py:412
  77.2 1.7 %shard_map.87 = (f32[1024,256]{1,0:T(8,128)}, f32[1024,256]{1,0:T(8,128)}) custom-call(s32[5,16]{1,0:T(8,128)S(1)} %dynamic-slice_bitcast_fusion.table.refs_0_, f32[512,128]{1,0:T(8,128)S(1)} %collective-permute-done.17.refs_0_, f32[512,128]{1,0:T(8,128)S(1)} %collective-permute-done.28.refs_1_, ...), custom_call_target="tpu_custom_call", output_to_operand_aliasing={{0}: (6, {}), {1}: (7, {})} | custom-call | flops 1048576 | bytes 2097152 | tf_op jit(solution)/shard_map/pallas_call | solution.py:412
  (46 shorter events, 0.4 us)
Async XLA Ops:
  0.6 8.4 %collective-permute-start = (f32[64,256]{1,0:T(8,128)}, f32[64,256]{1,0:T(8,128)S(1)}, u32[]{:S(2)}, u32[]{:S(2)}) collective-permute-start(f32[64,256]{1,0:T(8,128)} %refs_0_.1), channel_id=1, source_target_pairs={{0,9},{1,8},{2,11},{3,10},{4,13},{5,12},{6,15},{7,14},{8,1},{9,0},... | collective-permute-start | bytes 196616 | tf_op jit(solution)/shard_map/gather_parameters/ppermute | solution.py:74
  4.2 6.9 %collective-permute-start.3 = (f32[64,256]{1,0:T(8,128)}, f32[64,256]{1,0:T(8,128)S(1)}, u32[]{:S(2)}, u32[]{:S(2)}) collective-permute-start(f32[64,256]{1,0:T(8,128)} %refs_1_.1), channel_id=1, source_target_pairs={{0,9},{1,8},{2,11},{3,10},{4,13},{5,12},{6,15},{7,14},{8,1},{9,0},... | collective-permute-start | bytes 196616 | tf_op jit(solution)/shard_map/gather_parameters/ppermute | solution.py:74
  9.0 4.6 %collective-permute-start.1 = (f32[128,256]{1,0:T(8,128)S(1)}, f32[128,256]{1,0:T(8,128)S(1)}, u32[]{:S(2)}, u32[]{:S(2)}) collective-permute-start(f32[128,256]{1,0:T(8,128)S(1)} %pad_maximum_fusion.4), channel_id=1, source_target_pairs={{0,5},{1,2},{2,1},{3,6},{4,7},{5,0},{6,3},{7,4},{8,11},{9,12},{10,... | collective-permute-start | bytes 393224 | tf_op jit(solution)/shard_map/gather_parameters/ppermute | solution.py:74
  11.1 4.5 %collective-permute-start.4 = (f32[128,256]{1,0:T(8,128)S(1)}, f32[128,256]{1,0:T(8,128)S(1)}, u32[]{:S(2)}, u32[]{:S(2)}) collective-permute-start(f32[128,256]{1,0:T(8,128)S(1)} %pad_maximum_fusion.5), channel_id=1, source_target_pairs={{0,5},{1,2},{2,1},{3,6},{4,7},{5,0},{6,3},{7,4},{8,11},{9,12},{10,... | collective-permute-start | bytes 393224 | tf_op jit(solution)/shard_map/gather_parameters/ppermute | solution.py:74
  15.5 2.4 %collective-permute-start.6 = (f32[256,256]{1,0:T(8,128)S(1)}, f32[256,256]{1,0:T(8,128)S(1)}, u32[]{:S(2)}, u32[]{:S(2)}) collective-permute-start(f32[256,256]{1,0:T(8,128)S(1)} %constant_dynamic-update-slice_fusion.refs_1_), channel_id=1, source_target_pairs={{0,1},{1,0},{2,3},{3,2},{4,5},{5,4},{6,7},{7,6},{8,9},{9,8},{10,11... | collective-permute-start | bytes 786440 | tf_op jit(solution)/shard_map/gather_parameters/ppermute | solution.py:74
  16.0 1.9 %collective-permute-start.7 = (f32[256,256]{1,0:T(8,128)S(1)}, f32[256,256]{1,0:T(8,128)S(1)}, u32[]{:S(2)}, u32[]{:S(2)}) collective-permute-start(f32[256,256]{1,0:T(8,128)S(1)} %constant_dynamic-update-slice_fusion.3.refs_3_), channel_id=1, source_target_pairs={{0,1},{1,0},{2,3},{3,2},{4,5},{5,4},{6,7},{7,6},{8,9},{9,8},{10,11... | collective-permute-start | bytes 786440 | tf_op jit(solution)/shard_map/gather_parameters/ppermute | solution.py:74
  16.1 6.0 %collective-permute-start.2 = (f32[256,256]{1,0:T(8,128)S(1)}, f32[256,256]{1,0:T(8,128)S(1)}, u32[]{:S(2)}, u32[]{:S(2)}) collective-permute-start(f32[256,256]{1,0:T(8,128)S(1)} %constant_dynamic-update-slice_fusion.refs_1_), channel_id=1, source_target_pairs={{0,3},{1,4},{2,7},{3,0},{4,1},{5,6},{6,5},{7,2},{8,13},{9,10},{10,... | collective-permute-start | bytes 786440 | tf_op jit(solution)/shard_map/gather_parameters/ppermute | solution.py:74
  17.9 6.9 %collective-permute-start.5 = (f32[256,256]{1,0:T(8,128)S(1)}, f32[256,256]{1,0:T(8,128)S(1)}, u32[]{:S(2)}, u32[]{:S(2)}) collective-permute-start(f32[256,256]{1,0:T(8,128)S(1)} %constant_dynamic-update-slice_fusion.3.refs_3_), channel_id=1, source_target_pairs={{0,3},{1,4},{2,7},{3,0},{4,1},{5,6},{6,5},{7,2},{8,13},{9,10},{10,... | collective-permute-start | bytes 786440 | tf_op jit(solution)/shard_map/gather_parameters/ppermute | solution.py:74
  24.8 2.9 %collective-permute-start.8 = (f32[256,256]{1,0:T(8,128)S(1)}, f32[256,256]{1,0:T(8,128)S(1)}, u32[]{:S(2)}, u32[]{:S(2)}) collective-permute-start(f32[256,256]{1,0:T(8,128)S(1)} %collective-permute-done.2.refs_1_), channel_id=1, source_target_pairs={{0,1},{1,0},{2,3},{3,2},{4,5},{5,4},{6,7},{7,6},{8,9},{9,8},{10,11... | collective-permute-start | bytes 786440 | tf_op jit(solution)/shard_map/gather_parameters/ppermute | solution.py:74
  25.2 2.5 %collective-permute-start.9 = (f32[256,256]{1,0:T(8,128)S(1)}, f32[256,256]{1,0:T(8,128)S(1)}, u32[]{:S(2)}, u32[]{:S(2)}) collective-permute-start(f32[256,256]{1,0:T(8,128)S(1)} %collective-permute-done.5.refs_2_), channel_id=1, source_target_pairs={{0,1},{1,0},{2,3},{3,2},{4,5},{5,4},{6,7},{7,6},{8,9},{9,8},{10,11... | collective-permute-start | bytes 786440 | tf_op jit(solution)/shard_map/gather_parameters/ppermute | solution.py:74
  32.6 2.4 %collective-permute-start.10 = (f32[1032,128]{1,0:T(8,128)S(1)}, f32[1032,128]{1,0:T(8,128)S(1)}, u32[]{:S(2)}, u32[]{:S(2)}) collective-permute-start(f32[1032,128]{1,0:T(8,128)S(1)} %get-tuple-element.59), channel_id=1, source_target_pairs={{0,1},{1,0},{2,3},{3,2},{4,5},{5,4},{6,7},{7,6},{8,9},{9,8},{10,11... | collective-permute-start | bytes 1585160 | tf_op jit(solution)/shard_map/scatter_moments/ppermute | solution.py:74
  33.0 3.4 %collective-permute-start.19 = (f32[1024,128]{1,0:T(8,128)S(1)}, f32[1024,128]{1,0:T(8,128)S(1)}, u32[]{:S(2)}, u32[]{:S(2)}) collective-permute-start(f32[1024,128]{1,0:T(8,128)S(1)} %get-tuple-element.62), channel_id=1, source_target_pairs={{0,1},{1,0},{2,3},{3,2},{4,5},{5,4},{6,7},{7,6},{8,9},{9,8},{10,11... | collective-permute-start | bytes 1572872 | tf_op jit(solution)/shard_map/scatter_moments/ppermute | solution.py:74
  35.1 5.9 %collective-permute-start.11 = (f32[520,128]{1,0:T(8,128)S(1)}, f32[520,128]{1,0:T(8,128)S(1)}, u32[]{:S(2)}, u32[]{:S(2)}) collective-permute-start(f32[520,128]{1,0:T(8,128)S(1)} %pad_maximum_fusion), channel_id=1, source_target_pairs={{0,5},{1,17},{2,18},{3,6},{4,20},{5,0},{6,3},{7,23},{8,24},{9,12},... | collective-permute-start | bytes 798728 | tf_op jit(solution)/shard_map/scatter_moments/ppermute | solution.py:74
  36.6 6.7 %collective-permute-start.20 = (f32[512,128]{1,0:T(8,128)S(1)}, f32[512,128]{1,0:T(8,128)S(1)}, u32[]{:S(2)}, u32[]{:S(2)}) collective-permute-start(f32[512,128]{1,0:T(8,128)S(1)} %slice.104), channel_id=1, source_target_pairs={{0,3},{1,17},{2,18},{3,0},{4,20},{5,6},{6,5},{7,23},{8,24},{9,10},... | collective-permute-start | bytes 786440 | tf_op jit(solution)/shard_map/scatter_moments/ppermute | solution.py:74
  41.1 4.8 %collective-permute-start.12 = (f32[264,128]{1,0:T(8,128)S(1)}, f32[264,128]{1,0:T(8,128)S(1)}, u32[]{:S(2)}, u32[]{:S(2)}) collective-permute-start(f32[264,128]{1,0:T(8,128)S(1)} %pad_maximum_fusion.3), channel_id=1, source_target_pairs={{0,3},{1,4},{2,7},{3,0},{4,1},{5,6},{6,5},{7,2},{8,13},{9,10},{10,... | collective-permute-start | bytes 405512 | tf_op jit(solution)/shard_map/scatter_moments/ppermute | solution.py:74
  43.3 5.0 %collective-permute-start.21 = (f32[256,128]{1,0:T(8,128)S(1)}, f32[256,128]{1,0:T(8,128)S(1)}, u32[]{:S(2)}, u32[]{:S(2)}) collective-permute-start(f32[256,128]{1,0:T(8,128)S(1)} %slice.106), channel_id=1, source_target_pairs={{0,16},{1,4},{2,7},{3,19},{4,1},{5,21},{6,22},{7,2},{8,13},{9,25},... | collective-permute-start | bytes 393224 | tf_op jit(solution)/shard_map/scatter_moments/ppermute | solution.py:74
  46.0 4.4 %collective-permute-start.13 = (f32[136,128]{1,0:T(8,128)S(1)}, f32[136,128]{1,0:T(8,128)S(1)}, u32[]{:S(2)}, u32[]{:S(2)}) collective-permute-start(f32[136,128]{1,0:T(8,128)S(1)} %pad_maximum_fusion.8), channel_id=1, source_target_pairs={{0,16},{1,2},{2,1},{3,19},{4,7},{5,21},{6,22},{7,4},{8,11},{9,25},... | collective-permute-start | bytes 208904 | tf_op jit(solution)/shard_map/scatter_moments/ppermute | solution.py:74
  48.4 4.5 %collective-permute-start.22 = (f32[128,128]{1,0:T(8,128)S(1)}, f32[128,128]{1,0:T(8,128)S(1)}, u32[]{:S(2)}, u32[]{:S(2)}) collective-permute-start(f32[128,128]{1,0:T(8,128)S(1)} %slice.108), channel_id=1, source_target_pairs={{0,5},{1,2},{2,1},{3,6},{4,7},{5,0},{6,3},{7,4},{8,11},{9,12},{10,... | collective-permute-start | bytes 196616 | tf_op jit(solution)/shard_map/scatter_moments/ppermute | solution.py:74
  50.4 5.0 %collective-permute-start.14 = (f32[136,128]{1,0:T(8,128)S(1)}, f32[136,128]{1,0:T(8,128)S(1)}, u32[]{:S(2)}, u32[]{:S(2)}) collective-permute-start(f32[136,128]{1,0:T(8,128)S(1)} %pad_maximum_fusion.9), channel_id=1, source_target_pairs={{0,9},{1,8},{2,11},{3,10},{4,13},{5,12},{6,15},{7,14},{8,1},{9,0},... | collective-permute-start | bytes 208904 | tf_op jit(solution)/shard_map/scatter_moments/ppermute | solution.py:74
  52.9 7.4 %collective-permute-start.23 = (f32[128,128]{1,0:T(8,128)S(1)}, f32[128,128]{1,0:T(8,128)S(1)}, u32[]{:S(2)}, u32[]{:S(2)}) collective-permute-start(f32[128,128]{1,0:T(8,128)S(1)} %slice_add_fusion.5), channel_id=1, source_target_pairs={{0,9},{1,8},{2,11},{3,10},{4,13},{5,12},{6,15},{7,14},{8,1},{9,0},... | collective-permute-start | bytes 196616 | tf_op jit(solution)/shard_map/scatter_moments/ppermute | solution.py:74
  55.4 5.5 %collective-permute-start.15 = (f32[128,128]{1,0:T(8,128)S(1)}, f32[128,128]{1,0:T(8,128)S(1)}, u32[]{:S(2)}, u32[]{:S(2)}) collective-permute-start(f32[128,128]{1,0:T(8,128)S(1)} %slice_add_fusion.6), channel_id=1, source_target_pairs={{0,16},{1,2},{2,1},{3,19},{4,7},{5,21},{6,22},{7,4},{8,11},{9,25},... | collective-permute-start | bytes 196616 | tf_op jit(solution)/shard_map/gather_moments/ppermute | solution.py:74
  60.3 3.8 %collective-permute-start.24 = (f32[128,128]{1,0:T(8,128)S(1)}, f32[128,128]{1,0:T(8,128)S(1)}, u32[]{:S(2)}, u32[]{:S(2)}) collective-permute-start(f32[128,128]{1,0:T(8,128)S(1)} %add.70), channel_id=1, source_target_pairs={{0,5},{1,2},{2,1},{3,6},{4,7},{5,0},{6,3},{7,4},{8,11},{9,12},{10,... | collective-permute-start | bytes 196616 | tf_op jit(solution)/shard_map/gather_moments/ppermute | solution.py:74
  60.9 4.8 %collective-permute-start.16 = (f32[256,128]{1,0:T(8,128)S(1)}, f32[256,128]{1,0:T(8,128)S(1)}, u32[]{:S(2)}, u32[]{:S(2)}) collective-permute-start(f32[256,128]{1,0:T(8,128)S(1)} %pad_maximum_fusion.6), channel_id=1, source_target_pairs={{0,3},{1,4},{2,7},{3,0},{4,1},{5,6},{6,5},{7,2},{8,13},{9,10},{10,... | collective-permute-start | bytes 393224 | tf_op jit(solution)/shard_map/gather_moments/ppermute | solution.py:74
  64.1 5.0 %collective-permute-start.25 = (f32[256,128]{1,0:T(8,128)S(1)}, f32[256,128]{1,0:T(8,128)S(1)}, u32[]{:S(2)}, u32[]{:S(2)}) collective-permute-start(f32[256,128]{1,0:T(8,128)S(1)} %pad_maximum_fusion.7), channel_id=1, source_target_pairs={{0,16},{1,4},{2,7},{3,19},{4,1},{5,21},{6,22},{7,2},{8,13},{9,25},... | collective-permute-start | bytes 393224 | tf_op jit(solution)/shard_map/gather_moments/ppermute | solution.py:74
  65.8 7.5 %collective-permute-start.18 = (f32[512,128]{1,0:T(8,128)S(1)}, f32[512,128]{1,0:T(8,128)S(1)}, u32[]{:S(2)}, u32[]{:S(2)}) collective-permute-start(f32[512,128]{1,0:T(8,128)S(1)} %pad_maximum_fusion.1.refs_0_), channel_id=1, source_target_pairs={{0,5},{1,17},{2,18},{3,6},{4,20},{5,0},{6,3},{7,23},{8,24},{9,12},... | collective-permute-start | bytes 786440 | tf_op jit(solution)/shard_map/gather_moments/ppermute | solution.py:74
  69.1 5.9 %collective-permute-start.26 = (f32[512,128]{1,0:T(8,128)S(1)}, f32[512,128]{1,0:T(8,128)S(1)}, u32[]{:S(2)}, u32[]{:S(2)}) collective-permute-start(f32[512,128]{1,0:T(8,128)S(1)} %pad_maximum_fusion.2.refs_2_), channel_id=1, source_target_pairs={{0,3},{1,17},{2,18},{3,0},{4,20},{5,6},{6,5},{7,23},{8,24},{9,10},... | collective-permute-start | bytes 786440 | tf_op jit(solution)/shard_map/gather_moments/ppermute | solution.py:74
  70.0 1.5 %collective-permute-start.27 = (f32[8,128]{1,0:T(8,128)S(1)}, f32[8,128]{1,0:T(8,128)S(1)}, u32[]{:S(2)}, u32[]{:S(2)}) collective-permute-start(f32[8,128]{1,0:T(8,128)S(1)} %slice_add_fusion.8), channel_id=1, source_target_pairs={{0,1},{1,0},{2,3},{3,2},{4,5},{5,4},{6,7},{7,6},{8,9},{9,8},{10,11... | collective-permute-start | bytes 12296 | tf_op jit(solution)/shard_map/scatter_moments/ppermute | solution.py:74
  72.7 4.5 %collective-permute-start.17 = (f32[512,128]{1,0:T(8,128)S(1)}, f32[512,128]{1,0:T(8,128)S(1)}, u32[]{:S(2)}, u32[]{:S(2)}) collective-permute-start(f32[512,128]{1,0:T(8,128)S(1)} %pad_maximum_fusion.1.refs_0_), channel_id=1, source_target_pairs={{0,1},{1,0},{2,3},{3,2},{4,5},{5,4},{6,7},{7,6},{8,9},{9,8},{10,11... | collective-permute-start | bytes 786440 | tf_op jit(solution)/shard_map/gather_moments/ppermute | solution.py:74
  73.1 4.1 %collective-permute-start.29 = (f32[512,128]{1,0:T(8,128)S(1)}, f32[512,128]{1,0:T(8,128)S(1)}, u32[]{:S(2)}, u32[]{:S(2)}) collective-permute-start(f32[512,128]{1,0:T(8,128)S(1)} %pad_maximum_fusion.2.refs_2_), channel_id=1, source_target_pairs={{0,1},{1,0},{2,3},{3,2},{4,5},{5,4},{6,7},{7,6},{8,9},{9,8},{10,11... | collective-permute-start | bytes 786440 | tf_op jit(solution)/shard_map/gather_moments/ppermute | solution.py:74
  75.0 2.2 %collective-permute-start.28 = (f32[512,128]{1,0:T(8,128)S(1)}, f32[512,128]{1,0:T(8,128)S(1)}, u32[]{:S(2)}, u32[]{:S(2)}) collective-permute-start(f32[512,128]{1,0:T(8,128)S(1)} %collective-permute-done.18.refs_1_), channel_id=1, source_target_pairs={{0,1},{1,0},{2,3},{3,2},{4,5},{5,4},{6,7},{7,6},{8,9},{9,8},{10,11... | collective-permute-start | bytes 786440 | tf_op jit(solution)/shard_map/gather_moments/ppermute | solution.py:74
  75.0 2.2 %collective-permute-start.30 = (f32[512,128]{1,0:T(8,128)S(1)}, f32[512,128]{1,0:T(8,128)S(1)}, u32[]{:S(2)}, u32[]{:S(2)}) collective-permute-start(f32[512,128]{1,0:T(8,128)S(1)} %collective-permute-done.26.refs_3_), channel_id=1, source_target_pairs={{0,1},{1,0},{2,3},{3,2},{4,5},{5,4},{6,7},{7,6},{8,9},{9,8},{10,11... | collective-permute-start | bytes 786440 | tf_op jit(solution)/shard_map/gather_moments/ppermute | solution.py:74

commit v8 on v7

--- a/solution.py
+++ b/solution.py
@@ -253,17 +253,19 @@
     store_moments(plan, table, plan.units // 2, moments, sent_refs[::-1])
 
 
-def own_kernel(plan, table, own_ref, stack_ref, first_ref, second_ref, moments):
-    count, width = stack_ref.shape[0], stack_ref.shape[1] // 3
-    block = min(BLOCK, count)
-    for first in range(0, count, block):
-        here = slice(first, first + block)
-        added = jnp.dot(own_ref[:, here], stack_ref[here, width:], preferred_element_type=F32)
-        if first == 0:
-            moments[...] = added
-        else:
-            moments[...] += added
-    store_moments(plan, table, 0, moments, (second_ref, first_ref))
+def own_kernel(plan, stream, table, own_ref, stack_ref, moments_ref):
+    width = stack_ref.shape[1] // 3
+    unit = plan.unit
+    parts = width // LANES
+    inputs = stack_ref[:, (2 - stream) * width : (3 - stream) * width]
+    moments = jnp.dot(own_ref[...], inputs, preferred_element_type=F32)
+    for u in range(plan.units // 2):
+        slot = table[1 + stream, u] % (plan.units // 2)
+        first = pl.multiple_of(slot * (unit * parts), unit)
+        for part in range(parts):
+            moments_ref[pl.ds(first + part * unit, unit), :] = moments[
+                u * unit : (u + 1) * unit, part * LANES : (part + 1) * LANES
+            ]
 
 
 def call(kernel, plan, table, operands, shapes, scratch, flops, vmem_mib, space=pltpu.VMEM):
@@ -354,16 +356,19 @@
         9 * half * count * width,
         32,
     )
-    kept = call(
-        own_kernel,
-        plan,
-        table,
-        [own, stack],
-        [((rows, LANES), F32)] * 2,
-        [((half, 2 * width), F32)],
-        4 * half * count * width,
-        16,
-    )
+    kept = [
+        call(
+            lambda plan, *refs, stream=stream: own_kernel(plan, stream, *refs),
+            plan,
+            table,
+            [own, stack],
+            [((rows, LANES), F32)],
+            [],
+            2 * half * count * width,
+            16,
+        )[0]
+        for stream in (0, 1)
+    ]
     return sent, kept, counts, row_scores
 
 

time: 79.4 us -> 78.9 us (level)
  waiting for transfers between devices: 20.5 us -> 19 us
  Pallas kernels: 22 us -> 22.8 us
    ppermute x31, waiting for transfers between devices: 20.5 us -> 19 us  [swap(): return lax.ppermute(value, ('grp', 'comp'), pairs)]
    pallas_call x7 -> x8, Pallas kernels: 18.6 us -> 19.4 us  [call(): pl.pallas_call(functools.partial(kernel, plan), in_specs=[pl.BlockSpec(me...]
  transfers between devices with their start and end apart: 31 -> 31, of which waited for: 14 -> 15; matrix products, arithmetic and copies ran while one was open for 2% -> 2% of each run, Pallas kernels for 19% -> 20%
where the time goes in v8:
time: 78.9 us; the launch traced here: 78.7 us
  starting transfers between devices  34.8 us (44%)
  Pallas kernels  22.8 us (29%)
  waiting for transfers between devices  19 us (24%)
  between operations  0.97 us (1%)
  local copies, waits for them, and re-layouts  0.8 us (1%)
    ppermute x31, starting transfers between devices, swap(): return lax.ppermute(value, ('grp', 'comp'), pairs)  34.8 us
    pallas_call x8, Pallas kernels, call(): pl.pallas_call(functools.partial(kernel, plan), in_specs=[pl.BlockSpec(me...  19.4 us
    ppermute x31, waiting for transfers between devices, swap(): return lax.ppermute(value, ('grp', 'comp'), pairs)  19 us
    pallas_call x2, Pallas kernels, update(): pl.pallas_call(functools.partial(update_kernel, plan, first_slot), in_spe...  3.4 us
  transfers between devices with their start and end apart: 31, of which 15 were waited for; matrix products, arithmetic and copies ran while one was open for 2% of the time, Pallas kernels for 20%

profile of v8, /device:TPU:0, one launch (start us, length us, event | category | flops | bytes accessed | tf_op | source)
XLA Modules:
  0.0 78.7 jit_solution(3758770996117483100)
XLA Ops:
  0.6 3.5 %collective-permute-start = (f32[64,256]{1,0:T(8,128)}, f32[64,256]{1,0:T(8,128)S(1)}, u32[]{:S(2)}, u32[]{:S(2)}) collective-permute-start(f32[64,256]{1,0:T(8,128)} %refs_0_.1), channel_id=1, source_target_pairs={{0,9},{1,8},{2,11},{3,10},{4,13},{5,12},{6,15},{7,14},{8,1},{9,0},... | collective-permute-start | bytes 196616 | tf_op jit(solution)/shard_map/gather_parameters/ppermute | solution.py:74
  4.2 0.1 collective-permute-start.3
  4.3 0.7 dynamic-slice_bitcast_fusion.table.refs_0_
  4.9 2.0 %gather_parameters.4 = (f32[64,256]{1,0:T(8,128)S(1)}, f32[64,256]{1,0:T(8,128)S(1)}, f32[1024,128]{1,0:T(8,128)S(1)}) custom-call(s32[5,16]{1,0:T(8,128)S(1)} %dynamic-slice_bitcast_fusion.table.refs_0_, f32[64,256]{1,0:T(8,128)} %refs_0_.1, f32[64,256]{1,0:T(8,128)} %refs_1_.1, f32[8,128]{1,0:T(8,128)} %bitcast.5), custom_call_target="tpu_custom_call" | custom-call | bytes 270336 | tf_op jit(solution)/shard_map/gather_parameters/pallas_call | solution.py:274
  6.9 2.0 %gather_parameters.5.refs_6_.refs_4_.refs_3_.refs_2_ = bf16[2048,768]{1,0:T(8,128)(2,1)S(1)} custom-call(s32[5,16]{1,0:T(8,128)S(1)} %dynamic-slice_bitcast_fusion.table.refs_0_, bf16[2048,256]{1,0:T(8,128)(2,1)} %source.1), custom_call_target="tpu_custom_call" | custom-call | flops 4194304 | bytes 2097152 | tf_op jit(solution)/shard_map/gather_parameters/pallas_call | solution.py:274
  9.0 0.0 collective-permute-done
  9.0 2.0 %collective-permute-start.1 = (f32[128,256]{1,0:T(8,128)S(1)}, f32[128,256]{1,0:T(8,128)S(1)}, u32[]{:S(2)}, u32[]{:S(2)}) collective-permute-start(f32[128,256]{1,0:T(8,128)S(1)} %pad_maximum_fusion.4), channel_id=1, source_target_pairs={{0,5},{1,2},{2,1},{3,6},{4,7},{5,0},{6,3},{7,4},{8,11},{9,12},{10,... | collective-permute-start | bytes 393224 | tf_op jit(solution)/shard_map/gather_parameters/ppermute | solution.py:74
  11.1 1.4 %collective-permute-start.4 = (f32[128,256]{1,0:T(8,128)S(1)}, f32[128,256]{1,0:T(8,128)S(1)}, u32[]{:S(2)}, u32[]{:S(2)}) collective-permute-start(f32[128,256]{1,0:T(8,128)S(1)} %pad_maximum_fusion.5), channel_id=1, source_target_pairs={{0,5},{1,2},{2,1},{3,6},{4,7},{5,0},{6,3},{7,4},{8,11},{9,12},{10,... | collective-permute-start | bytes 393224 | tf_op jit(solution)/shard_map/gather_parameters/ppermute | solution.py:74
  12.5 1.2 %collective-permute-done.1 = f32[128,256]{1,0:T(8,128)S(1)} collective-permute-done((f32[128,256]{1,0:T(8,128)S(1)}, f32[128,256]{1,0:T(8,128)S(1)}, u32[]{:S(2)}, u32[]{:S(2)}) %collective-permute-start.1) | collective-permute-done | bytes 131104 | tf_op jit(solution)/shard_map/gather_parameters/ppermute | solution.py:74
  13.7 1.8 %collective-permute-done.4 = f32[128,256]{1,0:T(8,128)S(1)} collective-permute-done((f32[128,256]{1,0:T(8,128)S(1)}, f32[128,256]{1,0:T(8,128)S(1)}, u32[]{:S(2)}, u32[]{:S(2)}) %collective-permute-start.4) | collective-permute-done | bytes 131104 | tf_op jit(solution)/shard_map/gather_parameters/ppermute | solution.py:74
  15.5 0.5 collective-permute-start.6
  16.0 0.1 collective-permute-start.7
  16.1 1.8 %collective-permute-start.2 = (f32[256,256]{1,0:T(8,128)S(1)}, f32[256,256]{1,0:T(8,128)S(1)}, u32[]{:S(2)}, u32[]{:S(2)}) collective-permute-start(f32[256,256]{1,0:T(8,128)S(1)} %constant_dynamic-update-slice_fusion.refs_1_), channel_id=1, source_target_pairs={{0,3},{1,4},{2,7},{3,0},{4,1},{5,6},{6,5},{7,2},{8,13},{9,10},{10,... | collective-permute-start | bytes 786440 | tf_op jit(solution)/shard_map/gather_parameters/ppermute | solution.py:74
  17.9 0.0 collective-permute-start.5
  17.9 4.1 %gather_parameters.6 = (f32[512,2048]{1,0:T(8,128)S(1)}, f32[1,2048]{1,0:T(1,128)S(1)}, f32[1,2048]{1,0:T(1,128)S(1)}) custom-call(s32[5,16]{1,0:T(8,128)S(1)} %dynamic-slice_bitcast_fusion.table.refs_0_, f32[256,256]{1,0:T(8,128)S(1)} %constant_dynamic-update-slice_fusion.refs_1_, f32[256,256]{1,0:T(8,128)S(1)} %collective-permute-done.6.refs_2_, ...), custom_call_target="tpu_custom_call" | custom-call | flops 2684354560 | bytes 9437184 | tf_op jit(solution)/shard_map/gather_parameters/pallas_call | solution.py:274
  22.1 0.0 collective-permute-done.2.refs_1_
  22.1 2.7 %collective-permute-done.5.refs_2_ = f32[256,256]{1,0:T(8,128)S(1)} collective-permute-done((f32[256,256]{1,0:T(8,128)S(1)}, f32[256,256]{1,0:T(8,128)S(1)}, u32[]{:S(2)}, u32[]{:S(2)}) %collective-permute-start.5) | collective-permute-done | bytes 262176 | tf_op jit(solution)/shard_map/gather_parameters/ppermute | solution.py:74
  24.8 0.4 collective-permute-start.8
  25.2 0.1 collective-permute-start.9
  25.3 2.4 %gather_parameters.7 = (f32[256,2048]{1,0:T(8,128)S(1)}, f32[1,2048]{1,0:T(1,128)S(1)}, f32[1,2048]{1,0:T(1,128)S(1)}) custom-call(s32[5,16]{1,0:T(8,128)S(1)} %dynamic-slice_bitcast_fusion.table.refs_0_, f32[256,256]{1,0:T(8,128)S(1)} %collective-permute-done.2.refs_1_, f32[256,256]{1,0:T(8,128)S(1)} %collective-permute-done.5.refs_2_, ...), custom_call_target="tpu_custom_call" | custom-call | flops 1342177280 | bytes 8388608 | tf_op jit(solution)/shard_map/gather_parameters/pallas_call | solution.py:274
  27.6 0.0 collective-permute-done.9.refs_1_
  27.7 5.0 %shard_map.84 = (f32[1032,128]{1,0:T(8,128)S(1)}, f32[1024,128]{1,0:T(8,128)S(1)}, f32[8,128]{1,0:T(8,128)S(1)}, f32[1,2048]{1,0:T(1,128)}, bf16[512,2048]{1,0:T(8,128)(2,1)S(1)}) custom-call(s32[5,16]{1,0:T(8,128)S(1)} %dynamic-slice_bitcast_fusion.table.refs_0_, f32[256,256]{1,0:T(8,128)S(1)} %collective-permute-done.8.refs_0_, ...), custom_call_target="tpu_custom_call" | custom-call | flops 2415919104 | bytes 21037056 | tf_op jit(solution)/shard_map/pallas_call | solution.py:274
  32.6 0.4 collective-permute-start.10
  33.0 0.1 collective-permute-start.19
  33.1 1.3 %shard_map.85 = f32[1024,128]{1,0:T(8,128)S(1)} custom-call(s32[5,16]{1,0:T(8,128)S(1)} %dynamic-slice_bitcast_fusion.table.refs_0_, bf16[512,2048]{1,0:T(8,128)(2,1)S(1)} %get-tuple-element.55.refs_1_, bf16[2048,768]{1,0:T(8,128)(2,1)S(1)} %gather_parameters.5.refs_6_.refs_4_.refs_3_.refs_2_), custom_call_target="tpu_custom_call" | custom-call | flops 536870912 | bytes 10485760 | tf_op jit(solution)/shard_map/pallas_call | solution.py:274
  34.5 0.1 collective-permute-done.10
  34.6 0.1 slice_add_fusion
  34.7 1.3 %collective-permute-start.11 = (f32[520,128]{1,0:T(8,128)S(1)}, f32[520,128]{1,0:T(8,128)S(1)}, u32[]{:S(2)}, u32[]{:S(2)}) collective-permute-start(f32[520,128]{1,0:T(8,128)S(1)} %pad_maximum_fusion), channel_id=1, source_target_pairs={{0,5},{1,17},{2,18},{3,6},{4,20},{5,0},{6,3},{7,23},{8,24},{9,12},... | collective-permute-start | bytes 798728 | tf_op jit(solution)/shard_map/scatter_moments/ppermute | solution.py:74
  36.0 1.3 %shard_map.86 = f32[1024,128]{1,0:T(8,128)S(1)} custom-call(s32[5,16]{1,0:T(8,128)S(1)} %dynamic-slice_bitcast_fusion.table.refs_0_, bf16[512,2048]{1,0:T(8,128)(2,1)S(1)} %get-tuple-element.55.refs_1_, bf16[2048,768]{1,0:T(8,128)(2,1)S(1)} %gather_parameters.5.refs_6_.refs_4_.refs_3_.refs_2_), custom_call_target="tpu_custom_call" | custom-call | flops 536870912 | bytes 10485760 | tf_op jit(solution)/shard_map/pallas_call | solution.py:274
  37.4 0.0 collective-permute-done.19
  37.4 0.1 add.66
  37.5 1.5 %collective-permute-start.20 = (f32[512,128]{1,0:T(8,128)S(1)}, f32[512,128]{1,0:T(8,128)S(1)}, u32[]{:S(2)}, u32[]{:S(2)}) collective-permute-start(f32[512,128]{1,0:T(8,128)S(1)} %slice.104), channel_id=1, source_target_pairs={{0,3},{1,17},{2,18},{3,0},{4,20},{5,6},{6,5},{7,23},{8,24},{9,10},... | collective-permute-start | bytes 786440 | tf_op jit(solution)/shard_map/scatter_moments/ppermute | solution.py:74
  39.0 1.6 %collective-permute-done.11 = f32[520,128]{1,0:T(8,128)S(1)} collective-permute-done((f32[520,128]{1,0:T(8,128)S(1)}, f32[520,128]{1,0:T(8,128)S(1)}, u32[]{:S(2)}, u32[]{:S(2)}) %collective-permute-start.11) | collective-permute-done | bytes 266272 | tf_op jit(solution)/shard_map/scatter_moments/ppermute | solution.py:74
  40.7 2.1 %collective-permute-start.12 = (f32[264,128]{1,0:T(8,128)S(1)}, f32[264,128]{1,0:T(8,128)S(1)}, u32[]{:S(2)}, u32[]{:S(2)}) collective-permute-start(f32[264,128]{1,0:T(8,128)S(1)} %pad_maximum_fusion.3), channel_id=1, source_target_pairs={{0,3},{1,4},{2,7},{3,0},{4,1},{5,6},{6,5},{7,2},{8,13},{9,10},{10,... | collective-permute-start | bytes 405512 | tf_op jit(solution)/shard_map/scatter_moments/ppermute | solution.py:74
  42.8 0.5 collective-permute-done.20
  43.4 1.6 %collective-permute-start.21 = (f32[256,128]{1,0:T(8,128)S(1)}, f32[256,128]{1,0:T(8,128)S(1)}, u32[]{:S(2)}, u32[]{:S(2)}) collective-permute-start(f32[256,128]{1,0:T(8,128)S(1)} %slice.106), channel_id=1, source_target_pairs={{0,16},{1,4},{2,7},{3,19},{4,1},{5,21},{6,22},{7,2},{8,13},{9,25},... | collective-permute-start | bytes 393224 | tf_op jit(solution)/shard_map/scatter_moments/ppermute | solution.py:74
  45.0 0.5 collective-permute-done.12
  45.6 1.8 %collective-permute-start.13 = (f32[136,128]{1,0:T(8,128)S(1)}, f32[136,128]{1,0:T(8,128)S(1)}, u32[]{:S(2)}, u32[]{:S(2)}) collective-permute-start(f32[136,128]{1,0:T(8,128)S(1)} %pad_maximum_fusion.8), channel_id=1, source_target_pairs={{0,16},{1,2},{2,1},{3,19},{4,7},{5,21},{6,22},{7,4},{8,11},{9,25},... | collective-permute-start | bytes 208904 | tf_op jit(solution)/shard_map/scatter_moments/ppermute | solution.py:74
  47.3 1.1 %collective-permute-done.21 = f32[256,128]{1,0:T(8,128)S(1)} collective-permute-done((f32[256,128]{1,0:T(8,128)S(1)}, f32[256,128]{1,0:T(8,128)S(1)}, u32[]{:S(2)}, u32[]{:S(2)}) %collective-permute-start.21) | collective-permute-done | bytes 131104 | tf_op jit(solution)/shard_map/scatter_moments/ppermute | solution.py:74
  48.4 0.3 collective-permute-start.22
  48.7 1.2 %collective-permute-done.13 = f32[136,128]{1,0:T(8,128)S(1)} collective-permute-done((f32[136,128]{1,0:T(8,128)S(1)}, f32[136,128]{1,0:T(8,128)S(1)}, u32[]{:S(2)}, u32[]{:S(2)}) %collective-permute-start.13) | collective-permute-done | bytes 69664 | tf_op jit(solution)/shard_map/scatter_moments/ppermute | solution.py:74
  50.0 2.4 %collective-permute-start.14 = (f32[136,128]{1,0:T(8,128)S(1)}, f32[136,128]{1,0:T(8,128)S(1)}, u32[]{:S(2)}, u32[]{:S(2)}) collective-permute-start(f32[136,128]{1,0:T(8,128)S(1)} %pad_maximum_fusion.9), channel_id=1, source_target_pairs={{0,9},{1,8},{2,11},{3,10},{4,13},{5,12},{6,15},{7,14},{8,1},{9,0},... | collective-permute-start | bytes 208904 | tf_op jit(solution)/shard_map/scatter_moments/ppermute | solution.py:74
  52.4 0.0 collective-permute-done.22
  52.4 2.9 %collective-permute-start.23 = (f32[128,128]{1,0:T(8,128)S(1)}, f32[128,128]{1,0:T(8,128)S(1)}, u32[]{:S(2)}, u32[]{:S(2)}) collective-permute-start(f32[128,128]{1,0:T(8,128)S(1)} %slice_add_fusion.5), channel_id=1, source_target_pairs={{0,9},{1,8},{2,11},{3,10},{4,13},{5,12},{6,15},{7,14},{8,1},{9,0},... | collective-permute-start | bytes 196616 | tf_op jit(solution)/shard_map/scatter_moments/ppermute | solution.py:74
  55.3 1.6 %collective-permute-start.15 = (f32[128,128]{1,0:T(8,128)S(1)}, f32[128,128]{1,0:T(8,128)S(1)}, u32[]{:S(2)}, u32[]{:S(2)}) collective-permute-start(f32[128,128]{1,0:T(8,128)S(1)} %slice_add_fusion.6), channel_id=1, source_target_pairs={{0,16},{1,2},{2,1},{3,19},{4,7},{5,21},{6,22},{7,4},{8,11},{9,25},... | collective-permute-start | bytes 196616 | tf_op jit(solution)/shard_map/gather_moments/ppermute | solution.py:74
  56.9 3.1 %collective-permute-done.23 = f32[128,128]{1,0:T(8,128)S(1)} collective-permute-done((f32[128,128]{1,0:T(8,128)S(1)}, f32[128,128]{1,0:T(8,128)S(1)}, u32[]{:S(2)}, u32[]{:S(2)}) %collective-permute-start.23) | collective-permute-done | bytes 65568 | tf_op jit(solution)/shard_map/scatter_moments/ppermute | solution.py:74
  60.0 0.5 collective-permute-start.24
  60.5 1.6 %collective-permute-start.16 = (f32[256,128]{1,0:T(8,128)S(1)}, f32[256,128]{1,0:T(8,128)S(1)}, u32[]{:S(2)}, u32[]{:S(2)}) collective-permute-start(f32[256,128]{1,0:T(8,128)S(1)} %pad_maximum_fusion.6), channel_id=1, source_target_pairs={{0,3},{1,4},{2,7},{3,0},{4,1},{5,6},{6,5},{7,2},{8,13},{9,10},{10,... | collective-permute-start | bytes 393224 | tf_op jit(solution)/shard_map/gather_moments/ppermute | solution.py:74
  62.1 1.7 %collective-permute-done.24 = f32[128,128]{1,0:T(8,128)S(1)} collective-permute-done((f32[128,128]{1,0:T(8,128)S(1)}, f32[128,128]{1,0:T(8,128)S(1)}, u32[]{:S(2)}, u32[]{:S(2)}) %collective-permute-start.24) | collective-permute-done | bytes 65568 | tf_op jit(solution)/shard_map/gather_moments/ppermute | solution.py:74
  63.7 1.3 %collective-permute-start.25 = (f32[256,128]{1,0:T(8,128)S(1)}, f32[256,128]{1,0:T(8,128)S(1)}, u32[]{:S(2)}, u32[]{:S(2)}) collective-permute-start(f32[256,128]{1,0:T(8,128)S(1)} %pad_maximum_fusion.7), channel_id=1, source_target_pairs={{0,16},{1,4},{2,7},{3,19},{4,1},{5,21},{6,22},{7,2},{8,13},{9,25},... | collective-permute-start | bytes 393224 | tf_op jit(solution)/shard_map/gather_moments/ppermute | solution.py:74
  65.1 0.4 collective-permute-done.16
  65.5 2.5 %collective-permute-start.18 = (f32[512,128]{1,0:T(8,128)S(1)}, f32[512,128]{1,0:T(8,128)S(1)}, u32[]{:S(2)}, u32[]{:S(2)}) collective-permute-start(f32[512,128]{1,0:T(8,128)S(1)} %pad_maximum_fusion.1.refs_0_), channel_id=1, source_target_pairs={{0,5},{1,17},{2,18},{3,6},{4,20},{5,0},{6,3},{7,23},{8,24},{9,12},... | collective-permute-start | bytes 786440 | tf_op jit(solution)/shard_map/gather_moments/ppermute | solution.py:74
  68.0 0.9 %collective-permute-done.25 = f32[256,128]{1,0:T(8,128)S(1)} collective-permute-done((f32[256,128]{1,0:T(8,128)S(1)}, f32[256,128]{1,0:T(8,128)S(1)}, u32[]{:S(2)}, u32[]{:S(2)}) %collective-permute-start.25) | collective-permute-done | bytes 131104 | tf_op jit(solution)/shard_map/gather_moments/ppermute | solution.py:74
  68.9 0.6 collective-permute-start.26
  69.5 1.3 %collective-permute-start.27 = (f32[8,128]{1,0:T(8,128)S(1)}, f32[8,128]{1,0:T(8,128)S(1)}, u32[]{:S(2)}, u32[]{:S(2)}) collective-permute-start(f32[8,128]{1,0:T(8,128)S(1)} %slice_add_fusion.8), channel_id=1, source_target_pairs={{0,1},{1,0},{2,3},{3,2},{4,5},{5,4},{6,7},{7,6},{8,9},{9,8},{10,11... | collective-permute-start | bytes 12296 | tf_op jit(solution)/shard_map/scatter_moments/ppermute | solution.py:74
  70.9 0.8 %collective-permute-done.27 = f32[8,128]{1,0:T(8,128)S(1)} collective-permute-done((f32[8,128]{1,0:T(8,128)S(1)}, f32[8,128]{1,0:T(8,128)S(1)}, u32[]{:S(2)}, u32[]{:S(2)}) %collective-permute-start.27) | collective-permute-done | bytes 4128 | tf_op jit(solution)/shard_map/scatter_moments/ppermute | solution.py:74
  71.7 1.3 %gather_moments.1 = (f32[8,128]{1,0:T(8,128)}, f32[1024,128]{1,0:T(8,128)S(1)}) custom-call(s32[5,16]{1,0:T(8,128)S(1)} %dynamic-slice_bitcast_fusion.table.refs_0_, f32[8,128]{1,0:T(8,128)S(1)} %add_multiply_fusion.refs_1_), custom_call_target="tpu_custom_call" | custom-call | flops 1024 | bytes 8192 | tf_op jit(solution)/shard_map/gather_moments/pallas_call | solution.py:274
  73.0 0.3 collective-permute-start.17
  73.3 0.2 collective-permute-start.29
  73.5 1.3 %collective-permute-done.26.refs_3_ = f32[512,128]{1,0:T(8,128)S(1)} collective-permute-done((f32[512,128]{1,0:T(8,128)S(1)}, f32[512,128]{1,0:T(8,128)S(1)}, u32[]{:S(2)}, u32[]{:S(2)}) %collective-permute-start.26) | collective-permute-done | bytes 262176 | tf_op jit(solution)/shard_map/gather_moments/ppermute | solution.py:74
  74.8 0.1 collective-permute-start.28
  74.9 0.4 collective-permute-start.30
  75.3 1.7 %shard_map.87 = (f32[1024,256]{1,0:T(8,128)}, f32[1024,256]{1,0:T(8,128)}) custom-call(s32[5,16]{1,0:T(8,128)S(1)} %dynamic-slice_bitcast_fusion.table.refs_0_, f32[512,128]{1,0:T(8,128)S(1)} %pad_maximum_fusion.1.refs_0_, f32[512,128]{1,0:T(8,128)S(1)} %collective-permute-done.18.refs_1_, f32[512,128]{1,0:T(8,128)S(1)} %pad_maximum_fusion.2.refs_2_, ...), custom_call_target="tpu_custom_call" | custom-call | flops 1048576 | bytes 2097152 | tf_op jit(solution)/shard_map/pallas_call | solution.py:417
  77.0 1.7 %shard_map.88 = (f32[1024,256]{1,0:T(8,128)}, f32[1024,256]{1,0:T(8,128)}) custom-call(s32[5,16]{1,0:T(8,128)S(1)} %dynamic-slice_bitcast_fusion.table.refs_0_, f32[512,128]{1,0:T(8,128)S(1)} %collective-permute-done.17.refs_0_, f32[512,128]{1,0:T(8,128)S(1)} %collective-permute-done.28.refs_1_, ...), custom_call_target="tpu_custom_call", output_to_operand_aliasing={{0}: (6, {}), {1}: (7, {})} | custom-call | flops 1048576 | bytes 2097152 | tf_op jit(solution)/shard_map/pallas_call | solution.py:417
  (47 shorter events, 0.4 us)
Async XLA Ops:
  0.6 8.4 %collective-permute-start = (f32[64,256]{1,0:T(8,128)}, f32[64,256]{1,0:T(8,128)S(1)}, u32[]{:S(2)}, u32[]{:S(2)}) collective-permute-start(f32[64,256]{1,0:T(8,128)} %refs_0_.1), channel_id=1, source_target_pairs={{0,9},{1,8},{2,11},{3,10},{4,13},{5,12},{6,15},{7,14},{8,1},{9,0},... | collective-permute-start | bytes 196616 | tf_op jit(solution)/shard_map/gather_parameters/ppermute | solution.py:74
  4.2 6.9 %collective-permute-start.3 = (f32[64,256]{1,0:T(8,128)}, f32[64,256]{1,0:T(8,128)S(1)}, u32[]{:S(2)}, u32[]{:S(2)}) collective-permute-start(f32[64,256]{1,0:T(8,128)} %refs_1_.1), channel_id=1, source_target_pairs={{0,9},{1,8},{2,11},{3,10},{4,13},{5,12},{6,15},{7,14},{8,1},{9,0},... | collective-permute-start | bytes 196616 | tf_op jit(solution)/shard_map/gather_parameters/ppermute | solution.py:74
  9.0 4.6 %collective-permute-start.1 = (f32[128,256]{1,0:T(8,128)S(1)}, f32[128,256]{1,0:T(8,128)S(1)}, u32[]{:S(2)}, u32[]{:S(2)}) collective-permute-start(f32[128,256]{1,0:T(8,128)S(1)} %pad_maximum_fusion.4), channel_id=1, source_target_pairs={{0,5},{1,2},{2,1},{3,6},{4,7},{5,0},{6,3},{7,4},{8,11},{9,12},{10,... | collective-permute-start | bytes 393224 | tf_op jit(solution)/shard_map/gather_parameters/ppermute | solution.py:74
  11.1 4.5 %collective-permute-start.4 = (f32[128,256]{1,0:T(8,128)S(1)}, f32[128,256]{1,0:T(8,128)S(1)}, u32[]{:S(2)}, u32[]{:S(2)}) collective-permute-start(f32[128,256]{1,0:T(8,128)S(1)} %pad_maximum_fusion.5), channel_id=1, source_target_pairs={{0,5},{1,2},{2,1},{3,6},{4,7},{5,0},{6,3},{7,4},{8,11},{9,12},{10,... | collective-permute-start | bytes 393224 | tf_op jit(solution)/shard_map/gather_parameters/ppermute | solution.py:74
  15.5 2.4 %collective-permute-start.6 = (f32[256,256]{1,0:T(8,128)S(1)}, f32[256,256]{1,0:T(8,128)S(1)}, u32[]{:S(2)}, u32[]{:S(2)}) collective-permute-start(f32[256,256]{1,0:T(8,128)S(1)} %constant_dynamic-update-slice_fusion.refs_1_), channel_id=1, source_target_pairs={{0,1},{1,0},{2,3},{3,2},{4,5},{5,4},{6,7},{7,6},{8,9},{9,8},{10,11... | collective-permute-start | bytes 786440 | tf_op jit(solution)/shard_map/gather_parameters/ppermute | solution.py:74
  16.0 1.9 %collective-permute-start.7 = (f32[256,256]{1,0:T(8,128)S(1)}, f32[256,256]{1,0:T(8,128)S(1)}, u32[]{:S(2)}, u32[]{:S(2)}) collective-permute-start(f32[256,256]{1,0:T(8,128)S(1)} %constant_dynamic-update-slice_fusion.3.refs_3_), channel_id=1, source_target_pairs={{0,1},{1,0},{2,3},{3,2},{4,5},{5,4},{6,7},{7,6},{8,9},{9,8},{10,11... | collective-permute-start | bytes 786440 | tf_op jit(solution)/shard_map/gather_parameters/ppermute | solution.py:74
  16.1 6.0 %collective-permute-start.2 = (f32[256,256]{1,0:T(8,128)S(1)}, f32[256,256]{1,0:T(8,128)S(1)}, u32[]{:S(2)}, u32[]{:S(2)}) collective-permute-start(f32[256,256]{1,0:T(8,128)S(1)} %constant_dynamic-update-slice_fusion.refs_1_), channel_id=1, source_target_pairs={{0,3},{1,4},{2,7},{3,0},{4,1},{5,6},{6,5},{7,2},{8,13},{9,10},{10,... | collective-permute-start | bytes 786440 | tf_op jit(solution)/shard_map/gather_parameters/ppermute | solution.py:74
  17.9 6.9 %collective-permute-start.5 = (f32[256,256]{1,0:T(8,128)S(1)}, f32[256,256]{1,0:T(8,128)S(1)}, u32[]{:S(2)}, u32[]{:S(2)}) collective-permute-start(f32[256,256]{1,0:T(8,128)S(1)} %constant_dynamic-update-slice_fusion.3.refs_3_), channel_id=1, source_target_pairs={{0,3},{1,4},{2,7},{3,0},{4,1},{5,6},{6,5},{7,2},{8,13},{9,10},{10,... | collective-permute-start | bytes 786440 | tf_op jit(solution)/shard_map/gather_parameters/ppermute | solution.py:74
  24.8 2.9 %collective-permute-start.8 = (f32[256,256]{1,0:T(8,128)S(1)}, f32[256,256]{1,0:T(8,128)S(1)}, u32[]{:S(2)}, u32[]{:S(2)}) collective-permute-start(f32[256,256]{1,0:T(8,128)S(1)} %collective-permute-done.2.refs_1_), channel_id=1, source_target_pairs={{0,1},{1,0},{2,3},{3,2},{4,5},{5,4},{6,7},{7,6},{8,9},{9,8},{10,11... | collective-permute-start | bytes 786440 | tf_op jit(solution)/shard_map/gather_parameters/ppermute | solution.py:74
  25.2 2.5 %collective-permute-start.9 = (f32[256,256]{1,0:T(8,128)S(1)}, f32[256,256]{1,0:T(8,128)S(1)}, u32[]{:S(2)}, u32[]{:S(2)}) collective-permute-start(f32[256,256]{1,0:T(8,128)S(1)} %collective-permute-done.5.refs_2_), channel_id=1, source_target_pairs={{0,1},{1,0},{2,3},{3,2},{4,5},{5,4},{6,7},{7,6},{8,9},{9,8},{10,11... | collective-permute-start | bytes 786440 | tf_op jit(solution)/shard_map/gather_parameters/ppermute | solution.py:74
  32.6 2.0 %collective-permute-start.10 = (f32[1032,128]{1,0:T(8,128)S(1)}, f32[1032,128]{1,0:T(8,128)S(1)}, u32[]{:S(2)}, u32[]{:S(2)}) collective-permute-start(f32[1032,128]{1,0:T(8,128)S(1)} %get-tuple-element.56), channel_id=1, source_target_pairs={{0,1},{1,0},{2,3},{3,2},{4,5},{5,4},{6,7},{7,6},{8,9},{9,8},{10,11... | collective-permute-start | bytes 1585160 | tf_op jit(solution)/shard_map/scatter_moments/ppermute | solution.py:74
  33.0 4.3 %collective-permute-start.19 = (f32[1024,128]{1,0:T(8,128)S(1)}, f32[1024,128]{1,0:T(8,128)S(1)}, u32[]{:S(2)}, u32[]{:S(2)}) collective-permute-start(f32[1024,128]{1,0:T(8,128)S(1)} %get-tuple-element.58), channel_id=1, source_target_pairs={{0,1},{1,0},{2,3},{3,2},{4,5},{5,4},{6,7},{7,6},{8,9},{9,8},{10,11... | collective-permute-start | bytes 1572872 | tf_op jit(solution)/shard_map/scatter_moments/ppermute | solution.py:74
  34.7 5.9 %collective-permute-start.11 = (f32[520,128]{1,0:T(8,128)S(1)}, f32[520,128]{1,0:T(8,128)S(1)}, u32[]{:S(2)}, u32[]{:S(2)}) collective-permute-start(f32[520,128]{1,0:T(8,128)S(1)} %pad_maximum_fusion), channel_id=1, source_target_pairs={{0,5},{1,17},{2,18},{3,6},{4,20},{5,0},{6,3},{7,23},{8,24},{9,12},... | collective-permute-start | bytes 798728 | tf_op jit(solution)/shard_map/scatter_moments/ppermute | solution.py:74
  37.5 5.9 %collective-permute-start.20 = (f32[512,128]{1,0:T(8,128)S(1)}, f32[512,128]{1,0:T(8,128)S(1)}, u32[]{:S(2)}, u32[]{:S(2)}) collective-permute-start(f32[512,128]{1,0:T(8,128)S(1)} %slice.104), channel_id=1, source_target_pairs={{0,3},{1,17},{2,18},{3,0},{4,20},{5,6},{6,5},{7,23},{8,24},{9,10},... | collective-permute-start | bytes 786440 | tf_op jit(solution)/shard_map/scatter_moments/ppermute | solution.py:74
  40.7 4.8 %collective-permute-start.12 = (f32[264,128]{1,0:T(8,128)S(1)}, f32[264,128]{1,0:T(8,128)S(1)}, u32[]{:S(2)}, u32[]{:S(2)}) collective-permute-start(f32[264,128]{1,0:T(8,128)S(1)} %pad_maximum_fusion.3), channel_id=1, source_target_pairs={{0,3},{1,4},{2,7},{3,0},{4,1},{5,6},{6,5},{7,2},{8,13},{9,10},{10,... | collective-permute-start | bytes 405512 | tf_op jit(solution)/shard_map/scatter_moments/ppermute | solution.py:74
  43.4 5.0 %collective-permute-start.21 = (f32[256,128]{1,0:T(8,128)S(1)}, f32[256,128]{1,0:T(8,128)S(1)}, u32[]{:S(2)}, u32[]{:S(2)}) collective-permute-start(f32[256,128]{1,0:T(8,128)S(1)} %slice.106), channel_id=1, source_target_pairs={{0,16},{1,4},{2,7},{3,19},{4,1},{5,21},{6,22},{7,2},{8,13},{9,25},... | collective-permute-start | bytes 393224 | tf_op jit(solution)/shard_map/scatter_moments/ppermute | solution.py:74
  45.6 4.4 %collective-permute-start.13 = (f32[136,128]{1,0:T(8,128)S(1)}, f32[136,128]{1,0:T(8,128)S(1)}, u32[]{:S(2)}, u32[]{:S(2)}) collective-permute-start(f32[136,128]{1,0:T(8,128)S(1)} %pad_maximum_fusion.8), channel_id=1, source_target_pairs={{0,16},{1,2},{2,1},{3,19},{4,7},{5,21},{6,22},{7,4},{8,11},{9,25},... | collective-permute-start | bytes 208904 | tf_op jit(solution)/shard_map/scatter_moments/ppermute | solution.py:74
  48.4 3.9 %collective-permute-start.22 = (f32[128,128]{1,0:T(8,128)S(1)}, f32[128,128]{1,0:T(8,128)S(1)}, u32[]{:S(2)}, u32[]{:S(2)}) collective-permute-start(f32[128,128]{1,0:T(8,128)S(1)} %slice.108), channel_id=1, source_target_pairs={{0,5},{1,2},{2,1},{3,6},{4,7},{5,0},{6,3},{7,4},{8,11},{9,12},{10,... | collective-permute-start | bytes 196616 | tf_op jit(solution)/shard_map/scatter_moments/ppermute | solution.py:74
  50.0 5.3 %collective-permute-start.14 = (f32[136,128]{1,0:T(8,128)S(1)}, f32[136,128]{1,0:T(8,128)S(1)}, u32[]{:S(2)}, u32[]{:S(2)}) collective-permute-start(f32[136,128]{1,0:T(8,128)S(1)} %pad_maximum_fusion.9), channel_id=1, source_target_pairs={{0,9},{1,8},{2,11},{3,10},{4,13},{5,12},{6,15},{7,14},{8,1},{9,0},... | collective-permute-start | bytes 208904 | tf_op jit(solution)/shard_map/scatter_moments/ppermute | solution.py:74
  52.4 7.5 %collective-permute-start.23 = (f32[128,128]{1,0:T(8,128)S(1)}, f32[128,128]{1,0:T(8,128)S(1)}, u32[]{:S(2)}, u32[]{:S(2)}) collective-permute-start(f32[128,128]{1,0:T(8,128)S(1)} %slice_add_fusion.5), channel_id=1, source_target_pairs={{0,9},{1,8},{2,11},{3,10},{4,13},{5,12},{6,15},{7,14},{8,1},{9,0},... | collective-permute-start | bytes 196616 | tf_op jit(solution)/shard_map/scatter_moments/ppermute | solution.py:74
  55.3 5.2 %collective-permute-start.15 = (f32[128,128]{1,0:T(8,128)S(1)}, f32[128,128]{1,0:T(8,128)S(1)}, u32[]{:S(2)}, u32[]{:S(2)}) collective-permute-start(f32[128,128]{1,0:T(8,128)S(1)} %slice_add_fusion.6), channel_id=1, source_target_pairs={{0,16},{1,2},{2,1},{3,19},{4,7},{5,21},{6,22},{7,4},{8,11},{9,25},... | collective-permute-start | bytes 196616 | tf_op jit(solution)/shard_map/gather_moments/ppermute | solution.py:74
  60.0 3.8 %collective-permute-start.24 = (f32[128,128]{1,0:T(8,128)S(1)}, f32[128,128]{1,0:T(8,128)S(1)}, u32[]{:S(2)}, u32[]{:S(2)}) collective-permute-start(f32[128,128]{1,0:T(8,128)S(1)} %add.70), channel_id=1, source_target_pairs={{0,5},{1,2},{2,1},{3,6},{4,7},{5,0},{6,3},{7,4},{8,11},{9,12},{10,... | collective-permute-start | bytes 196616 | tf_op jit(solution)/shard_map/gather_moments/ppermute | solution.py:74
  60.5 5.0 %collective-permute-start.16 = (f32[256,128]{1,0:T(8,128)S(1)}, f32[256,128]{1,0:T(8,128)S(1)}, u32[]{:S(2)}, u32[]{:S(2)}) collective-permute-start(f32[256,128]{1,0:T(8,128)S(1)} %pad_maximum_fusion.6), channel_id=1, source_target_pairs={{0,3},{1,4},{2,7},{3,0},{4,1},{5,6},{6,5},{7,2},{8,13},{9,10},{10,... | collective-permute-start | bytes 393224 | tf_op jit(solution)/shard_map/gather_moments/ppermute | solution.py:74
  63.7 5.1 %collective-permute-start.25 = (f32[256,128]{1,0:T(8,128)S(1)}, f32[256,128]{1,0:T(8,128)S(1)}, u32[]{:S(2)}, u32[]{:S(2)}) collective-permute-start(f32[256,128]{1,0:T(8,128)S(1)} %pad_maximum_fusion.7), channel_id=1, source_target_pairs={{0,16},{1,4},{2,7},{3,19},{4,1},{5,21},{6,22},{7,2},{8,13},{9,25},... | collective-permute-start | bytes 393224 | tf_op jit(solution)/shard_map/gather_moments/ppermute | solution.py:74
  65.5 8.0 %collective-permute-start.18 = (f32[512,128]{1,0:T(8,128)S(1)}, f32[512,128]{1,0:T(8,128)S(1)}, u32[]{:S(2)}, u32[]{:S(2)}) collective-permute-start(f32[512,128]{1,0:T(8,128)S(1)} %pad_maximum_fusion.1.refs_0_), channel_id=1, source_target_pairs={{0,5},{1,17},{2,18},{3,6},{4,20},{5,0},{6,3},{7,23},{8,24},{9,12},... | collective-permute-start | bytes 786440 | tf_op jit(solution)/shard_map/gather_moments/ppermute | solution.py:74
  68.9 5.9 %collective-permute-start.26 = (f32[512,128]{1,0:T(8,128)S(1)}, f32[512,128]{1,0:T(8,128)S(1)}, u32[]{:S(2)}, u32[]{:S(2)}) collective-permute-start(f32[512,128]{1,0:T(8,128)S(1)} %pad_maximum_fusion.2.refs_2_), channel_id=1, source_target_pairs={{0,3},{1,17},{2,18},{3,0},{4,20},{5,6},{6,5},{7,23},{8,24},{9,10},... | collective-permute-start | bytes 786440 | tf_op jit(solution)/shard_map/gather_moments/ppermute | solution.py:74
  69.5 2.1 %collective-permute-start.27 = (f32[8,128]{1,0:T(8,128)S(1)}, f32[8,128]{1,0:T(8,128)S(1)}, u32[]{:S(2)}, u32[]{:S(2)}) collective-permute-start(f32[8,128]{1,0:T(8,128)S(1)} %slice_add_fusion.8), channel_id=1, source_target_pairs={{0,1},{1,0},{2,3},{3,2},{4,5},{5,4},{6,7},{7,6},{8,9},{9,8},{10,11... | collective-permute-start | bytes 12296 | tf_op jit(solution)/shard_map/scatter_moments/ppermute | solution.py:74
  73.0 4.0 %collective-permute-start.17 = (f32[512,128]{1,0:T(8,128)S(1)}, f32[512,128]{1,0:T(8,128)S(1)}, u32[]{:S(2)}, u32[]{:S(2)}) collective-permute-start(f32[512,128]{1,0:T(8,128)S(1)} %pad_maximum_fusion.1.refs_0_), channel_id=1, source_target_pairs={{0,1},{1,0},{2,3},{3,2},{4,5},{5,4},{6,7},{7,6},{8,9},{9,8},{10,11... | collective-permute-start | bytes 786440 | tf_op jit(solution)/shard_map/gather_moments/ppermute | solution.py:74
  73.3 3.7 %collective-permute-start.29 = (f32[512,128]{1,0:T(8,128)S(1)}, f32[512,128]{1,0:T(8,128)S(1)}, u32[]{:S(2)}, u32[]{:S(2)}) collective-permute-start(f32[512,128]{1,0:T(8,128)S(1)} %pad_maximum_fusion.2.refs_2_), channel_id=1, source_target_pairs={{0,1},{1,0},{2,3},{3,2},{4,5},{5,4},{6,7},{7,6},{8,9},{9,8},{10,11... | collective-permute-start | bytes 786440 | tf_op jit(solution)/shard_map/gather_moments/ppermute | solution.py:74
  74.8 2.2 %collective-permute-start.28 = (f32[512,128]{1,0:T(8,128)S(1)}, f32[512,128]{1,0:T(8,128)S(1)}, u32[]{:S(2)}, u32[]{:S(2)}) collective-permute-start(f32[512,128]{1,0:T(8,128)S(1)} %collective-permute-done.18.refs_1_), channel_id=1, source_target_pairs={{0,1},{1,0},{2,3},{3,2},{4,5},{5,4},{6,7},{7,6},{8,9},{9,8},{10,11... | collective-permute-start | bytes 786440 | tf_op jit(solution)/shard_map/gather_moments/ppermute | solution.py:74
  74.9 2.1 %collective-permute-start.30 = (f32[512,128]{1,0:T(8,128)S(1)}, f32[512,128]{1,0:T(8,128)S(1)}, u32[]{:S(2)}, u32[]{:S(2)}) collective-permute-start(f32[512,128]{1,0:T(8,128)S(1)} %collective-permute-done.26.refs_3_), channel_id=1, source_target_pairs={{0,1},{1,0},{2,3},{3,2},{4,5},{5,4},{6,7},{7,6},{8,9},{9,8},{10,11... | collective-permute-start | bytes 786440 | tf_op jit(solution)/shard_map/gather_moments/ppermute | solution.py:74

commit v9 on v8

--- a/solution.py
+++ b/solution.py
@@ -476,7 +476,7 @@
         pairs = [(h, plan.swap(b, (0, 0))) for h, b in zip(held, both)]
         firsts = (0, plan.units // 2)
         early = early_scores(plan, table, firsts, *pairs, log_weights, stack)
-        last, early = lax.optimization_barrier((last, early))
+        last[0], early = lax.optimization_barrier((last[0], early))
         mates = [plan.swap(l, (0, 0)) for l in last]
         firsts = (plan.units // 4,)
         early += early_scores(plan, table, firsts, last[:1], last[1:], log_weights, stack)
@@ -501,7 +501,7 @@
             held = double(plan, held, step)
         last = [plan.swap(h, at) for h, at in zip(held, steps[-1])]
         mates = [plan.swap(h, (0, 0)) for h in held]
-        last, scale = lax.optimization_barrier((last, scale))
+        last[0], scale = lax.optimization_barrier((last[0], scale))
         own = [[h, l] for h, l in zip(held, last)]
         others = [[m, plan.swap(l, (0, 0))] for m, l in zip(mates, last)]
     fresh = update(plan, table, 0, *own, scale, (comps, width))

time: 78.9 us -> 79.3 us (level)
  waiting for transfers between devices: 19 us -> 20.7 us
  starting transfers between devices: 34.8 us -> 33.4 us
    ppermute x31, waiting for transfers between devices: 19 us -> 20.7 us  [swap(): return lax.ppermute(value, ('grp', 'comp'), pairs)]
    ppermute x31, starting transfers between devices: 34.8 us -> 33.4 us  [swap(): return lax.ppermute(value, ('grp', 'comp'), pairs)]
where the time goes in v9:
time: 79.3 us; the launch traced here: 79 us
  starting transfers between devices  33.4 us (42%)
  Pallas kernels  22.8 us (29%)
  waiting for transfers between devices  20.7 us (26%)
  between operations  0.97 us (1%)
  local copies, waits for them, and re-layouts  0.8 us (1%)
    ppermute x31, starting transfers between devices, swap(): return lax.ppermute(value, ('grp', 'comp'), pairs)  33.4 us
    ppermute x31, waiting for transfers between devices, swap(): return lax.ppermute(value, ('grp', 'comp'), pairs)  20.7 us
    pallas_call x8, Pallas kernels, call(): pl.pallas_call(functools.partial(kernel, plan), in_specs=[pl.BlockSpec(me...  19.4 us
    pallas_call x2, Pallas kernels, update(): pl.pallas_call(functools.partial(update_kernel, plan, first_slot), in_spe...  3.4 us
  transfers between devices with their start and end apart: 31, of which 15 were waited for; matrix products, arithmetic and copies ran while one was open for 2% of the time, Pallas kernels for 20%

profile of v9, /device:TPU:0, one launch (start us, length us, event | category | flops | bytes accessed | tf_op | source)
XLA Modules:
  0.0 79.0 jit_solution(11025277426113300547)
XLA Ops:
  0.6 3.5 %collective-permute-start = (f32[64,256]{1,0:T(8,128)}, f32[64,256]{1,0:T(8,128)S(1)}, u32[]{:S(2)}, u32[]{:S(2)}) collective-permute-start(f32[64,256]{1,0:T(8,128)} %refs_0_.1), channel_id=1, source_target_pairs={{0,9},{1,8},{2,11},{3,10},{4,13},{5,12},{6,15},{7,14},{8,1},{9,0},... | collective-permute-start | bytes 196616 | tf_op jit(solution)/shard_map/gather_parameters/ppermute | solution.py:74
  4.2 0.1 collective-permute-start.3
  4.3 0.7 dynamic-slice_bitcast_fusion.table.refs_0_
  4.9 2.0 %gather_parameters.4 = (f32[64,256]{1,0:T(8,128)S(1)}, f32[64,256]{1,0:T(8,128)S(1)}, f32[1024,128]{1,0:T(8,128)S(1)}) custom-call(s32[5,16]{1,0:T(8,128)S(1)} %dynamic-slice_bitcast_fusion.table.refs_0_, f32[64,256]{1,0:T(8,128)} %refs_0_.1, f32[64,256]{1,0:T(8,128)} %refs_1_.1, f32[8,128]{1,0:T(8,128)} %bitcast.5), custom_call_target="tpu_custom_call" | custom-call | bytes 270336 | tf_op jit(solution)/shard_map/gather_parameters/pallas_call | solution.py:274
  6.9 2.0 %gather_parameters.5.refs_6_.refs_4_.refs_3_.refs_2_ = bf16[2048,768]{1,0:T(8,128)(2,1)S(1)} custom-call(s32[5,16]{1,0:T(8,128)S(1)} %dynamic-slice_bitcast_fusion.table.refs_0_, bf16[2048,256]{1,0:T(8,128)(2,1)} %source.1), custom_call_target="tpu_custom_call" | custom-call | flops 4194304 | bytes 2097152 | tf_op jit(solution)/shard_map/gather_parameters/pallas_call | solution.py:274
  9.0 0.0 collective-permute-done
  9.0 2.0 %collective-permute-start.1 = (f32[128,256]{1,0:T(8,128)S(1)}, f32[128,256]{1,0:T(8,128)S(1)}, u32[]{:S(2)}, u32[]{:S(2)}) collective-permute-start(f32[128,256]{1,0:T(8,128)S(1)} %pad_maximum_fusion.4), channel_id=1, source_target_pairs={{0,5},{1,2},{2,1},{3,6},{4,7},{5,0},{6,3},{7,4},{8,11},{9,12},{10,... | collective-permute-start | bytes 393224 | tf_op jit(solution)/shard_map/gather_parameters/ppermute | solution.py:74
  11.0 0.0 collective-permute-done.3
  11.1 1.4 %collective-permute-start.4 = (f32[128,256]{1,0:T(8,128)S(1)}, f32[128,256]{1,0:T(8,128)S(1)}, u32[]{:S(2)}, u32[]{:S(2)}) collective-permute-start(f32[128,256]{1,0:T(8,128)S(1)} %pad_maximum_fusion.5), channel_id=1, source_target_pairs={{0,5},{1,2},{2,1},{3,6},{4,7},{5,0},{6,3},{7,4},{8,11},{9,12},{10,... | collective-permute-start | bytes 393224 | tf_op jit(solution)/shard_map/gather_parameters/ppermute | solution.py:74
  12.5 1.2 %collective-permute-done.1 = f32[128,256]{1,0:T(8,128)S(1)} collective-permute-done((f32[128,256]{1,0:T(8,128)S(1)}, f32[128,256]{1,0:T(8,128)S(1)}, u32[]{:S(2)}, u32[]{:S(2)}) %collective-permute-start.1) | collective-permute-done | bytes 131104 | tf_op jit(solution)/shard_map/gather_parameters/ppermute | solution.py:74
  13.7 1.8 %collective-permute-done.4 = f32[128,256]{1,0:T(8,128)S(1)} collective-permute-done((f32[128,256]{1,0:T(8,128)S(1)}, f32[128,256]{1,0:T(8,128)S(1)}, u32[]{:S(2)}, u32[]{:S(2)}) %collective-permute-start.4) | collective-permute-done | bytes 131104 | tf_op jit(solution)/shard_map/gather_parameters/ppermute | solution.py:74
  15.5 0.5 collective-permute-start.5
  16.0 0.1 collective-permute-start.6
  16.1 1.8 %collective-permute-start.2 = (f32[256,256]{1,0:T(8,128)S(1)}, f32[256,256]{1,0:T(8,128)S(1)}, u32[]{:S(2)}, u32[]{:S(2)}) collective-permute-start(f32[256,256]{1,0:T(8,128)S(1)} %constant_dynamic-update-slice_fusion.refs_1_), channel_id=1, source_target_pairs={{0,3},{1,4},{2,7},{3,0},{4,1},{5,6},{6,5},{7,2},{8,13},{9,10},{10,... | collective-permute-start | bytes 786440 | tf_op jit(solution)/shard_map/gather_parameters/ppermute | solution.py:74
  17.9 0.0 collective-permute-start.8
  17.9 4.1 %gather_parameters.6 = (f32[512,2048]{1,0:T(8,128)S(1)}, f32[1,2048]{1,0:T(1,128)S(1)}, f32[1,2048]{1,0:T(1,128)S(1)}) custom-call(s32[5,16]{1,0:T(8,128)S(1)} %dynamic-slice_bitcast_fusion.table.refs_0_, f32[256,256]{1,0:T(8,128)S(1)} %constant_dynamic-update-slice_fusion.refs_1_, f32[256,256]{1,0:T(8,128)S(1)} %collective-permute-done.5.refs_2_, ...), custom_call_target="tpu_custom_call" | custom-call | flops 2684354560 | bytes 9437184 | tf_op jit(solution)/shard_map/gather_parameters/pallas_call | solution.py:274
  22.1 0.0 collective-permute-done.2.refs_1_
  22.1 2.7 %collective-permute-done.8.refs_2_ = f32[256,256]{1,0:T(8,128)S(1)} collective-permute-done((f32[256,256]{1,0:T(8,128)S(1)}, f32[256,256]{1,0:T(8,128)S(1)}, u32[]{:S(2)}, u32[]{:S(2)}) %collective-permute-start.8) | collective-permute-done | bytes 262176 | tf_op jit(solution)/shard_map/gather_parameters/ppermute | solution.py:74
  24.8 0.4 collective-permute-start.9
  25.2 0.1 collective-permute-start.7
  25.3 2.4 %gather_parameters.7 = (f32[256,2048]{1,0:T(8,128)S(1)}, f32[1,2048]{1,0:T(1,128)S(1)}, f32[1,2048]{1,0:T(1,128)S(1)}) custom-call(s32[5,16]{1,0:T(8,128)S(1)} %dynamic-slice_bitcast_fusion.table.refs_0_, f32[256,256]{1,0:T(8,128)S(1)} %collective-permute-done.2.refs_1_, f32[256,256]{1,0:T(8,128)S(1)} %collective-permute-done.8.refs_2_, ...), custom_call_target="tpu_custom_call" | custom-call | flops 1342177280 | bytes 8388608 | tf_op jit(solution)/shard_map/gather_parameters/pallas_call | solution.py:274
  27.6 0.0 collective-permute-done.9.refs_1_
  27.6 0.0 collective-permute-done.7.refs_0_
  27.7 5.0 %shard_map.84 = (f32[1032,128]{1,0:T(8,128)S(1)}, f32[1024,128]{1,0:T(8,128)S(1)}, f32[8,128]{1,0:T(8,128)S(1)}, f32[1,2048]{1,0:T(1,128)}, bf16[512,2048]{1,0:T(8,128)(2,1)S(1)}) custom-call(s32[5,16]{1,0:T(8,128)S(1)} %dynamic-slice_bitcast_fusion.table.refs_0_, f32[256,256]{1,0:T(8,128)S(1)} %collective-permute-done.7.refs_0_, ...), custom_call_target="tpu_custom_call" | custom-call | flops 2415919104 | bytes 21037056 | tf_op jit(solution)/shard_map/pallas_call | solution.py:274
  32.6 0.4 collective-permute-start.10
  33.0 0.1 collective-permute-start.21
  33.1 1.3 %shard_map.85 = f32[1024,128]{1,0:T(8,128)S(1)} custom-call(s32[5,16]{1,0:T(8,128)S(1)} %dynamic-slice_bitcast_fusion.table.refs_0_, bf16[512,2048]{1,0:T(8,128)(2,1)S(1)} %get-tuple-element.52.refs_1_, bf16[2048,768]{1,0:T(8,128)(2,1)S(1)} %gather_parameters.5.refs_6_.refs_4_.refs_3_.refs_2_), custom_call_target="tpu_custom_call" | custom-call | flops 536870912 | bytes 10485760 | tf_op jit(solution)/shard_map/pallas_call | solution.py:274
  34.5 0.1 collective-permute-done.10
  34.6 0.1 slice_add_fusion
  34.7 1.3 %collective-permute-start.11 = (f32[520,128]{1,0:T(8,128)S(1)}, f32[520,128]{1,0:T(8,128)S(1)}, u32[]{:S(2)}, u32[]{:S(2)}) collective-permute-start(f32[520,128]{1,0:T(8,128)S(1)} %pad_maximum_fusion), channel_id=1, source_target_pairs={{0,5},{1,17},{2,18},{3,6},{4,20},{5,0},{6,3},{7,23},{8,24},{9,12},... | collective-permute-start | bytes 798728 | tf_op jit(solution)/shard_map/scatter_moments/ppermute | solution.py:74
  36.0 1.3 %shard_map.86 = f32[1024,128]{1,0:T(8,128)S(1)} custom-call(s32[5,16]{1,0:T(8,128)S(1)} %dynamic-slice_bitcast_fusion.table.refs_0_, bf16[512,2048]{1,0:T(8,128)(2,1)S(1)} %get-tuple-element.52.refs_1_, bf16[2048,768]{1,0:T(8,128)(2,1)S(1)} %gather_parameters.5.refs_6_.refs_4_.refs_3_.refs_2_), custom_call_target="tpu_custom_call" | custom-call | flops 536870912 | bytes 10485760 | tf_op jit(solution)/shard_map/pallas_call | solution.py:274
  37.4 0.1 add.68
  37.5 1.5 %collective-permute-start.22 = (f32[512,128]{1,0:T(8,128)S(1)}, f32[512,128]{1,0:T(8,128)S(1)}, u32[]{:S(2)}, u32[]{:S(2)}) collective-permute-start(f32[512,128]{1,0:T(8,128)S(1)} %slice.105), channel_id=1, source_target_pairs={{0,3},{1,17},{2,18},{3,0},{4,20},{5,6},{6,5},{7,23},{8,24},{9,10},... | collective-permute-start | bytes 786440 | tf_op jit(solution)/shard_map/scatter_moments/ppermute | solution.py:74
  39.0 1.6 %collective-permute-done.11 = f32[520,128]{1,0:T(8,128)S(1)} collective-permute-done((f32[520,128]{1,0:T(8,128)S(1)}, f32[520,128]{1,0:T(8,128)S(1)}, u32[]{:S(2)}, u32[]{:S(2)}) %collective-permute-start.11) | collective-permute-done | bytes 266272 | tf_op jit(solution)/shard_map/scatter_moments/ppermute | solution.py:74
  40.7 2.1 %collective-permute-start.12 = (f32[264,128]{1,0:T(8,128)S(1)}, f32[264,128]{1,0:T(8,128)S(1)}, u32[]{:S(2)}, u32[]{:S(2)}) collective-permute-start(f32[264,128]{1,0:T(8,128)S(1)} %pad_maximum_fusion.3), channel_id=1, source_target_pairs={{0,3},{1,4},{2,7},{3,0},{4,1},{5,6},{6,5},{7,2},{8,13},{9,10},{10,... | collective-permute-start | bytes 405512 | tf_op jit(solution)/shard_map/scatter_moments/ppermute | solution.py:74
  42.8 0.5 collective-permute-done.22
  43.4 1.6 %collective-permute-start.23 = (f32[256,128]{1,0:T(8,128)S(1)}, f32[256,128]{1,0:T(8,128)S(1)}, u32[]{:S(2)}, u32[]{:S(2)}) collective-permute-start(f32[256,128]{1,0:T(8,128)S(1)} %slice.107), channel_id=1, source_target_pairs={{0,16},{1,4},{2,7},{3,19},{4,1},{5,21},{6,22},{7,2},{8,13},{9,25},... | collective-permute-start | bytes 393224 | tf_op jit(solution)/shard_map/scatter_moments/ppermute | solution.py:74
  44.9 0.5 collective-permute-done.12
  45.5 1.8 %collective-permute-start.13 = (f32[136,128]{1,0:T(8,128)S(1)}, f32[136,128]{1,0:T(8,128)S(1)}, u32[]{:S(2)}, u32[]{:S(2)}) collective-permute-start(f32[136,128]{1,0:T(8,128)S(1)} %pad_maximum_fusion.8), channel_id=1, source_target_pairs={{0,16},{1,2},{2,1},{3,19},{4,7},{5,21},{6,22},{7,4},{8,11},{9,25},... | collective-permute-start | bytes 208904 | tf_op jit(solution)/shard_map/scatter_moments/ppermute | solution.py:74
  47.3 1.1 %collective-permute-done.23 = f32[256,128]{1,0:T(8,128)S(1)} collective-permute-done((f32[256,128]{1,0:T(8,128)S(1)}, f32[256,128]{1,0:T(8,128)S(1)}, u32[]{:S(2)}, u32[]{:S(2)}) %collective-permute-start.23) | collective-permute-done | bytes 131104 | tf_op jit(solution)/shard_map/scatter_moments/ppermute | solution.py:74
  48.4 0.3 collective-permute-start.24
  48.7 1.2 %collective-permute-done.13 = f32[136,128]{1,0:T(8,128)S(1)} collective-permute-done((f32[136,128]{1,0:T(8,128)S(1)}, f32[136,128]{1,0:T(8,128)S(1)}, u32[]{:S(2)}, u32[]{:S(2)}) %collective-permute-start.13) | collective-permute-done | bytes 69664 | tf_op jit(solution)/shard_map/scatter_moments/ppermute | solution.py:74
  50.0 2.4 %collective-permute-start.14 = (f32[136,128]{1,0:T(8,128)S(1)}, f32[136,128]{1,0:T(8,128)S(1)}, u32[]{:S(2)}, u32[]{:S(2)}) collective-permute-start(f32[136,128]{1,0:T(8,128)S(1)} %pad_maximum_fusion.9), channel_id=1, source_target_pairs={{0,9},{1,8},{2,11},{3,10},{4,13},{5,12},{6,15},{7,14},{8,1},{9,0},... | collective-permute-start | bytes 208904 | tf_op jit(solution)/shard_map/scatter_moments/ppermute | solution.py:74
  52.4 2.9 %collective-permute-start.25 = (f32[128,128]{1,0:T(8,128)S(1)}, f32[128,128]{1,0:T(8,128)S(1)}, u32[]{:S(2)}, u32[]{:S(2)}) collective-permute-start(f32[128,128]{1,0:T(8,128)S(1)} %slice_add_fusion.5), channel_id=1, source_target_pairs={{0,9},{1,8},{2,11},{3,10},{4,13},{5,12},{6,15},{7,14},{8,1},{9,0},... | collective-permute-start | bytes 196616 | tf_op jit(solution)/shard_map/scatter_moments/ppermute | solution.py:74
  55.3 1.6 %collective-permute-start.15 = (f32[128,128]{1,0:T(8,128)S(1)}, f32[128,128]{1,0:T(8,128)S(1)}, u32[]{:S(2)}, u32[]{:S(2)}) collective-permute-start(f32[128,128]{1,0:T(8,128)S(1)} %slice_add_fusion.6), channel_id=1, source_target_pairs={{0,16},{1,2},{2,1},{3,19},{4,7},{5,21},{6,22},{7,4},{8,11},{9,25},... | collective-permute-start | bytes 196616 | tf_op jit(solution)/shard_map/gather_moments/ppermute | solution.py:74
  56.9 3.1 %collective-permute-done.25 = f32[128,128]{1,0:T(8,128)S(1)} collective-permute-done((f32[128,128]{1,0:T(8,128)S(1)}, f32[128,128]{1,0:T(8,128)S(1)}, u32[]{:S(2)}, u32[]{:S(2)}) %collective-permute-start.25) | collective-permute-done | bytes 65568 | tf_op jit(solution)/shard_map/scatter_moments/ppermute | solution.py:74
  60.0 0.5 collective-permute-start.26
  60.5 1.6 %collective-permute-start.16 = (f32[256,128]{1,0:T(8,128)S(1)}, f32[256,128]{1,0:T(8,128)S(1)}, u32[]{:S(2)}, u32[]{:S(2)}) collective-permute-start(f32[256,128]{1,0:T(8,128)S(1)} %pad_maximum_fusion.6), channel_id=1, source_target_pairs={{0,3},{1,4},{2,7},{3,0},{4,1},{5,6},{6,5},{7,2},{8,13},{9,10},{10,... | collective-permute-start | bytes 393224 | tf_op jit(solution)/shard_map/gather_moments/ppermute | solution.py:74
  62.0 1.7 %collective-permute-done.26 = f32[128,128]{1,0:T(8,128)S(1)} collective-permute-done((f32[128,128]{1,0:T(8,128)S(1)}, f32[128,128]{1,0:T(8,128)S(1)}, u32[]{:S(2)}, u32[]{:S(2)}) %collective-permute-start.26) | collective-permute-done | bytes 65568 | tf_op jit(solution)/shard_map/gather_moments/ppermute | solution.py:74
  63.7 1.3 %collective-permute-start.27 = (f32[256,128]{1,0:T(8,128)S(1)}, f32[256,128]{1,0:T(8,128)S(1)}, u32[]{:S(2)}, u32[]{:S(2)}) collective-permute-start(f32[256,128]{1,0:T(8,128)S(1)} %pad_maximum_fusion.7), channel_id=1, source_target_pairs={{0,16},{1,4},{2,7},{3,19},{4,1},{5,21},{6,22},{7,2},{8,13},{9,25},... | collective-permute-start | bytes 393224 | tf_op jit(solution)/shard_map/gather_moments/ppermute | solution.py:74
  65.1 0.4 collective-permute-done.16
  65.5 0.9 %collective-permute-start.18 = (f32[512,128]{1,0:T(8,128)S(1)}, f32[512,128]{1,0:T(8,128)S(1)}, u32[]{:S(2)}, u32[]{:S(2)}) collective-permute-start(f32[512,128]{1,0:T(8,128)S(1)} %pad_maximum_fusion.1.refs_0_), channel_id=1, source_target_pairs={{0,5},{1,17},{2,18},{3,6},{4,20},{5,0},{6,3},{7,23},{8,24},{9,12},... | collective-permute-start | bytes 786440 | tf_op jit(solution)/shard_map/gather_moments/ppermute | solution.py:74
  66.4 2.5 %collective-permute-done.27 = f32[256,128]{1,0:T(8,128)S(1)} collective-permute-done((f32[256,128]{1,0:T(8,128)S(1)}, f32[256,128]{1,0:T(8,128)S(1)}, u32[]{:S(2)}, u32[]{:S(2)}) %collective-permute-start.27) | collective-permute-done | bytes 131104 | tf_op jit(solution)/shard_map/gather_moments/ppermute | solution.py:74
  68.9 0.5 collective-permute-start.29
  69.4 1.5 %collective-permute-start.19 = (f32[8,128]{1,0:T(8,128)S(1)}, f32[8,128]{1,0:T(8,128)S(1)}, u32[]{:S(2)}, u32[]{:S(2)}) collective-permute-start(f32[8,128]{1,0:T(8,128)S(1)} %slice_add_fusion.8), channel_id=1, source_target_pairs={{0,1},{1,0},{2,3},{3,2},{4,5},{5,4},{6,7},{7,6},{8,9},{9,8},{10,11... | collective-permute-start | bytes 12296 | tf_op jit(solution)/shard_map/scatter_moments/ppermute | solution.py:74
  70.9 0.8 %collective-permute-done.19 = f32[8,128]{1,0:T(8,128)S(1)} collective-permute-done((f32[8,128]{1,0:T(8,128)S(1)}, f32[8,128]{1,0:T(8,128)S(1)}, u32[]{:S(2)}, u32[]{:S(2)}) %collective-permute-start.19) | collective-permute-done | bytes 4128 | tf_op jit(solution)/shard_map/scatter_moments/ppermute | solution.py:74
  71.7 1.3 %gather_moments.1 = (f32[8,128]{1,0:T(8,128)}, f32[1024,128]{1,0:T(8,128)S(1)}) custom-call(s32[5,16]{1,0:T(8,128)S(1)} %dynamic-slice_bitcast_fusion.table.refs_0_, f32[8,128]{1,0:T(8,128)S(1)} %add_multiply_fusion.refs_1_), custom_call_target="tpu_custom_call" | custom-call | flops 1024 | bytes 8192 | tf_op jit(solution)/shard_map/gather_moments/pallas_call | solution.py:274
  73.0 0.3 collective-permute-start.17
  73.3 0.2 collective-permute-start.28
  73.5 1.3 %collective-permute-done.29.refs_3_ = f32[512,128]{1,0:T(8,128)S(1)} collective-permute-done((f32[512,128]{1,0:T(8,128)S(1)}, f32[512,128]{1,0:T(8,128)S(1)}, u32[]{:S(2)}, u32[]{:S(2)}) %collective-permute-start.29) | collective-permute-done | bytes 262176 | tf_op jit(solution)/shard_map/gather_moments/ppermute | solution.py:74
  74.8 0.8 %collective-permute-start.30 = (f32[512,128]{1,0:T(8,128)S(1)}, f32[512,128]{1,0:T(8,128)S(1)}, u32[]{:S(2)}, u32[]{:S(2)}) collective-permute-start(f32[512,128]{1,0:T(8,128)S(1)} %collective-permute-done.29.refs_3_), channel_id=1, source_target_pairs={{0,1},{1,0},{2,3},{3,2},{4,5},{5,4},{6,7},{7,6},{8,9},{9,8},{10,11... | collective-permute-start | bytes 786440 | tf_op jit(solution)/shard_map/gather_moments/ppermute | solution.py:74
  75.6 0.0 collective-permute-start.20
  75.6 1.7 %shard_map.87 = (f32[1024,256]{1,0:T(8,128)}, f32[1024,256]{1,0:T(8,128)}) custom-call(s32[5,16]{1,0:T(8,128)S(1)} %dynamic-slice_bitcast_fusion.table.refs_0_, f32[512,128]{1,0:T(8,128)S(1)} %pad_maximum_fusion.1.refs_0_, f32[512,128]{1,0:T(8,128)S(1)} %collective-permute-done.18.refs_1_, f32[512,128]{1,0:T(8,128)S(1)} %pad_maximum_fusion.2.refs_2_, ...), custom_call_target="tpu_custom_call" | custom-call | flops 1048576 | bytes 2097152 | tf_op jit(solution)/shard_map/pallas_call | solution.py:417
  77.3 1.7 %shard_map.88 = (f32[1024,256]{1,0:T(8,128)}, f32[1024,256]{1,0:T(8,128)}) custom-call(s32[5,16]{1,0:T(8,128)S(1)} %dynamic-slice_bitcast_fusion.table.refs_0_, f32[512,128]{1,0:T(8,128)S(1)} %collective-permute-done.17.refs_0_, f32[512,128]{1,0:T(8,128)S(1)} %collective-permute-done.20.refs_1_, ...), custom_call_target="tpu_custom_call", output_to_operand_aliasing={{0}: (6, {}), {1}: (7, {})} | custom-call | flops 1048576 | bytes 2097152 | tf_op jit(solution)/shard_map/pallas_call | solution.py:417
  (47 shorter events, 0.4 us)
Async XLA Ops:
  0.6 8.4 %collective-permute-start = (f32[64,256]{1,0:T(8,128)}, f32[64,256]{1,0:T(8,128)S(1)}, u32[]{:S(2)}, u32[]{:S(2)}) collective-permute-start(f32[64,256]{1,0:T(8,128)} %refs_0_.1), channel_id=1, source_target_pairs={{0,9},{1,8},{2,11},{3,10},{4,13},{5,12},{6,15},{7,14},{8,1},{9,0},... | collective-permute-start | bytes 196616 | tf_op jit(solution)/shard_map/gather_parameters/ppermute | solution.py:74
  4.2 6.9 %collective-permute-start.3 = (f32[64,256]{1,0:T(8,128)}, f32[64,256]{1,0:T(8,128)S(1)}, u32[]{:S(2)}, u32[]{:S(2)}) collective-permute-start(f32[64,256]{1,0:T(8,128)} %refs_1_.1), channel_id=1, source_target_pairs={{0,9},{1,8},{2,11},{3,10},{4,13},{5,12},{6,15},{7,14},{8,1},{9,0},... | collective-permute-start | bytes 196616 | tf_op jit(solution)/shard_map/gather_parameters/ppermute | solution.py:74
  9.0 4.6 %collective-permute-start.1 = (f32[128,256]{1,0:T(8,128)S(1)}, f32[128,256]{1,0:T(8,128)S(1)}, u32[]{:S(2)}, u32[]{:S(2)}) collective-permute-start(f32[128,256]{1,0:T(8,128)S(1)} %pad_maximum_fusion.4), channel_id=1, source_target_pairs={{0,5},{1,2},{2,1},{3,6},{4,7},{5,0},{6,3},{7,4},{8,11},{9,12},{10,... | collective-permute-start | bytes 393224 | tf_op jit(solution)/shard_map/gather_parameters/ppermute | solution.py:74
  11.1 4.5 %collective-permute-start.4 = (f32[128,256]{1,0:T(8,128)S(1)}, f32[128,256]{1,0:T(8,128)S(1)}, u32[]{:S(2)}, u32[]{:S(2)}) collective-permute-start(f32[128,256]{1,0:T(8,128)S(1)} %pad_maximum_fusion.5), channel_id=1, source_target_pairs={{0,5},{1,2},{2,1},{3,6},{4,7},{5,0},{6,3},{7,4},{8,11},{9,12},{10,... | collective-permute-start | bytes 393224 | tf_op jit(solution)/shard_map/gather_parameters/ppermute | solution.py:74
  15.5 2.4 %collective-permute-start.5 = (f32[256,256]{1,0:T(8,128)S(1)}, f32[256,256]{1,0:T(8,128)S(1)}, u32[]{:S(2)}, u32[]{:S(2)}) collective-permute-start(f32[256,256]{1,0:T(8,128)S(1)} %constant_dynamic-update-slice_fusion.refs_1_), channel_id=1, source_target_pairs={{0,1},{1,0},{2,3},{3,2},{4,5},{5,4},{6,7},{7,6},{8,9},{9,8},{10,11... | collective-permute-start | bytes 786440 | tf_op jit(solution)/shard_map/gather_parameters/ppermute | solution.py:74
  16.0 1.9 %collective-permute-start.6 = (f32[256,256]{1,0:T(8,128)S(1)}, f32[256,256]{1,0:T(8,128)S(1)}, u32[]{:S(2)}, u32[]{:S(2)}) collective-permute-start(f32[256,256]{1,0:T(8,128)S(1)} %constant_dynamic-update-slice_fusion.3.refs_3_), channel_id=1, source_target_pairs={{0,1},{1,0},{2,3},{3,2},{4,5},{5,4},{6,7},{7,6},{8,9},{9,8},{10,11... | collective-permute-start | bytes 786440 | tf_op jit(solution)/shard_map/gather_parameters/ppermute | solution.py:74
  16.1 6.0 %collective-permute-start.2 = (f32[256,256]{1,0:T(8,128)S(1)}, f32[256,256]{1,0:T(8,128)S(1)}, u32[]{:S(2)}, u32[]{:S(2)}) collective-permute-start(f32[256,256]{1,0:T(8,128)S(1)} %constant_dynamic-update-slice_fusion.refs_1_), channel_id=1, source_target_pairs={{0,3},{1,4},{2,7},{3,0},{4,1},{5,6},{6,5},{7,2},{8,13},{9,10},{10,... | collective-permute-start | bytes 786440 | tf_op jit(solution)/shard_map/gather_parameters/ppermute | solution.py:74
  17.9 6.9 %collective-permute-start.8 = (f32[256,256]{1,0:T(8,128)S(1)}, f32[256,256]{1,0:T(8,128)S(1)}, u32[]{:S(2)}, u32[]{:S(2)}) collective-permute-start(f32[256,256]{1,0:T(8,128)S(1)} %constant_dynamic-update-slice_fusion.3.refs_3_), channel_id=1, source_target_pairs={{0,3},{1,4},{2,7},{3,0},{4,1},{5,6},{6,5},{7,2},{8,13},{9,10},{10,... | collective-permute-start | bytes 786440 | tf_op jit(solution)/shard_map/gather_parameters/ppermute | solution.py:74
  24.8 2.9 %collective-permute-start.9 = (f32[256,256]{1,0:T(8,128)S(1)}, f32[256,256]{1,0:T(8,128)S(1)}, u32[]{:S(2)}, u32[]{:S(2)}) collective-permute-start(f32[256,256]{1,0:T(8,128)S(1)} %collective-permute-done.8.refs_2_), channel_id=1, source_target_pairs={{0,1},{1,0},{2,3},{3,2},{4,5},{5,4},{6,7},{7,6},{8,9},{9,8},{10,11... | collective-permute-start | bytes 786440 | tf_op jit(solution)/shard_map/gather_parameters/ppermute | solution.py:74
  25.2 2.5 %collective-permute-start.7 = (f32[256,256]{1,0:T(8,128)S(1)}, f32[256,256]{1,0:T(8,128)S(1)}, u32[]{:S(2)}, u32[]{:S(2)}) collective-permute-start(f32[256,256]{1,0:T(8,128)S(1)} %collective-permute-done.2.refs_1_), channel_id=1, source_target_pairs={{0,1},{1,0},{2,3},{3,2},{4,5},{5,4},{6,7},{7,6},{8,9},{9,8},{10,11... | collective-permute-start | bytes 786440 | tf_op jit(solution)/shard_map/gather_parameters/ppermute | solution.py:74
  32.6 1.9 %collective-permute-start.10 = (f32[1032,128]{1,0:T(8,128)S(1)}, f32[1032,128]{1,0:T(8,128)S(1)}, u32[]{:S(2)}, u32[]{:S(2)}) collective-permute-start(f32[1032,128]{1,0:T(8,128)S(1)} %get-tuple-element.53), channel_id=1, source_target_pairs={{0,1},{1,0},{2,3},{3,2},{4,5},{5,4},{6,7},{7,6},{8,9},{9,8},{10,11... | collective-permute-start | bytes 1585160 | tf_op jit(solution)/shard_map/scatter_moments/ppermute | solution.py:74
  33.0 4.3 %collective-permute-start.21 = (f32[1024,128]{1,0:T(8,128)S(1)}, f32[1024,128]{1,0:T(8,128)S(1)}, u32[]{:S(2)}, u32[]{:S(2)}) collective-permute-start(f32[1024,128]{1,0:T(8,128)S(1)} %get-tuple-element.57), channel_id=1, source_target_pairs={{0,1},{1,0},{2,3},{3,2},{4,5},{5,4},{6,7},{7,6},{8,9},{9,8},{10,11... | collective-permute-start | bytes 1572872 | tf_op jit(solution)/shard_map/scatter_moments/ppermute | solution.py:74
  34.7 5.9 %collective-permute-start.11 = (f32[520,128]{1,0:T(8,128)S(1)}, f32[520,128]{1,0:T(8,128)S(1)}, u32[]{:S(2)}, u32[]{:S(2)}) collective-permute-start(f32[520,128]{1,0:T(8,128)S(1)} %pad_maximum_fusion), channel_id=1, source_target_pairs={{0,5},{1,17},{2,18},{3,6},{4,20},{5,0},{6,3},{7,23},{8,24},{9,12},... | collective-permute-start | bytes 798728 | tf_op jit(solution)/shard_map/scatter_moments/ppermute | solution.py:74
  37.5 5.9 %collective-permute-start.22 = (f32[512,128]{1,0:T(8,128)S(1)}, f32[512,128]{1,0:T(8,128)S(1)}, u32[]{:S(2)}, u32[]{:S(2)}) collective-permute-start(f32[512,128]{1,0:T(8,128)S(1)} %slice.105), channel_id=1, source_target_pairs={{0,3},{1,17},{2,18},{3,0},{4,20},{5,6},{6,5},{7,23},{8,24},{9,10},... | collective-permute-start | bytes 786440 | tf_op jit(solution)/shard_map/scatter_moments/ppermute | solution.py:74
  40.7 4.8 %collective-permute-start.12 = (f32[264,128]{1,0:T(8,128)S(1)}, f32[264,128]{1,0:T(8,128)S(1)}, u32[]{:S(2)}, u32[]{:S(2)}) collective-permute-start(f32[264,128]{1,0:T(8,128)S(1)} %pad_maximum_fusion.3), channel_id=1, source_target_pairs={{0,3},{1,4},{2,7},{3,0},{4,1},{5,6},{6,5},{7,2},{8,13},{9,10},{10,... | collective-permute-start | bytes 405512 | tf_op jit(solution)/shard_map/scatter_moments/ppermute | solution.py:74
  43.4 5.0 %collective-permute-start.23 = (f32[256,128]{1,0:T(8,128)S(1)}, f32[256,128]{1,0:T(8,128)S(1)}, u32[]{:S(2)}, u32[]{:S(2)}) collective-permute-start(f32[256,128]{1,0:T(8,128)S(1)} %slice.107), channel_id=1, source_target_pairs={{0,16},{1,4},{2,7},{3,19},{4,1},{5,21},{6,22},{7,2},{8,13},{9,25},... | collective-permute-start | bytes 393224 | tf_op jit(solution)/shard_map/scatter_moments/ppermute | solution.py:74
  45.5 4.4 %collective-permute-start.13 = (f32[136,128]{1,0:T(8,128)S(1)}, f32[136,128]{1,0:T(8,128)S(1)}, u32[]{:S(2)}, u32[]{:S(2)}) collective-permute-start(f32[136,128]{1,0:T(8,128)S(1)} %pad_maximum_fusion.8), channel_id=1, source_target_pairs={{0,16},{1,2},{2,1},{3,19},{4,7},{5,21},{6,22},{7,4},{8,11},{9,25},... | collective-permute-start | bytes 208904 | tf_op jit(solution)/shard_map/scatter_moments/ppermute | solution.py:74
  48.4 4.0 %collective-permute-start.24 = (f32[128,128]{1,0:T(8,128)S(1)}, f32[128,128]{1,0:T(8,128)S(1)}, u32[]{:S(2)}, u32[]{:S(2)}) collective-permute-start(f32[128,128]{1,0:T(8,128)S(1)} %slice.109), channel_id=1, source_target_pairs={{0,5},{1,2},{2,1},{3,6},{4,7},{5,0},{6,3},{7,4},{8,11},{9,12},{10,... | collective-permute-start | bytes 196616 | tf_op jit(solution)/shard_map/scatter_moments/ppermute | solution.py:74
  50.0 5.3 %collective-permute-start.14 = (f32[136,128]{1,0:T(8,128)S(1)}, f32[136,128]{1,0:T(8,128)S(1)}, u32[]{:S(2)}, u32[]{:S(2)}) collective-permute-start(f32[136,128]{1,0:T(8,128)S(1)} %pad_maximum_fusion.9), channel_id=1, source_target_pairs={{0,9},{1,8},{2,11},{3,10},{4,13},{5,12},{6,15},{7,14},{8,1},{9,0},... | collective-permute-start | bytes 208904 | tf_op jit(solution)/shard_map/scatter_moments/ppermute | solution.py:74
  52.4 7.6 %collective-permute-start.25 = (f32[128,128]{1,0:T(8,128)S(1)}, f32[128,128]{1,0:T(8,128)S(1)}, u32[]{:S(2)}, u32[]{:S(2)}) collective-permute-start(f32[128,128]{1,0:T(8,128)S(1)} %slice_add_fusion.5), channel_id=1, source_target_pairs={{0,9},{1,8},{2,11},{3,10},{4,13},{5,12},{6,15},{7,14},{8,1},{9,0},... | collective-permute-start | bytes 196616 | tf_op jit(solution)/shard_map/scatter_moments/ppermute | solution.py:74
  55.3 5.2 %collective-permute-start.15 = (f32[128,128]{1,0:T(8,128)S(1)}, f32[128,128]{1,0:T(8,128)S(1)}, u32[]{:S(2)}, u32[]{:S(2)}) collective-permute-start(f32[128,128]{1,0:T(8,128)S(1)} %slice_add_fusion.6), channel_id=1, source_target_pairs={{0,16},{1,2},{2,1},{3,19},{4,7},{5,21},{6,22},{7,4},{8,11},{9,25},... | collective-permute-start | bytes 196616 | tf_op jit(solution)/shard_map/gather_moments/ppermute | solution.py:74
  60.0 3.8 %collective-permute-start.26 = (f32[128,128]{1,0:T(8,128)S(1)}, f32[128,128]{1,0:T(8,128)S(1)}, u32[]{:S(2)}, u32[]{:S(2)}) collective-permute-start(f32[128,128]{1,0:T(8,128)S(1)} %add.72), channel_id=1, source_target_pairs={{0,5},{1,2},{2,1},{3,6},{4,7},{5,0},{6,3},{7,4},{8,11},{9,12},{10,... | collective-permute-start | bytes 196616 | tf_op jit(solution)/shard_map/gather_moments/ppermute | solution.py:74
  60.5 5.0 %collective-permute-start.16 = (f32[256,128]{1,0:T(8,128)S(1)}, f32[256,128]{1,0:T(8,128)S(1)}, u32[]{:S(2)}, u32[]{:S(2)}) collective-permute-start(f32[256,128]{1,0:T(8,128)S(1)} %pad_maximum_fusion.6), channel_id=1, source_target_pairs={{0,3},{1,4},{2,7},{3,0},{4,1},{5,6},{6,5},{7,2},{8,13},{9,10},{10,... | collective-permute-start | bytes 393224 | tf_op jit(solution)/shard_map/gather_moments/ppermute | solution.py:74
  63.7 5.1 %collective-permute-start.27 = (f32[256,128]{1,0:T(8,128)S(1)}, f32[256,128]{1,0:T(8,128)S(1)}, u32[]{:S(2)}, u32[]{:S(2)}) collective-permute-start(f32[256,128]{1,0:T(8,128)S(1)} %pad_maximum_fusion.7), channel_id=1, source_target_pairs={{0,16},{1,4},{2,7},{3,19},{4,1},{5,21},{6,22},{7,2},{8,13},{9,25},... | collective-permute-start | bytes 393224 | tf_op jit(solution)/shard_map/gather_moments/ppermute | solution.py:74
  65.5 8.0 %collective-permute-start.18 = (f32[512,128]{1,0:T(8,128)S(1)}, f32[512,128]{1,0:T(8,128)S(1)}, u32[]{:S(2)}, u32[]{:S(2)}) collective-permute-start(f32[512,128]{1,0:T(8,128)S(1)} %pad_maximum_fusion.1.refs_0_), channel_id=1, source_target_pairs={{0,5},{1,17},{2,18},{3,6},{4,20},{5,0},{6,3},{7,23},{8,24},{9,12},... | collective-permute-start | bytes 786440 | tf_op jit(solution)/shard_map/gather_moments/ppermute | solution.py:74
  68.9 5.9 %collective-permute-start.29 = (f32[512,128]{1,0:T(8,128)S(1)}, f32[512,128]{1,0:T(8,128)S(1)}, u32[]{:S(2)}, u32[]{:S(2)}) collective-permute-start(f32[512,128]{1,0:T(8,128)S(1)} %pad_maximum_fusion.2.refs_2_), channel_id=1, source_target_pairs={{0,3},{1,17},{2,18},{3,0},{4,20},{5,6},{6,5},{7,23},{8,24},{9,10},... | collective-permute-start | bytes 786440 | tf_op jit(solution)/shard_map/gather_moments/ppermute | solution.py:74
  69.4 2.3 %collective-permute-start.19 = (f32[8,128]{1,0:T(8,128)S(1)}, f32[8,128]{1,0:T(8,128)S(1)}, u32[]{:S(2)}, u32[]{:S(2)}) collective-permute-start(f32[8,128]{1,0:T(8,128)S(1)} %slice_add_fusion.8), channel_id=1, source_target_pairs={{0,1},{1,0},{2,3},{3,2},{4,5},{5,4},{6,7},{7,6},{8,9},{9,8},{10,11... | collective-permute-start | bytes 12296 | tf_op jit(solution)/shard_map/scatter_moments/ppermute | solution.py:74
  73.0 4.3 %collective-permute-start.17 = (f32[512,128]{1,0:T(8,128)S(1)}, f32[512,128]{1,0:T(8,128)S(1)}, u32[]{:S(2)}, u32[]{:S(2)}) collective-permute-start(f32[512,128]{1,0:T(8,128)S(1)} %pad_maximum_fusion.1.refs_0_), channel_id=1, source_target_pairs={{0,1},{1,0},{2,3},{3,2},{4,5},{5,4},{6,7},{7,6},{8,9},{9,8},{10,11... | collective-permute-start | bytes 786440 | tf_op jit(solution)/shard_map/gather_moments/ppermute | solution.py:74
  73.3 4.0 %collective-permute-start.28 = (f32[512,128]{1,0:T(8,128)S(1)}, f32[512,128]{1,0:T(8,128)S(1)}, u32[]{:S(2)}, u32[]{:S(2)}) collective-permute-start(f32[512,128]{1,0:T(8,128)S(1)} %pad_maximum_fusion.2.refs_2_), channel_id=1, source_target_pairs={{0,1},{1,0},{2,3},{3,2},{4,5},{5,4},{6,7},{7,6},{8,9},{9,8},{10,11... | collective-permute-start | bytes 786440 | tf_op jit(solution)/shard_map/gather_moments/ppermute | solution.py:74
  74.8 2.5 %collective-permute-start.30 = (f32[512,128]{1,0:T(8,128)S(1)}, f32[512,128]{1,0:T(8,128)S(1)}, u32[]{:S(2)}, u32[]{:S(2)}) collective-permute-start(f32[512,128]{1,0:T(8,128)S(1)} %collective-permute-done.29.refs_3_), channel_id=1, source_target_pairs={{0,1},{1,0},{2,3},{3,2},{4,5},{5,4},{6,7},{7,6},{8,9},{9,8},{10,11... | collective-permute-start | bytes 786440 | tf_op jit(solution)/shard_map/gather_moments/ppermute | solution.py:74
  75.6 1.7 %collective-permute-start.20 = (f32[512,128]{1,0:T(8,128)S(1)}, f32[512,128]{1,0:T(8,128)S(1)}, u32[]{:S(2)}, u32[]{:S(2)}) collective-permute-start(f32[512,128]{1,0:T(8,128)S(1)} %collective-permute-done.18.refs_1_), channel_id=1, source_target_pairs={{0,1},{1,0},{2,3},{3,2},{4,5},{5,4},{6,7},{7,6},{8,9},{9,8},{10,11... | collective-permute-start | bytes 786440 | tf_op jit(solution)/shard_map/gather_moments/ppermute | solution.py:74
